TPU v7x, 32 devices: a whole 2x2x4 slice. The times are simulated.
32 devices in a mesh: gx: 4 (over y, core), gy: 2 (over x), layer: 4 (over z).
Axes of the slice: x: 2, y: 2, z: 4, core: 2. Of those that a mesh axis runs over, the one named last changes fastest.
Arguments:
- source: float32 [3, 32, 32, 512], P(None, 'layer', 'gy', 'gx'), may hold values from -6 to 6
- active_cells: int32 [32, 32, 512], P('layer', 'gy', 'gx'), may hold values 0 or 1
- diag_blocks: float32 [9, 32, 32, 512], P(None, 'layer', 'gy', 'gx'), may hold values from -0.45 to 3, as said below
- frozen_inverses: float32 [9, 32, 32, 512], P(None, 'layer', 'gy', 'gx'), may hold values from -0.05 to 0.2, as said below
- transmissibility: float32 [3, 32, 32, 512], P(None, 'layer', 'gy', 'gx'), may hold values from 0.1 to 1
- pressure_weights: float32 [3, 32, 32, 512], P(None, 'layer', 'gy', 'gx'), may hold values from 1 to 4
- stencil_fine: float32 [7, 32, 32, 512], P(None, 'layer', 'gy', 'gx'), may hold values from -1 to 9, as said below
- coarse_one: float32 [7, 16, 16, 256], P(None, 'layer', 'gy', 'gx'), may hold values from -1 to 9, as said below
- coarse_two: float32 [7, 8, 8, 128], P(None, 'layer', 'gy', 'gx'), may hold values from -1 to 9, as said below
- coarse_three: float32 [7, 4, 4, 64], P(None, 'layer', 'gy', 'gx'), may hold values from -1 to 9, as said below
- pressure_state: float32 [32, 32, 512], P('layer', 'gy', 'gx'), may hold values from -6 to 6
- mobilities: float32 [3, 32, 32, 512], P(None, 'layer', 'gy', 'gx'), may hold values from 0.1 to 1
Outputs:
- adjoint: float32 [3, 32, 32, 512], P(None, 'layer', 'gy', 'gx')
- perm_grad: float32 [3, 32, 32, 512], P(None, 'layer', 'gy', 'gx')
Inputs may be any that keep to these rules, and one draw needn't show every extreme that they name: `diag_blocks`: entries 0, 4 and 8 are the blocks' diagonals. `frozen_inverses`: entries 0, 4 and 8 are the blocks' diagonals. `stencil_fine`: coefficient 0 exceeds the sum of the magnitudes of the other six. `coarse_one`: coefficient 0 exceeds the sum of the magnitudes of the other six. `coarse_two`: coefficient 0 exceeds the sum of the magnitudes of the other six. `coarse_three`: coefficient 0 exceeds the sum of the magnitudes of the other six.
All inputs are finite; a program needn't handle non-finite values. No bound on the sum of `active_cells` on one device may be relied on, other than what follows from the above.
Results may differ from a plain program's by a relative error of at most 0.00002.
Values sent between devices are 32-bit elements; how exact they have to be, the bound alone decides.
No kernel may reach another device: no remote copies, remote signals or barrier semaphores. Data moves between devices by JAX's collectives and lax.ppermute only.
A program may use at most 64 MiB of HBM per device.

v0:
```python
import jax
import jax.numpy as jnp
from jax import lax
from jax.sharding import PartitionSpec as P

SWEEPS = 3
LEVELS = 3
COARSE_SWEEPS = 4


OMEGA = 0.8


def padded_2(shard, sides, width):
    for axis, dim in sides:
        peers, length = (lax.axis_size(axis), shard.shape[dim])
        up = [(i, (i + 1) % peers) for i in range(peers - 1)]
        down = [(j, i) for i, j in up]
        last = lax.slice_in_dim(shard, length - width, length, axis=dim)
        first = lax.slice_in_dim(shard, 0, width, axis=dim)
        before = lax.ppermute(last, axis, up)
        after = lax.ppermute(first, axis, down)
        shard = jnp.concatenate([before, shard, after], axis=dim)
    return shard


def shifted(block, axis, distance):
    devices = range(lax.axis_size(axis))
    route = [(i - distance, i) for i in devices if i - distance in devices]
    return lax.ppermute(block, axis, route)


def leading(field):
    return (slice(None),) * (field.ndim - 3)


def interior(padded):
    return padded[leading(padded) + (slice(1, -1), slice(1, -1), slice(1, -1))]


def neighbour(padded, direction, lower):
    window = [slice(1, -1), slice(1, -1), slice(1, -1)]
    window[direction] = slice(0, -2) if lower else slice(2, None)
    return padded[leading(padded) + tuple(window)]


def face_slab(field, direction, start, stop):
    window = [slice(None), slice(None), slice(None)]
    window[direction] = slice(start, stop)
    return field[tuple(window)]


def pad_along(field, direction, before, after):
    widths = [(1, 1), (1, 1), (1, 1)]
    widths[direction] = (before, after)
    return jnp.pad(field, widths)


def stencil_used(off):
    faces = [
        jnp.concatenate(
            [
                face_slab(off[2 * direction], direction, 0, 1),
                face_slab(off[2 * direction + 1], direction, -1, None),
            ],
            axis=direction,
        )
        for direction in range(3)
    ]
    wide_layer = padded_2(faces[0], (("layer", 0),), 1)
    wide_y = padded_2(faces[1], (("gy", 1),), 1)
    wide_x = padded_2(faces[2], (("gx", 2),), 1)
    padded = [None] * 6
    for direction, wide in enumerate((wide_layer, wide_y, wide_x)):
        lower_rim = face_slab(wide, direction, 0, 1)
        upper_rim = face_slab(wide, direction, 3, 4)
        padded[2 * direction + 1] = pad_along(
            jnp.concatenate([lower_rim, off[2 * direction + 1]], axis=direction), direction, 0, 1
        )
        padded[2 * direction] = pad_along(
            jnp.concatenate([off[2 * direction], upper_rim], axis=direction), direction, 1, 0
        )
    return jnp.stack(padded)


def trans_used(transmissibility):
    lower_layer = shifted(face_slab(transmissibility[0], 0, -1, None), "layer", 1)
    lower_y = shifted(face_slab(transmissibility[1], 1, -1, None), "gy", 1)
    lower_x = shifted(face_slab(transmissibility[2], 2, -1, None), "gx", 1)
    padded = []
    for direction, lower_rim in enumerate((lower_layer, lower_y, lower_x)):
        padded.append(
            pad_along(
                jnp.concatenate([lower_rim, transmissibility[direction]], axis=direction),
                direction,
                0,
                1,
            )
        )
    return jnp.stack(padded)


def system_row(channel, values, padded_channel, trans_pad, blocks):
    total = (
        blocks[channel] * values[0]
        + blocks[3 + channel] * values[1]
        + blocks[6 + channel] * values[2]
    )
    center = interior(padded_channel)
    for direction in range(3):
        here = interior(trans_pad[direction])
        before = neighbour(trans_pad[direction], direction, True)
        total = total + here * (center - neighbour(padded_channel, direction, False))
        total = total + before * (center - neighbour(padded_channel, direction, True))
    return total


def system_apply(values, padded_values, trans_pad, blocks):
    return jnp.stack(
        [
            system_row(channel, values, padded_values[channel], trans_pad, blocks)
            for channel in range(3)
        ]
    )


def frozen_apply(inverses, residual):
    return jnp.stack(
        [
            inverses[channel] * residual[0]
            + inverses[3 + channel] * residual[1]
            + inverses[6 + channel] * residual[2]
            for channel in range(3)
        ]
    )


def stencil_apply(field, padded_field, center, off_pad):
    total = center * field
    for direction in range(3):
        upper_coef = off_pad[2 * direction + 1]
        lower_coef = off_pad[2 * direction]
        total = total + neighbour(upper_coef, direction, True) * neighbour(
            padded_field, direction, True
        )
        total = total + neighbour(lower_coef, direction, False) * neighbour(
            padded_field, direction, False
        )
    return total


def restrict(field):
    depth, height, width = field.shape
    return field.reshape(depth // 2, 2, height // 2, 2, width // 2, 2).sum(axis=(1, 3, 5))


def prolong(field):
    return jnp.repeat(jnp.repeat(jnp.repeat(field, 2, 0), 2, 1), 2, 2)


def coarsest_solve(rhs, stencil):
    center = stencil[0]
    off_pad = padded_2(stencil[1:], (("gx", 3), ("gy", 2), ("layer", 1)), 1)
    field = OMEGA * rhs / center
    for sweep in range(COARSE_SWEEPS - 1):
        padded_field = padded_2(field, (("gx", 2), ("gy", 1), ("layer", 0)), 1)
        field = field + OMEGA * (rhs - stencil_apply(field, padded_field, center, off_pad)) / center
    return field


def level_apply(field, center, off_pad):
    padded_field = padded_2(field, (("gx", 2), ("gy", 1), ("layer", 0)), 1)
    return stencil_apply(field, padded_field, center, off_pad)


def vcycle(rhs, stencils, off_pads, level):
    if level == LEVELS:
        return coarsest_solve(rhs, stencils[level])
    center = stencils[level][0]
    off_pad = off_pads[level]
    field = OMEGA * rhs / center
    residual = rhs - level_apply(field, center, off_pad)
    field = field + prolong(vcycle(restrict(residual), stencils, off_pads, level + 1))
    field = field + OMEGA * (rhs - level_apply(field, center, off_pad)) / center
    return field


def face_term(coef, lam_a, lam_b, mob_a, mob_b, pres_a, pres_b):
    total = (lam_a[0] - lam_b[0]) * (0.5 * (mob_a[0] + mob_b[0]))
    for channel in (1, 2):
        total = total + (lam_a[channel] - lam_b[channel]) * (
            0.5 * (mob_a[channel] + mob_b[channel])
        )
    return coef * total * (pres_a - pres_b)


def local(
    source,
    active_cells,
    diag_blocks,
    frozen_inverses,
    transmissibility,
    pressure_weights,
    stencil_fine,
    coarse_one,
    coarse_two,
    coarse_three,
    pressure_state,
    mobilities,
):
    mask = active_cells.astype(jnp.float32)
    rhs = source * mask
    trans_pad = trans_used(transmissibility)
    iterate = frozen_apply(frozen_inverses, rhs)
    for sweep in range(SWEEPS - 1):
        padded_iterate = padded_2(iterate, (("gx", 3), ("gy", 2), ("layer", 1)), 1)
        iterate = iterate + frozen_apply(
            frozen_inverses, rhs - system_apply(iterate, padded_iterate, trans_pad, diag_blocks)
        )
    first_pad = padded_2(iterate[0], (("gx", 2), ("gy", 1), ("layer", 0)), 1)
    row = system_row(0, iterate, first_pad, trans_pad, diag_blocks)
    pressure_rhs = rhs[0] - row
    stencils = (stencil_fine, coarse_one, coarse_two, coarse_three)
    off_pads = [stencil_used(stencils[level][1:]) for level in range(LEVELS)]
    correction = vcycle(pressure_rhs, stencils, off_pads, 0)
    adjoint = mask * (iterate + pressure_weights * correction[None])
    states = jnp.concatenate([adjoint, mobilities, pressure_state[None]])
    states_pad = padded_2(states, (("gx", 3), ("gy", 2), ("layer", 1)), 1)
    gradients = []
    for direction in range(3):
        above = neighbour(states_pad, direction, False)
        below = neighbour(states_pad, direction, True)
        here_term = face_term(
            transmissibility[direction],
            adjoint,
            above[0:3],
            mobilities,
            above[3:6],
            pressure_state,
            above[6],
        )
        below_term = face_term(
            neighbour(trans_pad[direction], direction, True),
            below[0:3],
            adjoint,
            below[3:6],
            mobilities,
            below[6],
            pressure_state,
        )
        gradients.append(0.5 * (here_term + below_term))
    return (adjoint, jnp.stack(gradients))


def solution(mesh):
    return jax.shard_map(
        local,
        mesh=mesh,
        in_specs=(
            P(None, "layer", "gy", "gx"),
            P("layer", "gy", "gx"),
            P(None, "layer", "gy", "gx"),
            P(None, "layer", "gy", "gx"),
            P(None, "layer", "gy", "gx"),
            P(None, "layer", "gy", "gx"),
            P(None, "layer", "gy", "gx"),
            P(None, "layer", "gy", "gx"),
            P(None, "layer", "gy", "gx"),
            P(None, "layer", "gy", "gx"),
            P("layer", "gy", "gx"),
            P(None, "layer", "gy", "gx"),
        ),
        out_specs=(P(None, "layer", "gy", "gx"), P(None, "layer", "gy", "gx")),
        check_vma=False,
    )
```

profile of v0, /device:TPU:12, one launch (start us, length us, event | category | flops | bytes accessed | tf_op | source)
XLA Modules:
  0.0 380.7 jit_solution(1820371623237344844)
XLA Ops:
  21.6 4.2 %collective-permute-done.3 = f32[3,8,1,130]{3,1,2,0:T(8,128)S(1)} collective-permute-done((f32[3,8,1,130]{3,1,2,0:T(8,128)S(1)}, f32[3,8,1,130]{3,1,2,0:T(8,128)S(1)}, u32[]{:S(2)}, u32[]{:S(2)}) %collective-permute-start.3) | collective-permute-done | bytes 12512 | tf_op jit(solution)/shard_map/ppermute | solution.py:22
  55.6 4.2 %collective-permute-done.12 = f32[3,8,1,130]{3,1,2,0:T(8,128)S(1)} collective-permute-done((f32[3,8,1,130]{3,1,2,0:T(8,128)S(1)}, f32[3,8,1,130]{3,1,2,0:T(8,128)S(1)}, u32[]{:S(2)}, u32[]{:S(2)}) %collective-permute-start.12) | collective-permute-done | bytes 12512 | tf_op jit(solution)/shard_map/ppermute | solution.py:22
  85.4 4.1 %collective-permute-done.18 = f32[8,1,130]{2,0,1:T(8,128)S(1)} collective-permute-done((f32[8,1,130]{2,0,1:T(8,128)S(1)}, f32[8,1,130]{2,0,1:T(8,128)S(1)}, u32[]{:S(2)}, u32[]{:S(2)}) %collective-permute-start.18) | collective-permute-done | bytes 4192 | tf_op jit(solution)/shard_map/ppermute | solution.py:22
  107.3 4.4 %collective-permute-start.24 = (f32[8,1,130]{2,0,1:T(8,128)S(1)}, f32[8,1,130]{2,0,1:T(8,128)S(1)}, u32[]{:S(2)}, u32[]{:S(2)}) collective-permute-start(f32[8,1,130]{2,0,1:T(8,128)S(1)} %copy.767), channel_id=1, source_target_pairs={{0,4},{1,5},{2,6},{3,7},{8,12},{9,13},{10,14},{11,15},{16,20},{17,... | collective-permute-start | bytes 12488 | tf_op jit(solution)/shard_map/ppermute | solution.py:21
  119.3 3.9 %collective-permute-start.26 = (f32[1,18,130]{2,1,0:T(8,128)S(1)}, f32[1,18,130]{2,1,0:T(8,128)S(1)}, u32[]{:S(2)}, u32[]{:S(2)}) collective-permute-start(f32[1,18,130]{2,1,0:T(8,128)S(1)} %get-tuple-element.59), channel_id=1, source_target_pairs={{0,1},{1,2},{2,3},{4,5},{5,6},{6,7},{8,9},{9,10},{10,11},{12,13},{... | collective-permute-start | bytes 28088 | tf_op jit(solution)/shard_map/ppermute | solution.py:21
  126.5 4.5 %collective-permute-start.41 = (f32[4,1,64]{2,0,1:T(4,128)S(1)}, f32[4,1,64]{2,0,1:T(4,128)S(1)}, u32[]{:S(2)}, u32[]{:S(2)}) collective-permute-start(f32[4,1,64]{2,0,1:T(4,128)S(1)} %slice.1867), channel_id=1, source_target_pairs={{0,4},{1,5},{2,6},{3,7},{8,12},{9,13},{10,14},{11,15},{16,20},{17,... | collective-permute-start | bytes 3080 | tf_op jit(solution)/shard_map/ppermute | solution.py:21
  133.3 5.6 %reshape.187 = f32[4,2,8,2,64,2]{5,4,3,2,1,0:T(8,128)} reshape(f32[8,16,128]{2,1,0:T(8,128)S(1)} %fusion.103) | data formatting | bytes 131072 | tf_op jit(solution)/shard_map/reshape | solution.py:154
  152.3 3.9 %collective-permute-start.33 = (f32[1,8,64]{2,1,0:T(8,128)S(1)}, f32[1,8,64]{2,1,0:T(8,128)S(1)}, u32[]{:S(2)}, u32[]{:S(2)}) collective-permute-start(f32[1,8,64]{2,1,0:T(8,128)S(1)} %get-tuple-element.83), channel_id=1, source_target_pairs={{0,1},{1,2},{2,3},{4,5},{5,6},{6,7},{8,9},{9,10},{10,11},{12,13},{... | collective-permute-start | bytes 6152 | tf_op jit(solution)/shard_map/ppermute | solution.py:21
  169.9 4.3 %collective-permute-start.53 = (f32[2,1,32]{2,1,0:T(1,128)S(1)}, f32[2,1,32]{2,1,0:T(1,128)S(1)}, u32[]{:S(2)}, u32[]{:S(2)}) collective-permute-start(f32[2,1,32]{2,1,0:T(1,128)S(1)} %slice.1875), channel_id=1, source_target_pairs={{0,4},{1,5},{2,6},{3,7},{8,12},{9,13},{10,14},{11,15},{16,20},{17,... | collective-permute-start | bytes 776 | tf_op jit(solution)/shard_map/ppermute | solution.py:21
  174.3 3.9 %collective-permute-start.61 = (f32[6,1,4,18]{3,2,1,0:T(4,128)S(1)}, f32[6,1,4,18]{3,2,1,0:T(4,128)S(1)}, u32[]{:S(2)}, u32[]{:S(2)}) collective-permute-start(f32[6,1,4,18]{3,2,1,0:T(4,128)S(1)} %pad_maximum_fusion.175), channel_id=1, source_target_pairs={{0,1},{1,2},{2,3},{4,5},{5,6},{6,7},{8,9},{9,10},{10,11},{12,13},{... | collective-permute-start | bytes 5192 | tf_op jit(solution)/shard_map/ppermute | solution.py:21
  223.7 4.1 %collective-permute-done.66 = f32[1,1,18]{2,1,0:T(1,128)S(1)} collective-permute-done((f32[1,1,18]{2,1,0:T(1,128)S(1)}, f32[1,1,18]{2,1,0:T(1,128)S(1)}, u32[]{:S(2)}, u32[]{:S(2)}) %collective-permute-start.66) | collective-permute-done | bytes 104 | tf_op jit(solution)/shard_map/ppermute | solution.py:22
  229.8 3.9 %collective-permute-start.68 = (f32[1,4,18]{2,1,0:T(4,128)S(1)}, f32[1,4,18]{2,1,0:T(4,128)S(1)}, u32[]{:S(2)}, u32[]{:S(2)}) collective-permute-start(f32[1,4,18]{2,1,0:T(4,128)S(1)} %pad_maximum_fusion.246), channel_id=1, source_target_pairs={{1,0},{2,1},{3,2},{5,4},{6,5},{7,6},{9,8},{10,9},{11,10},{13,12},{... | collective-permute-start | bytes 872 | tf_op jit(solution)/shard_map/ppermute | solution.py:22
  245.4 4.1 %collective-permute-done.72 = f32[1,1,18]{2,1,0:T(1,128)S(1)} collective-permute-done((f32[1,1,18]{2,1,0:T(1,128)S(1)}, f32[1,1,18]{2,1,0:T(1,128)S(1)}, u32[]{:S(2)}, u32[]{:S(2)}) %collective-permute-start.72) | collective-permute-done | bytes 104 | tf_op jit(solution)/shard_map/ppermute | solution.py:22
  251.6 3.9 %collective-permute-start.74 = (f32[1,4,18]{2,1,0:T(4,128)S(1)}, f32[1,4,18]{2,1,0:T(4,128)S(1)}, u32[]{:S(2)}, u32[]{:S(2)}) collective-permute-start(f32[1,4,18]{2,1,0:T(4,128)S(1)} %pad_maximum_fusion.248), channel_id=1, source_target_pairs={{1,0},{2,1},{3,2},{5,4},{6,5},{7,6},{9,8},{10,9},{11,10},{13,12},{... | collective-permute-start | bytes 872 | tf_op jit(solution)/shard_map/ppermute | solution.py:22
  267.3 4.1 %collective-permute-done.78 = f32[1,1,18]{2,1,0:T(1,128)S(1)} collective-permute-done((f32[1,1,18]{2,1,0:T(1,128)S(1)}, f32[1,1,18]{2,1,0:T(1,128)S(1)}, u32[]{:S(2)}, u32[]{:S(2)}) %collective-permute-start.78) | collective-permute-done | bytes 104 | tf_op jit(solution)/shard_map/ppermute | solution.py:22
  273.3 3.9 %collective-permute-start.80 = (f32[1,4,18]{2,1,0:T(4,128)S(1)}, f32[1,4,18]{2,1,0:T(4,128)S(1)}, u32[]{:S(2)}, u32[]{:S(2)}) collective-permute-start(f32[1,4,18]{2,1,0:T(4,128)S(1)} %pad_maximum_fusion.250), channel_id=1, source_target_pairs={{1,0},{2,1},{3,2},{5,4},{6,5},{7,6},{9,8},{10,9},{11,10},{13,12},{... | collective-permute-start | bytes 872 | tf_op jit(solution)/shard_map/ppermute | solution.py:22
  289.1 4.2 %collective-permute-done.84 = f32[2,1,34]{2,1,0:T(1,128)S(1)} collective-permute-done((f32[2,1,34]{2,1,0:T(1,128)S(1)}, f32[2,1,34]{2,1,0:T(1,128)S(1)}, u32[]{:S(2)}, u32[]{:S(2)}) %collective-permute-start.84) | collective-permute-done | bytes 304 | tf_op jit(solution)/shard_map/ppermute | solution.py:22
  295.3 3.9 %collective-permute-start.86 = (f32[1,6,34]{2,1,0:T(8,128)S(1)}, f32[1,6,34]{2,1,0:T(8,128)S(1)}, u32[]{:S(2)}, u32[]{:S(2)}) collective-permute-start(f32[1,6,34]{2,1,0:T(8,128)S(1)} %get-tuple-element.121), channel_id=1, source_target_pairs={{1,0},{2,1},{3,2},{5,4},{6,5},{7,6},{9,8},{10,9},{11,10},{13,12},{... | collective-permute-start | bytes 2456 | tf_op jit(solution)/shard_map/ppermute | solution.py:22
  311.3 4.2 %collective-permute-done.90 = f32[4,1,66]{2,1,0:T(1,128)S(1)} collective-permute-done((f32[4,1,66]{2,1,0:T(1,128)S(1)}, f32[4,1,66]{2,1,0:T(1,128)S(1)}, u32[]{:S(2)}, u32[]{:S(2)}) %collective-permute-start.90) | collective-permute-done | bytes 1088 | tf_op jit(solution)/shard_map/ppermute | solution.py:22
  334.5 4.2 %collective-permute-done.96 = f32[8,1,130]{2,0,1:T(8,128)S(1)} collective-permute-done((f32[8,1,130]{2,0,1:T(8,128)S(1)}, f32[8,1,130]{2,0,1:T(8,128)S(1)}, u32[]{:S(2)}, u32[]{:S(2)}) %collective-permute-start.96) | collective-permute-done | bytes 4192 | tf_op jit(solution)/shard_map/ppermute | solution.py:22
  340.7 3.9 %collective-permute-start.98 = (f32[1,18,130]{2,1,0:T(8,128)S(1)}, f32[1,18,130]{2,1,0:T(8,128)S(1)}, u32[]{:S(2)}, u32[]{:S(2)}) collective-permute-start(f32[1,18,130]{2,1,0:T(8,128)S(1)} %get-tuple-element.58), channel_id=1, source_target_pairs={{1,0},{2,1},{3,2},{5,4},{6,5},{7,6},{9,8},{10,9},{11,10},{13,12},{... | collective-permute-start | bytes 28088 | tf_op jit(solution)/shard_map/ppermute | solution.py:22
  362.7 4.2 %collective-permute-done.102 = f32[7,8,1,130]{3,1,2,0:T(8,128)S(1)} collective-permute-done((f32[7,8,1,130]{3,1,2,0:T(8,128)S(1)}, f32[7,8,1,130]{3,1,2,0:T(8,128)S(1)}, u32[]{:S(2)}, u32[]{:S(2)}) %collective-permute-start.102) | collective-permute-done | bytes 29152 | tf_op jit(solution)/shard_map/ppermute | solution.py:22
  367.2 3.9 %collective-permute-start.103 = (f32[7,1,18,130]{3,2,1,0:T(8,128)S(1)}, f32[7,1,18,130]{3,2,1,0:T(8,128)S(1)}, u32[]{:S(2)}, u32[]{:S(2)}) collective-permute-start(f32[7,1,18,130]{3,2,1,0:T(8,128)S(1)} %get-tuple-element.20), channel_id=1, source_target_pairs={{1,0},{2,1},{3,2},{5,4},{6,5},{7,6},{9,8},{10,9},{11,10},{13,12},{... | collective-permute-start | bytes 196568 | tf_op jit(solution)/shard_map/ppermute | solution.py:22
  374.5 3.9 %collective-permute-done.104 = f32[7,1,18,130]{3,2,1,0:T(8,128)S(1)} collective-permute-done((f32[7,1,18,130]{3,2,1,0:T(8,128)S(1)}, f32[7,1,18,130]{3,2,1,0:T(8,128)S(1)}, u32[]{:S(2)}, u32[]{:S(2)}) %collective-permute-start.104) | collective-permute-done | bytes 65552 | tf_op jit(solution)/shard_map/ppermute | solution.py:21
  (384 shorter events, 278.5 us)
Async XLA Ops:
  3.9 14.6 %collective-permute-start = (f32[3,8,16,1]{3,2,1,0:T(8,128)S(1)}, f32[3,8,16,1]{3,2,1,0:T(8,128)S(1)}, u32[]{:S(2)}, u32[]{:S(2)}) collective-permute-start(f32[3,8,16,1]{3,2,1,0:T(8,128)S(1)} %get-tuple-element.74), channel_id=1, source_target_pairs={{0,8},{8,16},{16,24},{1,9},{9,17},{17,25},{2,10},{10,18},{18,26},{... | collective-permute-start | bytes 4616 | tf_op jit(solution)/shard_map/ppermute | solution.py:21
  9.6 29.0 %collective-permute-start.8 = (f32[8,16,1]{2,1,0:T(8,128)S(1)}, f32[8,16,1]{2,1,0:T(8,128)S(1)}, u32[]{:S(2)}, u32[]{:S(2)}) collective-permute-start(f32[8,16,1]{2,1,0:T(8,128)S(1)} %slice.1801), channel_id=1, source_target_pairs={{0,8},{8,16},{16,24},{1,9},{9,17},{17,25},{2,10},{10,18},{18,26},{... | collective-permute-start | bytes 1544 | tf_op jit(solution)/shard_map/ppermute | solution.py:30
  11.5 29.0 %collective-permute-start.7 = (f32[8,1,128]{2,1,0:T(1,128)S(1)}, f32[8,1,128]{2,1,0:T(1,128)S(1)}, u32[]{:S(2)}, u32[]{:S(2)}) collective-permute-start(f32[8,1,128]{2,1,0:T(1,128)S(1)} %slice.1798), channel_id=1, source_target_pairs={{0,4},{1,5},{2,6},{3,7},{8,12},{9,13},{10,14},{11,15},{16,20},{17,... | collective-permute-start | bytes 12296 | tf_op jit(solution)/shard_map/ppermute | solution.py:30
  14.9 25.6 %collective-permute-start.6 = (f32[1,16,128]{2,1,0:T(8,128)S(1)}, f32[1,16,128]{2,1,0:T(8,128)S(1)}, u32[]{:S(2)}, u32[]{:S(2)}) collective-permute-start(f32[1,16,128]{2,1,0:T(8,128)S(1)} %slice_bitcast_fusion.27), channel_id=1, source_target_pairs={{0,1},{1,2},{2,3},{4,5},{5,6},{6,7},{8,9},{9,10},{10,11},{12,13},{... | collective-permute-start | bytes 24584 | tf_op jit(solution)/shard_map/ppermute | solution.py:30
  32.2 79.5 %collective-permute-start.30 = (f32[8,1,128]{2,0,1:T(8,128)S(1)}, f32[8,1,128]{2,0,1:T(8,128)S(1)}, u32[]{:S(2)}, u32[]{:S(2)}) collective-permute-start(f32[8,1,128]{2,0,1:T(8,128)S(1)} %slice.1862), channel_id=1, source_target_pairs={{4,0},{5,1},{6,2},{7,3},{12,8},{13,9},{14,10},{15,11},{20,16},{21,... | collective-permute-start | bytes 12296 | tf_op jit(solution)/shard_map/ppermute | solution.py:22
  35.7 87.6 %collective-permute-start.29 = (f32[8,1,128]{2,0,1:T(8,128)S(1)}, f32[8,1,128]{2,0,1:T(8,128)S(1)}, u32[]{:S(2)}, u32[]{:S(2)}) collective-permute-start(f32[8,1,128]{2,0,1:T(8,128)S(1)} %slice.1861), channel_id=1, source_target_pairs={{0,4},{1,5},{2,6},{3,7},{8,12},{9,13},{10,14},{11,15},{16,20},{17,... | collective-permute-start | bytes 12296 | tf_op jit(solution)/shard_map/ppermute | solution.py:21
  38.5 80.8 %collective-permute-start.31 = (f32[8,16,1]{2,1,0:T(8,128)S(1)}, f32[8,16,1]{2,1,0:T(8,128)S(1)}, u32[]{:S(2)}, u32[]{:S(2)}) collective-permute-start(f32[8,16,1]{2,1,0:T(8,128)S(1)} %slice.1863), channel_id=1, source_target_pairs={{0,8},{8,16},{16,24},{1,9},{9,17},{17,25},{2,10},{10,18},{18,26},{... | collective-permute-start | bytes 1544 | tf_op jit(solution)/shard_map/ppermute | solution.py:21
  105.3 19.9 %collective-permute-start.32 = (f32[8,16,1]{2,1,0:T(8,128)S(1)}, f32[8,16,1]{2,1,0:T(8,128)S(1)}, u32[]{:S(2)}, u32[]{:S(2)}) collective-permute-start(f32[8,16,1]{2,1,0:T(8,128)S(1)} %bitcast.519), channel_id=1, source_target_pairs={{8,0},{16,8},{24,16},{9,1},{17,9},{25,17},{10,2},{18,10},{26,18},{... | collective-permute-start | bytes 1544 | tf_op jit(solution)/shard_map/ppermute | solution.py:22
  113.1 13.5 %collective-permute-start.21 = (f32[1,16,128]{2,1,0:T(8,128)S(1)}, f32[1,16,128]{2,1,0:T(8,128)S(1)}, u32[]{:S(2)}, u32[]{:S(2)}) collective-permute-start(f32[1,16,128]{2,1,0:T(8,128)S(1)} %get-tuple-element.56), channel_id=1, source_target_pairs={{0,1},{1,2},{2,3},{4,5},{5,6},{6,7},{8,9},{9,10},{10,11},{12,13},{... | collective-permute-start | bytes 24584 | tf_op jit(solution)/shard_map/ppermute | solution.py:21
  117.3 13.8 %collective-permute-start.27 = (f32[1,16,128]{2,1,0:T(8,128)S(1)}, f32[1,16,128]{2,1,0:T(8,128)S(1)}, u32[]{:S(2)}, u32[]{:S(2)}) collective-permute-start(f32[1,16,128]{2,1,0:T(8,128)S(1)} %get-tuple-element.55), channel_id=1, source_target_pairs={{1,0},{2,1},{3,2},{5,4},{6,5},{7,6},{9,8},{10,9},{11,10},{13,12},{... | collective-permute-start | bytes 24584 | tf_op jit(solution)/shard_map/ppermute | solution.py:22
  119.3 13.7 %collective-permute-start.26 = (f32[1,18,130]{2,1,0:T(8,128)S(1)}, f32[1,18,130]{2,1,0:T(8,128)S(1)}, u32[]{:S(2)}, u32[]{:S(2)}) collective-permute-start(f32[1,18,130]{2,1,0:T(8,128)S(1)} %get-tuple-element.59), channel_id=1, source_target_pairs={{0,1},{1,2},{2,3},{4,5},{5,6},{6,7},{8,9},{9,10},{10,11},{12,13},{... | collective-permute-start | bytes 28088 | tf_op jit(solution)/shard_map/ppermute | solution.py:21
  125.2 25.7 %collective-permute-start.42 = (f32[4,1,64]{2,0,1:T(4,128)S(1)}, f32[4,1,64]{2,0,1:T(4,128)S(1)}, u32[]{:S(2)}, u32[]{:S(2)}) collective-permute-start(f32[4,1,64]{2,0,1:T(4,128)S(1)} %slice.1868), channel_id=1, source_target_pairs={{4,0},{5,1},{6,2},{7,3},{12,8},{13,9},{14,10},{15,11},{20,16},{21,... | collective-permute-start | bytes 3080 | tf_op jit(solution)/shard_map/ppermute | solution.py:22
  126.5 35.8 %collective-permute-start.41 = (f32[4,1,64]{2,0,1:T(4,128)S(1)}, f32[4,1,64]{2,0,1:T(4,128)S(1)}, u32[]{:S(2)}, u32[]{:S(2)}) collective-permute-start(f32[4,1,64]{2,0,1:T(4,128)S(1)} %slice.1867), channel_id=1, source_target_pairs={{0,4},{1,5},{2,6},{3,7},{8,12},{9,13},{10,14},{11,15},{16,20},{17,... | collective-permute-start | bytes 3080 | tf_op jit(solution)/shard_map/ppermute | solution.py:21
  131.1 27.3 %collective-permute-start.43 = (f32[4,8,1]{2,1,0:T(8,128)S(1)}, f32[4,8,1]{2,1,0:T(8,128)S(1)}, u32[]{:S(2)}, u32[]{:S(2)}) collective-permute-start(f32[4,8,1]{2,1,0:T(8,128)S(1)} %slice.1869), channel_id=1, source_target_pairs={{0,8},{8,16},{16,24},{1,9},{9,17},{17,25},{2,10},{10,18},{18,26},{... | collective-permute-start | bytes 392 | tf_op jit(solution)/shard_map/ppermute | solution.py:21
  147.1 17.2 %collective-permute-start.44 = (f32[4,8,1]{2,1,0:T(8,128)S(1)}, f32[4,8,1]{2,1,0:T(8,128)S(1)}, u32[]{:S(2)}, u32[]{:S(2)}) collective-permute-start(f32[4,8,1]{2,1,0:T(8,128)S(1)} %bitcast.527), channel_id=1, source_target_pairs={{8,0},{16,8},{24,16},{9,1},{17,9},{25,17},{10,2},{18,10},{26,18},{... | collective-permute-start | bytes 392 | tf_op jit(solution)/shard_map/ppermute | solution.py:22
  152.3 14.0 %collective-permute-start.33 = (f32[1,8,64]{2,1,0:T(8,128)S(1)}, f32[1,8,64]{2,1,0:T(8,128)S(1)}, u32[]{:S(2)}, u32[]{:S(2)}) collective-permute-start(f32[1,8,64]{2,1,0:T(8,128)S(1)} %get-tuple-element.83), channel_id=1, source_target_pairs={{0,1},{1,2},{2,3},{4,5},{5,6},{6,7},{8,9},{9,10},{10,11},{12,13},{... | collective-permute-start | bytes 6152 | tf_op jit(solution)/shard_map/ppermute | solution.py:21
  156.4 13.5 %collective-permute-start.39 = (f32[1,8,64]{2,1,0:T(8,128)S(1)}, f32[1,8,64]{2,1,0:T(8,128)S(1)}, u32[]{:S(2)}, u32[]{:S(2)}) collective-permute-start(f32[1,8,64]{2,1,0:T(8,128)S(1)} %get-tuple-element.82), channel_id=1, source_target_pairs={{1,0},{2,1},{3,2},{5,4},{6,5},{7,6},{9,8},{10,9},{11,10},{13,12},{... | collective-permute-start | bytes 6152 | tf_op jit(solution)/shard_map/ppermute | solution.py:22
  158.4 15.8 %collective-permute-start.38 = (f32[1,10,66]{2,1,0:T(8,128)S(1)}, f32[1,10,66]{2,1,0:T(8,128)S(1)}, u32[]{:S(2)}, u32[]{:S(2)}) collective-permute-start(f32[1,10,66]{2,1,0:T(8,128)S(1)} %get-tuple-element.92), channel_id=1, source_target_pairs={{0,1},{1,2},{2,3},{4,5},{5,6},{6,7},{8,9},{9,10},{10,11},{12,13},{... | collective-permute-start | bytes 7928 | tf_op jit(solution)/shard_map/ppermute | solution.py:21
  162.4 15.8 %collective-permute-start.40 = (f32[1,10,66]{2,1,0:T(8,128)S(1)}, f32[1,10,66]{2,1,0:T(8,128)S(1)}, u32[]{:S(2)}, u32[]{:S(2)}) collective-permute-start(f32[1,10,66]{2,1,0:T(8,128)S(1)} %get-tuple-element.93), channel_id=1, source_target_pairs={{1,0},{2,1},{3,2},{5,4},{6,5},{7,6},{9,8},{10,9},{11,10},{13,12},{... | collective-permute-start | bytes 7928 | tf_op jit(solution)/shard_map/ppermute | solution.py:22
  164.3 37.5 %collective-permute-start.55 = (f32[2,4,1]{2,1,0:T(4,128)S(1)}, f32[2,4,1]{2,1,0:T(4,128)S(1)}, u32[]{:S(2)}, u32[]{:S(2)}) collective-permute-start(f32[2,4,1]{2,1,0:T(4,128)S(1)} %slice.1877), channel_id=1, source_target_pairs={{0,8},{8,16},{16,24},{1,9},{9,17},{17,25},{2,10},{10,18},{18,26},{... | collective-permute-start | bytes 104 | tf_op jit(solution)/shard_map/ppermute | solution.py:21
  166.2 38.0 %collective-permute-start.56 = (f32[2,4,1]{2,1,0:T(4,128)S(1)}, f32[2,4,1]{2,1,0:T(4,128)S(1)}, u32[]{:S(2)}, u32[]{:S(2)}) collective-permute-start(f32[2,4,1]{2,1,0:T(4,128)S(1)} %bitcast.539), channel_id=1, source_target_pairs={{8,0},{16,8},{24,16},{9,1},{17,9},{25,17},{10,2},{18,10},{26,18},{... | collective-permute-start | bytes 104 | tf_op jit(solution)/shard_map/ppermute | solution.py:22
  169.9 37.8 %collective-permute-start.53 = (f32[2,1,32]{2,1,0:T(1,128)S(1)}, f32[2,1,32]{2,1,0:T(1,128)S(1)}, u32[]{:S(2)}, u32[]{:S(2)}) collective-permute-start(f32[2,1,32]{2,1,0:T(1,128)S(1)} %slice.1875), channel_id=1, source_target_pairs={{0,4},{1,5},{2,6},{3,7},{8,12},{9,13},{10,14},{11,15},{16,20},{17,... | collective-permute-start | bytes 776 | tf_op jit(solution)/shard_map/ppermute | solution.py:21
  174.3 15.0 %collective-permute-start.61 = (f32[6,1,4,18]{3,2,1,0:T(4,128)S(1)}, f32[6,1,4,18]{3,2,1,0:T(4,128)S(1)}, u32[]{:S(2)}, u32[]{:S(2)}) collective-permute-start(f32[6,1,4,18]{3,2,1,0:T(4,128)S(1)} %pad_maximum_fusion.175), channel_id=1, source_target_pairs={{0,1},{1,2},{2,3},{4,5},{5,6},{6,7},{8,9},{9,10},{10,11},{12,13},{... | collective-permute-start | bytes 5192 | tf_op jit(solution)/shard_map/ppermute | solution.py:21
  194.2 15.9 %collective-permute-start.54 = (f32[2,1,32]{2,1,0:T(1,128)S(1)}, f32[2,1,32]{2,1,0:T(1,128)S(1)}, u32[]{:S(2)}, u32[]{:S(2)}) collective-permute-start(f32[2,1,32]{2,1,0:T(1,128)S(1)} %slice.1876), channel_id=1, source_target_pairs={{4,0},{5,1},{6,2},{7,3},{12,8},{13,9},{14,10},{15,11},{20,16},{21,... | collective-permute-start | bytes 776 | tf_op jit(solution)/shard_map/ppermute | solution.py:22
  (93 other events, 638.9 us)
where the time goes:
time: 384 us; the launch traced here: 381 us
  starting transfers between devices  253 us (66%)
  waiting for transfers between devices  98.9 us (26%)
  other arithmetic  16.6 us (4%)
  local copies, waits for them, and re-layouts  9.76 us (3%)
    ppermute x51, starting transfers between devices, padded_2(): after = lax.ppermute(first, axis, down)  125 us
    ppermute x51, starting transfers between devices, padded_2(): before = lax.ppermute(last, axis, up)  119 us
    ppermute x51, waiting for transfers between devices, padded_2(): after = lax.ppermute(first, axis, down)  82.7 us
    ppermute x51, waiting for transfers between devices, padded_2(): before = lax.ppermute(last, axis, up)  16.2 us
    ppermute x3, starting transfers between devices, shifted(): return lax.ppermute(block, axis, route)  8.8 us
  transfers between devices with their start and end apart: 105, of which 43 were waited for; matrix products, arithmetic and copies ran while one was open for 4% of the time, Pallas kernels for 0%

commit v1 on v0

v1 whole, which is shorter than its diff:
```python
import itertools

import jax
import jax.numpy as jnp
from jax import lax
from jax.sharding import PartitionSpec as P

SWEEPS = 3
LEVELS = 3
COARSE_SWEEPS = 4
OMEGA = 0.8
AXES = ("gx", "gy", "layer")
DIMS = (("layer", 0), ("gy", 1), ("gx", 2))
HIGHEST = lax.Precision.HIGHEST


def pair_route(axis, phase):
    sizes = [lax.axis_size(name) for name in AXES]
    k = AXES.index(axis)
    n = sizes[k]
    route = []
    for index in itertools.product(*[range(size) for size in sizes]):
        target = list(index)
        if phase == 0:
            target[k] = index[k] ^ 1
        elif 0 < index[k] < n - 1 or k == 0:
            target[k] = (((index[k] + 1) % n ^ 1) - 1) % n
        else:
            target[0] = index[0] ^ 1 if sizes[0] % 2 == 0 else index[0]
        flat = [(i[0] * sizes[1] + i[1]) * sizes[2] + i[2] for i in (index, target)]
        route.append(tuple(flat))
    return route


def swap(axis, first, last):
    n, me = lax.axis_size(axis), lax.axis_index(axis)
    if n == 1:
        return jnp.zeros_like(last), jnp.zeros_like(first)
    if n % 2:
        before = lax.ppermute(last, axis, [(i, (i + 1) % n) for i in range(n)])
        after = lax.ppermute(first, axis, [(i, (i - 1) % n) for i in range(n)])
    else:
        even = me % 2 == 0
        one = lax.ppermute(jnp.where(even, last, first), AXES, pair_route(axis, 0))
        if n == 2:
            return jnp.where(even, 0.0, one), jnp.where(even, one, 0.0)
        two = lax.ppermute(jnp.where(even, first, last), AXES, pair_route(axis, 1))
        before, after = jnp.where(even, two, one), jnp.where(even, one, two)
    return jnp.where(me > 0, before, 0.0), jnp.where(me < n - 1, after, 0.0)


def face(field, dim, last):
    axis = field.ndim - 3 + dim
    size = field.shape[axis]
    return lax.slice_in_dim(field, size - 1, size, axis=axis) if last else lax.slice_in_dim(field, 0, 1, axis=axis)


def previous(field, before, dim):
    axis = field.ndim - 3 + dim
    return jnp.concatenate([before, lax.slice_in_dim(field, 0, field.shape[axis] - 1, axis=axis)], axis=axis)


def following(field, after, dim):
    axis = field.ndim - 3 + dim
    return jnp.concatenate([lax.slice_in_dim(field, 1, field.shape[axis], axis=axis), after], axis=axis)


def exchange(firsts, lasts):
    return [swap(axis, firsts[dim], lasts[dim]) for axis, dim in DIMS]


def faces(field):
    return [face(field, dim, False) for dim in range(3)], [face(field, dim, True) for dim in range(3)]


def block_apply(blocks, values):
    return jnp.stack([blocks[c] * values[0] + blocks[3 + c] * values[1] + blocks[6 + c] * values[2] for c in range(3)])


def laplacian(field, halos, trans, trans_before):
    total = 0.0
    for dim in range(3):
        before, after = halos[dim]
        flux = trans[dim] * (field - following(field, after, dim))
        rim = trans_before[dim] * (before - face(field, dim, False))
        total = total + flux - previous(flux, jnp.broadcast_to(rim, before.shape), dim)
    return total


def product_faces(stencil, field):
    firsts = [face(stencil[1 + 2 * dim], dim, False) * face(field, dim, False) for dim in range(3)]
    lasts = [face(stencil[2 + 2 * dim], dim, True) * face(field, dim, True) for dim in range(3)]
    return firsts, lasts


def off_apply(stencil, field, halos):
    total = 0.0
    for dim in range(3):
        before, after = halos[dim]
        total = total + previous(stencil[2 + 2 * dim] * field, before, dim)
        total = total + following(stencil[1 + 2 * dim] * field, after, dim)
    return total


def pool_matrix(size):
    return (jnp.arange(size)[:, None] // 2 == jnp.arange(size // 2)[None, :]).astype(jnp.float32)


def restrict(field):
    depth, height, width = field.shape
    field = field.reshape(depth // 2, 2, height // 2, 2, width).sum(axis=(1, 3))
    return jnp.einsum("lyx,xX->lyX", field, pool_matrix(width), precision=HIGHEST)


def prolong_x(field):
    return jnp.einsum("...X,xX->...x", field, pool_matrix(2 * field.shape[-1]), precision=HIGHEST)


def prolong(field):
    return jnp.repeat(jnp.repeat(prolong_x(field), 2, 1), 2, 0)


def zero_halos(field):
    return [(jnp.zeros_like(face(field, dim, False)),) * 2 for dim in range(3)]


def apply_whole(stencil, field):
    return stencil[0] * field + off_apply(stencil, field, zero_halos(field))


def cycle_whole(rhs, stencils, level):
    stencil = stencils[level]
    scale = OMEGA / stencil[0]
    field = rhs * scale
    if level == LEVELS:
        for sweep in range(COARSE_SWEEPS - 1):
            field = field + (rhs - apply_whole(stencil, field)) * scale
        return field
    residual = rhs - apply_whole(stencil, field)
    field = field + prolong(cycle_whole(restrict(residual), stencils, level + 1))
    return field + (rhs - apply_whole(stencil, field)) * scale


def gather_whole(arrays):
    sizes = [lax.axis_size(name) for name in AXES]
    count = sizes[0] * sizes[1] * sizes[2]
    flat = jnp.concatenate([array.reshape(-1) for array in arrays])
    width = flat.shape[0]
    rows = -(-width // 128)
    flat = jnp.pad(flat, (0, rows * 128 - width)).reshape(rows, 128)
    sent = jnp.broadcast_to(flat[None], (count,) + flat.shape)
    got = lax.all_to_all(sent, AXES, 0, 0).reshape(sizes[0], sizes[1], sizes[2], rows * 128)
    wholes, start = [], 0
    for array in arrays:
        part = got[..., start : start + array.size]
        start += array.size
        lead = array.shape[:-3]
        d, h, w = array.shape[-3:]
        part = part.reshape(sizes + [-1, d, h, w])
        part = part.transpose(3, 2, 4, 1, 5, 0, 6)
        wholes.append(part.reshape(lead + (sizes[2] * d, sizes[1] * h, sizes[0] * w)))
    return wholes


def level_one(rhs, stencil, coarse_two, coarse_three):
    scale = OMEGA / stencil[0]
    field = rhs * scale
    product_firsts, product_lasts = product_faces(stencil, field)
    firsts = [jnp.stack([product_firsts[dim], face(stencil[1 + 2 * dim], dim, False)]) for dim in range(3)]
    lasts = [jnp.stack([product_lasts[dim], face(stencil[2 + 2 * dim], dim, True)]) for dim in range(3)]
    halos = exchange(firsts, lasts)
    off = off_apply(stencil, field, [(b[0], a[0]) for b, a in halos])
    residual = (1.0 - OMEGA) * rhs - off
    next_rhs = restrict(residual)
    d, h, w = next_rhs.shape
    rhs_two, whole_two, whole_three = gather_whole([next_rhs, coarse_two, coarse_three])
    coarse = cycle_whole(rhs_two, [None, None, whole_two, whole_three], 2)
    wide = jnp.pad(coarse, 1)
    starts = [lax.axis_index(axis) * size for axis, size in zip(("layer", "gy", "gx"), (d, h, w))]
    box = lax.dynamic_slice(wide, starts, (d + 2, h + 2, w + 2))
    addition = prolong(box[1:-1, 1:-1, 1:-1])
    rims = []
    for dim in range(3):
        pair = []
        for last in (False, True):
            window = [slice(1, -1)] * 3
            window[dim] = slice(-1, None) if last else slice(0, 1)
            rim = box[tuple(window)]
            for other in range(3):
                if other != dim:
                    rim = prolong_x(rim) if other == 2 else jnp.repeat(rim, 2, other)
            pair.append(rim)
        rims.append(pair)
    add_halos = [(halos[dim][0][1] * rims[dim][0], halos[dim][1][1] * rims[dim][1]) for dim in range(3)]
    off = off + off_apply(stencil, addition, add_halos)
    field = field + addition
    return field + (rhs - stencil[0] * field - off) * scale


def local(
    source,
    active_cells,
    diag_blocks,
    frozen_inverses,
    transmissibility,
    pressure_weights,
    stencil_fine,
    coarse_one,
    coarse_two,
    coarse_three,
    pressure_state,
    mobilities,
):
    mask = active_cells.astype(jnp.float32)
    rhs = source * mask
    iterate = block_apply(frozen_inverses, rhs)
    trans_before = None
    for sweep in range(SWEEPS - 1):
        if sweep == 0:
            extra = [transmissibility[dim][None] for dim in range(3)]
        elif sweep == 1:
            extra = [jnp.concatenate([mobilities, pressure_state[None]])] * 3
        else:
            extra = [iterate[:0]] * 3
        firsts = [jnp.concatenate([face(iterate, dim, False), face(extra[dim], dim, False)]) for dim in range(3)]
        lasts = [jnp.concatenate([face(iterate, dim, True), face(extra[dim], dim, True)]) for dim in range(3)]
        halos = exchange(firsts, lasts)
        if sweep == 0:
            trans_before = [before[3] for before, after in halos]
        elif sweep == 1:
            state_halos = [(before[3:7], after[3:7]) for before, after in halos]
        halos = [(before[0:3], after[0:3]) for before, after in halos]
        applied = block_apply(diag_blocks, iterate) + laplacian(iterate, halos, transmissibility, trans_before)
        iterate = iterate + block_apply(frozen_inverses, rhs - applied)
    halos = exchange(*faces(iterate[0]))
    row = (
        diag_blocks[0] * iterate[0]
        + diag_blocks[3] * iterate[1]
        + diag_blocks[6] * iterate[2]
        + laplacian(iterate[0], halos, transmissibility, trans_before)
    )
    pressure_rhs = rhs[0] - row
    scale = OMEGA / stencil_fine[0]
    field = pressure_rhs * scale
    halos = exchange(*product_faces(stencil_fine, field))
    residual = (1.0 - OMEGA) * pressure_rhs - off_apply(stencil_fine, field, halos)
    field = field + prolong(level_one(restrict(residual), coarse_one, coarse_two, coarse_three))
    halos = exchange(*product_faces(stencil_fine, field))
    correction = (1.0 - OMEGA) * field + (pressure_rhs - off_apply(stencil_fine, field, halos)) * scale
    adjoint = mask * (iterate + pressure_weights * correction[None])
    halos = exchange(*faces(adjoint))
    gradients = []
    for dim in range(3):
        (adj_b, adj_a), (sta_b, sta_a) = halos[dim], state_halos[dim]
        mean = 0.5 * (mobilities + following(mobilities, sta_a[0:3], dim))
        drop = adjoint - following(adjoint, adj_a, dim)
        total = drop[0] * mean[0] + drop[1] * mean[1] + drop[2] * mean[2]
        here = transmissibility[dim] * total * (pressure_state - following(pressure_state, sta_a[3], dim))
        mean = 0.5 * (sta_b[0:3] + face(mobilities, dim, False))
        drop = adj_b - face(adjoint, dim, False)
        total = drop[0] * mean[0] + drop[1] * mean[1] + drop[2] * mean[2]
        rim = trans_before[dim] * total * (sta_b[3] - face(pressure_state, dim, False))
        gradients.append(0.5 * (here + previous(here, rim, dim)))
    return (adjoint, jnp.stack(gradients))


def solution(mesh):
    cells = P("layer", "gy", "gx")
    fields = P(None, "layer", "gy", "gx")
    return jax.shard_map(
        local,
        mesh=mesh,
        in_specs=(
            fields,
            cells,
            fields,
            fields,
            fields,
            fields,
            fields,
            fields,
            fields,
            fields,
            cells,
            fields,
        ),
        out_specs=(fields, fields),
        check_vma=False,
    )
```

time: 384 us -> 154 us (0.40)
  the two profiles are of different devices: /device:TPU:12 before, /device:TPU:0 now
where the time goes in v1:
time: 154 us; the launch traced here: 151 us
  local copies, waits for them, and re-layouts  62.7 us (41%)
  starting transfers between devices  36.2 us (24%)
  other arithmetic  24.2 us (16%)
  waiting for transfers between devices  22.2 us (14%)
  matrix products  2.99 us (2%)
  between operations  2.95 us (2%)
    unnamed x281, local copies, waits for them, and re-layouts  32.6 us
    ppermute x21, starting transfers between devices, swap(): one = lax.ppermute(jnp.where(even, last, first), AXES, pair_route(axis, 0))  27.4 us
    ppermute x14, waiting for transfers between devices, swap(): two = lax.ppermute(jnp.where(even, first, last), AXES, pair_route(axis, 1))  14 us
    ppermute x14, starting transfers between devices, swap(): two = lax.ppermute(jnp.where(even, first, last), AXES, pair_route(axis, 1))  5.84 us
    slice x21, local copies, waits for them, and re-layouts, following(): lax.slice_in_dim(field, 1, field.shape[axis], axis=axis)  5.28 us
    ppermute x21, waiting for transfers between devices, swap(): one = lax.ppermute(jnp.where(even, last, first), AXES, pair_route(axis, 0))  4.49 us
    select_n x14, other arithmetic, swap(): one = lax.ppermute(jnp.where(even, last, first), AXES, pair_route(axis, 0))  3.85 us
    all_to_all x1, waiting for transfers between devices, gather_whole(): lax.all_to_all(sent, AXES, 0, 0)  3.74 us
  transfers between devices with their start and end apart: 36, of which 8 were waited for; matrix products, arithmetic and copies ran while one was open for 17% of the time, Pallas kernels for 0%

profile of v1, /device:TPU:0, one launch (start us, length us, event | category | flops | bytes accessed | tf_op | source)
XLA Modules:
  0.0 151.3 jit_solution(2545903559476771340)
XLA Ops:
  3.3 1.6 %multiply_add_fusion.11 = (f32[1,8,16,128]{3,2,1,0:T(8,128)}, f32[1,8,16,128]{3,2,1,0:T(8,128)S(1)}, f32[1,8,16,128]{3,2,1,0:T(8,128)S(1)}, f32[1,8,16,128]{3,2,1,0:T(8,128)S(1)}, f32[1,8,16,128]{3,2,1,0:T(8,128)}) fusion(f32[9,8,16,128]{3,2,1,0:T(8,128)} %param.14, f32[3,8,16,128]{3,2,1,0:T(8,128)S(1)} %broadcast_multiply_fusion, ...), kind=kLoop, calls=%fused_computation.215 | loop fusion | flops 327680 | bytes 1310720 | tf_op jit(solution)/shard_map/add | solution.py:77
  5.6 2.9 %collective-permute-start.2 = (f32[4,8,1,128]{3,2,1,0:T(1,128)}, f32[4,8,1,128]{3,2,1,0:T(1,128)}, u32[]{:S(2)}, u32[]{:S(2)}) collective-permute-start(f32[4,8,1,128]{3,2,1,0:T(1,128)} %broadcast_select_fusion.7), channel_id=1, source_target_pairs={{0,4},{1,5},{2,6},{3,7},{4,0},{5,1},{6,2},{7,3},{8,12},{9,13},{10,... | collective-permute-start | bytes 49160 | tf_op jit(solution)/shard_map/ppermute | solution.py:44
  9.2 1.6 %collective-permute-start = (f32[4,1,16,128]{3,2,1,0:T(8,128)}, f32[4,1,16,128]{3,2,1,0:T(8,128)}, u32[]{:S(2)}, u32[]{:S(2)}) collective-permute-start(f32[4,1,16,128]{3,2,1,0:T(8,128)} %get-tuple-element.185), channel_id=1, source_target_pairs={{0,1},{1,0},{2,3},{3,2},{4,5},{5,4},{6,7},{7,6},{8,9},{9,8},{10,11... | collective-permute-start | bytes 98312 | tf_op jit(solution)/shard_map/ppermute | solution.py:44
  12.4 1.1 collective-permute-start.4
  29.5 1.3 collective-permute-start.7
  31.6 3.2 %collective-permute-start.5 = (f32[7,1,16,128]{3,2,1,0:T(8,128)S(1)}, f32[7,1,16,128]{3,2,1,0:T(8,128)S(1)}, u32[]{:S(2)}, u32[]{:S(2)}) collective-permute-start(f32[7,1,16,128]{3,2,1,0:T(8,128)S(1)} %broadcast_select_fusion.9), channel_id=1, source_target_pairs={{0,1},{1,0},{2,3},{3,2},{4,5},{5,4},{6,7},{7,6},{8,9},{9,8},{10,11... | collective-permute-start | bytes 172040 | tf_op jit(solution)/shard_map/ppermute | solution.py:44
  34.8 8.6 %collective-permute-done.9 = f32[7,8,16,1]{3,2,1,0:T(8,128)S(1)} collective-permute-done((f32[7,8,16,1]{3,2,1,0:T(8,128)S(1)}, f32[7,8,16,1]{3,2,1,0:T(8,128)S(1)}, u32[]{:S(2)}, u32[]{:S(2)}) %collective-permute-start.9) | collective-permute-done | bytes 3616 | tf_op jit(solution)/shard_map/ppermute | solution.py:47
  50.3 3.3 %collective-permute-start.10 = (f32[1,16,128]{2,1,0:T(8,128)S(1)}, f32[1,16,128]{2,1,0:T(8,128)S(1)}, u32[]{:S(2)}, u32[]{:S(2)}) collective-permute-start(f32[1,16,128]{2,1,0:T(8,128)S(1)} %get-tuple-element.249), channel_id=1, source_target_pairs={{0,1},{1,0},{2,3},{3,2},{4,5},{5,4},{6,7},{7,6},{8,9},{9,8},{10,11... | collective-permute-start | bytes 24584 | tf_op jit(solution)/shard_map/ppermute | solution.py:44
  54.6 2.8 %collective-permute-done.12 = f32[8,1,128]{2,1,0:T(1,128)S(1)} collective-permute-done((f32[8,1,128]{2,1,0:T(1,128)S(1)}, f32[8,1,128]{2,1,0:T(1,128)S(1)}, u32[]{:S(2)}, u32[]{:S(2)}) %collective-permute-start.12) | collective-permute-done | bytes 4128 | tf_op jit(solution)/shard_map/ppermute | solution.py:44
  62.9 1.6 %collective-permute-start.18 = (f32[8,16,1]{2,1,0:T(8,128)S(1)}, f32[8,16,1]{2,1,0:T(8,128)S(1)}, u32[]{:S(2)}, u32[]{:S(2)}) collective-permute-start(f32[8,16,1]{2,1,0:T(8,128)S(1)} %get-tuple-element.107), channel_id=1, source_target_pairs={{0,24},{1,25},{2,26},{3,27},{4,28},{5,29},{6,30},{7,31},{8,16},{9,... | collective-permute-start | bytes 1544 | tf_op jit(solution)/shard_map/ppermute | solution.py:47
  64.6 2.1 %collective-permute-done.18 = f32[8,16,1]{2,1,0:T(8,128)S(1)} collective-permute-done((f32[8,16,1]{2,1,0:T(8,128)S(1)}, f32[8,16,1]{2,1,0:T(8,128)S(1)}, u32[]{:S(2)}, u32[]{:S(2)}) %collective-permute-start.18) | collective-permute-done | bytes 544 | tf_op jit(solution)/shard_map/ppermute | solution.py:47
  70.9 1.3 collective-permute-start.22
  72.2 4.6 %collective-permute-start.21 = (f32[2,1,8,64]{3,2,1,0:T(8,128)S(1)}, f32[2,1,8,64]{3,2,1,0:T(8,128)S(1)}, u32[]{:S(2)}, u32[]{:S(2)}) collective-permute-start(f32[2,1,8,64]{3,2,1,0:T(8,128)S(1)} %get-tuple-element.237), channel_id=1, source_target_pairs={{0,1},{1,0},{2,3},{3,2},{4,5},{5,4},{6,7},{7,6},{8,9},{9,8},{10,11... | collective-permute-start | bytes 12296 | tf_op jit(solution)/shard_map/ppermute | solution.py:44
  85.9 2.9 %all-to-all-start = ((f32[32,18,128]{2,1,0:T(8,128)}), f32[32,18,128]{2,1,0:T(8,128)S(1)}, u32[]{:S(2)}, u32[]{:S(2)}) async-start(f32[32,18,128]{2,1,0:T(8,128)} %broadcast_in_dim.197), calls=%async_computation | async-start | bytes 786432 | tf_op jit(solution)/shard_map/all_to_all | solution.py:152
  94.3 1.3 slice_bitcast_fusion.9
  96.2 1.3 slice.1708
  98.1 3.7 %all-to-all-done = f32[32,18,128]{2,1,0:T(8,128)S(1)} async-done(((f32[32,18,128]{2,1,0:T(8,128)}), f32[32,18,128]{2,1,0:T(8,128)S(1)}, u32[]{:S(2)}, u32[]{:S(2)}) %all-to-all-start) | async-done | bytes 294944 | tf_op jit(solution)/shard_map/all_to_all | solution.py:152
  126.6 1.1 collective-permute-start.28
  130.7 1.4 collective-permute-done.27
  133.3 1.1 fusion.81
  135.6 1.6 %collective-permute-start.33 = (f32[3,8,16,1]{3,2,1,0:T(8,128)S(1)}, f32[3,8,16,1]{3,2,1,0:T(8,128)S(1)}, u32[]{:S(2)}, u32[]{:S(2)}) collective-permute-start(f32[3,8,16,1]{3,2,1,0:T(8,128)S(1)} %get-tuple-element.97), channel_id=1, source_target_pairs={{0,8},{1,9},{2,10},{3,11},{4,12},{5,13},{6,14},{7,15},{8,0},{9,1},... | collective-permute-start | bytes 4616 | tf_op jit(solution)/shard_map/ppermute | solution.py:44
  137.3 1.1 collective-permute-start.32
  138.4 2.0 %collective-permute-start.30 = (f32[3,1,16,128]{3,2,1,0:T(8,128)S(1)}, f32[3,1,16,128]{3,2,1,0:T(8,128)S(1)}, u32[]{:S(2)}, u32[]{:S(2)}) collective-permute-start(f32[3,1,16,128]{3,2,1,0:T(8,128)S(1)} %get-tuple-element.88), channel_id=1, source_target_pairs={{0,1},{1,0},{2,3},{3,2},{4,5},{5,4},{6,7},{7,6},{8,9},{9,8},{10,11... | collective-permute-start | bytes 73736 | tf_op jit(solution)/shard_map/ppermute | solution.py:44
  140.4 2.3 %collective-permute-done.34 = f32[3,8,16,1]{3,2,1,0:T(8,128)S(1)} collective-permute-done((f32[3,8,16,1]{3,2,1,0:T(8,128)S(1)}, f32[3,8,16,1]{3,2,1,0:T(8,128)S(1)}, u32[]{:S(2)}, u32[]{:S(2)}) %collective-permute-start.34) | collective-permute-done | bytes 1568 | tf_op jit(solution)/shard_map/ppermute | solution.py:47
  (625 shorter events, 92.5 us)
Async XLA Ops:
  5.6 18.9 %collective-permute-start.2 = (f32[4,8,1,128]{3,2,1,0:T(1,128)}, f32[4,8,1,128]{3,2,1,0:T(1,128)}, u32[]{:S(2)}, u32[]{:S(2)}) collective-permute-start(f32[4,8,1,128]{3,2,1,0:T(1,128)} %broadcast_select_fusion.7), channel_id=1, source_target_pairs={{0,4},{1,5},{2,6},{3,7},{4,0},{5,1},{6,2},{7,3},{8,12},{9,13},{10,... | collective-permute-start | bytes 49160 | tf_op jit(solution)/shard_map/ppermute | solution.py:44
  9.2 16.7 %collective-permute-start = (f32[4,1,16,128]{3,2,1,0:T(8,128)}, f32[4,1,16,128]{3,2,1,0:T(8,128)}, u32[]{:S(2)}, u32[]{:S(2)}) collective-permute-start(f32[4,1,16,128]{3,2,1,0:T(8,128)} %get-tuple-element.185), channel_id=1, source_target_pairs={{0,1},{1,0},{2,3},{3,2},{4,5},{5,4},{6,7},{7,6},{8,9},{9,8},{10,11... | collective-permute-start | bytes 98312 | tf_op jit(solution)/shard_map/ppermute | solution.py:44
  10.8 15.1 %collective-permute-start.1 = (f32[4,1,16,128]{3,2,1,0:T(8,128)}, f32[4,1,16,128]{3,2,1,0:T(8,128)}, u32[]{:S(2)}, u32[]{:S(2)}) collective-permute-start(f32[4,1,16,128]{3,2,1,0:T(8,128)} %get-tuple-element.186), channel_id=1, source_target_pairs={{0,8},{1,2},{2,1},{3,11},{4,12},{5,6},{6,5},{7,15},{8,0},{9,10},{1... | collective-permute-start | bytes 98312 | tf_op jit(solution)/shard_map/ppermute | solution.py:47
  11.9 12.3 %collective-permute-start.3 = (f32[4,8,16,1]{3,2,1,0:T(8,128)}, f32[4,8,16,1]{3,2,1,0:T(8,128)S(1)}, u32[]{:S(2)}, u32[]{:S(2)}) collective-permute-start(f32[4,8,16,1]{3,2,1,0:T(8,128)} %get-tuple-element.60), channel_id=1, source_target_pairs={{0,8},{1,9},{2,10},{3,11},{4,12},{5,13},{6,14},{7,15},{8,0},{9,1},... | collective-permute-start | bytes 6152 | tf_op jit(solution)/shard_map/ppermute | solution.py:44
  12.4 11.8 %collective-permute-start.4 = (f32[4,8,16,1]{3,2,1,0:T(8,128)}, f32[4,8,16,1]{3,2,1,0:T(8,128)S(1)}, u32[]{:S(2)}, u32[]{:S(2)}) collective-permute-start(f32[4,8,16,1]{3,2,1,0:T(8,128)} %get-tuple-element.61), channel_id=1, source_target_pairs={{0,24},{1,25},{2,26},{3,27},{4,28},{5,29},{6,30},{7,31},{8,16},{9,... | collective-permute-start | bytes 6152 | tf_op jit(solution)/shard_map/ppermute | solution.py:47
  29.5 14.8 %collective-permute-start.7 = (f32[7,8,1,128]{3,2,1,0:T(1,128)S(1)}, f32[7,8,1,128]{3,2,1,0:T(1,128)S(1)}, u32[]{:S(2)}, u32[]{:S(2)}) collective-permute-start(f32[7,8,1,128]{3,2,1,0:T(1,128)S(1)} %broadcast_select_fusion.2), channel_id=1, source_target_pairs={{0,4},{1,5},{2,6},{3,7},{4,0},{5,1},{6,2},{7,3},{8,12},{9,13},{10,... | collective-permute-start | bytes 86024 | tf_op jit(solution)/shard_map/ppermute | solution.py:44
  30.9 12.6 %collective-permute-start.9 = (f32[7,8,16,1]{3,2,1,0:T(8,128)S(1)}, f32[7,8,16,1]{3,2,1,0:T(8,128)S(1)}, u32[]{:S(2)}, u32[]{:S(2)}) collective-permute-start(f32[7,8,16,1]{3,2,1,0:T(8,128)S(1)} %get-tuple-element.42), channel_id=1, source_target_pairs={{0,24},{1,25},{2,26},{3,27},{4,28},{5,29},{6,30},{7,31},{8,16},{9,... | collective-permute-start | bytes 10760 | tf_op jit(solution)/shard_map/ppermute | solution.py:47
  31.3 12.2 %collective-permute-start.8 = (f32[7,8,16,1]{3,2,1,0:T(8,128)S(1)}, f32[7,8,16,1]{3,2,1,0:T(8,128)S(1)}, u32[]{:S(2)}, u32[]{:S(2)}) collective-permute-start(f32[7,8,16,1]{3,2,1,0:T(8,128)S(1)} %get-tuple-element.43), channel_id=1, source_target_pairs={{0,8},{1,9},{2,10},{3,11},{4,12},{5,13},{6,14},{7,15},{8,0},{9,1},... | collective-permute-start | bytes 10760 | tf_op jit(solution)/shard_map/ppermute | solution.py:44
  31.6 13.4 %collective-permute-start.5 = (f32[7,1,16,128]{3,2,1,0:T(8,128)S(1)}, f32[7,1,16,128]{3,2,1,0:T(8,128)S(1)}, u32[]{:S(2)}, u32[]{:S(2)}) collective-permute-start(f32[7,1,16,128]{3,2,1,0:T(8,128)S(1)} %broadcast_select_fusion.9), channel_id=1, source_target_pairs={{0,1},{1,0},{2,3},{3,2},{4,5},{5,4},{6,7},{7,6},{8,9},{9,8},{10,11... | collective-permute-start | bytes 172040 | tf_op jit(solution)/shard_map/ppermute | solution.py:44
  34.8 10.2 %collective-permute-start.6 = (f32[7,1,16,128]{3,2,1,0:T(8,128)S(1)}, f32[7,1,16,128]{3,2,1,0:T(8,128)S(1)}, u32[]{:S(2)}, u32[]{:S(2)}) collective-permute-start(f32[7,1,16,128]{3,2,1,0:T(8,128)S(1)} %get-tuple-element.26), channel_id=1, source_target_pairs={{0,8},{1,2},{2,1},{3,11},{4,12},{5,6},{6,5},{7,15},{8,0},{9,10},{1... | collective-permute-start | bytes 172040 | tf_op jit(solution)/shard_map/ppermute | solution.py:47
  49.5 5.0 %collective-permute-start.14 = (f32[8,16,1]{2,1,0:T(8,128)S(1)}, f32[8,16,1]{2,1,0:T(8,128)S(1)}, u32[]{:S(2)}, u32[]{:S(2)}) collective-permute-start(f32[8,16,1]{2,1,0:T(8,128)S(1)} %get-tuple-element.183), channel_id=1, source_target_pairs={{0,24},{1,25},{2,26},{3,27},{4,28},{5,29},{6,30},{7,31},{8,16},{9,... | collective-permute-start | bytes 1544 | tf_op jit(solution)/shard_map/ppermute | solution.py:47
  49.7 4.8 %collective-permute-start.13 = (f32[8,16,1]{2,1,0:T(8,128)S(1)}, f32[8,16,1]{2,1,0:T(8,128)S(1)}, u32[]{:S(2)}, u32[]{:S(2)}) collective-permute-start(f32[8,16,1]{2,1,0:T(8,128)S(1)} %get-tuple-element.184), channel_id=1, source_target_pairs={{0,8},{1,9},{2,10},{3,11},{4,12},{5,13},{6,14},{7,15},{8,0},{9,1},... | collective-permute-start | bytes 1544 | tf_op jit(solution)/shard_map/ppermute | solution.py:44
  50.1 7.3 %collective-permute-start.11 = (f32[1,16,128]{2,1,0:T(8,128)S(1)}, f32[1,16,128]{2,1,0:T(8,128)S(1)}, u32[]{:S(2)}, u32[]{:S(2)}) collective-permute-start(f32[1,16,128]{2,1,0:T(8,128)S(1)} %get-tuple-element.248), channel_id=1, source_target_pairs={{0,8},{1,2},{2,1},{3,11},{4,12},{5,6},{6,5},{7,15},{8,0},{9,10},{1... | collective-permute-start | bytes 24584 | tf_op jit(solution)/shard_map/ppermute | solution.py:47
  50.3 7.1 %collective-permute-start.10 = (f32[1,16,128]{2,1,0:T(8,128)S(1)}, f32[1,16,128]{2,1,0:T(8,128)S(1)}, u32[]{:S(2)}, u32[]{:S(2)}) collective-permute-start(f32[1,16,128]{2,1,0:T(8,128)S(1)} %get-tuple-element.249), channel_id=1, source_target_pairs={{0,1},{1,0},{2,3},{3,2},{4,5},{5,4},{6,7},{7,6},{8,9},{9,8},{10,11... | collective-permute-start | bytes 24584 | tf_op jit(solution)/shard_map/ppermute | solution.py:44
  62.1 4.6 %collective-permute-start.17 = (f32[8,1,128]{2,1,0:T(1,128)S(1)}, f32[8,1,128]{2,1,0:T(1,128)S(1)}, u32[]{:S(2)}, u32[]{:S(2)}) collective-permute-start(f32[8,1,128]{2,1,0:T(1,128)S(1)} %broadcast_select_fusion.20), channel_id=1, source_target_pairs={{0,4},{1,5},{2,6},{3,7},{4,0},{5,1},{6,2},{7,3},{8,12},{9,13},{10,... | collective-permute-start | bytes 12296 | tf_op jit(solution)/shard_map/ppermute | solution.py:44
  70.9 10.9 %collective-permute-start.22 = (f32[2,4,1,64]{3,1,2,0:T(4,128)S(1)}, f32[2,4,1,64]{3,1,2,0:T(4,128)S(1)}, u32[]{:S(2)}, u32[]{:S(2)}) collective-permute-start(f32[2,4,1,64]{3,1,2,0:T(4,128)S(1)} %maximum_select_fusion), channel_id=1, source_target_pairs={{0,4},{1,5},{2,6},{3,7},{4,0},{5,1},{6,2},{7,3},{8,12},{9,13},{10,... | collective-permute-start | bytes 6152 | tf_op jit(solution)/shard_map/ppermute | solution.py:44
  72.2 10.2 %collective-permute-start.21 = (f32[2,1,8,64]{3,2,1,0:T(8,128)S(1)}, f32[2,1,8,64]{3,2,1,0:T(8,128)S(1)}, u32[]{:S(2)}, u32[]{:S(2)}) collective-permute-start(f32[2,1,8,64]{3,2,1,0:T(8,128)S(1)} %get-tuple-element.237), channel_id=1, source_target_pairs={{0,1},{1,0},{2,3},{3,2},{4,5},{5,4},{6,7},{7,6},{8,9},{9,8},{10,11... | collective-permute-start | bytes 12296 | tf_op jit(solution)/shard_map/ppermute | solution.py:44
  76.8 5.6 %collective-permute-start.20 = (f32[2,1,8,64]{3,2,1,0:T(8,128)S(1)}, f32[2,1,8,64]{3,2,1,0:T(8,128)S(1)}, u32[]{:S(2)}, u32[]{:S(2)}) collective-permute-start(f32[2,1,8,64]{3,2,1,0:T(8,128)S(1)} %get-tuple-element.238), channel_id=1, source_target_pairs={{0,8},{1,2},{2,1},{3,11},{4,12},{5,6},{6,5},{7,15},{8,0},{9,10},{1... | collective-permute-start | bytes 12296 | tf_op jit(solution)/shard_map/ppermute | solution.py:47
  85.9 15.9 %all-to-all-start = ((f32[32,18,128]{2,1,0:T(8,128)}), f32[32,18,128]{2,1,0:T(8,128)S(1)}, u32[]{:S(2)}, u32[]{:S(2)}) async-start(f32[32,18,128]{2,1,0:T(8,128)} %broadcast_in_dim.197), calls=%async_computation | async-start | bytes 786432 | tf_op jit(solution)/shard_map/all_to_all | solution.py:152
  135.5 7.2 %collective-permute-start.34 = (f32[3,8,16,1]{3,2,1,0:T(8,128)S(1)}, f32[3,8,16,1]{3,2,1,0:T(8,128)S(1)}, u32[]{:S(2)}, u32[]{:S(2)}) collective-permute-start(f32[3,8,16,1]{3,2,1,0:T(8,128)S(1)} %get-tuple-element.96), channel_id=1, source_target_pairs={{0,24},{1,25},{2,26},{3,27},{4,28},{5,29},{6,30},{7,31},{8,16},{9,... | collective-permute-start | bytes 4616 | tf_op jit(solution)/shard_map/ppermute | solution.py:47
  135.6 7.2 %collective-permute-start.33 = (f32[3,8,16,1]{3,2,1,0:T(8,128)S(1)}, f32[3,8,16,1]{3,2,1,0:T(8,128)S(1)}, u32[]{:S(2)}, u32[]{:S(2)}) collective-permute-start(f32[3,8,16,1]{3,2,1,0:T(8,128)S(1)} %get-tuple-element.97), channel_id=1, source_target_pairs={{0,8},{1,9},{2,10},{3,11},{4,12},{5,13},{6,14},{7,15},{8,0},{9,1},... | collective-permute-start | bytes 4616 | tf_op jit(solution)/shard_map/ppermute | solution.py:44
  137.3 8.4 %collective-permute-start.32 = (f32[3,8,1,128]{3,2,1,0:T(1,128)S(1)}, f32[3,8,1,128]{3,2,1,0:T(1,128)S(1)}, u32[]{:S(2)}, u32[]{:S(2)}) collective-permute-start(f32[3,8,1,128]{3,2,1,0:T(1,128)S(1)} %broadcast_select_fusion.12), channel_id=1, source_target_pairs={{0,4},{1,5},{2,6},{3,7},{4,0},{5,1},{6,2},{7,3},{8,12},{9,13},{10,... | collective-permute-start | bytes 36872 | tf_op jit(solution)/shard_map/ppermute | solution.py:44
  138.4 9.4 %collective-permute-start.31 = (f32[3,1,16,128]{3,2,1,0:T(8,128)S(1)}, f32[3,1,16,128]{3,2,1,0:T(8,128)S(1)}, u32[]{:S(2)}, u32[]{:S(2)}) collective-permute-start(f32[3,1,16,128]{3,2,1,0:T(8,128)S(1)} %get-tuple-element.87), channel_id=1, source_target_pairs={{0,8},{1,2},{2,1},{3,11},{4,12},{5,6},{6,5},{7,15},{8,0},{9,10},{1... | collective-permute-start | bytes 73736 | tf_op jit(solution)/shard_map/ppermute | solution.py:47
  138.4 9.4 %collective-permute-start.30 = (f32[3,1,16,128]{3,2,1,0:T(8,128)S(1)}, f32[3,1,16,128]{3,2,1,0:T(8,128)S(1)}, u32[]{:S(2)}, u32[]{:S(2)}) collective-permute-start(f32[3,1,16,128]{3,2,1,0:T(8,128)S(1)} %get-tuple-element.88), channel_id=1, source_target_pairs={{0,1},{1,0},{2,3},{3,2},{4,5},{5,4},{6,7},{7,6},{8,9},{9,8},{10,11... | collective-permute-start | bytes 73736 | tf_op jit(solution)/shard_map/ppermute | solution.py:44
  (150 other events, 422.0 us)

commit v2 on v1

v2 whole, which is shorter than its diff:
```python
import itertools

import jax
import jax.numpy as jnp
from jax import lax
from jax.experimental import pallas as pl
from jax.experimental.pallas import tpu as pltpu
from jax.sharding import PartitionSpec as P

SWEEPS = 3
LEVELS = 3
COARSE_SWEEPS = 4
OMEGA = 0.8
LANES = 128
AXES = ("gx", "gy", "layer")
BY_DIM = ("layer", "gy", "gx")
ORDER = ((0, 1), (0, 0), (1, 1), (1, 0), (2, 1), (2, 0))
HIGHEST = lax.Precision.HIGHEST
F32 = jnp.float32


def pair_route(axis, phase):
    sizes = [lax.axis_size(name) for name in AXES]
    k = AXES.index(axis)
    n = sizes[k]
    route = []
    for index in itertools.product(*[range(size) for size in sizes]):
        target = list(index)
        if phase == 0:
            target[k] = index[k] ^ 1
        elif 0 < index[k] < n - 1 or k == 0:
            target[k] = (((index[k] + 1) % n ^ 1) - 1) % n
        else:
            target[0] = index[0] ^ 1
        flat = [(i[0] * sizes[1] + i[1]) * sizes[2] + i[2] for i in (index, target)]
        route.append(tuple(flat))
    return route


def phases(dim):
    return min(lax.axis_size(BY_DIM[dim]), 3) - 1


def sends():
    return [(dim, phase) for dim, phase in ORDER if phase < phases(dim)]


def swap(buffers):
    return [lax.ppermute(b, AXES, pair_route(BY_DIM[dim], phase)) for b, (dim, phase) in zip(buffers, sends())]


class Grid:
    def __init__(self, depth, height, dup):
        self.depth, self.height, self.dup = depth, height, dup
        self.rows = depth * height

    def buffers(self, channels):
        shapes = ((channels, self.height, LANES), (channels, self.depth, LANES), (8, LANES))
        return [jax.ShapeDtypeStruct(shapes[dim], F32) for dim, phase in sends()]

    def emit(self, channels, out):
        out = dict(zip(sends(), out))
        lane = lax.broadcasted_iota(jnp.int32, (8, LANES), 1)
        for dim in range(3):
            if phases(dim) == 0:
                continue
            even = lax.axis_index(BY_DIM[dim]) % 2 == 0
            if dim == 2:
                firsts, lasts = jnp.zeros((8, LANES), F32), jnp.zeros((8, LANES), F32)
                for c, (first, last) in enumerate(channels[dim]):
                    for k in range(self.rows // 8):
                        at = 8 * k + self.dup * c
                        here = (lane >= at) & (lane < at + self.dup)
                        rows = slice(8 * k, 8 * k + 8)
                        firsts = jnp.where(here, roll(first(rows), at, 1), firsts)
                        lasts = jnp.where(here, roll(last(rows), at + self.dup, 1), lasts)
                pairs = [(slice(None), firsts, lasts)]
            else:
                if dim == 0:
                    low, high = slice(0, self.height), slice(self.rows - self.height, self.rows)
                else:
                    low, high = (pl.ds(s, self.depth, stride=self.height) for s in (0, self.height - 1))
                pairs = [(c, first(low), last(high)) for c, (first, last) in enumerate(channels[dim])]
            for c, first, last in pairs:
                out[dim, 0][c] = jnp.where(even, last, first)
                if phases(dim) == 2:
                    out[dim, 1][c] = jnp.where(even, first, last)

    def halos(self, got, count, scratch):
        got = dict(zip(sends(), got))
        result = [[None] * 3 for _ in range(count)]
        for dim in range(3):
            me, n = lax.axis_index(BY_DIM[dim]), lax.axis_size(BY_DIM[dim])
            even = me % 2 == 0
            for c in range(count if dim < 2 else 1):
                key = c if dim < 2 else slice(None)
                if phases(dim) == 0:
                    before = after = jnp.zeros((self.height, self.depth, 8)[dim : dim + 1] + (LANES,), F32)
                elif phases(dim) == 1:
                    one = got[dim, 0][key]
                    before, after = jnp.where(even, 0.0, one), jnp.where(even, one, 0.0)
                else:
                    one, two = got[dim, 0][key], got[dim, 1][key]
                    before, after = jnp.where(even, two, one), jnp.where(even, one, two)
                    before, after = jnp.where(me > 0, before, 0.0), jnp.where(me < n - 1, after, 0.0)
                if dim < 2:
                    result[c][dim] = (before, after)
                else:
                    for ch in range(count):
                        parts = []
                        for side, start in ((before, 0), (after, LANES - self.dup)):
                            pieces = [roll(side, start - 8 * k - self.dup * ch, 1) for k in range(self.rows // 8)]
                            parts.append(jnp.concatenate(pieces))
                        result[ch][dim] = tuple(parts)
        return [Rim(self, r, scratch, c) for c, r in enumerate(result)]


class Rim:
    def __init__(self, grid, faces, scratch, c):
        self.grid, self.faces = grid, faces
        ends = scratch.at[c]
        ends[pl.ds(0, grid.depth, stride=grid.height), :] = faces[1][0]
        ends[pl.ds(grid.height - 1, grid.depth, stride=grid.height), :] = faces[1][1]
        self.y_ends = ends[...]

    def previous(self, value, dim):
        g = self.grid
        if dim == 0:
            return jnp.concatenate([self.faces[0][0], value[: g.rows - g.height]])
        if dim == 1:
            return jnp.where(row_y(value, g.height) == 0, self.y_ends, roll(value, 1, 0))
        return jnp.where(lane_of(value) < g.dup, self.faces[2][0], roll(value, g.dup, 1))

    def following(self, value, dim):
        g = self.grid
        if dim == 0:
            return jnp.concatenate([value[g.height :], self.faces[0][1]])
        if dim == 1:
            return jnp.where(row_y(value, g.height) == g.height - 1, self.y_ends, roll(value, -1, 0))
        return jnp.where(lane_of(value) >= value.shape[1] - g.dup, self.faces[2][1], roll(value, -g.dup, 1))


class Closed:
    def __init__(self, height, dup):
        self.height, self.dup = height, dup

    def previous(self, value, dim):
        if dim == 0:
            return jnp.concatenate([jnp.zeros_like(value[: self.height]), value[: -self.height]])
        if dim == 1:
            return jnp.where(row_y(value, self.height) == 0, 0.0, roll(value, 1, 0))
        return jnp.where(lane_of(value) < self.dup, 0.0, roll(value, self.dup, 1))

    def following(self, value, dim):
        if dim == 0:
            return jnp.concatenate([value[self.height :], jnp.zeros_like(value[: self.height])])
        if dim == 1:
            return jnp.where(row_y(value, self.height) == self.height - 1, 0.0, roll(value, -1, 0))
        return jnp.where(lane_of(value) >= value.shape[1] - self.dup, 0.0, roll(value, -self.dup, 1))


def roll(value, shift, axis):
    shift %= value.shape[axis]
    return pltpu.roll(value, shift, axis) if shift else value


def row_y(value, height):
    return lax.broadcasted_iota(jnp.int32, value.shape, 0) % height


def lane_of(value):
    return lax.broadcasted_iota(jnp.int32, value.shape, 1)


def loader(ref, c):
    return lambda rows: ref[c, rows, :]


def product(coefs, k, ref):
    return lambda rows: coefs[k, rows, :] * ref[rows, :]


def off_apply(stencil, field, rim):
    total = 0.0
    for dim in range(3):
        total = total + rim.previous(stencil[2 + 2 * dim] * field, dim)
        total = total + rim.following(stencil[1 + 2 * dim] * field, dim)
    return total


def block_row(blocks, c, values):
    return blocks[c] * values[0] + blocks[3 + c] * values[1] + blocks[6 + c] * values[2]


def system_row(c, values, rim, blocks, trans, trans_before):
    total = block_row(blocks, c, values)
    v = values[c]
    for dim in range(3):
        total = total + trans[dim] * (v - rim.following(v, dim))
        total = total + trans_before[dim] * (v - rim.previous(v, dim))
    return total


def pair_sum_x(value, dup):
    odd = (lane_of(value) // dup) % 2 == 1
    return value + jnp.where(odd, roll(value, dup, 1), roll(value, -dup, 1))


def pair_sum_rows(value, depth, height, scratch):
    half = depth // 2
    parts = [value[2 * a * height : (2 * a + 1) * height] + value[(2 * a + 1) * height : (2 * a + 2) * height] for a in range(half)]
    whole = jnp.concatenate(parts)
    count = half * height // 2
    sums = []
    for at in range(0, whole.shape[1], LANES):
        scratch[: half * height, :] = whole[:, at : at + LANES]
        sums.append(scratch[pl.ds(0, count, stride=2), :] + scratch[pl.ds(1, count, stride=2), :])
    return jnp.concatenate(sums, axis=1)


def spread_rows(value, depth, height, scratch):
    count = depth * height
    tiles = []
    for at in range(0, value.shape[1], LANES):
        scratch[pl.ds(0, count, stride=2), :] = value[:, at : at + LANES]
        scratch[pl.ds(1, count, stride=2), :] = value[:, at : at + LANES]
        wide = scratch[: 2 * count, :]
        tiles.append(jnp.concatenate([wide[2 * height * (a // 2) : 2 * height * (a // 2 + 1)] for a in range(2 * depth)]))
    return jnp.concatenate(tiles, axis=1)


def one_hot(shape, hit):
    return jnp.where(hit(lax.broadcasted_iota(jnp.int32, shape, 0), lax.broadcasted_iota(jnp.int32, shape, 1)), 1.0, 0.0).astype(F32)


def matmul(a, b):
    return jnp.dot(a, b, precision=HIGHEST, preferred_element_type=F32)


def call(kernel, inputs, outputs, scratch=()):
    return pl.pallas_call(
        kernel,
        out_shape=list(outputs),
        scratch_shapes=[pltpu.VMEM(shape, F32) for shape in scratch],
        compiler_params=pltpu.CompilerParams(vmem_limit_bytes=40 * 2**20),
    )(*inputs)


def local(
    source,
    active_cells,
    diag_blocks,
    frozen_inverses,
    transmissibility,
    pressure_weights,
    stencil_fine,
    coarse_one,
    coarse_two,
    coarse_three,
    pressure_state,
    mobilities,
):
    depth, height, width = active_cells.shape
    fine, mid = Grid(depth, height, 1), Grid(depth // 2, height // 2, 2)
    sizes = [lax.axis_size(name) for name in AXES]
    count = sizes[0] * sizes[1] * sizes[2]
    swaps = len(sends())
    rows = fine.rows

    def flat(array):
        return array.reshape(array.shape[:-3] + (rows, width))

    def out(*shape):
        return jax.ShapeDtypeStruct(shape, F32)

    source, active, diag, frozen, trans, weights, stencil, pressure, mobility = (
        flat(a)
        for a in (
            source,
            active_cells,
            diag_blocks,
            frozen_inverses,
            transmissibility,
            pressure_weights,
            stencil_fine,
            pressure_state,
            mobilities,
        )
    )
    pressure = pressure[None]

    def start_kernel(source, active, frozen, trans, rhs_out, it_out, *buffers):
        mask = active[...].astype(F32)
        rhs = [source[c] * mask for c in range(3)]
        for c in range(3):
            rhs_out[c] = rhs[c]
            it_out[c] = block_row(frozen, c, rhs)
        its = [(loader(it_out, c),) * 2 for c in range(3)]
        fine.emit([its + [(loader(trans, dim),) * 2] for dim in range(3)], buffers)

    rhs, iterate, *buffers = call(
        start_kernel, (source, active, frozen, trans), [out(3, rows, LANES)] * 2 + fine.buffers(4)
    )
    got = swap(buffers)

    def sweep_one(rhs, it, frozen, diag, trans, mobility, pressure, *rest):
        got, (it_out, before_out), buffers, (ends,) = rest[:swaps], rest[swaps : swaps + 2], rest[swaps + 2 : -1], rest[-1:]
        rims = fine.halos(got, 4, ends)
        trans_before = [rims[3].previous(trans[dim], dim) for dim in range(3)]
        values = [it[c] for c in range(3)]
        rest = [rhs[c] - system_row(c, values, rims[c], diag, trans, trans_before) for c in range(3)]
        for c in range(3):
            before_out[c] = trans_before[c]
            it_out[c] = values[c] + block_row(frozen, c, rest)
        channels = [(loader(it_out, c),) * 2 for c in range(3)]
        channels += [(loader(mobility, c),) * 2 for c in range(3)] + [(loader(pressure, 0),) * 2]
        fine.emit([channels] * 3, buffers)

    iterate, trans_before, *buffers = call(
        sweep_one,
        (rhs, iterate, frozen, diag, trans, mobility, pressure, *got),
        [out(3, rows, LANES)] * 2 + fine.buffers(7),
        [(4, rows, LANES)],
    )
    state_got = got = swap(buffers)

    def sweep_two(rhs, it, frozen, diag, trans, trans_before, *rest):
        got, it_out, buffers, ends = rest[:swaps], rest[swaps], rest[swaps + 1 : -1], rest[-1]
        rims = fine.halos(got, 3, ends)
        values = [it[c] for c in range(3)]
        rest = [rhs[c] - system_row(c, values, rims[c], diag, trans, trans_before) for c in range(3)]
        for c in range(3):
            it_out[c] = values[c] + block_row(frozen, c, rest)
        fine.emit([[(loader(it_out, 0),) * 2]] * 3, buffers)

    iterate, *buffers = call(
        sweep_two,
        (rhs, iterate, frozen, diag, trans, trans_before, *got),
        [out(3, rows, LANES)] + fine.buffers(1),
        [(3, rows, LANES)],
    )
    got = swap(buffers)

    def emit_products(grid, coefs, field, buffers, with_coefs=False):
        channels = []
        for dim in range(3):
            pairs = [(product(coefs, 1 + 2 * dim, field), product(coefs, 2 + 2 * dim, field))]
            if with_coefs:
                pairs.append((loader(coefs, 1 + 2 * dim), loader(coefs, 2 + 2 * dim)))
            channels.append(pairs)
        grid.emit(channels, buffers)

    def pressure_kernel(rhs, it, diag, trans, trans_before, stencil, *rest):
        got, (b_out, x_out), buffers, ends = rest[:swaps], rest[swaps : swaps + 2], rest[swaps + 2 : -1], rest[-1]
        (rim,) = fine.halos(got, 1, ends)
        b = rhs[0] - system_row(0, [it[c] for c in range(3)], rim, diag, trans, trans_before)
        b_out[...] = b
        x_out[...] = b * (OMEGA / stencil[0])
        emit_products(fine, stencil, x_out, buffers)

    b_fine, x_fine, *buffers = call(
        pressure_kernel,
        (rhs, iterate, diag, trans, trans_before, stencil, *got),
        [out(rows, LANES)] * 2 + fine.buffers(1),
        [(1, rows, LANES)],
    )
    got = swap(buffers)

    one = coarse_one.reshape(7, mid.rows, width // 2)
    one = jnp.repeat(one, 2, axis=2)
    low_depth, low_height, low_width = coarse_two.shape[1:]
    groups = LANES // low_width

    def pack(array, channels, dup):
        lead = array.shape[1] * array.shape[2]
        array = jnp.repeat(array, dup, axis=3) if dup > 1 else array
        array = jnp.pad(array, ((0, channels - array.shape[0]), (0, 0), (0, 0), (0, 0)))
        array = array.reshape(groups, channels // groups, lead, low_width).transpose(1, 2, 0, 3)
        return array.reshape(channels // groups * lead, LANES)

    packed = jnp.concatenate([pack(coarse_two, 8, 1), pack(coarse_three, 8, 2)])
    block = packed.shape[0]
    low_rows = low_depth * low_height

    def residual_kernel(b, x, stencil, one, *rest):
        got, (b_out, x_out), buffers, (ends, temp) = rest[:swaps], rest[swaps : swaps + 2], rest[swaps + 2 : -2], rest[-2:]
        (rim,) = fine.halos(got, 1, ends)
        residual = (1.0 - OMEGA) * b[...] - off_apply(stencil, x[...], rim)
        coarse = pair_sum_rows(pair_sum_x(residual, 1), depth, height, temp)
        b_out[...] = coarse
        x_out[...] = coarse * (OMEGA / one[0])
        emit_products(mid, one, x_out, buffers, True)

    b_mid, x_mid, *buffers = call(
        residual_kernel,
        (b_fine, x_fine, stencil, one, *got),
        [out(mid.rows, LANES)] * 2 + mid.buffers(2),
        [(1, rows, LANES), (rows // 2, LANES)],
    )
    mid_got = got = swap(buffers)

    def low_kernel(b, x, one, packed, *rest):
        got, (off_out, sent), (ends, temp) = rest[:swaps], rest[swaps : swaps + 2], rest[-2:]
        rim, _ = mid.halos(got, 2, ends)
        off = off_apply(one, x[...], rim)
        off_out[...] = off
        residual = (1.0 - OMEGA) * b[...] - off
        coarse = pair_sum_rows(residual, mid.depth, mid.height, temp)
        first = LANES - low_width
        place = one_hot((LANES, LANES), lambda i, j: (i // 4 == j - first) & (i % 2 == 0))
        filled = jnp.concatenate([packed[:low_rows], packed[low_rows : 2 * low_rows] + matmul(coarse, place), packed[2 * low_rows :]])
        sent[...] = jnp.broadcast_to(filled[None], (count, block, LANES))

    off_mid, sent = call(
        low_kernel,
        (b_mid, x_mid, one, packed, *got),
        [out(mid.rows, LANES), out(count, block, LANES)],
        [(2, mid.rows, LANES), (mid.rows // 2, LANES)],
    )
    everyone = lax.all_to_all(sent, AXES, 0, 0)

    two_rows, two_width = sizes[2] * low_depth * sizes[1] * low_height, sizes[0] * low_width
    two_height = sizes[1] * low_height
    three_height = two_height // 2
    three_rows = two_rows // 4

    def assemble(everyone, two, three):
        per = sizes[1] * sizes[2]
        for tile in range(two_width // LANES):
            parts = [everyone[(tile * groups + g) * per : (tile * groups + g + 1) * per].reshape(per * block, LANES) for g in range(groups)]
            lane = lane_of(parts[0])
            for q in range(groups):
                value = parts[0] if q == 0 else roll(parts[0], -low_width * q, 1)
                for g in range(1, groups):
                    value = jnp.where(lane // low_width == g, roll(parts[g], low_width * (g - q), 1), value)
                value = value.reshape(per, block, LANES)
                lanes = slice(tile * LANES, (tile + 1) * LANES)
                for y in range(sizes[1]):
                    for z in range(sizes[2]):
                        for half in range(8 // groups):
                            c = q * (8 // groups) + half
                            mine = value[y * sizes[2] + z]
                            for a in range(low_depth):
                                at = (z * low_depth + a) * two_height + y * low_height
                                start = (half * low_depth + a) * low_height
                                two[c, at : at + low_height, lanes] = mine[start : start + low_height]
                            low = low_height // 2
                            for a in range(low_depth // 2):
                                at = (z * (low_depth // 2) + a) * three_height + y * low
                                start = 8 // groups * low_rows + (half * (low_depth // 2) + a) * low
                                three[c, at : at + low, lanes] = mine[start : start + low]

    def solve_low(two, three, temp):
        closed = Closed(two_height, 1)
        b = two[7]
        scale = OMEGA / two[0]
        x = b * scale
        residual = (1.0 - OMEGA) * b - off_apply(two, x, closed)
        coarse = pair_sum_rows(pair_sum_x(residual, 1), sizes[2] * low_depth, two_height, temp)
        inner = Closed(three_height, 2)
        inner_scale = OMEGA / three[0]
        field = start = coarse * inner_scale
        for sweep in range(COARSE_SWEEPS - 1):
            field = start + (1.0 - OMEGA) * field - off_apply(three, field, inner) * inner_scale
        x = x + spread_rows(field, sizes[2] * low_depth // 2, three_height, temp)
        return (1.0 - OMEGA) * x + (b - off_apply(two, x, closed)) * scale

    def up_kernel(everyone, b, x, off, one, x_fine, stencil, *rest):
        got, field_out, buffers = rest[:swaps], rest[swaps], rest[swaps + 1 : -5]
        ends, two, three, low_temp, temp = rest[-5:]
        assemble(everyone, two, three)
        low = solve_low(two, three, low_temp)
        gx, gy, gz = (lax.axis_index(name) for name in AXES)
        h, d = mid.height, mid.depth
        own = one_hot((two_width, LANES), lambda i, j: i == gx * low_width + j // 4)
        beside = one_hot(
            (two_width, LANES),
            lambda i, j: ((j < 2) & (i == gx * low_width - 1)) | ((j >= LANES - 2) & (i == (gx + 1) * low_width)),
        )

        def picked(n, layer, y):
            def hit(i, j):
                return j == (gz * low_depth + layer(i)) * two_height + gy * low_height + y(i)

            return one_hot((n, two_rows), hit)

        picks = jnp.concatenate(
            [
                picked(d * h, lambda i: i // h // 2, lambda i: i % h // 2),
                picked(h, lambda i: -1, lambda i: i // 2),
                picked(h, lambda i: low_depth, lambda i: i // 2),
                picked(8, lambda i: i % d // 2, lambda i: jnp.where(i < d, -1, low_height)),
            ]
        )
        chosen = matmul(picks, low)
        around = matmul(chosen, own)
        add = around[: d * h]
        add_x = matmul(chosen[: d * h], beside)
        _, coefs = mid.halos(got, 2, ends)
        starts = d * h
        faces = [
            (coefs.faces[0][0] * around[starts : starts + h], coefs.faces[0][1] * around[starts + h : starts + 2 * h]),
            (
                coefs.faces[1][0] * around[starts + 2 * h : starts + 2 * h + d],
                coefs.faces[1][1] * around[starts + 2 * h + d : starts + 2 * h + 2 * d],
            ),
            (coefs.faces[2][0] * add_x, coefs.faces[2][1] * add_x),
        ]
        off_all = off[...] + off_apply(one, add, Rim(mid, faces, ends, 0))
        field = (1.0 - OMEGA) * (x[...] + add) + (b[...] - off_all) * (OMEGA / one[0])
        field_out[...] = x_fine[...] + spread_rows(field, d, h, temp)
        emit_products(fine, stencil, field_out, buffers)

    field, *buffers = call(
        up_kernel,
        (everyone, b_mid, x_mid, off_mid, one, x_fine, stencil, *got),
        [out(rows, LANES)] + fine.buffers(1),
        [(2, mid.rows, LANES), (8, two_rows, two_width), (8, three_rows, two_width), (two_rows, LANES), (rows // 2, LANES)],
    )
    got = swap(buffers)

    def adjoint_kernel(field, b, stencil, it, active, weights, *rest):
        got, adj_out, buffers, ends = rest[:swaps], rest[swaps], rest[swaps + 1 : -1], rest[-1]
        (rim,) = fine.halos(got, 1, ends)
        value = field[...]
        correction = (1.0 - OMEGA) * value + (b[...] - off_apply(stencil, value, rim)) * (OMEGA / stencil[0])
        mask = active[...].astype(F32)
        for c in range(3):
            adj_out[c] = mask * (it[c] + weights[c] * correction)
        fine.emit([[(loader(adj_out, c),) * 2 for c in range(3)]] * 3, buffers)

    adjoint, *buffers = call(
        adjoint_kernel,
        (field, b_fine, stencil, iterate, active, weights, *got),
        [out(3, rows, LANES)] + fine.buffers(3),
        [(1, rows, LANES)],
    )
    got = swap(buffers)

    def gradient_kernel(adj, mobility, pressure, trans, trans_before, *rest):
        got, state_got, grad_out, (ends, state_ends) = rest[:swaps], rest[swaps : 2 * swaps], rest[2 * swaps], rest[-2:]
        adj_rims = fine.halos(got, 3, ends)
        state_rims = fine.halos(state_got, 7, state_ends)[3:]
        values = [adj[c] for c in range(3)]
        for dim in range(3):

            def term(trans, shift):
                total = 0.0
                for c in range(3):
                    mean = 0.5 * (mobility[c] + shift(state_rims[c], mobility[c]))
                    total = total + (values[c] - shift(adj_rims[c], values[c])) * mean
                return trans * total * (pressure[0] - shift(state_rims[3], pressure[0]))

            here = term(trans[dim], lambda rim, v: rim.following(v, dim))
            below = term(trans_before[dim], lambda rim, v: rim.previous(v, dim))
            grad_out[dim] = 0.5 * (here + below)

    (gradient,) = call(
        gradient_kernel,
        (adjoint, mobility, pressure, trans, trans_before, *got, *state_got),
        [out(3, rows, LANES)],
        [(3, rows, LANES), (7, rows, LANES)],
    )
    shape = (3, depth, height, width)
    return adjoint.reshape(shape), gradient.reshape(shape)


def solution(mesh):
    cells = P("layer", "gy", "gx")
    fields = P(None, "layer", "gy", "gx")
    return jax.shard_map(
        local,
        mesh=mesh,
        in_specs=(
            fields,
            cells,
            fields,
            fields,
            fields,
            fields,
            fields,
            fields,
            fields,
            fields,
            cells,
            fields,
        ),
        out_specs=(fields, fields),
        check_vma=False,
    )
```

time: 154 us -> 72.3 us (0.47); the launches traced: 151 us -> 71.9 us
  local copies, waits for them, and re-layouts: 62.7 us -> 7.35 us
  other arithmetic: 24.2 us -> 0.01 us
  blocking collectives: 0 us -> 16.2 us
  waiting for transfers between devices: 22.2 us -> 10.9 us
  Pallas kernels: 0 us -> 5.83 us
  starting transfers between devices: 36.2 us -> 30.7 us
  matrix products: 2.99 us -> 0 us
  between operations: 2.95 us -> 0.91 us
    unnamed x281 -> x33, local copies, waits for them, and re-layouts: 32.6 us -> 6.6 us
    all_to_all x0 -> x1, blocking collectives: none -> 16.2 us  [local(): everyone = lax.all_to_all(sent, AXES, 0, 0)]
    slice x74 -> x0, local copies, waits for them, and re-layouts: 12.7 us -> none  [the longest x21 5.28 us: following(): lax.slice_in_dim(field, 1, field.shape[axis], axis=axis)]
    squeeze x25 -> x0, local copies, waits for them, and re-layouts: 9.79 us -> none  [the longest x6 2.41 us: off_apply(): total = total + previous(stencil[2 + 2 * dim] * field, before, dim)]
    mul x54 -> x0, other arithmetic: 8.96 us -> none  [the longest x3 1.97 us: local(): mean = 0.5 * (sta_b[0:3] + face(mobilities, dim, False))]
    select_n x39 -> x0, other arithmetic: 7.89 us -> none  [the longest x14 3.85 us: swap(): one = lax.ppermute(jnp.where(even, last, first), AXES, pair_route(axis, 0))]
    ppermute x35, waiting for transfers between devices: 18.5 us -> 10.9 us  [swap(): lax.ppermute(b, AXES, pair_route(BY_DIM[dim], phase))]
    pallas_call x0 -> x9, Pallas kernels: none -> 5.83 us  [call(): pl.pallas_call(kernel, out_shape=list(outputs), scratch_shapes=[pltpu.VME...]
  transfers between devices with their start and end apart: 36 -> 35, of which waited for: 8 -> 9; matrix products, arithmetic and copies ran while one was open for 17% -> 1% of each run, Pallas kernels for 0% -> 0%
where the time goes in v2:
time: 72.3 us; the launch traced here: 71.9 us
  starting transfers between devices  30.7 us (42%)
  blocking collectives  16.2 us (22%)
  waiting for transfers between devices  10.9 us (15%)
  local copies, waits for them, and re-layouts  7.35 us (10%)
  Pallas kernels  5.83 us (8%)
  between operations  0.91 us (1%)
    ppermute x35, starting transfers between devices, swap(): lax.ppermute(b, AXES, pair_route(BY_DIM[dim], phase))  30.7 us
    all_to_all x1, blocking collectives, local(): everyone = lax.all_to_all(sent, AXES, 0, 0)  16.2 us
    ppermute x35, waiting for transfers between devices, swap(): lax.ppermute(b, AXES, pair_route(BY_DIM[dim], phase))  10.9 us
    unnamed x33, local copies, waits for them, and re-layouts  6.6 us
    pallas_call x9, Pallas kernels, call(): pl.pallas_call(kernel, out_shape=list(outputs), scratch_shapes=[pltpu.VME...  5.83 us
  transfers between devices with their start and end apart: 35, of which 9 were waited for; matrix products, arithmetic and copies ran while one was open for 1% of the time, Pallas kernels for 0%

profile of v2, /device:TPU:0, one launch (start us, length us, event | category | flops | bytes accessed | tf_op | source)
XLA Modules:
  0.0 71.9 jit_solution(16471861290256454810)
XLA Ops:
  0.7 1.1 %copy-done.2 = f32[9,8,16,128]{3,2,1,0:T(8,128)S(1)} copy-done((f32[9,8,16,128]{3,2,1,0:T(8,128)S(1)}, f32[9,8,16,128]{3,2,1,0:T(8,128)}, u32[]{:S(2)}) %copy-start.2) | copy-done | bytes 589848
  5.2 4.1 %collective-permute-start.1 = (f32[4,16,128]{2,1,0:T(8,128)S(1)}, f32[4,16,128]{2,1,0:T(8,128)S(1)}, u32[]{:S(2)}, u32[]{:S(2)}) collective-permute-start(f32[4,16,128]{2,1,0:T(8,128)S(1)} %get-tuple-element.53), channel_id=1, source_target_pairs={{0,1},{1,0},{2,3},{3,2},{4,5},{5,4},{6,7},{7,6},{8,9},{9,8},{10,11... | collective-permute-start | bytes 98312 | tf_op jit(solution)/shard_map/ppermute | solution.py:49
  9.4 1.5 %collective-permute-start.2 = (f32[4,8,128]{2,1,0:T(8,128)S(1)}, f32[4,8,128]{2,1,0:T(8,128)S(1)}, u32[]{:S(2)}, u32[]{:S(2)}) collective-permute-start(f32[4,8,128]{2,1,0:T(8,128)S(1)} %get-tuple-element.54), channel_id=1, source_target_pairs={{0,4},{1,5},{2,6},{3,7},{4,0},{5,1},{6,2},{7,3},{8,12},{9,13},{10,... | collective-permute-start | bytes 49160 | tf_op jit(solution)/shard_map/ppermute | solution.py:49
  11.0 1.5 %collective-permute-start.4 = (f32[8,128]{1,0:T(8,128)S(1)}, f32[8,128]{1,0:T(8,128)S(1)}, u32[]{:S(2)}, u32[]{:S(2)}) collective-permute-start(f32[8,128]{1,0:T(8,128)S(1)} %get-tuple-element.56), channel_id=1, source_target_pairs={{0,8},{1,9},{2,10},{3,11},{4,12},{5,13},{6,14},{7,15},{8,0},{9,1},... | collective-permute-start | bytes 12296 | tf_op jit(solution)/shard_map/ppermute | solution.py:49
  12.5 1.4 %collective-permute-done.3.rest_3_ = f32[8,128]{1,0:T(8,128)S(1)} collective-permute-done((f32[8,128]{1,0:T(8,128)S(1)}, f32[8,128]{1,0:T(8,128)S(1)}, u32[]{:S(2)}, u32[]{:S(2)}) %collective-permute-start.3) | collective-permute-done | bytes 4128 | tf_op jit(solution)/shard_map/ppermute | solution.py:49
  15.9 1.5 %collective-permute-start.6 = (f32[7,16,128]{2,1,0:T(8,128)S(1)}, f32[7,16,128]{2,1,0:T(8,128)S(1)}, u32[]{:S(2)}, u32[]{:S(2)}) collective-permute-start(f32[7,16,128]{2,1,0:T(8,128)S(1)} %get-tuple-element.60), channel_id=1, source_target_pairs={{0,1},{1,0},{2,3},{3,2},{4,5},{5,4},{6,7},{7,6},{8,9},{9,8},{10,11... | collective-permute-start | bytes 172040 | tf_op jit(solution)/shard_map/ppermute | solution.py:49
  18.5 1.3 %collective-permute-start.9 = (f32[8,128]{1,0:T(8,128)S(1)}, f32[8,128]{1,0:T(8,128)S(1)}, u32[]{:S(2)}, u32[]{:S(2)}) collective-permute-start(f32[8,128]{1,0:T(8,128)S(1)} %get-tuple-element.63), channel_id=1, source_target_pairs={{0,8},{1,9},{2,10},{3,11},{4,12},{5,13},{6,14},{7,15},{8,0},{9,1},... | collective-permute-start | bytes 12296 | tf_op jit(solution)/shard_map/ppermute | solution.py:49
  19.8 1.4 %collective-permute-done.8.rest_3_.rest_8_ = f32[8,128]{1,0:T(8,128)S(1)} collective-permute-done((f32[8,128]{1,0:T(8,128)S(1)}, f32[8,128]{1,0:T(8,128)S(1)}, u32[]{:S(2)}, u32[]{:S(2)}) %collective-permute-start.8) | collective-permute-done | bytes 4128 | tf_op jit(solution)/shard_map/ppermute | solution.py:49
  22.9 1.3 %collective-permute-start.12 = (f32[1,8,128]{2,1,0:T(8,128)S(1)}, f32[1,8,128]{2,1,0:T(8,128)S(1)}, u32[]{:S(2)}, u32[]{:S(2)}) collective-permute-start(f32[1,8,128]{2,1,0:T(8,128)S(1)} %get-tuple-element.67), channel_id=1, source_target_pairs={{0,4},{1,5},{2,6},{3,7},{4,0},{5,1},{6,2},{7,3},{8,12},{9,13},{10,... | collective-permute-start | bytes 12296 | tf_op jit(solution)/shard_map/ppermute | solution.py:49
  24.5 1.2 %collective-permute-start.14 = (f32[8,128]{1,0:T(8,128)S(1)}, f32[8,128]{1,0:T(8,128)S(1)}, u32[]{:S(2)}, u32[]{:S(2)}) collective-permute-start(f32[8,128]{1,0:T(8,128)S(1)} %get-tuple-element.69), channel_id=1, source_target_pairs={{0,8},{1,9},{2,10},{3,11},{4,12},{5,13},{6,14},{7,15},{8,0},{9,1},... | collective-permute-start | bytes 12296 | tf_op jit(solution)/shard_map/ppermute | solution.py:49
  27.6 1.5 %collective-permute-start.16 = (f32[1,16,128]{2,1,0:T(8,128)S(1)}, f32[1,16,128]{2,1,0:T(8,128)S(1)}, u32[]{:S(2)}, u32[]{:S(2)}) collective-permute-start(f32[1,16,128]{2,1,0:T(8,128)S(1)} %get-tuple-element.73), channel_id=1, source_target_pairs={{0,1},{1,0},{2,3},{3,2},{4,5},{5,4},{6,7},{7,6},{8,9},{9,8},{10,11... | collective-permute-start | bytes 24584 | tf_op jit(solution)/shard_map/ppermute | solution.py:49
  30.2 1.2 %collective-permute-start.19 = (f32[8,128]{1,0:T(8,128)S(1)}, f32[8,128]{1,0:T(8,128)S(1)}, u32[]{:S(2)}, u32[]{:S(2)}) collective-permute-start(f32[8,128]{1,0:T(8,128)S(1)} %get-tuple-element.76), channel_id=1, source_target_pairs={{0,8},{1,9},{2,10},{3,11},{4,12},{5,13},{6,14},{7,15},{8,0},{9,1},... | collective-permute-start | bytes 12296 | tf_op jit(solution)/shard_map/ppermute | solution.py:49
  33.4 1.2 %collective-permute-start.22 = (f32[2,4,128]{2,1,0:T(4,128)S(1)}, f32[2,4,128]{2,1,0:T(4,128)S(1)}, u32[]{:S(2)}, u32[]{:S(2)}) collective-permute-start(f32[2,4,128]{2,1,0:T(4,128)S(1)} %get-tuple-element.81), channel_id=1, source_target_pairs={{0,4},{1,5},{2,6},{3,7},{4,0},{5,1},{6,2},{7,3},{8,12},{9,13},{10,... | collective-permute-start | bytes 12296 | tf_op jit(solution)/shard_map/ppermute | solution.py:49
  34.7 1.3 %collective-permute-start.24 = (f32[8,128]{1,0:T(8,128)S(1)}, f32[8,128]{1,0:T(8,128)S(1)}, u32[]{:S(2)}, u32[]{:S(2)}) collective-permute-start(f32[8,128]{1,0:T(8,128)S(1)} %get-tuple-element.83), channel_id=1, source_target_pairs={{0,8},{1,9},{2,10},{3,11},{4,12},{5,13},{6,14},{7,15},{8,0},{9,1},... | collective-permute-start | bytes 12296 | tf_op jit(solution)/shard_map/ppermute | solution.py:49
  36.0 2.1 %collective-permute-start.21 = (f32[2,8,128]{2,1,0:T(8,128)S(1)}, f32[2,8,128]{2,1,0:T(8,128)S(1)}, u32[]{:S(2)}, u32[]{:S(2)}) collective-permute-start(f32[2,8,128]{2,1,0:T(8,128)S(1)} %get-tuple-element.80), channel_id=1, source_target_pairs={{0,1},{1,0},{2,3},{3,2},{4,5},{5,4},{6,7},{7,6},{8,9},{9,8},{10,11... | collective-permute-start | bytes 24584 | tf_op jit(solution)/shard_map/ppermute | solution.py:49
  38.1 1.6 %collective-permute-done.21.rest_1_ = f32[2,8,128]{2,1,0:T(8,128)S(1)} collective-permute-done((f32[2,8,128]{2,1,0:T(8,128)S(1)}, f32[2,8,128]{2,1,0:T(8,128)S(1)}, u32[]{:S(2)}, u32[]{:S(2)}) %collective-permute-start.21) | collective-permute-done | bytes 8224 | tf_op jit(solution)/shard_map/ppermute | solution.py:49
  40.0 16.2 %all_to_all.5.everyone = f32[32,20,128]{2,1,0:T(8,128)S(1)} all-to-all(f32[32,20,128]{2,1,0:T(8,128)S(1)} %get-tuple-element.84), channel_id=1, replica_groups=mesh['gx'=4,'gy'=2,'layer'=4] {'gx','gy','layer'}, dimensions={0} | all-to-all | bytes 655360 | tf_op jit(solution)/shard_map/all_to_all | solution.py:420
  56.2 1.3 %shard_map.140 = (f32[128,128]{1,0:T(8,128)S(1)}, f32[1,16,128]{2,1,0:T(8,128)S(1)}, f32[1,16,128]{2,1,0:T(8,128)S(1)}, f32[1,8,128]{2,1,0:T(8,128)S(1)}, f32[8,128]{1,0:T(8,128)S(1)}, /*index=5*/f32[8,128]{1,0:T(8,128)S(1)}) custom-call(f32[32,20,128]{2,1,0:T(8,128)S(1)} %all_to_all.5.everyone, f32[32,128]{1,0:T(8,128)S(1)} %get-tuple-element.77.b, ...), custom_call_target="tpu_custom_call" | custom-call | tf_op jit(solution)/shard_map/pallas_call | solution.py:241
  57.9 1.4 %collective-permute-start.26 = (f32[1,16,128]{2,1,0:T(8,128)S(1)}, f32[1,16,128]{2,1,0:T(8,128)S(1)}, u32[]{:S(2)}, u32[]{:S(2)}) collective-permute-start(f32[1,16,128]{2,1,0:T(8,128)S(1)} %get-tuple-element.88), channel_id=1, source_target_pairs={{0,1},{1,0},{2,3},{3,2},{4,5},{5,4},{6,7},{7,6},{8,9},{9,8},{10,11... | collective-permute-start | bytes 24584 | tf_op jit(solution)/shard_map/ppermute | solution.py:49
  60.7 2.1 %collective-permute-done.27.rest_2_ = f32[1,8,128]{2,1,0:T(8,128)S(1)} collective-permute-done((f32[1,8,128]{2,1,0:T(8,128)S(1)}, f32[1,8,128]{2,1,0:T(8,128)S(1)}, u32[]{:S(2)}, u32[]{:S(2)}) %collective-permute-start.27) | collective-permute-done | bytes 4128 | tf_op jit(solution)/shard_map/ppermute | solution.py:49
  64.1 1.1 %collective-permute-start.31 = (f32[3,16,128]{2,1,0:T(8,128)S(1)}, f32[3,16,128]{2,1,0:T(8,128)S(1)}, u32[]{:S(2)}, u32[]{:S(2)}) collective-permute-start(f32[3,16,128]{2,1,0:T(8,128)S(1)} %get-tuple-element.94), channel_id=1, source_target_pairs={{0,1},{1,0},{2,3},{3,2},{4,5},{5,4},{6,7},{7,6},{8,9},{9,8},{10,11... | collective-permute-start | bytes 73736 | tf_op jit(solution)/shard_map/ppermute | solution.py:49
  65.3 1.3 %collective-permute-start.32 = (f32[3,8,128]{2,1,0:T(8,128)S(1)}, f32[3,8,128]{2,1,0:T(8,128)S(1)}, u32[]{:S(2)}, u32[]{:S(2)}) collective-permute-start(f32[3,8,128]{2,1,0:T(8,128)S(1)} %get-tuple-element.95), channel_id=1, source_target_pairs={{0,4},{1,5},{2,6},{3,7},{4,0},{5,1},{6,2},{7,3},{8,12},{9,13},{10,... | collective-permute-start | bytes 36872 | tf_op jit(solution)/shard_map/ppermute | solution.py:49
  67.2 2.4 %collective-permute-done.33.rest_3_ = f32[8,128]{1,0:T(8,128)S(1)} collective-permute-done((f32[8,128]{1,0:T(8,128)S(1)}, f32[8,128]{1,0:T(8,128)S(1)}, u32[]{:S(2)}, u32[]{:S(2)}) %collective-permute-start.33) | collective-permute-done | bytes 4128 | tf_op jit(solution)/shard_map/ppermute | solution.py:49
  70.6 1.3 %shard_map.142 = f32[3,128,128]{2,1,0:T(8,128)} custom-call(f32[3,128,128]{2,1,0:T(8,128)S(1)} %copy-done.11, f32[3,128,128]{2,1,0:T(8,128)S(1)} %bitcast.38, f32[1,128,128]{2,1,0:T(8,128)S(1)} %bitcast.42, f32[3,128,128]{2,1,0:T(8,128)S(1)} %bitcast.36, f32[3,128,128]{2,1,0:T(8,128)S(1)} %get-tuple-element.58.trans_before, ...), custom_call_target="tpu_custom_call" | custom-call | tf_op jit(solution)/shard_map/pallas_call | solution.py:241
  (101 shorter events, 18.5 us)
Async XLA Ops:
  4.7 9.2 %collective-permute-start = (f32[4,16,128]{2,1,0:T(8,128)S(1)}, f32[4,16,128]{2,1,0:T(8,128)S(1)}, u32[]{:S(2)}, u32[]{:S(2)}) collective-permute-start(f32[4,16,128]{2,1,0:T(8,128)S(1)} %get-tuple-element.52), channel_id=1, source_target_pairs={{0,8},{1,2},{2,1},{3,11},{4,12},{5,6},{6,5},{7,15},{8,0},{9,10},{1... | collective-permute-start | bytes 98312 | tf_op jit(solution)/shard_map/ppermute | solution.py:49
  5.2 8.7 %collective-permute-start.1 = (f32[4,16,128]{2,1,0:T(8,128)S(1)}, f32[4,16,128]{2,1,0:T(8,128)S(1)}, u32[]{:S(2)}, u32[]{:S(2)}) collective-permute-start(f32[4,16,128]{2,1,0:T(8,128)S(1)} %get-tuple-element.53), channel_id=1, source_target_pairs={{0,1},{1,0},{2,3},{3,2},{4,5},{5,4},{6,7},{7,6},{8,9},{9,8},{10,11... | collective-permute-start | bytes 98312 | tf_op jit(solution)/shard_map/ppermute | solution.py:49
  9.4 4.5 %collective-permute-start.2 = (f32[4,8,128]{2,1,0:T(8,128)S(1)}, f32[4,8,128]{2,1,0:T(8,128)S(1)}, u32[]{:S(2)}, u32[]{:S(2)}) collective-permute-start(f32[4,8,128]{2,1,0:T(8,128)S(1)} %get-tuple-element.54), channel_id=1, source_target_pairs={{0,4},{1,5},{2,6},{3,7},{4,0},{5,1},{6,2},{7,3},{8,12},{9,13},{10,... | collective-permute-start | bytes 49160 | tf_op jit(solution)/shard_map/ppermute | solution.py:49
  15.8 5.6 %collective-permute-start.5 = (f32[7,16,128]{2,1,0:T(8,128)S(1)}, f32[7,16,128]{2,1,0:T(8,128)S(1)}, u32[]{:S(2)}, u32[]{:S(2)}) collective-permute-start(f32[7,16,128]{2,1,0:T(8,128)S(1)} %get-tuple-element.59), channel_id=1, source_target_pairs={{0,8},{1,2},{2,1},{3,11},{4,12},{5,6},{6,5},{7,15},{8,0},{9,10},{1... | collective-permute-start | bytes 172040 | tf_op jit(solution)/shard_map/ppermute | solution.py:49
  15.9 5.4 %collective-permute-start.6 = (f32[7,16,128]{2,1,0:T(8,128)S(1)}, f32[7,16,128]{2,1,0:T(8,128)S(1)}, u32[]{:S(2)}, u32[]{:S(2)}) collective-permute-start(f32[7,16,128]{2,1,0:T(8,128)S(1)} %get-tuple-element.60), channel_id=1, source_target_pairs={{0,1},{1,0},{2,3},{3,2},{4,5},{5,4},{6,7},{7,6},{8,9},{9,8},{10,11... | collective-permute-start | bytes 172040 | tf_op jit(solution)/shard_map/ppermute | solution.py:49
  17.5 3.9 %collective-permute-start.7 = (f32[7,8,128]{2,1,0:T(8,128)S(1)}, f32[7,8,128]{2,1,0:T(8,128)S(1)}, u32[]{:S(2)}, u32[]{:S(2)}) collective-permute-start(f32[7,8,128]{2,1,0:T(8,128)S(1)} %get-tuple-element.61), channel_id=1, source_target_pairs={{0,4},{1,5},{2,6},{3,7},{4,0},{5,1},{6,2},{7,3},{8,12},{9,13},{10,... | collective-permute-start | bytes 86024 | tf_op jit(solution)/shard_map/ppermute | solution.py:49
  21.9 5.3 %collective-permute-start.10 = (f32[1,16,128]{2,1,0:T(8,128)S(1)}, f32[1,16,128]{2,1,0:T(8,128)S(1)}, u32[]{:S(2)}, u32[]{:S(2)}) collective-permute-start(f32[1,16,128]{2,1,0:T(8,128)S(1)} %get-tuple-element.65), channel_id=1, source_target_pairs={{0,8},{1,2},{2,1},{3,11},{4,12},{5,6},{6,5},{7,15},{8,0},{9,10},{1... | collective-permute-start | bytes 24584 | tf_op jit(solution)/shard_map/ppermute | solution.py:49
  22.0 5.2 %collective-permute-start.11 = (f32[1,16,128]{2,1,0:T(8,128)S(1)}, f32[1,16,128]{2,1,0:T(8,128)S(1)}, u32[]{:S(2)}, u32[]{:S(2)}) collective-permute-start(f32[1,16,128]{2,1,0:T(8,128)S(1)} %get-tuple-element.66), channel_id=1, source_target_pairs={{0,1},{1,0},{2,3},{3,2},{4,5},{5,4},{6,7},{7,6},{8,9},{9,8},{10,11... | collective-permute-start | bytes 24584 | tf_op jit(solution)/shard_map/ppermute | solution.py:49
  22.9 3.6 %collective-permute-start.12 = (f32[1,8,128]{2,1,0:T(8,128)S(1)}, f32[1,8,128]{2,1,0:T(8,128)S(1)}, u32[]{:S(2)}, u32[]{:S(2)}) collective-permute-start(f32[1,8,128]{2,1,0:T(8,128)S(1)} %get-tuple-element.67), channel_id=1, source_target_pairs={{0,4},{1,5},{2,6},{3,7},{4,0},{5,1},{6,2},{7,3},{8,12},{9,13},{10,... | collective-permute-start | bytes 12296 | tf_op jit(solution)/shard_map/ppermute | solution.py:49
  24.1 3.0 %collective-permute-start.13 = (f32[8,128]{1,0:T(8,128)S(1)}, f32[8,128]{1,0:T(8,128)S(1)}, u32[]{:S(2)}, u32[]{:S(2)}) collective-permute-start(f32[8,128]{1,0:T(8,128)S(1)} %get-tuple-element.68), channel_id=1, source_target_pairs={{0,24},{1,25},{2,26},{3,27},{4,28},{5,29},{6,30},{7,31},{8,16},{9,... | collective-permute-start | bytes 12296 | tf_op jit(solution)/shard_map/ppermute | solution.py:49
  27.4 5.6 %collective-permute-start.15 = (f32[1,16,128]{2,1,0:T(8,128)S(1)}, f32[1,16,128]{2,1,0:T(8,128)S(1)}, u32[]{:S(2)}, u32[]{:S(2)}) collective-permute-start(f32[1,16,128]{2,1,0:T(8,128)S(1)} %get-tuple-element.72), channel_id=1, source_target_pairs={{0,8},{1,2},{2,1},{3,11},{4,12},{5,6},{6,5},{7,15},{8,0},{9,10},{1... | collective-permute-start | bytes 24584 | tf_op jit(solution)/shard_map/ppermute | solution.py:49
  27.6 5.5 %collective-permute-start.16 = (f32[1,16,128]{2,1,0:T(8,128)S(1)}, f32[1,16,128]{2,1,0:T(8,128)S(1)}, u32[]{:S(2)}, u32[]{:S(2)}) collective-permute-start(f32[1,16,128]{2,1,0:T(8,128)S(1)} %get-tuple-element.73), channel_id=1, source_target_pairs={{0,1},{1,0},{2,3},{3,2},{4,5},{5,4},{6,7},{7,6},{8,9},{9,8},{10,11... | collective-permute-start | bytes 24584 | tf_op jit(solution)/shard_map/ppermute | solution.py:49
  29.1 3.9 %collective-permute-start.17 = (f32[1,8,128]{2,1,0:T(8,128)S(1)}, f32[1,8,128]{2,1,0:T(8,128)S(1)}, u32[]{:S(2)}, u32[]{:S(2)}) collective-permute-start(f32[1,8,128]{2,1,0:T(8,128)S(1)} %get-tuple-element.74), channel_id=1, source_target_pairs={{0,4},{1,5},{2,6},{3,7},{4,0},{5,1},{6,2},{7,3},{8,12},{9,13},{10,... | collective-permute-start | bytes 12296 | tf_op jit(solution)/shard_map/ppermute | solution.py:49
  29.9 3.1 %collective-permute-start.18 = (f32[8,128]{1,0:T(8,128)S(1)}, f32[8,128]{1,0:T(8,128)S(1)}, u32[]{:S(2)}, u32[]{:S(2)}) collective-permute-start(f32[8,128]{1,0:T(8,128)S(1)} %get-tuple-element.75), channel_id=1, source_target_pairs={{0,24},{1,25},{2,26},{3,27},{4,28},{5,29},{6,30},{7,31},{8,16},{9,... | collective-permute-start | bytes 12296 | tf_op jit(solution)/shard_map/ppermute | solution.py:49
  33.4 4.7 %collective-permute-start.22 = (f32[2,4,128]{2,1,0:T(4,128)S(1)}, f32[2,4,128]{2,1,0:T(4,128)S(1)}, u32[]{:S(2)}, u32[]{:S(2)}) collective-permute-start(f32[2,4,128]{2,1,0:T(4,128)S(1)} %get-tuple-element.81), channel_id=1, source_target_pairs={{0,4},{1,5},{2,6},{3,7},{4,0},{5,1},{6,2},{7,3},{8,12},{9,13},{10,... | collective-permute-start | bytes 12296 | tf_op jit(solution)/shard_map/ppermute | solution.py:49
  34.6 3.5 %collective-permute-start.23 = (f32[8,128]{1,0:T(8,128)S(1)}, f32[8,128]{1,0:T(8,128)S(1)}, u32[]{:S(2)}, u32[]{:S(2)}) collective-permute-start(f32[8,128]{1,0:T(8,128)S(1)} %get-tuple-element.82), channel_id=1, source_target_pairs={{0,24},{1,25},{2,26},{3,27},{4,28},{5,29},{6,30},{7,31},{8,16},{9,... | collective-permute-start | bytes 12296 | tf_op jit(solution)/shard_map/ppermute | solution.py:49
  34.7 3.4 %collective-permute-start.24 = (f32[8,128]{1,0:T(8,128)S(1)}, f32[8,128]{1,0:T(8,128)S(1)}, u32[]{:S(2)}, u32[]{:S(2)}) collective-permute-start(f32[8,128]{1,0:T(8,128)S(1)} %get-tuple-element.83), channel_id=1, source_target_pairs={{0,8},{1,9},{2,10},{3,11},{4,12},{5,13},{6,14},{7,15},{8,0},{9,1},... | collective-permute-start | bytes 12296 | tf_op jit(solution)/shard_map/ppermute | solution.py:49
  36.0 3.7 %collective-permute-start.21 = (f32[2,8,128]{2,1,0:T(8,128)S(1)}, f32[2,8,128]{2,1,0:T(8,128)S(1)}, u32[]{:S(2)}, u32[]{:S(2)}) collective-permute-start(f32[2,8,128]{2,1,0:T(8,128)S(1)} %get-tuple-element.80), channel_id=1, source_target_pairs={{0,1},{1,0},{2,3},{3,2},{4,5},{5,4},{6,7},{7,6},{8,9},{9,8},{10,11... | collective-permute-start | bytes 24584 | tf_op jit(solution)/shard_map/ppermute | solution.py:49
  57.6 5.6 %collective-permute-start.25 = (f32[1,16,128]{2,1,0:T(8,128)S(1)}, f32[1,16,128]{2,1,0:T(8,128)S(1)}, u32[]{:S(2)}, u32[]{:S(2)}) collective-permute-start(f32[1,16,128]{2,1,0:T(8,128)S(1)} %get-tuple-element.87), channel_id=1, source_target_pairs={{0,8},{1,2},{2,1},{3,11},{4,12},{5,6},{6,5},{7,15},{8,0},{9,10},{1... | collective-permute-start | bytes 24584 | tf_op jit(solution)/shard_map/ppermute | solution.py:49
  57.9 5.3 %collective-permute-start.26 = (f32[1,16,128]{2,1,0:T(8,128)S(1)}, f32[1,16,128]{2,1,0:T(8,128)S(1)}, u32[]{:S(2)}, u32[]{:S(2)}) collective-permute-start(f32[1,16,128]{2,1,0:T(8,128)S(1)} %get-tuple-element.88), channel_id=1, source_target_pairs={{0,1},{1,0},{2,3},{3,2},{4,5},{5,4},{6,7},{7,6},{8,9},{9,8},{10,11... | collective-permute-start | bytes 24584 | tf_op jit(solution)/shard_map/ppermute | solution.py:49
  59.3 3.6 %collective-permute-start.27 = (f32[1,8,128]{2,1,0:T(8,128)S(1)}, f32[1,8,128]{2,1,0:T(8,128)S(1)}, u32[]{:S(2)}, u32[]{:S(2)}) collective-permute-start(f32[1,8,128]{2,1,0:T(8,128)S(1)} %get-tuple-element.89), channel_id=1, source_target_pairs={{0,4},{1,5},{2,6},{3,7},{4,0},{5,1},{6,2},{7,3},{8,12},{9,13},{10,... | collective-permute-start | bytes 12296 | tf_op jit(solution)/shard_map/ppermute | solution.py:49
  64.1 5.5 %collective-permute-start.30 = (f32[3,16,128]{2,1,0:T(8,128)S(1)}, f32[3,16,128]{2,1,0:T(8,128)S(1)}, u32[]{:S(2)}, u32[]{:S(2)}) collective-permute-start(f32[3,16,128]{2,1,0:T(8,128)S(1)} %get-tuple-element.93), channel_id=1, source_target_pairs={{0,8},{1,2},{2,1},{3,11},{4,12},{5,6},{6,5},{7,15},{8,0},{9,10},{1... | collective-permute-start | bytes 73736 | tf_op jit(solution)/shard_map/ppermute | solution.py:49
  64.1 5.5 %collective-permute-start.31 = (f32[3,16,128]{2,1,0:T(8,128)S(1)}, f32[3,16,128]{2,1,0:T(8,128)S(1)}, u32[]{:S(2)}, u32[]{:S(2)}) collective-permute-start(f32[3,16,128]{2,1,0:T(8,128)S(1)} %get-tuple-element.94), channel_id=1, source_target_pairs={{0,1},{1,0},{2,3},{3,2},{4,5},{5,4},{6,7},{7,6},{8,9},{9,8},{10,11... | collective-permute-start | bytes 73736 | tf_op jit(solution)/shard_map/ppermute | solution.py:49
  65.3 4.4 %collective-permute-start.32 = (f32[3,8,128]{2,1,0:T(8,128)S(1)}, f32[3,8,128]{2,1,0:T(8,128)S(1)}, u32[]{:S(2)}, u32[]{:S(2)}) collective-permute-start(f32[3,8,128]{2,1,0:T(8,128)S(1)} %get-tuple-element.95), channel_id=1, source_target_pairs={{0,4},{1,5},{2,6},{3,7},{4,0},{5,1},{6,2},{7,3},{8,12},{9,13},{10,... | collective-permute-start | bytes 36872 | tf_op jit(solution)/shard_map/ppermute | solution.py:49
  (27 other events, 104.3 us)

commit v3 on v2

--- a/solution.py
+++ b/solution.py
@@ -237,12 +237,21 @@
     return jnp.dot(a, b, precision=HIGHEST, preferred_element_type=F32)
 
 
-def call(kernel, inputs, outputs, scratch=()):
+def call(kernel, inputs, outputs, scratch=(), far_inputs=0, far_outputs=0):
+    inputs = list(inputs)
+    for i in range(far_inputs):
+        inputs[i] = pltpu.with_memory_space_constraint(inputs[i], pltpu.HBM)
+
+    def specs(count, far):
+        return [pl.BlockSpec(memory_space=pltpu.HBM if i < far else pltpu.VMEM) for i in range(count)]
+
     return pl.pallas_call(
         kernel,
         out_shape=list(outputs),
-        scratch_shapes=[pltpu.VMEM(shape, F32) for shape in scratch],
-        compiler_params=pltpu.CompilerParams(vmem_limit_bytes=40 * 2**20),
+        in_specs=specs(len(inputs), far_inputs),
+        out_specs=specs(len(outputs), far_outputs),
+        scratch_shapes=[pltpu.VMEM(shape, F32) if isinstance(shape, tuple) else shape for shape in scratch],
+        compiler_params=pltpu.CompilerParams(vmem_limit_bytes=24 * 2**20),
     )(*inputs)
 
 
@@ -289,17 +298,34 @@
     )
     pressure = pressure[None]
 
-    def start_kernel(source, active, frozen, trans, rhs_out, it_out, *buffers):
-        mask = active[...].astype(F32)
-        rhs = [source[c] * mask for c in range(3)]
+    def start_kernel(source, active, frozen, trans, rhs_out, it_out, frozen_out, trans_out, *rest):
+        buffers, (source_in, active_in, sems) = rest[:-3], rest[-3:]
+        order = [k for c in range(3) for k in (c, 3 + c, 6 + c)]
+        pairs = [(active, active_in), (source, source_in)] + [(frozen.at[k], frozen_out.at[k]) for k in order]
+        pairs.append((trans, trans_out))
+        copies = [pltpu.make_async_copy(a, b, sems.at[i]) for i, (a, b) in enumerate(pairs)]
+        for copy in copies:
+            copy.start()
+        copies[0].wait()
+        mask = active_in[...].astype(F32)
+        copies[1].wait()
+        rhs = [source_in[c] * mask for c in range(3)]
         for c in range(3):
             rhs_out[c] = rhs[c]
-            it_out[c] = block_row(frozen, c, rhs)
+        for c in range(3):
+            for copy in copies[2 + 3 * c : 5 + 3 * c]:
+                copy.wait()
+            it_out[c] = block_row(frozen_out, c, rhs)
+        copies[-1].wait()
         its = [(loader(it_out, c),) * 2 for c in range(3)]
-        fine.emit([its + [(loader(trans, dim),) * 2] for dim in range(3)], buffers)
-
-    rhs, iterate, *buffers = call(
-        start_kernel, (source, active, frozen, trans), [out(3, rows, LANES)] * 2 + fine.buffers(4)
+        fine.emit([its + [(loader(trans_out, dim),) * 2] for dim in range(3)], buffers)
+
+    rhs, iterate, frozen, trans, *buffers = call(
+        start_kernel,
+        (source, active, frozen, trans),
+        [out(3, rows, LANES)] * 2 + [out(9, rows, LANES), out(3, rows, LANES)] + fine.buffers(4),
+        [(3, rows, LANES), pltpu.VMEM((rows, LANES), jnp.int32), pltpu.SemaphoreType.DMA((12,))],
+        far_inputs=4,
     )
     got = swap(buffers)
 
@@ -538,7 +564,10 @@
     got = swap(buffers)
 
     def gradient_kernel(adj, mobility, pressure, trans, trans_before, *rest):
-        got, state_got, grad_out, (ends, state_ends) = rest[:swaps], rest[swaps : 2 * swaps], rest[2 * swaps], rest[-2:]
+        got, state_got, (adj_out, grad_out) = rest[:swaps], rest[swaps : 2 * swaps], rest[2 * swaps : 2 * swaps + 2]
+        ends, state_ends, grad, sems = rest[-4:]
+        copies = [pltpu.make_async_copy(adj, adj_out, sems.at[3])]
+        copies[0].start()
         adj_rims = fine.halos(got, 3, ends)
         state_rims = fine.halos(state_got, 7, state_ends)[3:]
         values = [adj[c] for c in range(3)]
@@ -553,13 +582,18 @@
 
             here = term(trans[dim], lambda rim, v: rim.following(v, dim))
             below = term(trans_before[dim], lambda rim, v: rim.previous(v, dim))
-            grad_out[dim] = 0.5 * (here + below)
-
-    (gradient,) = call(
+            grad[dim] = 0.5 * (here + below)
+            copies.append(pltpu.make_async_copy(grad.at[dim], grad_out.at[dim], sems.at[dim]))
+            copies[-1].start()
+        for copy in copies:
+            copy.wait()
+
+    adjoint, gradient = call(
         gradient_kernel,
         (adjoint, mobility, pressure, trans, trans_before, *got, *state_got),
-        [out(3, rows, LANES)],
-        [(3, rows, LANES), (7, rows, LANES)],
+        [out(3, rows, LANES)] * 2,
+        [(3, rows, LANES), (7, rows, LANES), (3, rows, LANES), pltpu.SemaphoreType.DMA((4,))],
+        far_outputs=2,
     )
     shape = (3, depth, height, width)
     return adjoint.reshape(shape), gradient.reshape(shape)

time: 72.3 us -> 66.8 us (0.924)
  local copies, waits for them, and re-layouts: 7.35 us -> 2.05 us
  blocking collectives: 16.2 us -> 15.2 us
  Pallas kernels: 5.83 us -> 6.74 us
    unnamed x33 -> x19, local copies, waits for them, and re-layouts: 6.6 us -> 1.29 us
    all_to_all x1, blocking collectives: 16.2 us -> 15.2 us  [local(): everyone = lax.all_to_all(sent, AXES, 0, 0)]
    pallas_call x9, Pallas kernels: 5.83 us -> 6.74 us  [call(): pl.pallas_call(kernel, out_shape=list(outputs), in_specs=specs(len(inputs...]
  transfers between devices with their start and end apart: 35 -> 35, of which waited for: 9 -> 10; matrix products, arithmetic and copies ran while one was open for 1% -> 1% of each run, Pallas kernels for 0% -> 0%
where the time goes in v3:
time: 66.8 us; the launch traced here: 66.5 us
  starting transfers between devices  30.2 us (45%)
  blocking collectives  15.2 us (23%)
  waiting for transfers between devices  11.4 us (17%)
  Pallas kernels  6.74 us (10%)
  local copies, waits for them, and re-layouts  2.05 us (3%)
  between operations  0.9 us (1%)
    ppermute x35, starting transfers between devices, swap(): lax.ppermute(b, AXES, pair_route(BY_DIM[dim], phase))  30.2 us
    all_to_all x1, blocking collectives, local(): everyone = lax.all_to_all(sent, AXES, 0, 0)  15.2 us
    ppermute x35, waiting for transfers between devices, swap(): lax.ppermute(b, AXES, pair_route(BY_DIM[dim], phase))  11.4 us
    pallas_call x9, Pallas kernels, call(): pl.pallas_call(kernel, out_shape=list(outputs), in_specs=specs(len(inputs...  6.74 us
  transfers between devices with their start and end apart: 35, of which 10 were waited for; matrix products, arithmetic and copies ran while one was open for 1% of the time, Pallas kernels for 0%

profile of v3, /device:TPU:0, one launch (start us, length us, event | category | flops | bytes accessed | tf_op | source)
XLA Modules:
  0.0 66.5 jit_solution(13518919922568500308)
XLA Ops:
  0.7 1.7 %shard_map.134 = (f32[3,128,128]{2,1,0:T(8,128)S(1)}, f32[3,128,128]{2,1,0:T(8,128)S(1)}, f32[9,128,128]{2,1,0:T(8,128)S(1)}, f32[3,128,128]{2,1,0:T(8,128)S(1)}...) custom-call(f32[3,128,128]{2,1,0:T(8,128)} %bitcast.38, ...), custom_call_target="tpu_custom_call" | custom-call | tf_op jit(solution)/shard_map/pallas_call | solution.py:248
  2.8 4.1 %collective-permute-start.1 = (f32[4,16,128]{2,1,0:T(8,128)S(1)}, f32[4,16,128]{2,1,0:T(8,128)S(1)}, u32[]{:S(2)}, u32[]{:S(2)}) collective-permute-start(f32[4,16,128]{2,1,0:T(8,128)S(1)} %get-tuple-element.59), channel_id=1, source_target_pairs={{0,1},{1,0},{2,3},{3,2},{4,5},{5,4},{6,7},{7,6},{8,9},{9,8},{10,11... | collective-permute-start | bytes 98312 | tf_op jit(solution)/shard_map/ppermute | solution.py:49
  7.0 1.5 %collective-permute-start.2 = (f32[4,8,128]{2,1,0:T(8,128)S(1)}, f32[4,8,128]{2,1,0:T(8,128)S(1)}, u32[]{:S(2)}, u32[]{:S(2)}) collective-permute-start(f32[4,8,128]{2,1,0:T(8,128)S(1)} %get-tuple-element.60), channel_id=1, source_target_pairs={{0,4},{1,5},{2,6},{3,7},{4,0},{5,1},{6,2},{7,3},{8,12},{9,13},{10,... | collective-permute-start | bytes 49160 | tf_op jit(solution)/shard_map/ppermute | solution.py:49
  8.6 1.5 %collective-permute-start.4 = (f32[8,128]{1,0:T(8,128)S(1)}, f32[8,128]{1,0:T(8,128)S(1)}, u32[]{:S(2)}, u32[]{:S(2)}) collective-permute-start(f32[8,128]{1,0:T(8,128)S(1)} %get-tuple-element.62), channel_id=1, source_target_pairs={{0,8},{1,9},{2,10},{3,11},{4,12},{5,13},{6,14},{7,15},{8,0},{9,1},... | collective-permute-start | bytes 12296 | tf_op jit(solution)/shard_map/ppermute | solution.py:49
  10.1 1.4 %collective-permute-done.3.rest_3_ = f32[8,128]{1,0:T(8,128)S(1)} collective-permute-done((f32[8,128]{1,0:T(8,128)S(1)}, f32[8,128]{1,0:T(8,128)S(1)}, u32[]{:S(2)}, u32[]{:S(2)}) %collective-permute-start.3) | collective-permute-done | bytes 4128 | tf_op jit(solution)/shard_map/ppermute | solution.py:49
  12.5 1.5 %collective-permute-start.6 = (f32[7,16,128]{2,1,0:T(8,128)S(1)}, f32[7,16,128]{2,1,0:T(8,128)S(1)}, u32[]{:S(2)}, u32[]{:S(2)}) collective-permute-start(f32[7,16,128]{2,1,0:T(8,128)S(1)} %get-tuple-element.66), channel_id=1, source_target_pairs={{0,1},{1,0},{2,3},{3,2},{4,5},{5,4},{6,7},{7,6},{8,9},{9,8},{10,11... | collective-permute-start | bytes 172040 | tf_op jit(solution)/shard_map/ppermute | solution.py:49
  15.1 1.3 %collective-permute-start.9 = (f32[8,128]{1,0:T(8,128)S(1)}, f32[8,128]{1,0:T(8,128)S(1)}, u32[]{:S(2)}, u32[]{:S(2)}) collective-permute-start(f32[8,128]{1,0:T(8,128)S(1)} %get-tuple-element.69), channel_id=1, source_target_pairs={{0,8},{1,9},{2,10},{3,11},{4,12},{5,13},{6,14},{7,15},{8,0},{9,1},... | collective-permute-start | bytes 12296 | tf_op jit(solution)/shard_map/ppermute | solution.py:49
  16.4 1.4 %collective-permute-done.8.rest_3_.rest_8_ = f32[8,128]{1,0:T(8,128)S(1)} collective-permute-done((f32[8,128]{1,0:T(8,128)S(1)}, f32[8,128]{1,0:T(8,128)S(1)}, u32[]{:S(2)}, u32[]{:S(2)}) %collective-permute-start.8) | collective-permute-done | bytes 4128 | tf_op jit(solution)/shard_map/ppermute | solution.py:49
  19.5 1.3 %collective-permute-start.12 = (f32[1,8,128]{2,1,0:T(8,128)S(1)}, f32[1,8,128]{2,1,0:T(8,128)S(1)}, u32[]{:S(2)}, u32[]{:S(2)}) collective-permute-start(f32[1,8,128]{2,1,0:T(8,128)S(1)} %get-tuple-element.73), channel_id=1, source_target_pairs={{0,4},{1,5},{2,6},{3,7},{4,0},{5,1},{6,2},{7,3},{8,12},{9,13},{10,... | collective-permute-start | bytes 12296 | tf_op jit(solution)/shard_map/ppermute | solution.py:49
  21.1 1.2 %collective-permute-start.14 = (f32[8,128]{1,0:T(8,128)S(1)}, f32[8,128]{1,0:T(8,128)S(1)}, u32[]{:S(2)}, u32[]{:S(2)}) collective-permute-start(f32[8,128]{1,0:T(8,128)S(1)} %get-tuple-element.75), channel_id=1, source_target_pairs={{0,8},{1,9},{2,10},{3,11},{4,12},{5,13},{6,14},{7,15},{8,0},{9,1},... | collective-permute-start | bytes 12296 | tf_op jit(solution)/shard_map/ppermute | solution.py:49
  24.2 1.5 %collective-permute-start.16 = (f32[1,16,128]{2,1,0:T(8,128)S(1)}, f32[1,16,128]{2,1,0:T(8,128)S(1)}, u32[]{:S(2)}, u32[]{:S(2)}) collective-permute-start(f32[1,16,128]{2,1,0:T(8,128)S(1)} %get-tuple-element.79), channel_id=1, source_target_pairs={{0,1},{1,0},{2,3},{3,2},{4,5},{5,4},{6,7},{7,6},{8,9},{9,8},{10,11... | collective-permute-start | bytes 24584 | tf_op jit(solution)/shard_map/ppermute | solution.py:49
  26.8 1.2 %collective-permute-start.19 = (f32[8,128]{1,0:T(8,128)S(1)}, f32[8,128]{1,0:T(8,128)S(1)}, u32[]{:S(2)}, u32[]{:S(2)}) collective-permute-start(f32[8,128]{1,0:T(8,128)S(1)} %get-tuple-element.82), channel_id=1, source_target_pairs={{0,8},{1,9},{2,10},{3,11},{4,12},{5,13},{6,14},{7,15},{8,0},{9,1},... | collective-permute-start | bytes 12296 | tf_op jit(solution)/shard_map/ppermute | solution.py:49
  30.5 2.1 %collective-permute-start.21 = (f32[2,8,128]{2,1,0:T(8,128)S(1)}, f32[2,8,128]{2,1,0:T(8,128)S(1)}, u32[]{:S(2)}, u32[]{:S(2)}) collective-permute-start(f32[2,8,128]{2,1,0:T(8,128)S(1)} %get-tuple-element.86), channel_id=1, source_target_pairs={{0,1},{1,0},{2,3},{3,2},{4,5},{5,4},{6,7},{7,6},{8,9},{9,8},{10,11... | collective-permute-start | bytes 24584 | tf_op jit(solution)/shard_map/ppermute | solution.py:49
  32.6 1.2 %collective-permute-start.22 = (f32[2,4,128]{2,1,0:T(4,128)S(1)}, f32[2,4,128]{2,1,0:T(4,128)S(1)}, u32[]{:S(2)}, u32[]{:S(2)}) collective-permute-start(f32[2,4,128]{2,1,0:T(4,128)S(1)} %get-tuple-element.87), channel_id=1, source_target_pairs={{0,4},{1,5},{2,6},{3,7},{4,0},{5,1},{6,2},{7,3},{8,12},{9,13},{10,... | collective-permute-start | bytes 12296 | tf_op jit(solution)/shard_map/ppermute | solution.py:49
  33.8 0.9 %collective-permute-start.24 = (f32[8,128]{1,0:T(8,128)S(1)}, f32[8,128]{1,0:T(8,128)S(1)}, u32[]{:S(2)}, u32[]{:S(2)}) collective-permute-start(f32[8,128]{1,0:T(8,128)S(1)} %get-tuple-element.89), channel_id=1, source_target_pairs={{0,8},{1,9},{2,10},{3,11},{4,12},{5,13},{6,14},{7,15},{8,0},{9,1},... | collective-permute-start | bytes 12296 | tf_op jit(solution)/shard_map/ppermute | solution.py:49
  34.7 1.4 %collective-permute-done.22.rest_2_ = f32[2,4,128]{2,1,0:T(4,128)S(1)} collective-permute-done((f32[2,4,128]{2,1,0:T(4,128)S(1)}, f32[2,4,128]{2,1,0:T(4,128)S(1)}, u32[]{:S(2)}, u32[]{:S(2)}) %collective-permute-start.22) | collective-permute-done | bytes 4128 | tf_op jit(solution)/shard_map/ppermute | solution.py:49
  37.1 15.2 %all_to_all.5.everyone = f32[32,20,128]{2,1,0:T(8,128)S(1)} all-to-all(f32[32,20,128]{2,1,0:T(8,128)S(1)} %get-tuple-element.90), channel_id=1, replica_groups=mesh['gx'=4,'gy'=2,'layer'=4] {'gx','gy','layer'}, dimensions={0} | all-to-all | bytes 655360 | tf_op jit(solution)/shard_map/all_to_all | solution.py:446
  52.3 1.3 %shard_map.140 = (f32[128,128]{1,0:T(8,128)S(1)}, f32[1,16,128]{2,1,0:T(8,128)S(1)}, f32[1,16,128]{2,1,0:T(8,128)S(1)}, f32[1,8,128]{2,1,0:T(8,128)S(1)}, f32[8,128]{1,0:T(8,128)S(1)}, /*index=5*/f32[8,128]{1,0:T(8,128)S(1)}) custom-call(f32[32,20,128]{2,1,0:T(8,128)S(1)} %all_to_all.5.everyone, f32[32,128]{1,0:T(8,128)S(1)} %get-tuple-element.83.b, ...), custom_call_target="tpu_custom_call" | custom-call | tf_op jit(solution)/shard_map/pallas_call | solution.py:248
  54.0 1.4 %collective-permute-start.26 = (f32[1,16,128]{2,1,0:T(8,128)S(1)}, f32[1,16,128]{2,1,0:T(8,128)S(1)}, u32[]{:S(2)}, u32[]{:S(2)}) collective-permute-start(f32[1,16,128]{2,1,0:T(8,128)S(1)} %get-tuple-element.94), channel_id=1, source_target_pairs={{0,1},{1,0},{2,3},{3,2},{4,5},{5,4},{6,7},{7,6},{8,9},{9,8},{10,11... | collective-permute-start | bytes 24584 | tf_op jit(solution)/shard_map/ppermute | solution.py:49
  56.8 2.1 %collective-permute-done.27.rest_2_ = f32[1,8,128]{2,1,0:T(8,128)S(1)} collective-permute-done((f32[1,8,128]{2,1,0:T(8,128)S(1)}, f32[1,8,128]{2,1,0:T(8,128)S(1)}, u32[]{:S(2)}, u32[]{:S(2)}) %collective-permute-start.27) | collective-permute-done | bytes 4128 | tf_op jit(solution)/shard_map/ppermute | solution.py:49
  59.7 1.1 %collective-permute-start.31 = (f32[3,16,128]{2,1,0:T(8,128)S(1)}, f32[3,16,128]{2,1,0:T(8,128)S(1)}, u32[]{:S(2)}, u32[]{:S(2)}) collective-permute-start(f32[3,16,128]{2,1,0:T(8,128)S(1)} %get-tuple-element.100), channel_id=1, source_target_pairs={{0,1},{1,0},{2,3},{3,2},{4,5},{5,4},{6,7},{7,6},{8,9},{9,8},{10,11... | collective-permute-start | bytes 73736 | tf_op jit(solution)/shard_map/ppermute | solution.py:49
  60.8 1.3 %collective-permute-start.32 = (f32[3,8,128]{2,1,0:T(8,128)S(1)}, f32[3,8,128]{2,1,0:T(8,128)S(1)}, u32[]{:S(2)}, u32[]{:S(2)}) collective-permute-start(f32[3,8,128]{2,1,0:T(8,128)S(1)} %get-tuple-element.101), channel_id=1, source_target_pairs={{0,4},{1,5},{2,6},{3,7},{4,0},{5,1},{6,2},{7,3},{8,12},{9,13},{10,... | collective-permute-start | bytes 36872 | tf_op jit(solution)/shard_map/ppermute | solution.py:49
  62.8 2.4 %collective-permute-done.33.rest_3_ = f32[8,128]{1,0:T(8,128)S(1)} collective-permute-done((f32[8,128]{1,0:T(8,128)S(1)}, f32[8,128]{1,0:T(8,128)S(1)}, u32[]{:S(2)}, u32[]{:S(2)}) %collective-permute-start.33) | collective-permute-done | bytes 4128 | tf_op jit(solution)/shard_map/ppermute | solution.py:49
  65.2 1.3 %shard_map.142 = (f32[3,128,128]{2,1,0:T(8,128)}, f32[3,128,128]{2,1,0:T(8,128)}) custom-call(f32[3,128,128]{2,1,0:T(8,128)S(1)} %get-tuple-element.98.adj, f32[3,128,128]{2,1,0:T(8,128)S(1)} %bitcast.30, f32[1,128,128]{2,1,0:T(8,128)S(1)} %bitcast.34, f32[3,128,128]{2,1,0:T(8,128)S(1)} %get-tuple-element.57.trans, ...), custom_call_target="tpu_custom_call" | custom-call | tf_op jit(solution)/shard_map/pallas_call | solution.py:248
  (87 shorter events, 14.1 us)
Async XLA Ops:
  2.3 9.2 %collective-permute-start = (f32[4,16,128]{2,1,0:T(8,128)S(1)}, f32[4,16,128]{2,1,0:T(8,128)S(1)}, u32[]{:S(2)}, u32[]{:S(2)}) collective-permute-start(f32[4,16,128]{2,1,0:T(8,128)S(1)} %get-tuple-element.58), channel_id=1, source_target_pairs={{0,8},{1,2},{2,1},{3,11},{4,12},{5,6},{6,5},{7,15},{8,0},{9,10},{1... | collective-permute-start | bytes 98312 | tf_op jit(solution)/shard_map/ppermute | solution.py:49
  2.8 8.7 %collective-permute-start.1 = (f32[4,16,128]{2,1,0:T(8,128)S(1)}, f32[4,16,128]{2,1,0:T(8,128)S(1)}, u32[]{:S(2)}, u32[]{:S(2)}) collective-permute-start(f32[4,16,128]{2,1,0:T(8,128)S(1)} %get-tuple-element.59), channel_id=1, source_target_pairs={{0,1},{1,0},{2,3},{3,2},{4,5},{5,4},{6,7},{7,6},{8,9},{9,8},{10,11... | collective-permute-start | bytes 98312 | tf_op jit(solution)/shard_map/ppermute | solution.py:49
  7.0 4.5 %collective-permute-start.2 = (f32[4,8,128]{2,1,0:T(8,128)S(1)}, f32[4,8,128]{2,1,0:T(8,128)S(1)}, u32[]{:S(2)}, u32[]{:S(2)}) collective-permute-start(f32[4,8,128]{2,1,0:T(8,128)S(1)} %get-tuple-element.60), channel_id=1, source_target_pairs={{0,4},{1,5},{2,6},{3,7},{4,0},{5,1},{6,2},{7,3},{8,12},{9,13},{10,... | collective-permute-start | bytes 49160 | tf_op jit(solution)/shard_map/ppermute | solution.py:49
  12.4 5.6 %collective-permute-start.5 = (f32[7,16,128]{2,1,0:T(8,128)S(1)}, f32[7,16,128]{2,1,0:T(8,128)S(1)}, u32[]{:S(2)}, u32[]{:S(2)}) collective-permute-start(f32[7,16,128]{2,1,0:T(8,128)S(1)} %get-tuple-element.65), channel_id=1, source_target_pairs={{0,8},{1,2},{2,1},{3,11},{4,12},{5,6},{6,5},{7,15},{8,0},{9,10},{1... | collective-permute-start | bytes 172040 | tf_op jit(solution)/shard_map/ppermute | solution.py:49
  12.5 5.4 %collective-permute-start.6 = (f32[7,16,128]{2,1,0:T(8,128)S(1)}, f32[7,16,128]{2,1,0:T(8,128)S(1)}, u32[]{:S(2)}, u32[]{:S(2)}) collective-permute-start(f32[7,16,128]{2,1,0:T(8,128)S(1)} %get-tuple-element.66), channel_id=1, source_target_pairs={{0,1},{1,0},{2,3},{3,2},{4,5},{5,4},{6,7},{7,6},{8,9},{9,8},{10,11... | collective-permute-start | bytes 172040 | tf_op jit(solution)/shard_map/ppermute | solution.py:49
  14.1 3.9 %collective-permute-start.7 = (f32[7,8,128]{2,1,0:T(8,128)S(1)}, f32[7,8,128]{2,1,0:T(8,128)S(1)}, u32[]{:S(2)}, u32[]{:S(2)}) collective-permute-start(f32[7,8,128]{2,1,0:T(8,128)S(1)} %get-tuple-element.67), channel_id=1, source_target_pairs={{0,4},{1,5},{2,6},{3,7},{4,0},{5,1},{6,2},{7,3},{8,12},{9,13},{10,... | collective-permute-start | bytes 86024 | tf_op jit(solution)/shard_map/ppermute | solution.py:49
  18.5 5.3 %collective-permute-start.10 = (f32[1,16,128]{2,1,0:T(8,128)S(1)}, f32[1,16,128]{2,1,0:T(8,128)S(1)}, u32[]{:S(2)}, u32[]{:S(2)}) collective-permute-start(f32[1,16,128]{2,1,0:T(8,128)S(1)} %get-tuple-element.71), channel_id=1, source_target_pairs={{0,8},{1,2},{2,1},{3,11},{4,12},{5,6},{6,5},{7,15},{8,0},{9,10},{1... | collective-permute-start | bytes 24584 | tf_op jit(solution)/shard_map/ppermute | solution.py:49
  18.6 5.2 %collective-permute-start.11 = (f32[1,16,128]{2,1,0:T(8,128)S(1)}, f32[1,16,128]{2,1,0:T(8,128)S(1)}, u32[]{:S(2)}, u32[]{:S(2)}) collective-permute-start(f32[1,16,128]{2,1,0:T(8,128)S(1)} %get-tuple-element.72), channel_id=1, source_target_pairs={{0,1},{1,0},{2,3},{3,2},{4,5},{5,4},{6,7},{7,6},{8,9},{9,8},{10,11... | collective-permute-start | bytes 24584 | tf_op jit(solution)/shard_map/ppermute | solution.py:49
  19.5 3.6 %collective-permute-start.12 = (f32[1,8,128]{2,1,0:T(8,128)S(1)}, f32[1,8,128]{2,1,0:T(8,128)S(1)}, u32[]{:S(2)}, u32[]{:S(2)}) collective-permute-start(f32[1,8,128]{2,1,0:T(8,128)S(1)} %get-tuple-element.73), channel_id=1, source_target_pairs={{0,4},{1,5},{2,6},{3,7},{4,0},{5,1},{6,2},{7,3},{8,12},{9,13},{10,... | collective-permute-start | bytes 12296 | tf_op jit(solution)/shard_map/ppermute | solution.py:49
  20.8 3.0 %collective-permute-start.13 = (f32[8,128]{1,0:T(8,128)S(1)}, f32[8,128]{1,0:T(8,128)S(1)}, u32[]{:S(2)}, u32[]{:S(2)}) collective-permute-start(f32[8,128]{1,0:T(8,128)S(1)} %get-tuple-element.74), channel_id=1, source_target_pairs={{0,24},{1,25},{2,26},{3,27},{4,28},{5,29},{6,30},{7,31},{8,16},{9,... | collective-permute-start | bytes 12296 | tf_op jit(solution)/shard_map/ppermute | solution.py:49
  24.1 6.1 %collective-permute-start.15 = (f32[1,16,128]{2,1,0:T(8,128)S(1)}, f32[1,16,128]{2,1,0:T(8,128)S(1)}, u32[]{:S(2)}, u32[]{:S(2)}) collective-permute-start(f32[1,16,128]{2,1,0:T(8,128)S(1)} %get-tuple-element.78), channel_id=1, source_target_pairs={{0,8},{1,2},{2,1},{3,11},{4,12},{5,6},{6,5},{7,15},{8,0},{9,10},{1... | collective-permute-start | bytes 24584 | tf_op jit(solution)/shard_map/ppermute | solution.py:49
  24.2 6.0 %collective-permute-start.16 = (f32[1,16,128]{2,1,0:T(8,128)S(1)}, f32[1,16,128]{2,1,0:T(8,128)S(1)}, u32[]{:S(2)}, u32[]{:S(2)}) collective-permute-start(f32[1,16,128]{2,1,0:T(8,128)S(1)} %get-tuple-element.79), channel_id=1, source_target_pairs={{0,1},{1,0},{2,3},{3,2},{4,5},{5,4},{6,7},{7,6},{8,9},{9,8},{10,11... | collective-permute-start | bytes 24584 | tf_op jit(solution)/shard_map/ppermute | solution.py:49
  25.7 4.4 %collective-permute-start.17 = (f32[1,8,128]{2,1,0:T(8,128)S(1)}, f32[1,8,128]{2,1,0:T(8,128)S(1)}, u32[]{:S(2)}, u32[]{:S(2)}) collective-permute-start(f32[1,8,128]{2,1,0:T(8,128)S(1)} %get-tuple-element.80), channel_id=1, source_target_pairs={{0,4},{1,5},{2,6},{3,7},{4,0},{5,1},{6,2},{7,3},{8,12},{9,13},{10,... | collective-permute-start | bytes 12296 | tf_op jit(solution)/shard_map/ppermute | solution.py:49
  26.5 3.6 %collective-permute-start.18 = (f32[8,128]{1,0:T(8,128)S(1)}, f32[8,128]{1,0:T(8,128)S(1)}, u32[]{:S(2)}, u32[]{:S(2)}) collective-permute-start(f32[8,128]{1,0:T(8,128)S(1)} %get-tuple-element.81), channel_id=1, source_target_pairs={{0,24},{1,25},{2,26},{3,27},{4,28},{5,29},{6,30},{7,31},{8,16},{9,... | collective-permute-start | bytes 12296 | tf_op jit(solution)/shard_map/ppermute | solution.py:49
  26.8 3.3 %collective-permute-start.19 = (f32[8,128]{1,0:T(8,128)S(1)}, f32[8,128]{1,0:T(8,128)S(1)}, u32[]{:S(2)}, u32[]{:S(2)}) collective-permute-start(f32[8,128]{1,0:T(8,128)S(1)} %get-tuple-element.82), channel_id=1, source_target_pairs={{0,8},{1,9},{2,10},{3,11},{4,12},{5,13},{6,14},{7,15},{8,0},{9,1},... | collective-permute-start | bytes 12296 | tf_op jit(solution)/shard_map/ppermute | solution.py:49
  30.5 6.4 %collective-permute-start.20 = (f32[2,8,128]{2,1,0:T(8,128)S(1)}, f32[2,8,128]{2,1,0:T(8,128)S(1)}, u32[]{:S(2)}, u32[]{:S(2)}) collective-permute-start(f32[2,8,128]{2,1,0:T(8,128)S(1)} %get-tuple-element.85), channel_id=1, source_target_pairs={{0,8},{1,2},{2,1},{3,11},{4,12},{5,6},{6,5},{7,15},{8,0},{9,10},{1... | collective-permute-start | bytes 24584 | tf_op jit(solution)/shard_map/ppermute | solution.py:49
  30.5 6.3 %collective-permute-start.21 = (f32[2,8,128]{2,1,0:T(8,128)S(1)}, f32[2,8,128]{2,1,0:T(8,128)S(1)}, u32[]{:S(2)}, u32[]{:S(2)}) collective-permute-start(f32[2,8,128]{2,1,0:T(8,128)S(1)} %get-tuple-element.86), channel_id=1, source_target_pairs={{0,1},{1,0},{2,3},{3,2},{4,5},{5,4},{6,7},{7,6},{8,9},{9,8},{10,11... | collective-permute-start | bytes 24584 | tf_op jit(solution)/shard_map/ppermute | solution.py:49
  32.6 3.6 %collective-permute-start.22 = (f32[2,4,128]{2,1,0:T(4,128)S(1)}, f32[2,4,128]{2,1,0:T(4,128)S(1)}, u32[]{:S(2)}, u32[]{:S(2)}) collective-permute-start(f32[2,4,128]{2,1,0:T(4,128)S(1)} %get-tuple-element.87), channel_id=1, source_target_pairs={{0,4},{1,5},{2,6},{3,7},{4,0},{5,1},{6,2},{7,3},{8,12},{9,13},{10,... | collective-permute-start | bytes 12296 | tf_op jit(solution)/shard_map/ppermute | solution.py:49
  53.6 5.6 %collective-permute-start.25 = (f32[1,16,128]{2,1,0:T(8,128)S(1)}, f32[1,16,128]{2,1,0:T(8,128)S(1)}, u32[]{:S(2)}, u32[]{:S(2)}) collective-permute-start(f32[1,16,128]{2,1,0:T(8,128)S(1)} %get-tuple-element.93), channel_id=1, source_target_pairs={{0,8},{1,2},{2,1},{3,11},{4,12},{5,6},{6,5},{7,15},{8,0},{9,10},{1... | collective-permute-start | bytes 24584 | tf_op jit(solution)/shard_map/ppermute | solution.py:49
  54.0 5.3 %collective-permute-start.26 = (f32[1,16,128]{2,1,0:T(8,128)S(1)}, f32[1,16,128]{2,1,0:T(8,128)S(1)}, u32[]{:S(2)}, u32[]{:S(2)}) collective-permute-start(f32[1,16,128]{2,1,0:T(8,128)S(1)} %get-tuple-element.94), channel_id=1, source_target_pairs={{0,1},{1,0},{2,3},{3,2},{4,5},{5,4},{6,7},{7,6},{8,9},{9,8},{10,11... | collective-permute-start | bytes 24584 | tf_op jit(solution)/shard_map/ppermute | solution.py:49
  55.3 3.6 %collective-permute-start.27 = (f32[1,8,128]{2,1,0:T(8,128)S(1)}, f32[1,8,128]{2,1,0:T(8,128)S(1)}, u32[]{:S(2)}, u32[]{:S(2)}) collective-permute-start(f32[1,8,128]{2,1,0:T(8,128)S(1)} %get-tuple-element.95), channel_id=1, source_target_pairs={{0,4},{1,5},{2,6},{3,7},{4,0},{5,1},{6,2},{7,3},{8,12},{9,13},{10,... | collective-permute-start | bytes 12296 | tf_op jit(solution)/shard_map/ppermute | solution.py:49
  59.6 5.6 %collective-permute-start.30 = (f32[3,16,128]{2,1,0:T(8,128)S(1)}, f32[3,16,128]{2,1,0:T(8,128)S(1)}, u32[]{:S(2)}, u32[]{:S(2)}) collective-permute-start(f32[3,16,128]{2,1,0:T(8,128)S(1)} %get-tuple-element.99), channel_id=1, source_target_pairs={{0,8},{1,2},{2,1},{3,11},{4,12},{5,6},{6,5},{7,15},{8,0},{9,10},{1... | collective-permute-start | bytes 73736 | tf_op jit(solution)/shard_map/ppermute | solution.py:49
  59.7 5.5 %collective-permute-start.31 = (f32[3,16,128]{2,1,0:T(8,128)S(1)}, f32[3,16,128]{2,1,0:T(8,128)S(1)}, u32[]{:S(2)}, u32[]{:S(2)}) collective-permute-start(f32[3,16,128]{2,1,0:T(8,128)S(1)} %get-tuple-element.100), channel_id=1, source_target_pairs={{0,1},{1,0},{2,3},{3,2},{4,5},{5,4},{6,7},{7,6},{8,9},{9,8},{10,11... | collective-permute-start | bytes 73736 | tf_op jit(solution)/shard_map/ppermute | solution.py:49
  60.8 4.4 %collective-permute-start.32 = (f32[3,8,128]{2,1,0:T(8,128)S(1)}, f32[3,8,128]{2,1,0:T(8,128)S(1)}, u32[]{:S(2)}, u32[]{:S(2)}) collective-permute-start(f32[3,8,128]{2,1,0:T(8,128)S(1)} %get-tuple-element.101), channel_id=1, source_target_pairs={{0,4},{1,5},{2,6},{3,7},{4,0},{5,1},{6,2},{7,3},{8,12},{9,13},{10,... | collective-permute-start | bytes 36872 | tf_op jit(solution)/shard_map/ppermute | solution.py:49
  (20 other events, 90.8 us)

commit v4 on v3

--- a/solution.py
+++ b/solution.py
@@ -53,66 +53,93 @@
     def __init__(self, depth, height, dup):
         self.depth, self.height, self.dup = depth, height, dup
         self.rows = depth * height
-
-    def buffers(self, channels):
-        shapes = ((channels, self.height, LANES), (channels, self.depth, LANES), (8, LANES))
-        return [jax.ShapeDtypeStruct(shapes[dim], F32) for dim, phase in sends()]
-
-    def emit(self, channels, out):
+        self.groups = self.rows // 8
+        self.stride = LANES // self.groups
+
+    def lines(self, dim):
+        return (self.height, self.depth)[dim]
+
+
+class Message:
+    def __init__(self, *parts):
+        self.parts = parts
+
+    def start(self, part, dim):
+        return sum(8 if dim == 2 else count * grid.lines(dim) for grid, count in self.parts[:part])
+
+    def buffers(self):
+        return [jax.ShapeDtypeStruct((self.start(len(self.parts), dim), LANES), F32) for dim, phase in sends()]
+
+    def emit(self, part, channels, out):
         out = dict(zip(sends(), out))
+        grid, count = self.parts[part]
         lane = lax.broadcasted_iota(jnp.int32, (8, LANES), 1)
         for dim in range(3):
             if phases(dim) == 0:
                 continue
             even = lax.axis_index(BY_DIM[dim]) % 2 == 0
+            start = self.start(part, dim)
             if dim == 2:
                 firsts, lasts = jnp.zeros((8, LANES), F32), jnp.zeros((8, LANES), F32)
                 for c, (first, last) in enumerate(channels[dim]):
-                    for k in range(self.rows // 8):
-                        at = 8 * k + self.dup * c
-                        here = (lane >= at) & (lane < at + self.dup)
+                    for k in range(grid.groups):
+                        at = grid.stride * k + grid.dup * c
+                        here = (lane >= at) & (lane < at + grid.dup)
                         rows = slice(8 * k, 8 * k + 8)
                         firsts = jnp.where(here, roll(first(rows), at, 1), firsts)
-                        lasts = jnp.where(here, roll(last(rows), at + self.dup, 1), lasts)
-                pairs = [(slice(None), firsts, lasts)]
+                        lasts = jnp.where(here, roll(last(rows), at + grid.dup, 1), lasts)
+                pairs = [(slice(start, start + 8), firsts, lasts)]
             else:
                 if dim == 0:
-                    low, high = slice(0, self.height), slice(self.rows - self.height, self.rows)
+                    low, high = slice(0, grid.height), slice(grid.rows - grid.height, grid.rows)
                 else:
-                    low, high = (pl.ds(s, self.depth, stride=self.height) for s in (0, self.height - 1))
-                pairs = [(c, first(low), last(high)) for c, (first, last) in enumerate(channels[dim])]
-            for c, first, last in pairs:
-                out[dim, 0][c] = jnp.where(even, last, first)
+                    low, high = (pl.ds(s, grid.depth, stride=grid.height) for s in (0, grid.height - 1))
+                n = grid.lines(dim)
+                pairs = [
+                    (slice(start + c * n, start + (c + 1) * n), first(low), last(high))
+                    for c, (first, last) in enumerate(channels[dim])
+                ]
+            for rows, first, last in pairs:
+                out[dim, 0][rows] = jnp.where(even, last, first)
                 if phases(dim) == 2:
-                    out[dim, 1][c] = jnp.where(even, first, last)
-
-    def halos(self, got, count, scratch):
+                    out[dim, 1][rows] = jnp.where(even, first, last)
+
+    def faces(self, part, got, channels=None):
         got = dict(zip(sends(), got))
-        result = [[None] * 3 for _ in range(count)]
+        grid, count = self.parts[part]
+        channels = range(count) if channels is None else channels
+        result = [[None] * 3 for _ in channels]
         for dim in range(3):
             me, n = lax.axis_index(BY_DIM[dim]), lax.axis_size(BY_DIM[dim])
             even = me % 2 == 0
-            for c in range(count if dim < 2 else 1):
-                key = c if dim < 2 else slice(None)
+            start = self.start(part, dim)
+
+            def both(rows):
                 if phases(dim) == 0:
-                    before = after = jnp.zeros((self.height, self.depth, 8)[dim : dim + 1] + (LANES,), F32)
-                elif phases(dim) == 1:
-                    one = got[dim, 0][key]
-                    before, after = jnp.where(even, 0.0, one), jnp.where(even, one, 0.0)
-                else:
-                    one, two = got[dim, 0][key], got[dim, 1][key]
-                    before, after = jnp.where(even, two, one), jnp.where(even, one, two)
-                    before, after = jnp.where(me > 0, before, 0.0), jnp.where(me < n - 1, after, 0.0)
-                if dim < 2:
-                    result[c][dim] = (before, after)
-                else:
-                    for ch in range(count):
-                        parts = []
-                        for side, start in ((before, 0), (after, LANES - self.dup)):
-                            pieces = [roll(side, start - 8 * k - self.dup * ch, 1) for k in range(self.rows // 8)]
-                            parts.append(jnp.concatenate(pieces))
-                        result[ch][dim] = tuple(parts)
-        return [Rim(self, r, scratch, c) for c, r in enumerate(result)]
+                    return (jnp.zeros((rows.stop - rows.start, LANES), F32),) * 2
+                one = got[dim, 0][rows]
+                if phases(dim) == 1:
+                    return jnp.where(even, 0.0, one), jnp.where(even, one, 0.0)
+                two = got[dim, 1][rows]
+                before, after = jnp.where(even, two, one), jnp.where(even, one, two)
+                return jnp.where(me > 0, before, 0.0), jnp.where(me < n - 1, after, 0.0)
+
+            if dim == 2:
+                sides = both(slice(start, start + 8))
+                for i, c in enumerate(channels):
+                    parts = []
+                    for side, lane in zip(sides, (0, LANES - grid.dup)):
+                        pieces = [roll(side, lane - grid.stride * k - grid.dup * c, 1) for k in range(grid.groups)]
+                        parts.append(jnp.concatenate(pieces))
+                    result[i][dim] = tuple(parts)
+            else:
+                size = grid.lines(dim)
+                for i, c in enumerate(channels):
+                    result[i][dim] = both(slice(start + c * size, start + (c + 1) * size))
+        return result
+
+    def halos(self, part, got, scratch, channels=None):
+        return [Rim(self.parts[part][0], r, scratch, c) for c, r in enumerate(self.faces(part, got, channels))]
 
 
 class Rim:
@@ -227,6 +254,23 @@
         wide = scratch[: 2 * count, :]
         tiles.append(jnp.concatenate([wide[2 * height * (a // 2) : 2 * height * (a // 2 + 1)] for a in range(2 * depth)]))
     return jnp.concatenate(tiles, axis=1)
+
+
+def spread_lines(value, scratch):
+    count = value.shape[0]
+    scratch[pl.ds(0, count, stride=2), :] = value
+    scratch[pl.ds(1, count, stride=2), :] = value
+    return scratch[: 2 * count, :]
+
+
+def fold(value):
+    half = value.shape[0] // 2
+    return jnp.where(lane_of(value[:half]) % 2 == 0, value[:half], value[half:])
+
+
+def unfold(value):
+    even = lane_of(value) % 2 == 0
+    return jnp.concatenate([jnp.where(even, value, roll(value, 1, 1)), jnp.where(even, roll(value, -1, 1), value)])
 
 
 def one_hot(shape, hit):
@@ -274,6 +318,12 @@
     sizes = [lax.axis_size(name) for name in AXES]
     count = sizes[0] * sizes[1] * sizes[2]
     swaps = len(sends())
+    first_round = Message((fine, 4))
+    second_round = Message((fine, 8), (mid, 1))
+    third_round = Message((fine, 1))
+    fourth_round = Message((fine, 1), (mid, 6))
+    fifth_round = Message((mid, 1))
+    last_round = Message((fine, 3))
     rows = fine.rows
 
     def flat(array):
@@ -318,20 +368,25 @@
             it_out[c] = block_row(frozen_out, c, rhs)
         copies[-1].wait()
         its = [(loader(it_out, c),) * 2 for c in range(3)]
-        fine.emit([its + [(loader(trans_out, dim),) * 2] for dim in range(3)], buffers)
+        first_round.emit(0, [its + [(loader(trans_out, dim),) * 2] for dim in range(3)], buffers)
 
     rhs, iterate, frozen, trans, *buffers = call(
         start_kernel,
         (source, active, frozen, trans),
-        [out(3, rows, LANES)] * 2 + [out(9, rows, LANES), out(3, rows, LANES)] + fine.buffers(4),
+        [out(3, rows, LANES)] * 2 + [out(9, rows, LANES), out(3, rows, LANES)] + first_round.buffers(),
         [(3, rows, LANES), pltpu.VMEM((rows, LANES), jnp.int32), pltpu.SemaphoreType.DMA((12,))],
         far_inputs=4,
     )
     got = swap(buffers)
 
-    def sweep_one(rhs, it, frozen, diag, trans, mobility, pressure, *rest):
-        got, (it_out, before_out), buffers, (ends,) = rest[:swaps], rest[swaps : swaps + 2], rest[swaps + 2 : -1], rest[-1:]
-        rims = fine.halos(got, 4, ends)
+    one = jnp.repeat(coarse_one.reshape(7, mid.rows, width // 2), 2, axis=2)
+
+    def coupling_faces(coefs):
+        return [[(loader(coefs, 1 + 2 * dim), loader(coefs, 2 + 2 * dim))] for dim in range(3)]
+
+    def sweep_one(rhs, it, frozen, diag, trans, mobility, pressure, stencil, one, *rest):
+        got, (it_out, before_out), buffers, ends = rest[:swaps], rest[swaps : swaps + 2], rest[swaps + 2 : -1], rest[-1]
+        rims = first_round.halos(0, got, ends)
         trans_before = [rims[3].previous(trans[dim], dim) for dim in range(3)]
         values = [it[c] for c in range(3)]
         rest = [rhs[c] - system_row(c, values, rims[c], diag, trans, trans_before) for c in range(3)]
@@ -340,60 +395,70 @@
             it_out[c] = values[c] + block_row(frozen, c, rest)
         channels = [(loader(it_out, c),) * 2 for c in range(3)]
         channels += [(loader(mobility, c),) * 2 for c in range(3)] + [(loader(pressure, 0),) * 2]
-        fine.emit([channels] * 3, buffers)
+        second_round.emit(0, [channels + faces for faces in coupling_faces(stencil)], buffers)
+        second_round.emit(1, coupling_faces(one), buffers)
 
     iterate, trans_before, *buffers = call(
         sweep_one,
-        (rhs, iterate, frozen, diag, trans, mobility, pressure, *got),
-        [out(3, rows, LANES)] * 2 + fine.buffers(7),
+        (rhs, iterate, frozen, diag, trans, mobility, pressure, stencil, one, *got),
+        [out(3, rows, LANES)] * 2 + second_round.buffers(),
         [(4, rows, LANES)],
     )
-    state_got = got = swap(buffers)
+    second_got = swap(buffers)
+
+    def couplings_kernel(stencil, one, *rest):
+        got, outs, scratch = rest[:swaps], rest[swaps : swaps + 2], rest[swaps + 2 :]
+        for part, channel, coefs, coupling, ends in ((0, 7, stencil, outs[0], scratch[0]), (1, 0, one, outs[1], scratch[1])):
+            (rim,) = second_round.halos(part, got, ends, [channel])
+            scale = OMEGA / coefs[0]
+            for dim in range(3):
+                coupling[2 * dim] = scale * rim.previous(coefs[2 + 2 * dim], dim)
+                coupling[2 * dim + 1] = scale * rim.following(coefs[1 + 2 * dim], dim)
+
+    fine_couplings, mid_couplings = call(
+        couplings_kernel,
+        (stencil, one, *second_got),
+        [out(6, rows, LANES), out(6, mid.rows, LANES)],
+        [(1, rows, LANES), (1, mid.rows, LANES)],
+    )
 
     def sweep_two(rhs, it, frozen, diag, trans, trans_before, *rest):
         got, it_out, buffers, ends = rest[:swaps], rest[swaps], rest[swaps + 1 : -1], rest[-1]
-        rims = fine.halos(got, 3, ends)
+        rims = second_round.halos(0, got, ends, range(3))
         values = [it[c] for c in range(3)]
         rest = [rhs[c] - system_row(c, values, rims[c], diag, trans, trans_before) for c in range(3)]
         for c in range(3):
             it_out[c] = values[c] + block_row(frozen, c, rest)
-        fine.emit([[(loader(it_out, 0),) * 2]] * 3, buffers)
+        third_round.emit(0, [[(loader(it_out, 0),) * 2]] * 3, buffers)
 
     iterate, *buffers = call(
         sweep_two,
-        (rhs, iterate, frozen, diag, trans, trans_before, *got),
-        [out(3, rows, LANES)] + fine.buffers(1),
+        (rhs, iterate, frozen, diag, trans, trans_before, *second_got),
+        [out(3, rows, LANES)] + third_round.buffers(),
         [(3, rows, LANES)],
     )
     got = swap(buffers)
 
-    def emit_products(grid, coefs, field, buffers, with_coefs=False):
-        channels = []
-        for dim in range(3):
-            pairs = [(product(coefs, 1 + 2 * dim, field), product(coefs, 2 + 2 * dim, field))]
-            if with_coefs:
-                pairs.append((loader(coefs, 1 + 2 * dim), loader(coefs, 2 + 2 * dim)))
-            channels.append(pairs)
-        grid.emit(channels, buffers)
-
-    def pressure_kernel(rhs, it, diag, trans, trans_before, stencil, *rest):
+    def products(coefs, field):
+        return [[(product(coefs, 1 + 2 * dim, field), product(coefs, 2 + 2 * dim, field))] for dim in range(3)]
+
+    def pressure_kernel(rhs, it, diag, trans, trans_before, stencil, mid_couplings, *rest):
         got, (b_out, x_out), buffers, ends = rest[:swaps], rest[swaps : swaps + 2], rest[swaps + 2 : -1], rest[-1]
-        (rim,) = fine.halos(got, 1, ends)
+        (rim,) = third_round.halos(0, got, ends)
         b = rhs[0] - system_row(0, [it[c] for c in range(3)], rim, diag, trans, trans_before)
         b_out[...] = b
         x_out[...] = b * (OMEGA / stencil[0])
-        emit_products(fine, stencil, x_out, buffers)
+        fourth_round.emit(0, products(stencil, x_out), buffers)
+        fourth_round.emit(1, [[(loader(mid_couplings, c),) * 2 for c in range(6)]] * 3, buffers)
 
     b_fine, x_fine, *buffers = call(
         pressure_kernel,
-        (rhs, iterate, diag, trans, trans_before, stencil, *got),
-        [out(rows, LANES)] * 2 + fine.buffers(1),
+        (rhs, iterate, diag, trans, trans_before, stencil, mid_couplings, *got),
+        [out(rows, LANES)] * 2 + fourth_round.buffers(),
         [(1, rows, LANES)],
     )
-    got = swap(buffers)
-
-    one = coarse_one.reshape(7, mid.rows, width // 2)
-    one = jnp.repeat(one, 2, axis=2)
+    fourth_got = swap(buffers)
+
     low_depth, low_height, low_width = coarse_two.shape[1:]
     groups = LANES // low_width
 
@@ -405,43 +470,109 @@
         return array.reshape(channels // groups * lead, LANES)
 
     packed = jnp.concatenate([pack(coarse_two, 8, 1), pack(coarse_three, 8, 2)])
-    block = packed.shape[0]
+    own_lines = mid.height // 2
+    face_at = packed.shape[0]
+    block = face_at + own_lines
     low_rows = low_depth * low_height
 
     def residual_kernel(b, x, stencil, one, *rest):
-        got, (b_out, x_out), buffers, (ends, temp) = rest[:swaps], rest[swaps : swaps + 2], rest[swaps + 2 : -2], rest[-2:]
-        (rim,) = fine.halos(got, 1, ends)
-        residual = (1.0 - OMEGA) * b[...] - off_apply(stencil, x[...], rim)
+        got, (b_out, x_out, q_out), buffers = rest[:swaps], rest[swaps : swaps + 3], rest[swaps + 3 : -2]
+        ends, temp = rest[-2:]
+        (rim,) = fourth_round.halos(0, got, ends, [0])
+        off = off_apply(stencil, x[...], rim)
+        residual = (1.0 - OMEGA) * b[...] - off
+        q_out[...] = (1.0 - OMEGA) * x[...] + (b[...] - off) * (OMEGA / stencil[0])
         coarse = pair_sum_rows(pair_sum_x(residual, 1), depth, height, temp)
         b_out[...] = coarse
         x_out[...] = coarse * (OMEGA / one[0])
-        emit_products(mid, one, x_out, buffers, True)
-
-    b_mid, x_mid, *buffers = call(
+        fifth_round.emit(0, products(one, x_out), buffers)
+
+    b_mid, x_mid, q_fine, *buffers = call(
         residual_kernel,
-        (b_fine, x_fine, stencil, one, *got),
-        [out(mid.rows, LANES)] * 2 + mid.buffers(2),
+        (b_fine, x_fine, stencil, one, *fourth_got),
+        [out(mid.rows, LANES)] * 2 + [out(rows, LANES)] + fifth_round.buffers(),
         [(1, rows, LANES), (rows // 2, LANES)],
     )
-    mid_got = got = swap(buffers)
+    got = swap(buffers)
+
+    rim_y = 4
+    line = mid.height + 2 * rim_y
+    window = (mid.depth + 4) * line
+
+    def fill_window(ref, own, faces):
+        for a in range(mid.depth):
+            at = (a + 2) * line + rim_y
+            ref[at : at + mid.height, :] = own[a * mid.height : (a + 1) * mid.height]
+        if faces is not None:
+            for a, value in ((1, faces[0][0]), (mid.depth + 2, faces[0][1])):
+                ref[a * line + rim_y : a * line + rim_y + mid.height, :] = value
+            for y, value in ((rim_y - 1, faces[1][0]), (rim_y + mid.height, faces[1][1])):
+                ref[pl.ds(2 * line + y, mid.depth, stride=line), :] = value
+
+    def beside_of(faces):
+        return jnp.where(lane_of(faces[0]) < LANES // 2, faces[0], faces[1])
+
+    def window_kernel(couplings, *rest):
+        got, (around, beside) = rest[:swaps], rest[swaps:]
+        around[...] = jnp.zeros(around.shape, F32)
+        beside[...] = jnp.zeros(beside.shape, F32)
+        for c, faces in enumerate(fourth_round.faces(1, got)):
+            fill_window(around.at[c], couplings[c], faces)
+            fill_window(beside.at[c], beside_of(faces[2]), None)
+
+    around_couplings, beside_couplings = call(
+        window_kernel, (mid_couplings, *fourth_got), [out(6, window, LANES)] * 2
+    )
+
+    def device(*steps):
+        at = [lax.axis_index(name) for name in AXES]
+        inside, flat = True, 0
+        for position, size, step in zip(at, sizes, steps):
+            inside = inside & (position + step >= 0) & (position + step < size)
+        for position, size, step in zip(at, sizes, steps):
+            flat = flat * size + jnp.where(inside, position + step, position)
+        return flat
+
+    steps = {(dim, sign): tuple(sign if name == BY_DIM[dim] else 0 for name in AXES) for dim in range(3) for sign in (-1, 1)}
+    x_step = mid.stride
 
     def low_kernel(b, x, one, packed, *rest):
-        got, (off_out, sent), (ends, temp) = rest[:swaps], rest[swaps : swaps + 2], rest[-2:]
-        rim, _ = mid.halos(got, 2, ends)
+        got, (q_out, sent), (ends, temp) = rest[:swaps], rest[swaps : swaps + 2], rest[-2:]
+        (rim,) = fifth_round.halos(0, got, ends, [0])
         off = off_apply(one, x[...], rim)
-        off_out[...] = off
         residual = (1.0 - OMEGA) * b[...] - off
+        q = (1.0 - OMEGA) * x[...] + (b[...] - off) * (OMEGA / one[0])
+        q_out[...] = q
         coarse = pair_sum_rows(residual, mid.depth, mid.height, temp)
         first = LANES - low_width
         place = one_hot((LANES, LANES), lambda i, j: (i // 4 == j - first) & (i % 2 == 0))
-        filled = jnp.concatenate([packed[:low_rows], packed[low_rows : 2 * low_rows] + matmul(coarse, place), packed[2 * low_rows :]])
+        filled = jnp.concatenate(
+            [
+                packed[:low_rows],
+                packed[low_rows : 2 * low_rows] + matmul(coarse, place),
+                packed[2 * low_rows :],
+                jnp.zeros((own_lines, LANES), F32),
+            ]
+        )
         sent[...] = jnp.broadcast_to(filled[None], (count, block, LANES))
-
-    off_mid, sent = call(
+        lane = lax.broadcasted_iota(jnp.int32, (8, LANES), 1)
+        for sign in (-1, 1):
+            value = fold(q[: mid.height] if sign < 0 else q[mid.rows - mid.height :])
+            sent[device(*steps[0, sign]), face_at : face_at + own_lines, :] = value
+            value = q_out[pl.ds(0 if sign < 0 else mid.height - 1, mid.depth, stride=mid.height), :]
+            sent[device(*steps[1, sign]), face_at : face_at + mid.depth, :] = value
+            value = jnp.zeros((8, LANES), F32)
+            for k in range(mid.groups):
+                at = x_step * k
+                here = (lane >= at) & (lane < at + 2)
+                value = jnp.where(here, roll(q[8 * k : 8 * k + 8], at if sign < 0 else at + 2, 1), value)
+            sent[device(*steps[2, sign]), face_at : face_at + 4, :] = value[:4] + roll(value[4:], 2, 1)
+
+    q_mid, sent = call(
         low_kernel,
         (b_mid, x_mid, one, packed, *got),
         [out(mid.rows, LANES), out(count, block, LANES)],
-        [(2, mid.rows, LANES), (mid.rows // 2, LANES)],
+        [(1, mid.rows, LANES), (mid.rows // 2, LANES)],
     )
     everyone = lax.all_to_all(sent, AXES, 0, 0)
 
@@ -491,75 +622,100 @@
         x = x + spread_rows(field, sizes[2] * low_depth // 2, three_height, temp)
         return (1.0 - OMEGA) * x + (b - off_apply(two, x, closed)) * scale
 
-    def up_kernel(everyone, b, x, off, one, x_fine, stencil, *rest):
-        got, field_out, buffers = rest[:swaps], rest[swaps], rest[swaps + 1 : -5]
-        ends, two, three, low_temp, temp = rest[-5:]
+    def smooth_mid(low, everyone, q, around_couplings, beside_couplings, q_around, q_beside):
+        gx, gy, gz = (lax.axis_index(name) for name in AXES)
+        q_around[...] = jnp.zeros((window, LANES), F32)
+        q_beside[...] = jnp.zeros((window, LANES), F32)
+        got = {key: everyone[device(*step), face_at : face_at + own_lines, :] for key, step in steps.items()}
+        layers = [unfold(got[0, sign]) for sign in (-1, 1)]
+        lines = [got[1, sign][: mid.depth] for sign in (-1, 1)]
+        sides = []
+        for sign, start in ((-1, 0), (1, LANES - 2)):
+            pieces = [roll(got[2, sign], start - x_step * k - 2 * half, 1) for k in range(mid.groups) for half in range(2)]
+            sides.append(jnp.concatenate(pieces))
+        fill_window(q_around, q, (layers, lines))
+        fill_window(q_beside, beside_of(sides), None)
+
+        def picked(i, j):
+            layer, y = i // (2 * line) - 1, i % line // 2 - rim_y // 2
+            return j == (gz * low_depth + layer) * two_height + gy * low_height + y
+
+        def columns(i, j):
+            own = (j < LANES) & (i == gx * low_width + j // 4)
+            before = (j >= LANES) & (j < LANES + 2) & (i == gx * low_width - 1)
+            after = (j >= 2 * LANES - 2) & (i == (gx + 1) * low_width)
+            return own | before | after
+
+        chosen = matmul(one_hot((window, two_rows), picked), low)
+        both = matmul(chosen, one_hot((two_width, 2 * LANES), columns))
+        around, beside = both[:, :LANES], both[:, LANES:]
+        lane = lane_of(around)
+        none = jnp.zeros((line, LANES), F32)
+        results = []
+        for value, q, couplings in ((around, q_around, around_couplings), (beside, q_beside, beside_couplings)):
+            if value is around:
+                shifts = [jnp.where(lane < 2, beside, roll(around, 2, 1)), jnp.where(lane >= LANES - 2, beside, roll(around, -2, 1))]
+            else:
+                shifts = [jnp.where(lane < LANES // 2, beside, around), jnp.where(lane < LANES // 2, around, beside)]
+            shifts = [roll(value, 1, 0), roll(value, -1, 0)] + shifts
+            shifts = [jnp.concatenate([none, value[:-line]]), jnp.concatenate([value[line:], none])] + shifts
+            total = q[...] + (1.0 - OMEGA) * value
+            for k in range(6):
+                total = total - couplings[k] * shifts[k]
+            results.append(total)
+        return results
+
+    def correct_fine(around, beside, q, couplings, ends, temp):
+        def own(ref):
+            lines = [ref[(a + 2) * line + rim_y : (a + 2) * line + rim_y + mid.height, :] for a in range(mid.depth)]
+            return spread_rows(jnp.concatenate(lines), mid.depth, mid.height, temp)
+
+        def layer(ref, a):
+            return spread_lines(ref[a * line + rim_y : a * line + rim_y + mid.height, :], temp)
+
+        def row(ref, y):
+            return spread_lines(ref[pl.ds(2 * line + y, mid.depth, stride=line), :], temp)
+
+        value, side = own(around), own(beside)
+        faces = [
+            (layer(around, 1), layer(around, mid.depth + 2)),
+            (row(around, rim_y - 1), row(around, rim_y + mid.height)),
+            (side, side),
+        ]
+        rim = Rim(fine, faces, ends, 0)
+        total = q + (1.0 - OMEGA) * value
+        for dim in range(3):
+            total = total - couplings[2 * dim] * rim.previous(value, dim)
+            total = total - couplings[2 * dim + 1] * rim.following(value, dim)
+        return total
+
+    def up_kernel(everyone, q_mid, around_couplings, beside_couplings, q_fine, fine_couplings, it, active, weights, *rest):
+        adj_out, buffers = rest[0], rest[1:-7]
+        ends, two, three, low_temp, temp, first, second = rest[-7:]
         assemble(everyone, two, three)
         low = solve_low(two, three, low_temp)
-        gx, gy, gz = (lax.axis_index(name) for name in AXES)
-        h, d = mid.height, mid.depth
-        own = one_hot((two_width, LANES), lambda i, j: i == gx * low_width + j // 4)
-        beside = one_hot(
-            (two_width, LANES),
-            lambda i, j: ((j < 2) & (i == gx * low_width - 1)) | ((j >= LANES - 2) & (i == (gx + 1) * low_width)),
-        )
-
-        def picked(n, layer, y):
-            def hit(i, j):
-                return j == (gz * low_depth + layer(i)) * two_height + gy * low_height + y(i)
-
-            return one_hot((n, two_rows), hit)
-
-        picks = jnp.concatenate(
-            [
-                picked(d * h, lambda i: i // h // 2, lambda i: i % h // 2),
-                picked(h, lambda i: -1, lambda i: i // 2),
-                picked(h, lambda i: low_depth, lambda i: i // 2),
-                picked(8, lambda i: i % d // 2, lambda i: jnp.where(i < d, -1, low_height)),
-            ]
-        )
-        chosen = matmul(picks, low)
-        around = matmul(chosen, own)
-        add = around[: d * h]
-        add_x = matmul(chosen[: d * h], beside)
-        _, coefs = mid.halos(got, 2, ends)
-        starts = d * h
-        faces = [
-            (coefs.faces[0][0] * around[starts : starts + h], coefs.faces[0][1] * around[starts + h : starts + 2 * h]),
-            (
-                coefs.faces[1][0] * around[starts + 2 * h : starts + 2 * h + d],
-                coefs.faces[1][1] * around[starts + 2 * h + d : starts + 2 * h + 2 * d],
-            ),
-            (coefs.faces[2][0] * add_x, coefs.faces[2][1] * add_x),
-        ]
-        off_all = off[...] + off_apply(one, add, Rim(mid, faces, ends, 0))
-        field = (1.0 - OMEGA) * (x[...] + add) + (b[...] - off_all) * (OMEGA / one[0])
-        field_out[...] = x_fine[...] + spread_rows(field, d, h, temp)
-        emit_products(fine, stencil, field_out, buffers)
-
-    field, *buffers = call(
-        up_kernel,
-        (everyone, b_mid, x_mid, off_mid, one, x_fine, stencil, *got),
-        [out(rows, LANES)] + fine.buffers(1),
-        [(2, mid.rows, LANES), (8, two_rows, two_width), (8, three_rows, two_width), (two_rows, LANES), (rows // 2, LANES)],
-    )
-    got = swap(buffers)
-
-    def adjoint_kernel(field, b, stencil, it, active, weights, *rest):
-        got, adj_out, buffers, ends = rest[:swaps], rest[swaps], rest[swaps + 1 : -1], rest[-1]
-        (rim,) = fine.halos(got, 1, ends)
-        value = field[...]
-        correction = (1.0 - OMEGA) * value + (b[...] - off_apply(stencil, value, rim)) * (OMEGA / stencil[0])
+        around, beside = smooth_mid(low, everyone, q_mid[...], around_couplings, beside_couplings, first, second)
+        first[...] = around
+        second[...] = beside
+        correction = correct_fine(first, second, q_fine[...], fine_couplings, ends, temp)
         mask = active[...].astype(F32)
         for c in range(3):
             adj_out[c] = mask * (it[c] + weights[c] * correction)
-        fine.emit([[(loader(adj_out, c),) * 2 for c in range(3)]] * 3, buffers)
+        last_round.emit(0, [[(loader(adj_out, c),) * 2 for c in range(3)]] * 3, buffers)
 
     adjoint, *buffers = call(
-        adjoint_kernel,
-        (field, b_fine, stencil, iterate, active, weights, *got),
-        [out(3, rows, LANES)] + fine.buffers(3),
-        [(1, rows, LANES)],
+        up_kernel,
+        (everyone, q_mid, around_couplings, beside_couplings, q_fine, fine_couplings, iterate, active, weights),
+        [out(3, rows, LANES)] + last_round.buffers(),
+        [
+            (1, rows, LANES),
+            (8, two_rows, two_width),
+            (8, three_rows, two_width),
+            (two_rows, LANES),
+            (rows // 2, LANES),
+            (window, LANES),
+            (window, LANES),
+        ],
     )
     got = swap(buffers)
 
@@ -568,8 +724,8 @@
         ends, state_ends, grad, sems = rest[-4:]
         copies = [pltpu.make_async_copy(adj, adj_out, sems.at[3])]
         copies[0].start()
-        adj_rims = fine.halos(got, 3, ends)
-        state_rims = fine.halos(state_got, 7, state_ends)[3:]
+        adj_rims = last_round.halos(0, got, ends)
+        state_rims = second_round.halos(0, state_got, state_ends, range(3, 7))
         values = [adj[c] for c in range(3)]
         for dim in range(3):
 
@@ -590,9 +746,9 @@
 
     adjoint, gradient = call(
         gradient_kernel,
-        (adjoint, mobility, pressure, trans, trans_before, *got, *state_got),
+        (adjoint, mobility, pressure, trans, trans_before, *got, *second_got),
         [out(3, rows, LANES)] * 2,
-        [(3, rows, LANES), (7, rows, LANES), (3, rows, LANES), pltpu.SemaphoreType.DMA((4,))],
+        [(3, rows, LANES), (4, rows, LANES), (3, rows, LANES), pltpu.SemaphoreType.DMA((4,))],
         far_outputs=2,
     )
     shape = (3, depth, height, width)

time: 66.8 us -> 62.2 us (0.931)
  blocking collectives: 15.2 us -> 0 us
  waiting for transfers between devices: 11.4 us -> 21.4 us
  Pallas kernels: 6.74 us -> 7.7 us
    all_to_all x1 -> x0, blocking collectives: 15.2 us -> none  [local(): everyone = lax.all_to_all(sent, AXES, 0, 0)]
    all_to_all x0 -> x1, waiting for transfers between devices: none -> 13 us  [local(): everyone = lax.all_to_all(sent, AXES, 0, 0)]
    ppermute x35 -> x30, waiting for transfers between devices: 11.4 us -> 8.41 us  [swap(): lax.ppermute(b, AXES, pair_route(BY_DIM[dim], phase))]
    all_to_all x0 -> x1, starting transfers between devices: none -> 2.81 us  [local(): everyone = lax.all_to_all(sent, AXES, 0, 0)]
    ppermute x35 -> x30, starting transfers between devices: 30.2 us -> 27.6 us  [swap(): lax.ppermute(b, AXES, pair_route(BY_DIM[dim], phase))]
    pallas_call x9 -> x10, Pallas kernels: 6.74 us -> 7.7 us  [call(): pl.pallas_call(kernel, out_shape=list(outputs), in_specs=specs(len(inputs...]
  transfers between devices with their start and end apart: 35 -> 31, of which waited for: 10 -> 10; matrix products, arithmetic and copies ran while one was open for 1% -> 1% of each run, Pallas kernels for 0% -> 1%
where the time goes in v4:
time: 62.2 us; the launch traced here: 61.9 us
  starting transfers between devices  30.4 us (49%)
  waiting for transfers between devices  21.4 us (34%)
  Pallas kernels  7.7 us (12%)
  local copies, waits for them, and re-layouts  1.53 us (2%)
  between operations  0.87 us (1%)
    ppermute x30, starting transfers between devices, swap(): lax.ppermute(b, AXES, pair_route(BY_DIM[dim], phase))  27.6 us
    all_to_all x1, waiting for transfers between devices, local(): everyone = lax.all_to_all(sent, AXES, 0, 0)  13 us
    ppermute x30, waiting for transfers between devices, swap(): lax.ppermute(b, AXES, pair_route(BY_DIM[dim], phase))  8.41 us
    pallas_call x10, Pallas kernels, call(): pl.pallas_call(kernel, out_shape=list(outputs), in_specs=specs(len(inputs...  7.7 us
    all_to_all x1, starting transfers between devices, local(): everyone = lax.all_to_all(sent, AXES, 0, 0)  2.81 us
  transfers between devices with their start and end apart: 31, of which 10 were waited for; matrix products, arithmetic and copies ran while one was open for 1% of the time, Pallas kernels for 1%

profile of v4, /device:TPU:0, one launch (start us, length us, event | category | flops | bytes accessed | tf_op | source)
XLA Modules:
  0.0 61.9 jit_solution(7396218502351984227)
XLA Ops:
  0.6 1.6 %shard_map.134 = (f32[3,128,128]{2,1,0:T(8,128)S(1)}, f32[3,128,128]{2,1,0:T(8,128)S(1)}, f32[9,128,128]{2,1,0:T(8,128)S(1)}, f32[3,128,128]{2,1,0:T(8,128)S(1)}...) custom-call(f32[3,128,128]{2,1,0:T(8,128)} %bitcast.38, ...), custom_call_target="tpu_custom_call" | custom-call | tf_op jit(solution)/shard_map/pallas_call | solution.py:292
  2.8 4.1 %collective-permute-start.1 = (f32[64,128]{1,0:T(8,128)S(1)}, f32[64,128]{1,0:T(8,128)S(1)}, u32[]{:S(2)}, u32[]{:S(2)}) collective-permute-start(f32[64,128]{1,0:T(8,128)S(1)} %get-tuple-element.58), channel_id=1, source_target_pairs={{0,1},{1,0},{2,3},{3,2},{4,5},{5,4},{6,7},{7,6},{8,9},{9,8},{10,11... | collective-permute-start | bytes 98312 | tf_op jit(solution)/shard_map/ppermute | solution.py:49
  6.9 1.5 %collective-permute-start.2 = (f32[32,128]{1,0:T(8,128)S(1)}, f32[32,128]{1,0:T(8,128)S(1)}, u32[]{:S(2)}, u32[]{:S(2)}) collective-permute-start(f32[32,128]{1,0:T(8,128)S(1)} %get-tuple-element.59), channel_id=1, source_target_pairs={{0,4},{1,5},{2,6},{3,7},{4,0},{5,1},{6,2},{7,3},{8,12},{9,13},{10,... | collective-permute-start | bytes 49160 | tf_op jit(solution)/shard_map/ppermute | solution.py:49
  8.6 1.5 %collective-permute-start.4 = (f32[8,128]{1,0:T(8,128)S(1)}, f32[8,128]{1,0:T(8,128)S(1)}, u32[]{:S(2)}, u32[]{:S(2)}) collective-permute-start(f32[8,128]{1,0:T(8,128)S(1)} %get-tuple-element.61), channel_id=1, source_target_pairs={{0,8},{1,9},{2,10},{3,11},{4,12},{5,13},{6,14},{7,15},{8,0},{9,1},... | collective-permute-start | bytes 12296 | tf_op jit(solution)/shard_map/ppermute | solution.py:49
  10.6 0.9 %collective-permute-done.3.rest_3_ = f32[8,128]{1,0:T(8,128)S(1)} collective-permute-done((f32[8,128]{1,0:T(8,128)S(1)}, f32[8,128]{1,0:T(8,128)S(1)}, u32[]{:S(2)}, u32[]{:S(2)}) %collective-permute-start.3) | collective-permute-done | bytes 4128 | tf_op jit(solution)/shard_map/ppermute | solution.py:49
  12.5 1.5 %collective-permute-start.6 = (f32[136,128]{1,0:T(8,128)S(1)}, f32[136,128]{1,0:T(8,128)S(1)}, u32[]{:S(2)}, u32[]{:S(2)}) collective-permute-start(f32[136,128]{1,0:T(8,128)S(1)} %get-tuple-element.65), channel_id=1, source_target_pairs={{0,1},{1,0},{2,3},{3,2},{4,5},{5,4},{6,7},{7,6},{8,9},{9,8},{10,11... | collective-permute-start | bytes 208904 | tf_op jit(solution)/shard_map/ppermute | solution.py:49
  15.0 1.3 %collective-permute-start.9 = (f32[16,128]{1,0:T(8,128)S(1)}, f32[16,128]{1,0:T(8,128)S(1)}, u32[]{:S(2)}, u32[]{:S(2)}) collective-permute-start(f32[16,128]{1,0:T(8,128)S(1)} %get-tuple-element.68), channel_id=1, source_target_pairs={{0,8},{1,9},{2,10},{3,11},{4,12},{5,13},{6,14},{7,15},{8,0},{9,1},... | collective-permute-start | bytes 24584 | tf_op jit(solution)/shard_map/ppermute | solution.py:49
  16.4 1.5 %collective-permute-done.8.rest_3_.rest_8_ = f32[16,128]{1,0:T(8,128)S(1)} collective-permute-done((f32[16,128]{1,0:T(8,128)S(1)}, f32[16,128]{1,0:T(8,128)S(1)}, u32[]{:S(2)}, u32[]{:S(2)}) %collective-permute-start.8) | collective-permute-done | bytes 8224 | tf_op jit(solution)/shard_map/ppermute | solution.py:49
  18.5 0.9 %collective-permute-start.11 = (f32[16,128]{1,0:T(8,128)S(1)}, f32[16,128]{1,0:T(8,128)S(1)}, u32[]{:S(2)}, u32[]{:S(2)}) collective-permute-start(f32[16,128]{1,0:T(8,128)S(1)} %get-tuple-element.72), channel_id=1, source_target_pairs={{0,1},{1,0},{2,3},{3,2},{4,5},{5,4},{6,7},{7,6},{8,9},{9,8},{10,11... | collective-permute-start | bytes 24584 | tf_op jit(solution)/shard_map/ppermute | solution.py:49
  19.5 1.3 %collective-permute-start.12 = (f32[8,128]{1,0:T(8,128)S(1)}, f32[8,128]{1,0:T(8,128)S(1)}, u32[]{:S(2)}, u32[]{:S(2)}) collective-permute-start(f32[8,128]{1,0:T(8,128)S(1)} %get-tuple-element.73), channel_id=1, source_target_pairs={{0,4},{1,5},{2,6},{3,7},{4,0},{5,1},{6,2},{7,3},{8,12},{9,13},{10,... | collective-permute-start | bytes 12296 | tf_op jit(solution)/shard_map/ppermute | solution.py:49
  21.0 1.2 %collective-permute-start.14 = (f32[8,128]{1,0:T(8,128)S(1)}, f32[8,128]{1,0:T(8,128)S(1)}, u32[]{:S(2)}, u32[]{:S(2)}) collective-permute-start(f32[8,128]{1,0:T(8,128)S(1)} %get-tuple-element.75), channel_id=1, source_target_pairs={{0,8},{1,9},{2,10},{3,11},{4,12},{5,13},{6,14},{7,15},{8,0},{9,1},... | collective-permute-start | bytes 12296 | tf_op jit(solution)/shard_map/ppermute | solution.py:49
  24.2 1.6 %collective-permute-start.16 = (f32[64,128]{1,0:T(8,128)S(1)}, f32[64,128]{1,0:T(8,128)S(1)}, u32[]{:S(2)}, u32[]{:S(2)}) collective-permute-start(f32[64,128]{1,0:T(8,128)S(1)} %get-tuple-element.79), channel_id=1, source_target_pairs={{0,1},{1,0},{2,3},{3,2},{4,5},{5,4},{6,7},{7,6},{8,9},{9,8},{10,11... | collective-permute-start | bytes 98312 | tf_op jit(solution)/shard_map/ppermute | solution.py:49
  26.8 1.2 %collective-permute-start.19 = (f32[16,128]{1,0:T(8,128)S(1)}, f32[16,128]{1,0:T(8,128)S(1)}, u32[]{:S(2)}, u32[]{:S(2)}) collective-permute-start(f32[16,128]{1,0:T(8,128)S(1)} %get-tuple-element.82), channel_id=1, source_target_pairs={{0,8},{1,9},{2,10},{3,11},{4,12},{5,13},{6,14},{7,15},{8,0},{9,1},... | collective-permute-start | bytes 24584 | tf_op jit(solution)/shard_map/ppermute | solution.py:49
  30.0 1.2 %collective-permute-start.22 = (f32[4,128]{1,0:T(4,128)S(1)}, f32[4,128]{1,0:T(4,128)S(1)}, u32[]{:S(2)}, u32[]{:S(2)}) collective-permute-start(f32[4,128]{1,0:T(4,128)S(1)} %get-tuple-element.87), channel_id=1, source_target_pairs={{0,4},{1,5},{2,6},{3,7},{4,0},{5,1},{6,2},{7,3},{8,12},{9,13},{10,... | collective-permute-start | bytes 6152 | tf_op jit(solution)/shard_map/ppermute | solution.py:49
  31.2 2.1 %collective-permute-start.21 = (f32[8,128]{1,0:T(8,128)S(1)}, f32[8,128]{1,0:T(8,128)S(1)}, u32[]{:S(2)}, u32[]{:S(2)}) collective-permute-start(f32[8,128]{1,0:T(8,128)S(1)} %get-tuple-element.86), channel_id=1, source_target_pairs={{0,1},{1,0},{2,3},{3,2},{4,5},{5,4},{6,7},{7,6},{8,9},{9,8},{10,11... | collective-permute-start | bytes 12296 | tf_op jit(solution)/shard_map/ppermute | solution.py:49
  33.6 1.2 %collective-permute-start.24 = (f32[8,128]{1,0:T(8,128)S(1)}, f32[8,128]{1,0:T(8,128)S(1)}, u32[]{:S(2)}, u32[]{:S(2)}) collective-permute-start(f32[8,128]{1,0:T(8,128)S(1)} %get-tuple-element.89), channel_id=1, source_target_pairs={{0,8},{1,9},{2,10},{3,11},{4,12},{5,13},{6,14},{7,15},{8,0},{9,1},... | collective-permute-start | bytes 12296 | tf_op jit(solution)/shard_map/ppermute | solution.py:49
  34.9 1.4 %collective-permute-done.23.rest_3_ = f32[8,128]{1,0:T(8,128)S(1)} collective-permute-done((f32[8,128]{1,0:T(8,128)S(1)}, f32[8,128]{1,0:T(8,128)S(1)}, u32[]{:S(2)}, u32[]{:S(2)}) %collective-permute-start.23) | collective-permute-done | bytes 4128 | tf_op jit(solution)/shard_map/ppermute | solution.py:49
  36.3 1.0 %shard_map.140 = (f32[32,128]{1,0:T(8,128)S(1)}, f32[32,24,128]{2,1,0:T(8,128)}) custom-call(f32[32,128]{1,0:T(8,128)S(1)} %get-tuple-element.83.b, f32[32,128]{1,0:T(8,128)S(1)} %get-tuple-element.84.x, f32[7,32,128]{2,1,0:T(8,128)S(1)} %copy.16.one, f32[20,128]{1,0:T(8,128)S(1)} %pad_maximum_fusion.packed, f32[8,128]{1,0:T(8,128)S(1)} %collective-permute-done.20.rest_0_, ...), custom_call_target="tpu_custom_call" | custom-call | tf_op jit(solution)/shard_map/pallas_call | solution.py:292
  37.4 2.8 %all-to-all-start = ((f32[32,24,128]{2,1,0:T(8,128)}), f32[32,24,128]{2,1,0:T(8,128)S(1)}, u32[]{:S(2)}, u32[]{:S(2)}) async-start(f32[32,24,128]{2,1,0:T(8,128)} %get-tuple-element.90), calls=%async_computation | async-start | bytes 786432 | tf_op jit(solution)/shard_map/all_to_all | solution.py:577
  40.3 13.0 %all-to-all-done.everyone = f32[32,24,128]{2,1,0:T(8,128)S(1)} async-done(((f32[32,24,128]{2,1,0:T(8,128)}), f32[32,24,128]{2,1,0:T(8,128)S(1)}, u32[]{:S(2)}, u32[]{:S(2)}) %all-to-all-start) | async-done | bytes 393248 | tf_op jit(solution)/shard_map/all_to_all | solution.py:577
  53.4 1.5 %shard_map.142 = (f32[3,128,128]{2,1,0:T(8,128)S(1)}, f32[48,128]{1,0:T(8,128)S(1)}, f32[48,128]{1,0:T(8,128)S(1)}, f32[24,128]{1,0:T(8,128)S(1)}, f32[8,128]{1,0:T(8,128)S(1)}, /*index=5*/f32[8,128]{1,0:T(8,128)S(1)}) custom-call(f32[32,24,128]{2,1,0:T(8,128)S(1)} %all-to-all-done.everyone, f32[32,128]{1,0:T(8,128)S(1)} %get-tuple-element.91.q_mid, ...), custom_call_target="tpu_custom_call" | custom-call | tf_op jit(solution)/shard_map/pallas_call | solution.py:292
  55.2 1.4 %collective-permute-start.26 = (f32[48,128]{1,0:T(8,128)S(1)}, f32[48,128]{1,0:T(8,128)S(1)}, u32[]{:S(2)}, u32[]{:S(2)}) collective-permute-start(f32[48,128]{1,0:T(8,128)S(1)} %get-tuple-element.98), channel_id=1, source_target_pairs={{0,1},{1,0},{2,3},{3,2},{4,5},{5,4},{6,7},{7,6},{8,9},{9,8},{10,11... | collective-permute-start | bytes 73736 | tf_op jit(solution)/shard_map/ppermute | solution.py:49
  58.1 2.4 %collective-permute-done.28.rest_3_ = f32[8,128]{1,0:T(8,128)S(1)} collective-permute-done((f32[8,128]{1,0:T(8,128)S(1)}, f32[8,128]{1,0:T(8,128)S(1)}, u32[]{:S(2)}, u32[]{:S(2)}) %collective-permute-start.28) | collective-permute-done | bytes 4128 | tf_op jit(solution)/shard_map/ppermute | solution.py:49
  60.5 1.4 %shard_map.143 = (f32[3,128,128]{2,1,0:T(8,128)}, f32[3,128,128]{2,1,0:T(8,128)}) custom-call(f32[3,128,128]{2,1,0:T(8,128)S(1)} %get-tuple-element.96.adj, f32[3,128,128]{2,1,0:T(8,128)S(1)} %bitcast.30, f32[1,128,128]{2,1,0:T(8,128)S(1)} %bitcast.34, f32[3,128,128]{2,1,0:T(8,128)S(1)} %get-tuple-element.56.trans, ...), custom_call_target="tpu_custom_call" | custom-call | tf_op jit(solution)/shard_map/pallas_call | solution.py:292
  (79 shorter events, 11.3 us)
Async XLA Ops:
  2.3 9.2 %collective-permute-start = (f32[64,128]{1,0:T(8,128)S(1)}, f32[64,128]{1,0:T(8,128)S(1)}, u32[]{:S(2)}, u32[]{:S(2)}) collective-permute-start(f32[64,128]{1,0:T(8,128)S(1)} %get-tuple-element.57), channel_id=1, source_target_pairs={{0,8},{1,2},{2,1},{3,11},{4,12},{5,6},{6,5},{7,15},{8,0},{9,10},{1... | collective-permute-start | bytes 98312 | tf_op jit(solution)/shard_map/ppermute | solution.py:49
  2.8 8.7 %collective-permute-start.1 = (f32[64,128]{1,0:T(8,128)S(1)}, f32[64,128]{1,0:T(8,128)S(1)}, u32[]{:S(2)}, u32[]{:S(2)}) collective-permute-start(f32[64,128]{1,0:T(8,128)S(1)} %get-tuple-element.58), channel_id=1, source_target_pairs={{0,1},{1,0},{2,3},{3,2},{4,5},{5,4},{6,7},{7,6},{8,9},{9,8},{10,11... | collective-permute-start | bytes 98312 | tf_op jit(solution)/shard_map/ppermute | solution.py:49
  6.9 4.5 %collective-permute-start.2 = (f32[32,128]{1,0:T(8,128)S(1)}, f32[32,128]{1,0:T(8,128)S(1)}, u32[]{:S(2)}, u32[]{:S(2)}) collective-permute-start(f32[32,128]{1,0:T(8,128)S(1)} %get-tuple-element.59), channel_id=1, source_target_pairs={{0,4},{1,5},{2,6},{3,7},{4,0},{5,1},{6,2},{7,3},{8,12},{9,13},{10,... | collective-permute-start | bytes 49160 | tf_op jit(solution)/shard_map/ppermute | solution.py:49
  8.4 3.0 %collective-permute-start.3 = (f32[8,128]{1,0:T(8,128)S(1)}, f32[8,128]{1,0:T(8,128)S(1)}, u32[]{:S(2)}, u32[]{:S(2)}) collective-permute-start(f32[8,128]{1,0:T(8,128)S(1)} %get-tuple-element.60), channel_id=1, source_target_pairs={{0,24},{1,25},{2,26},{3,27},{4,28},{5,29},{6,30},{7,31},{8,16},{9,... | collective-permute-start | bytes 12296 | tf_op jit(solution)/shard_map/ppermute | solution.py:49
  12.3 5.7 %collective-permute-start.5 = (f32[136,128]{1,0:T(8,128)S(1)}, f32[136,128]{1,0:T(8,128)S(1)}, u32[]{:S(2)}, u32[]{:S(2)}) collective-permute-start(f32[136,128]{1,0:T(8,128)S(1)} %get-tuple-element.64), channel_id=1, source_target_pairs={{0,8},{1,2},{2,1},{3,11},{4,12},{5,6},{6,5},{7,15},{8,0},{9,10},{1... | collective-permute-start | bytes 208904 | tf_op jit(solution)/shard_map/ppermute | solution.py:49
  12.5 5.5 %collective-permute-start.6 = (f32[136,128]{1,0:T(8,128)S(1)}, f32[136,128]{1,0:T(8,128)S(1)}, u32[]{:S(2)}, u32[]{:S(2)}) collective-permute-start(f32[136,128]{1,0:T(8,128)S(1)} %get-tuple-element.65), channel_id=1, source_target_pairs={{0,1},{1,0},{2,3},{3,2},{4,5},{5,4},{6,7},{7,6},{8,9},{9,8},{10,11... | collective-permute-start | bytes 208904 | tf_op jit(solution)/shard_map/ppermute | solution.py:49
  14.0 4.0 %collective-permute-start.7 = (f32[68,128]{1,0:T(8,128)S(1)}, f32[68,128]{1,0:T(8,128)S(1)}, u32[]{:S(2)}, u32[]{:S(2)}) collective-permute-start(f32[68,128]{1,0:T(8,128)S(1)} %get-tuple-element.66), channel_id=1, source_target_pairs={{0,4},{1,5},{2,6},{3,7},{4,0},{5,1},{6,2},{7,3},{8,12},{9,13},{10,... | collective-permute-start | bytes 104456 | tf_op jit(solution)/shard_map/ppermute | solution.py:49
  14.7 3.1 %collective-permute-start.8 = (f32[16,128]{1,0:T(8,128)S(1)}, f32[16,128]{1,0:T(8,128)S(1)}, u32[]{:S(2)}, u32[]{:S(2)}) collective-permute-start(f32[16,128]{1,0:T(8,128)S(1)} %get-tuple-element.67), channel_id=1, source_target_pairs={{0,24},{1,25},{2,26},{3,27},{4,28},{5,29},{6,30},{7,31},{8,16},{9,... | collective-permute-start | bytes 24584 | tf_op jit(solution)/shard_map/ppermute | solution.py:49
  18.5 5.3 %collective-permute-start.10 = (f32[16,128]{1,0:T(8,128)S(1)}, f32[16,128]{1,0:T(8,128)S(1)}, u32[]{:S(2)}, u32[]{:S(2)}) collective-permute-start(f32[16,128]{1,0:T(8,128)S(1)} %get-tuple-element.71), channel_id=1, source_target_pairs={{0,8},{1,2},{2,1},{3,11},{4,12},{5,6},{6,5},{7,15},{8,0},{9,10},{1... | collective-permute-start | bytes 24584 | tf_op jit(solution)/shard_map/ppermute | solution.py:49
  18.5 5.2 %collective-permute-start.11 = (f32[16,128]{1,0:T(8,128)S(1)}, f32[16,128]{1,0:T(8,128)S(1)}, u32[]{:S(2)}, u32[]{:S(2)}) collective-permute-start(f32[16,128]{1,0:T(8,128)S(1)} %get-tuple-element.72), channel_id=1, source_target_pairs={{0,1},{1,0},{2,3},{3,2},{4,5},{5,4},{6,7},{7,6},{8,9},{9,8},{10,11... | collective-permute-start | bytes 24584 | tf_op jit(solution)/shard_map/ppermute | solution.py:49
  19.5 3.6 %collective-permute-start.12 = (f32[8,128]{1,0:T(8,128)S(1)}, f32[8,128]{1,0:T(8,128)S(1)}, u32[]{:S(2)}, u32[]{:S(2)}) collective-permute-start(f32[8,128]{1,0:T(8,128)S(1)} %get-tuple-element.73), channel_id=1, source_target_pairs={{0,4},{1,5},{2,6},{3,7},{4,0},{5,1},{6,2},{7,3},{8,12},{9,13},{10,... | collective-permute-start | bytes 12296 | tf_op jit(solution)/shard_map/ppermute | solution.py:49
  20.7 3.0 %collective-permute-start.13 = (f32[8,128]{1,0:T(8,128)S(1)}, f32[8,128]{1,0:T(8,128)S(1)}, u32[]{:S(2)}, u32[]{:S(2)}) collective-permute-start(f32[8,128]{1,0:T(8,128)S(1)} %get-tuple-element.74), channel_id=1, source_target_pairs={{0,24},{1,25},{2,26},{3,27},{4,28},{5,29},{6,30},{7,31},{8,16},{9,... | collective-permute-start | bytes 12296 | tf_op jit(solution)/shard_map/ppermute | solution.py:49
  24.1 5.6 %collective-permute-start.15 = (f32[64,128]{1,0:T(8,128)S(1)}, f32[64,128]{1,0:T(8,128)S(1)}, u32[]{:S(2)}, u32[]{:S(2)}) collective-permute-start(f32[64,128]{1,0:T(8,128)S(1)} %get-tuple-element.78), channel_id=1, source_target_pairs={{0,8},{1,2},{2,1},{3,11},{4,12},{5,6},{6,5},{7,15},{8,0},{9,10},{1... | collective-permute-start | bytes 98312 | tf_op jit(solution)/shard_map/ppermute | solution.py:49
  24.2 5.5 %collective-permute-start.16 = (f32[64,128]{1,0:T(8,128)S(1)}, f32[64,128]{1,0:T(8,128)S(1)}, u32[]{:S(2)}, u32[]{:S(2)}) collective-permute-start(f32[64,128]{1,0:T(8,128)S(1)} %get-tuple-element.79), channel_id=1, source_target_pairs={{0,1},{1,0},{2,3},{3,2},{4,5},{5,4},{6,7},{7,6},{8,9},{9,8},{10,11... | collective-permute-start | bytes 98312 | tf_op jit(solution)/shard_map/ppermute | solution.py:49
  25.7 3.9 %collective-permute-start.17 = (f32[32,128]{1,0:T(8,128)S(1)}, f32[32,128]{1,0:T(8,128)S(1)}, u32[]{:S(2)}, u32[]{:S(2)}) collective-permute-start(f32[32,128]{1,0:T(8,128)S(1)} %get-tuple-element.80), channel_id=1, source_target_pairs={{0,4},{1,5},{2,6},{3,7},{4,0},{5,1},{6,2},{7,3},{8,12},{9,13},{10,... | collective-permute-start | bytes 49160 | tf_op jit(solution)/shard_map/ppermute | solution.py:49
  26.6 3.1 %collective-permute-start.18 = (f32[16,128]{1,0:T(8,128)S(1)}, f32[16,128]{1,0:T(8,128)S(1)}, u32[]{:S(2)}, u32[]{:S(2)}) collective-permute-start(f32[16,128]{1,0:T(8,128)S(1)} %get-tuple-element.81), channel_id=1, source_target_pairs={{0,24},{1,25},{2,26},{3,27},{4,28},{5,29},{6,30},{7,31},{8,16},{9,... | collective-permute-start | bytes 24584 | tf_op jit(solution)/shard_map/ppermute | solution.py:49
  30.0 4.8 %collective-permute-start.22 = (f32[4,128]{1,0:T(4,128)S(1)}, f32[4,128]{1,0:T(4,128)S(1)}, u32[]{:S(2)}, u32[]{:S(2)}) collective-permute-start(f32[4,128]{1,0:T(4,128)S(1)} %get-tuple-element.87), channel_id=1, source_target_pairs={{0,4},{1,5},{2,6},{3,7},{4,0},{5,1},{6,2},{7,3},{8,12},{9,13},{10,... | collective-permute-start | bytes 6152 | tf_op jit(solution)/shard_map/ppermute | solution.py:49
  31.2 3.6 %collective-permute-start.20 = (f32[8,128]{1,0:T(8,128)S(1)}, f32[8,128]{1,0:T(8,128)S(1)}, u32[]{:S(2)}, u32[]{:S(2)}) collective-permute-start(f32[8,128]{1,0:T(8,128)S(1)} %get-tuple-element.85), channel_id=1, source_target_pairs={{0,8},{1,2},{2,1},{3,11},{4,12},{5,6},{6,5},{7,15},{8,0},{9,10},{1... | collective-permute-start | bytes 12296 | tf_op jit(solution)/shard_map/ppermute | solution.py:49
  31.2 3.7 %collective-permute-start.21 = (f32[8,128]{1,0:T(8,128)S(1)}, f32[8,128]{1,0:T(8,128)S(1)}, u32[]{:S(2)}, u32[]{:S(2)}) collective-permute-start(f32[8,128]{1,0:T(8,128)S(1)} %get-tuple-element.86), channel_id=1, source_target_pairs={{0,1},{1,0},{2,3},{3,2},{4,5},{5,4},{6,7},{7,6},{8,9},{9,8},{10,11... | collective-permute-start | bytes 12296 | tf_op jit(solution)/shard_map/ppermute | solution.py:49
  37.4 16.0 %all-to-all-start = ((f32[32,24,128]{2,1,0:T(8,128)}), f32[32,24,128]{2,1,0:T(8,128)S(1)}, u32[]{:S(2)}, u32[]{:S(2)}) async-start(f32[32,24,128]{2,1,0:T(8,128)} %get-tuple-element.90), calls=%async_computation | async-start | bytes 786432 | tf_op jit(solution)/shard_map/all_to_all | solution.py:577
  54.9 5.6 %collective-permute-start.25 = (f32[48,128]{1,0:T(8,128)S(1)}, f32[48,128]{1,0:T(8,128)S(1)}, u32[]{:S(2)}, u32[]{:S(2)}) collective-permute-start(f32[48,128]{1,0:T(8,128)S(1)} %get-tuple-element.97), channel_id=1, source_target_pairs={{0,8},{1,2},{2,1},{3,11},{4,12},{5,6},{6,5},{7,15},{8,0},{9,10},{1... | collective-permute-start | bytes 73736 | tf_op jit(solution)/shard_map/ppermute | solution.py:49
  55.2 5.3 %collective-permute-start.26 = (f32[48,128]{1,0:T(8,128)S(1)}, f32[48,128]{1,0:T(8,128)S(1)}, u32[]{:S(2)}, u32[]{:S(2)}) collective-permute-start(f32[48,128]{1,0:T(8,128)S(1)} %get-tuple-element.98), channel_id=1, source_target_pairs={{0,1},{1,0},{2,3},{3,2},{4,5},{5,4},{6,7},{7,6},{8,9},{9,8},{10,11... | collective-permute-start | bytes 73736 | tf_op jit(solution)/shard_map/ppermute | solution.py:49
  56.6 3.9 %collective-permute-start.27 = (f32[24,128]{1,0:T(8,128)S(1)}, f32[24,128]{1,0:T(8,128)S(1)}, u32[]{:S(2)}, u32[]{:S(2)}) collective-permute-start(f32[24,128]{1,0:T(8,128)S(1)} %get-tuple-element.99), channel_id=1, source_target_pairs={{0,4},{1,5},{2,6},{3,7},{4,0},{5,1},{6,2},{7,3},{8,12},{9,13},{10,... | collective-permute-start | bytes 36872 | tf_op jit(solution)/shard_map/ppermute | solution.py:49
  57.5 3.0 %collective-permute-start.28 = (f32[8,128]{1,0:T(8,128)S(1)}, f32[8,128]{1,0:T(8,128)S(1)}, u32[]{:S(2)}, u32[]{:S(2)}) collective-permute-start(f32[8,128]{1,0:T(8,128)S(1)} %get-tuple-element.100), channel_id=1, source_target_pairs={{0,24},{1,25},{2,26},{3,27},{4,28},{5,29},{6,30},{7,31},{8,16},{9,... | collective-permute-start | bytes 12296 | tf_op jit(solution)/shard_map/ppermute | solution.py:49
  (16 other events, 68.6 us)

commit v5 on v4

v5 whole, which is shorter than its diff:
```python
import itertools

import jax
import jax.numpy as jnp
from jax import lax
from jax.experimental import pallas as pl
from jax.experimental.pallas import tpu as pltpu
from jax.sharding import PartitionSpec as P

SWEEPS = 3
LEVELS = 3
COARSE_SWEEPS = 4
OMEGA = 0.8
LANES = 128
AXES = ("gx", "gy", "layer")
BY_DIM = ("layer", "gy", "gx")
ORDER = ((0, 1), (0, 0), (1, 1), (1, 0), (2, 1), (2, 0))
HIGHEST = lax.Precision.HIGHEST
F32 = jnp.float32


def pair_route(axis, phase):
    sizes = [lax.axis_size(name) for name in AXES]
    k = AXES.index(axis)
    n = sizes[k]
    route = []
    for index in itertools.product(*[range(size) for size in sizes]):
        target = list(index)
        if phase == 0:
            target[k] = index[k] ^ 1
        elif 0 < index[k] < n - 1 or k == 0:
            target[k] = (((index[k] + 1) % n ^ 1) - 1) % n
        else:
            target[0] = index[0] ^ 1
        flat = [(i[0] * sizes[1] + i[1]) * sizes[2] + i[2] for i in (index, target)]
        route.append(tuple(flat))
    return route


def phases(dim):
    return min(lax.axis_size(BY_DIM[dim]), 3) - 1


def sends():
    return [(dim, phase) for dim, phase in ORDER if phase < phases(dim)]


def swap(buffers):
    return [lax.ppermute(b, AXES, pair_route(BY_DIM[dim], phase)) for b, (dim, phase) in zip(buffers, sends())]


class Grid:
    def __init__(self, depth, height, dup):
        self.depth, self.height, self.dup = depth, height, dup
        self.rows = depth * height
        self.width = LANES // dup
        self.groups = self.rows // 8
        self.stride = LANES // self.groups

    def lines(self, dim):
        return (self.height, self.depth)[dim]


class Message:
    def __init__(self, *parts):
        self.parts = parts

    def size(self, part, dim):
        part = self.parts[part]
        if isinstance(part, dict):
            return part.get(dim, 0)
        if dim not in part[2:] and len(part) > 2:
            return 0
        return 8 if dim == 2 else part[1] * part[0].lines(dim)

    def start(self, part, dim):
        return sum(self.size(i, dim) for i in range(part))

    def buffers(self):
        return [jax.ShapeDtypeStruct((self.start(len(self.parts), dim), LANES), F32) for dim, phase in sends()]

    def put(self, dim, rows, first, last, out):
        if phases(dim) == 0:
            return
        out = dict(zip(sends(), out))
        even = lax.axis_index(BY_DIM[dim]) % 2 == 0
        out[dim, 0][rows] = jnp.where(even, last, first)
        if phases(dim) == 2:
            out[dim, 1][rows] = jnp.where(even, first, last)

    def put_rows(self, part, dim, first, last, out):
        start = self.start(part, dim)
        self.put(dim, slice(start, start + self.size(part, dim)), first, last, out)

    def emit(self, part, channels, out):
        grid = self.parts[part][0]
        lane = lax.broadcasted_iota(jnp.int32, (8, LANES), 1)
        for dim in range(3):
            if self.size(part, dim) == 0:
                continue
            start = self.start(part, dim)
            if dim == 2:
                firsts, lasts = jnp.zeros((8, LANES), F32), jnp.zeros((8, LANES), F32)
                for c, (first, last) in enumerate(channels[dim]):
                    for k in range(grid.groups):
                        at = grid.stride * k + grid.dup * c
                        here = (lane >= at) & (lane < at + grid.dup)
                        rows = slice(8 * k, 8 * k + 8)
                        firsts = jnp.where(here, roll(first(rows), at, 1), firsts)
                        lasts = jnp.where(here, roll(last(rows), at + grid.dup, 1), lasts)
                self.put(dim, slice(start, start + 8), firsts, lasts, out)
                continue
            if dim == 0:
                low, high = slice(0, grid.height), slice(grid.rows - grid.height, grid.rows)
            else:
                low, high = (pl.ds(s, grid.depth, stride=grid.height) for s in (0, grid.height - 1))
            n = grid.lines(dim)
            for c, (first, last) in enumerate(channels[dim]):
                self.put(dim, slice(start + c * n, start + (c + 1) * n), first(low), last(high), out)

    def both(self, dim, rows, got):
        if phases(dim) == 0:
            return (jnp.zeros((rows.stop - rows.start, LANES), F32),) * 2
        got = dict(zip(sends(), got))
        me, n = lax.axis_index(BY_DIM[dim]), lax.axis_size(BY_DIM[dim])
        even = me % 2 == 0
        one = got[dim, 0][rows]
        if phases(dim) == 1:
            return jnp.where(even, 0.0, one), jnp.where(even, one, 0.0)
        two = got[dim, 1][rows]
        before, after = jnp.where(even, two, one), jnp.where(even, one, two)
        return jnp.where(me > 0, before, 0.0), jnp.where(me < n - 1, after, 0.0)

    def rows(self, part, dim, got):
        start = self.start(part, dim)
        return self.both(dim, slice(start, start + self.size(part, dim)), got)

    def faces(self, part, got, channels=None):
        grid, count = self.parts[part][:2]
        channels = range(count) if channels is None else channels
        result = [[None] * 3 for _ in channels]
        for dim in range(3):
            if self.size(part, dim) == 0:
                continue
            start = self.start(part, dim)
            if dim == 2:
                sides = self.both(dim, slice(start, start + 8), got)
                for i, c in enumerate(channels):
                    parts = []
                    for side, lane in zip(sides, (0, LANES - grid.dup)):
                        pieces = [roll(side, lane - grid.stride * k - grid.dup * c, 1) for k in range(grid.groups)]
                        parts.append(jnp.concatenate(pieces))
                    result[i][dim] = tuple(parts)
            else:
                size = grid.lines(dim)
                for i, c in enumerate(channels):
                    result[i][dim] = self.both(dim, slice(start + c * size, start + (c + 1) * size), got)
        return result

    def halos(self, part, got, scratch, channels=None):
        return [Rim(self.parts[part][0], r, scratch, c) for c, r in enumerate(self.faces(part, got, channels))]


class Window:
    def __init__(self, grid, rim):
        self.grid, self.rim = grid, rim
        self.line = grid.height + 2 * rim
        self.rows = (grid.depth + 4) * self.line

    def at(self, layer, y):
        return (layer + 2) * self.line + self.rim + y

    def layer(self, layer):
        return slice(self.at(layer, 0), self.at(layer, self.grid.height))

    def row(self, y):
        return pl.ds(self.at(0, y), self.grid.depth, stride=self.line)

    def fill(self, ref, own):
        height = self.grid.height
        for a in range(self.grid.depth):
            ref[self.layer(a), :] = own[a * height : (a + 1) * height]


class Rim:
    def __init__(self, grid, faces, scratch, c):
        self.grid, self.faces = grid, faces
        ends = scratch.at[c]
        ends[pl.ds(0, grid.depth, stride=grid.height), :] = faces[1][0]
        ends[pl.ds(grid.height - 1, grid.depth, stride=grid.height), :] = faces[1][1]
        self.y_ends = ends[...]

    def previous(self, value, dim):
        g = self.grid
        if dim == 0:
            return jnp.concatenate([self.faces[0][0], value[: g.rows - g.height]])
        if dim == 1:
            return jnp.where(row_y(value, g.height) == 0, self.y_ends, roll(value, 1, 0))
        return jnp.where(lane_of(value) < g.dup, self.faces[2][0], roll(value, g.dup, 1))

    def following(self, value, dim):
        g = self.grid
        if dim == 0:
            return jnp.concatenate([value[g.height :], self.faces[0][1]])
        if dim == 1:
            return jnp.where(row_y(value, g.height) == g.height - 1, self.y_ends, roll(value, -1, 0))
        return jnp.where(lane_of(value) >= value.shape[1] - g.dup, self.faces[2][1], roll(value, -g.dup, 1))


class Closed:
    def __init__(self, height, dup):
        self.height, self.dup = height, dup

    def previous(self, value, dim):
        if dim == 0:
            return jnp.concatenate([jnp.zeros_like(value[: self.height]), value[: -self.height]])
        if dim == 1:
            return jnp.where(row_y(value, self.height) == 0, 0.0, roll(value, 1, 0))
        return jnp.where(lane_of(value) < self.dup, 0.0, roll(value, self.dup, 1))

    def following(self, value, dim):
        if dim == 0:
            return jnp.concatenate([value[self.height :], jnp.zeros_like(value[: self.height])])
        if dim == 1:
            return jnp.where(row_y(value, self.height) == self.height - 1, 0.0, roll(value, -1, 0))
        return jnp.where(lane_of(value) >= value.shape[1] - self.dup, 0.0, roll(value, -self.dup, 1))


def roll(value, shift, axis):
    shift %= value.shape[axis]
    return pltpu.roll(value, shift, axis) if shift else value


def row_y(value, height):
    return lax.broadcasted_iota(jnp.int32, value.shape, 0) % height


def lane_of(value):
    return lax.broadcasted_iota(jnp.int32, value.shape, 1)


def loader(ref, c):
    return lambda rows: ref[c, rows, :]


def product(coefs, k, ref):
    return lambda rows: coefs[k, rows, :] * ref[rows, :]


def off_apply(stencil, field, rim):
    total = 0.0
    for dim in range(3):
        total = total + rim.previous(stencil[2 + 2 * dim] * field, dim)
        total = total + rim.following(stencil[1 + 2 * dim] * field, dim)
    return total


def block_row(blocks, c, values):
    return blocks[c] * values[0] + blocks[3 + c] * values[1] + blocks[6 + c] * values[2]


def system_row(c, values, rim, blocks, trans, trans_before):
    total = block_row(blocks, c, values)
    v = values[c]
    for dim in range(3):
        total = total + trans[dim] * (v - rim.following(v, dim))
        total = total + trans_before[dim] * (v - rim.previous(v, dim))
    return total


def pair_sum_x(value, dup):
    odd = (lane_of(value) // dup) % 2 == 1
    return value + jnp.where(odd, roll(value, dup, 1), roll(value, -dup, 1))


def pair_sum_rows(value, depth, height, scratch):
    half = depth // 2
    parts = [value[2 * a * height : (2 * a + 1) * height] + value[(2 * a + 1) * height : (2 * a + 2) * height] for a in range(half)]
    whole = jnp.concatenate(parts)
    count = half * height // 2
    sums = []
    for at in range(0, whole.shape[1], LANES):
        scratch[: half * height, :] = whole[:, at : at + LANES]
        sums.append(scratch[pl.ds(0, count, stride=2), :] + scratch[pl.ds(1, count, stride=2), :])
    return jnp.concatenate(sums, axis=1)


def spread_rows(value, depth, height, scratch):
    count = depth * height
    tiles = []
    for at in range(0, value.shape[1], LANES):
        scratch[pl.ds(0, count, stride=2), :] = value[:, at : at + LANES]
        scratch[pl.ds(1, count, stride=2), :] = value[:, at : at + LANES]
        wide = scratch[: 2 * count, :]
        tiles.append(jnp.concatenate([wide[2 * height * (a // 2) : 2 * height * (a // 2 + 1)] for a in range(2 * depth)]))
    return jnp.concatenate(tiles, axis=1)


def spread_lines(value, scratch):
    count = value.shape[0]
    scratch[pl.ds(0, count, stride=2), :] = value
    scratch[pl.ds(1, count, stride=2), :] = value
    return scratch[: 2 * count, :]


def fold(value):
    half = value.shape[0] // 2
    return jnp.where(lane_of(value[:half]) % 2 == 0, value[:half], value[half:])


def unfold(value):
    even = lane_of(value) % 2 == 0
    return jnp.concatenate([jnp.where(even, value, roll(value, 1, 1)), jnp.where(even, roll(value, -1, 1), value)])


def beside_of(before, after):
    return jnp.where(lane_of(before) < LANES // 2, before, after)


def pack_sides(values, dup):
    total = jnp.zeros_like(values[0])
    lane = lane_of(total)
    for c, value in enumerate(values):
        total = jnp.where((lane >= dup * c) & (lane < dup * (c + 1)), roll(value, dup * c, 1), total)
        high = LANES - dup * c
        total = jnp.where((lane >= high - dup) & (lane < high), roll(value, -dup * c, 1), total)
    return total


def unpack_side(value, c, dup):
    return beside_of(roll(value, -dup * c, 1), roll(value, dup * c, 1))


def moved(rows, by):
    if isinstance(rows, slice):
        return slice(rows.start + by, rows.stop + by)
    return pl.ds(rows.start + by, rows.size, stride=rows.stride)


def shifts_of(value, inner, outer, line, dup, beside):
    none = jnp.zeros((line, LANES), F32)
    lane = lane_of(value)
    if beside:
        low, high = jnp.where(lane < LANES // 2, outer, inner), jnp.where(lane < LANES // 2, inner, outer)
    else:
        low, high = jnp.where(lane < dup, outer, roll(value, dup, 1)), jnp.where(lane >= LANES - dup, outer, roll(value, -dup, 1))
    return [
        jnp.concatenate([none, value[:-line]]),
        jnp.concatenate([value[line:], none]),
        roll(value, 1, 0),
        roll(value, -1, 0),
        low,
        high,
    ]


def smooth(x, added, couplings, line, dup):
    around, beside, second = x[0] + added[0], x[1] + added[1], x[2] + added[1]
    results = []
    for k, (value, shifts) in enumerate(
        (
            (around, shifts_of(around, None, beside, line, dup, False)),
            (beside, shifts_of(beside, around, second, line, dup, True)),
        )
    ):
        total = x[k] + (1.0 - OMEGA) * value
        for c in range(6):
            total = total - couplings[k](c) * shifts[c]
        results.append(total)
    return results


def one_hot(shape, hit):
    return jnp.where(hit(lax.broadcasted_iota(jnp.int32, shape, 0), lax.broadcasted_iota(jnp.int32, shape, 1)), 1.0, 0.0).astype(F32)


def matmul(a, b):
    return jnp.dot(a, b, precision=HIGHEST, preferred_element_type=F32)


def call(kernel, inputs, outputs, scratch=(), far_inputs=0, far_outputs=0):
    inputs = list(inputs)
    for i in range(far_inputs):
        inputs[i] = pltpu.with_memory_space_constraint(inputs[i], pltpu.HBM)

    def specs(count, far):
        return [pl.BlockSpec(memory_space=pltpu.HBM if i < far else pltpu.VMEM) for i in range(count)]

    return pl.pallas_call(
        kernel,
        out_shape=list(outputs),
        in_specs=specs(len(inputs), far_inputs),
        out_specs=specs(len(outputs), far_outputs),
        scratch_shapes=[pltpu.VMEM(shape, F32) if isinstance(shape, tuple) else shape for shape in scratch],
        compiler_params=pltpu.CompilerParams(vmem_limit_bytes=24 * 2**20),
    )(*inputs)


def local(
    source,
    active_cells,
    diag_blocks,
    frozen_inverses,
    transmissibility,
    pressure_weights,
    stencil_fine,
    coarse_one,
    coarse_two,
    coarse_three,
    pressure_state,
    mobilities,
):
    depth, height, width = active_cells.shape
    low_depth, low_height, low_width = coarse_two.shape[1:]
    last_height, last_width = coarse_three.shape[2:]
    fine = Grid(depth, height, 1)
    mid = Grid(depth // 2, height // 2, 2)
    low = Grid(low_depth, low_height, 4)
    mid_window, low_window = Window(mid, 4), Window(low, 2)
    sizes = [lax.axis_size(name) for name in AXES]
    count = sizes[0] * sizes[1] * sizes[2]
    swaps = len(sends())
    rows = fine.rows
    first_round = Message((fine, 4), (mid, 1), (low, 1))
    second_round = Message((fine, 8))
    third_round = Message((fine, 4), (mid, 6, 2), (low, 6, 2))
    fourth_round = Message((fine, 7), {1: 7 * mid.depth}, {1: 7 * low.depth})
    fifth_round = Message((fine, 3), (mid, 2), {0: 4 * mid_window.line}, {0: 4 * low_window.line})

    def flat(array):
        return array.reshape(array.shape[:-3] + (rows, width))

    def out(*shape):
        return jax.ShapeDtypeStruct(shape, F32)

    source, active, diag, frozen, trans, weights, stencil, pressure, mobility = (
        flat(a)
        for a in (
            source,
            active_cells,
            diag_blocks,
            frozen_inverses,
            transmissibility,
            pressure_weights,
            stencil_fine,
            pressure_state,
            mobilities,
        )
    )
    pressure = pressure[None]

    def coupling_faces(coefs):
        return [[(loader(coefs, 1 + 2 * dim), loader(coefs, 2 + 2 * dim))] for dim in range(3)]

    def widen(values, dup):
        wide = matmul(values, one_hot((values.shape[1], LANES), lambda i, j: i == j // dup))
        return wide.reshape(7, wide.shape[0] // 7, LANES)

    def start_kernel(source, active, frozen, trans, one, two, rhs_out, it_out, frozen_out, trans_out, one_out, two_out, *rest):
        buffers, (source_in, active_in, one_in, two_in, two_flat, sems) = rest[:-6], rest[-6:]
        order = [k for c in range(3) for k in (c, 3 + c, 6 + c)]
        pairs = [(active, active_in), (source, source_in)] + [(frozen.at[k], frozen_out.at[k]) for k in order]
        pairs += [(trans, trans_out), (one, one_in), (two, two_in)]
        copies = [pltpu.make_async_copy(a, b, sems.at[i]) for i, (a, b) in enumerate(pairs)]
        for copy in copies[-2:] + copies[:-2]:
            copy.start()
        copies[-2].wait()
        copies[-1].wait()
        one_out[...] = widen(one_in[...].reshape(7 * mid.rows, mid.width), mid.dup)
        for c in range(7):
            for a in range(low.depth):
                at = c * low.rows + a * low.height
                two_flat[at : at + low.height, :] = two_in[c, a]
        two_out[...] = widen(two_flat[...], low.dup)
        first_round.emit(1, coupling_faces(one_out), buffers)
        first_round.emit(2, coupling_faces(two_out), buffers)
        copies[0].wait()
        mask = active_in[...].astype(F32)
        copies[1].wait()
        rhs = [source_in[c] * mask for c in range(3)]
        for c in range(3):
            rhs_out[c] = rhs[c]
        for c in range(3):
            for copy in copies[2 + 3 * c : 5 + 3 * c]:
                copy.wait()
            it_out[c] = block_row(frozen_out, c, rhs)
        copies[-3].wait()
        its = [(loader(it_out, c),) * 2 for c in range(3)]
        first_round.emit(0, [its + [(loader(trans_out, dim),) * 2] for dim in range(3)], buffers)

    rhs, iterate, frozen, trans, one, two, *buffers = call(
        start_kernel,
        (source, active, frozen, trans, coarse_one.reshape(7, mid.rows, mid.width), coarse_two),
        [out(3, rows, LANES)] * 2
        + [out(9, rows, LANES), out(3, rows, LANES), out(7, mid.rows, LANES), out(7, low.rows, LANES)]
        + first_round.buffers(),
        [
            (3, rows, LANES),
            pltpu.VMEM((rows, LANES), jnp.int32),
            (7, mid.rows, mid.width),
            (7, low.depth, low.height, low.width),
            (7 * low.rows, low.width),
            pltpu.SemaphoreType.DMA((14,)),
        ],
        far_inputs=6,
    )
    got = swap(buffers)

    def couplings(coefs, rim, result):
        scale = OMEGA / coefs[0]
        for dim in range(3):
            result[2 * dim] = scale * rim.previous(coefs[2 + 2 * dim], dim)
            result[2 * dim + 1] = scale * rim.following(coefs[1 + 2 * dim], dim)

    def coarse_couplings(one, two, *rest):
        got, outs, scratch = rest[:swaps], rest[swaps : swaps + 2], rest[swaps + 2 :]
        for part, coefs, result, ends in ((1, one, outs[0], scratch[0]), (2, two, outs[1], scratch[1])):
            couplings(coefs, first_round.halos(part, got, ends)[0], result)

    mid_couplings, low_couplings = call(
        coarse_couplings,
        (one, two, *got),
        [out(6, mid.rows, LANES), out(6, low.rows, LANES)],
        [(1, mid.rows, LANES), (1, low.rows, LANES)],
    )

    def sweep_one(rhs, it, frozen, diag, trans, mobility, pressure, stencil, *rest):
        got, (it_out, before_out), buffers, ends = rest[:swaps], rest[swaps : swaps + 2], rest[swaps + 2 : -1], rest[-1]
        rims = first_round.halos(0, got, ends)
        trans_before = [rims[3].previous(trans[dim], dim) for dim in range(3)]
        values = [it[c] for c in range(3)]
        rest = [rhs[c] - system_row(c, values, rims[c], diag, trans, trans_before) for c in range(3)]
        for c in range(3):
            before_out[c] = trans_before[c]
            it_out[c] = values[c] + block_row(frozen, c, rest)
        channels = [(loader(it_out, c),) * 2 for c in range(3)]
        channels += [(loader(mobility, c),) * 2 for c in range(3)] + [(loader(pressure, 0),) * 2]
        second_round.emit(0, [channels + faces for faces in coupling_faces(stencil)], buffers)

    iterate, trans_before, *buffers = call(
        sweep_one,
        (rhs, iterate, frozen, diag, trans, mobility, pressure, stencil, *got),
        [out(3, rows, LANES)] * 2 + second_round.buffers(),
        [(4, rows, LANES)],
    )
    second_got = swap(buffers)

    def same(ref, channels):
        return [(loader(ref, c),) * 2 for c in channels]

    def sweep_two(rhs, it, frozen, diag, trans, trans_before, active, weights, mid_couplings, low_couplings, *rest):
        got, it_out, buffers, ends = rest[:swaps], rest[swaps], rest[swaps + 1 : -1], rest[-1]
        rims = second_round.halos(0, got, ends, range(3))
        values = [it[c] for c in range(3)]
        rest = [rhs[c] - system_row(c, values, rims[c], diag, trans, trans_before) for c in range(3)]
        for c in range(3):
            it_out[c] = values[c] + block_row(frozen, c, rest)
        factors = [(lambda at, c=c: active[at, :].astype(F32) * weights[c, at, :],) * 2 for c in range(3)]
        third_round.emit(0, [same(it_out, range(1)) + factors] * 3, buffers)
        third_round.emit(1, [same(mid_couplings, range(6))] * 3, buffers)
        third_round.emit(2, [same(low_couplings, range(6))] * 3, buffers)

    iterate, *buffers = call(
        sweep_two,
        (rhs, iterate, frozen, diag, trans, trans_before, active, weights, mid_couplings, low_couplings, *second_got),
        [out(3, rows, LANES)] + third_round.buffers(),
        [(3, rows, LANES)],
    )
    third_got = swap(buffers)

    def fine_kernel(stencil, *rest):
        got, (result, ends) = rest[:swaps], rest[swaps:]
        couplings(stencil, second_round.halos(0, got, ends, [7])[0], result)

    (fine_couplings,) = call(fine_kernel, (stencil, *second_got), [out(6, rows, LANES)], [(1, rows, LANES)])

    def products(coefs, field):
        return [[(product(coefs, 1 + 2 * dim, field), product(coefs, 2 + 2 * dim, field))] for dim in range(3)]

    def pressure_kernel(rhs, it, diag, trans, trans_before, stencil, fine_couplings, mid_couplings, low_couplings, *rest):
        got, (b_out, x_out, mid_side, low_side), buffers = rest[:swaps], rest[swaps : swaps + 4], rest[swaps + 4 : -1]
        (rim,) = third_round.halos(0, got, rest[-1], [0])
        b = rhs[0] - system_row(0, [it[c] for c in range(3)], rim, diag, trans, trans_before)
        b_out[...] = b
        x_out[...] = b * (OMEGA / stencil[0])
        ours = same(fine_couplings, range(6))
        fourth_round.emit(0, [faces + ours for faces in products(stencil, x_out)], buffers)
        for part, grid, values, side in ((1, mid, mid_couplings, mid_side), (2, low, low_couplings, low_side)):
            side[...] = pack_sides([beside_of(*faces[2]) for faces in third_round.faces(part, got)], grid.dup)
            ends = []
            for y in (0, grid.height - 1):
                lines = pl.ds(y, grid.depth, stride=grid.height)
                parts = [values[c, lines, :] for c in range(6)]
                ends.append(jnp.concatenate(parts + [side[lines, :]]))
            fourth_round.put_rows(part, 1, *ends, buffers)

    b_fine, x_fine, mid_side, low_side, *buffers = call(
        pressure_kernel,
        (rhs, iterate, diag, trans, trans_before, stencil, fine_couplings, mid_couplings, low_couplings, *third_got),
        [out(rows, LANES)] * 2 + [out(mid.rows, LANES), out(low.rows, LANES)] + fourth_round.buffers(),
        [(1, rows, LANES)],
    )
    fourth_got = swap(buffers)

    def residual_kernel(b, x, stencil, one, it, active, weights, mid_own, mid_side, low_own, low_side, *rest):
        got, (x_out, adj_out, factor_out), windows = rest[:swaps], rest[swaps : swaps + 3], rest[swaps + 3 : swaps + 7]
        buffers, (ends, temp) = rest[swaps + 7 : -2], rest[-2:]
        (rim,) = fourth_round.halos(0, got, ends, [0])
        off = off_apply(stencil, x[...], rim)
        residual = (1.0 - OMEGA) * b[...] - off
        q = (1.0 - OMEGA) * x[...] + (b[...] - off) * (OMEGA / stencil[0])
        mask = active[...].astype(F32)
        for c in range(3):
            factor = mask * weights[c]
            factor_out[c] = factor
            adj_out[c] = mask * it[c] + factor * q
        coarse = pair_sum_rows(pair_sum_x(residual, 1), depth, height, temp)
        x_out[...] = coarse * (OMEGA / one[0])
        fifth_round.emit(0, [same(adj_out, range(3))] * 3, buffers)
        near = (lambda at: x_out[at, :],) * 2
        channels = []
        for step in (mid.height, 1):
            channels.append([near, (lambda at, s=step: x_out[moved(at, s), :], lambda at, s=step: x_out[moved(at, -s), :])])
        channels.append([near, (lambda at: roll(x_out[at, :], -mid.dup, 1), lambda at: roll(x_out[at, :], mid.dup, 1))])
        fifth_round.emit(1, channels, buffers)
        for part, window, own, side, ours, theirs in (
            (1, mid_window, mid_own, mid_side, windows[0], windows[1]),
            (2, low_window, low_own, low_side, windows[2], windows[3]),
        ):
            grid, line = window.grid, window.line
            halves = fourth_round.rows(part, 1, got)
            ours[...] = jnp.zeros(ours.shape, F32)
            theirs[...] = jnp.zeros(theirs.shape, F32)
            pairs = [(ours.at[c], own.at[c], c) for c in range(6)] + [(theirs, side, 6)]
            for ref, source, c in pairs:
                for a in range(grid.depth):
                    at = a * line + window.rim
                    ref[at : at + grid.height, :] = source[a * grid.height : (a + 1) * grid.height, :]
                for y, half in zip((-1, grid.height), halves):
                    ref[pl.ds(window.rim + y, grid.depth, stride=line), :] = half[c * grid.depth : (c + 1) * grid.depth]
            ends = []
            for a in (0, grid.depth - 1):
                lines = slice(a * line, (a + 1) * line)
                parts = [fold(jnp.concatenate([ours[c, lines, :], ours[c + 1, lines, :]])) for c in (0, 2, 4)]
                ends.append(jnp.concatenate(parts + [theirs[lines, :]]))
            fifth_round.put_rows(part + 1, 0, *ends, buffers)

    mid_lines, low_lines = (mid.depth * mid_window.line, LANES), (low.depth * low_window.line, LANES)
    x_mid, adj_known, adj_factor, mid_around, mid_beside, low_around, low_beside, *buffers = call(
        residual_kernel,
        (b_fine, x_fine, stencil, one, iterate, active, weights, mid_couplings, mid_side, low_couplings, low_side, *fourth_got),
        [out(mid.rows, LANES), out(3, rows, LANES), out(3, rows, LANES)]
        + [out(6, *mid_lines), out(*mid_lines), out(6, *low_lines), out(*low_lines)]
        + fifth_round.buffers(),
        [(1, rows, LANES), (rows // 2, LANES)],
    )
    fifth_got = swap(buffers)

    def device(*steps):
        at = [lax.axis_index(name) for name in AXES]
        inside, flat = True, 0
        for position, size, step in zip(at, sizes, steps):
            inside = inside & (position + step >= 0) & (position + step < size)
        for position, size, step in zip(at, sizes, steps):
            flat = flat * size + jnp.where(inside, position + step, position)
        return flat

    last_groups = LANES // last_width
    last = jnp.concatenate([OMEGA / coarse_three[:1], coarse_three[1:]]).reshape(7, last_height, last_width)
    last = jnp.pad(last, ((0, 2 * last_groups - 7), (0, 0), (0, 0)))
    last = last.reshape(2, last_groups, last_height, last_width).transpose(0, 2, 1, 3).reshape(2 * last_height, LANES)
    keep = low.rows // low.dup
    own_at = keep + 2 * last_height
    block = own_at + 2
    signs = (-1, 1)

    def columns(near, far, sign):
        if sign < 0:
            parts = near, roll(far, 2, 1), roll(near, 2, 1)
        else:
            parts = roll(near, 2, 1), roll(far, 4, 1), roll(near, 8, 1)
        lane = lane_of(near)
        return jnp.where(lane < 2, parts[0], jnp.where(lane < 4, parts[1], jnp.where(lane < 6, parts[2], 0.0)))

    def low_kernel(x, one, mid_couplings, two, last, *rest):
        got, (sent, ends, temp) = rest[:swaps], rest[swaps:]
        (rim,) = fifth_round.halos(1, got, ends, [0])
        value = x[...]
        total = (1.0 - OMEGA) * value
        for dim in range(3):
            total = total - mid_couplings[2 * dim] * rim.previous(value, dim)
            total = total - mid_couplings[2 * dim + 1] * rim.following(value, dim)
        residual = total * (one[0] * (1.0 / OMEGA))
        b = pair_sum_rows(pair_sum_x(residual, mid.dup), mid.depth, mid.height, temp)
        field = b * (OMEGA / two[0])
        to_next = [two[2 + 2 * dim] * field for dim in range(3)]
        to_previous = [two[1 + 2 * dim] * field for dim in range(3)]
        closed = Closed(low.height, low.dup)
        inner = (1.0 - OMEGA) * b
        for dim in range(3):
            inner = inner - closed.previous(to_next[dim], dim) - closed.following(to_previous[dim], dim)
        row, lane = lax.broadcasted_iota(jnp.int32, field.shape, 0), lane_of(field)
        layer, y = row // low.height, row % low.height
        outer = [
            jnp.where(layer == 0, -to_previous[0], 0.0),
            jnp.where(layer == low.depth - 1, -to_next[0], 0.0),
            jnp.where(y == 0, -to_previous[1], jnp.where(y == low.height - 1, -to_next[1], 0.0)),
            jnp.where(lane < low.dup, -to_previous[2], jnp.where(lane >= LANES - low.dup, -to_next[2], 0.0)),
        ]
        parts = [pair_sum_rows(pair_sum_x(v, low.dup), low.depth, low.height, temp) for v in [inner] + outer]
        parts = matmul(jnp.concatenate(parts), one_hot((LANES, LANES), lambda i, j: i == 2 * low.dup * j))
        parts = [parts[k * last_height : (k + 1) * last_height] for k in range(5)]
        upper = last[:last_height] + roll(parts[0], 7 * last_width, 1)
        lower = last[last_height:]
        for k in range(4):
            lower = lower + roll(parts[1 + k], k * last_width, 1)
        packed = jnp.zeros((keep, LANES), F32)
        phase = lane_of(packed) % low.dup
        for k in range(low.dup):
            packed = jnp.where(phase == k, field[k * keep : (k + 1) * keep], packed)
        filled = jnp.concatenate([packed, upper, lower, jnp.zeros((2, LANES), F32)])
        sent[...] = jnp.broadcast_to(filled[None], (count, block, LANES))

        def near(sign, size):
            return 0 if sign < 0 else size - 1

        def line(a, y):
            return x[a * mid.height + y : a * mid.height + y + 1, :]

        def across(a):
            return x[a * mid.height : (a + 1) * mid.height, :]

        def along(y):
            return x[pl.ds(y, mid.depth, stride=mid.height), :]

        def folded(value):
            return sum(roll(value[2 * k : 2 * k + 2], 6 * k, 1) for k in range(value.shape[0] // 2))

        for sz in signs:
            a = near(sz, mid.depth)
            for sy in signs:
                y = near(sy, mid.height)
                pair = fold(jnp.concatenate([line(a, y), line(a - sz, y)]))
                sent[device(0, sy, sz), own_at : own_at + 2, :] = jnp.concatenate([pair, line(a, y - sy)])
                for sx in signs:
                    corner = columns(line(a, y), line(a, y), sx)
                    sent[device(sx, sy, sz), own_at : own_at + 1, :] = corner
            for sx in signs:
                sent[device(sx, 0, sz), own_at : own_at + 2, :] = folded(columns(across(a), across(a - sz), sx))
        for sy in signs:
            y = near(sy, mid.height)
            for sx in signs:
                sent[device(sx, sy, 0), own_at : own_at + 2, :] = folded(columns(along(y), along(y - sy), sx))

    (sent,) = call(
        low_kernel,
        (x_mid, one, mid_couplings, two, last, *fifth_got),
        [out(count, block, LANES)],
        [(1, mid.rows, LANES), (mid.rows // 2, LANES)],
    )
    everyone = lax.all_to_all(sent, AXES, 0, 0)

    def window_kernel(x, *rest):
        gots, (x_out, *lines, layers_out, lines_out, sides_out) = [rest[k * swaps : (k + 1) * swaps] for k in range(3)], rest[3 * swaps :]
        third, fourth, fifth = gots
        x_out[...] = jnp.zeros(x_out.shape, F32)
        near, far = fifth_round.faces(1, fifth)
        mid_window.fill(x_out.at[0], x[...])
        mid_window.fill(x_out.at[1], beside_of(*near[2]))
        mid_window.fill(x_out.at[2], beside_of(*far[2]))
        for faces, step in ((near, 0), (far, 1)):
            for layer, value in zip((-1 - step, mid.depth + step), faces[0]):
                x_out[0, mid_window.layer(layer), :] = value
            for y, value in zip((-1 - step, mid.height + step), faces[1]):
                x_out[0, mid_window.row(y), :] = value
        for part, window, ours, theirs in ((2, mid_window, *lines[:2]), (3, low_window, *lines[2:])):
            line = window.line
            for k, half in enumerate(fifth_round.rows(part, 0, fifth)):
                at = slice(k * line, (k + 1) * line)
                for pair in range(3):
                    both = unfold(half[pair * line : (pair + 1) * line])
                    ours[2 * pair, at, :] = both[:line]
                    ours[2 * pair + 1, at, :] = both[line:]
                theirs[at, :] = half[3 * line :]
        channels = fourth_round.faces(0, fourth, range(1, 7)) + third_round.faces(0, third, range(1, 4)) + fifth_round.faces(0, fifth)
        for c, faces in enumerate(channels):
            layers_out[c] = jnp.concatenate(faces[0])
            lines_out[c] = jnp.concatenate(faces[1])
        sides = [beside_of(*faces[2]) for faces in channels]
        for c in range(6):
            sides_out[c] = pack_sides(sides[2 * c : 2 * c + 2], 1)

    mid_ends, low_ends = (2 * mid_window.line, LANES), (2 * low_window.line, LANES)
    x_windows, *halo_inputs = call(
        window_kernel,
        (x_mid, *third_got, *fourth_got, *fifth_got),
        [out(3, mid_window.rows, LANES), out(6, *mid_ends), out(*mid_ends), out(6, *low_ends), out(*low_ends)]
        + [out(12, 2 * height, LANES), out(12, 2 * depth, LANES), out(6, rows, LANES)],
    )

    last_rows, last_line = sizes[2] * sizes[1] * last_height, sizes[1] * last_height

    def solve_last(everyone, temp):
        channels = [[] for _ in range(2 * last_groups)]
        for first in range(0, sizes[0], last_groups):
            here = range(min(last_groups, sizes[0] - first))
            for g in here:
                for y in range(sizes[1]):
                    for z in range(sizes[2]):
                        sender = ((first + g) * sizes[1] + y) * sizes[2] + z
                        for half in range(2):
                            at = half * last_rows + z * last_line + y * last_height
                            start = keep + half * last_height
                            temp[g, at : at + last_height, :] = everyone[sender, start : start + last_height, :]
            parts = [temp[g] for g in here]
            group = lane_of(parts[0]) // last_width
            for q in range(last_groups):
                value = jnp.zeros_like(parts[0])
                for g in here:
                    value = jnp.where(group == g, roll(parts[g], last_width * (g - q), 1), value)
                channels[q].append(value[:last_rows])
                channels[last_groups + q].append(value[last_rows:])
        parts = [jnp.concatenate(tiles, axis=1) for tiles in channels[: last_groups + 4]]
        stencil, (inner, back, on, beside_y, beside_x) = parts[:7], parts[7:]
        y, x = row_y(inner, last_line), lane_of(inner)
        none = jnp.zeros((last_line, inner.shape[1]), F32)
        b = inner + jnp.concatenate([back[last_line:], none]) + jnp.concatenate([none, on[:-last_line]])
        b = b + jnp.where((y % last_height == 0) & (y > 0), roll(beside_y, 1, 0), 0.0)
        b = b + jnp.where((y % last_height == last_height - 1) & (y < last_line - 1), roll(beside_y, -1, 0), 0.0)
        b = b + jnp.where((x % last_width == 0) & (x > 0), roll(beside_x, 1, 1), 0.0)
        b = b + jnp.where((x % last_width == last_width - 1) & (x < inner.shape[1] - 1), roll(beside_x, -1, 1), 0.0)
        closed = Closed(last_line, 1)
        field = start = b * stencil[0]
        for sweep in range(COARSE_SWEEPS - 1):
            field = start + (1.0 - OMEGA) * field - off_apply(stencil, field, closed) * stencil[0]
        return field

    def spread_last(field, temp):
        gx, gy, gz = (lax.axis_index(name) for name in AXES)
        half, reach = low_window.line // 2, low_window.rim // 2
        layers = low.depth // 2 + 2
        dup = 2 * low.dup

        def picked(i, j):
            return j == (gz * (low.depth // 2) + i // half - 1) * last_line + gy * last_height + i % half - reach

        def taken(i, j):
            own = (j < LANES) & (i == gx * last_width + j // dup)
            before = (j >= LANES) & (j < LANES + low.dup) & (i == gx * last_width - 1)
            after = (j >= 2 * LANES - low.dup) & (i == (gx + 1) * last_width)
            return own | before | after

        chosen = matmul(one_hot((layers * half, last_rows), picked), field)
        both = matmul(chosen, one_hot((field.shape[1], 2 * LANES), taken))
        return [spread_rows(both[:, k * LANES : (k + 1) * LANES], layers, half, temp) for k in range(2)]

    def low_windows(everyone, temp, result):
        around = [(sy, sz) for sz in (-1, 0, 1) for sy in (-1, 0, 1)]
        per = -(-len(around) * keep // 8) * 8
        for k, sx in enumerate((0, -1, 1)):
            for i, (sy, sz) in enumerate(around):
                temp[k * per + keep * i : k * per + keep * (i + 1), :] = everyone[device(sx, sy, sz), 0:keep, :]
        packed = temp[: 3 * per, :]
        lane = lane_of(packed)
        turned = {by: roll(packed, by, 1) for by in range(1 - low.dup, low.dup)}
        for k in range(low.dup):
            value = turned[-k]
            for m in range(1, low.dup):
                value = jnp.where(lane % low.dup == m, turned[m - k], value)
            own, before, after = (value[i * per : (i + 1) * per] for i in range(3))
            forms = [own]
            for cells in (1, 2):
                forms.append(beside_of(roll(before, low.dup * cells, 1), roll(after, -low.dup * cells, 1)))
            for i, (sy, sz) in enumerate(around):
                for j in range(keep):
                    a, y = divmod(k * keep + j, low.height)
                    a, y = a + sz * low.depth, y + sy * low.height
                    if -2 <= a < low.depth + 2 and -low_window.rim <= y < low.height + low_window.rim:
                        at = low_window.at(a, y)
                        for form, source in enumerate(forms):
                            result[form, at : at + 1, :] = source[keep * i + j : keep * i + j + 1]
        return [result[form] for form in range(3)]

    def mid_edges(everyone, x):
        def lines(*steps):
            return everyone[device(*steps), own_at : own_at + 2, :]

        def unfolded(value, n):
            return jnp.concatenate([roll(value, -6 * k, 1) for k in range(n // 2)])

        def sides(values, k):
            return beside_of(roll(values[0], -2 * k, 1), roll(values[1], -2 * k - 2, 1))

        for sz in signs:
            a = -1 if sz < 0 else mid.depth
            for sy in signs:
                y = -1 if sy < 0 else mid.height
                got = lines(0, sy, sz)
                pair = unfold(got[:1])
                for layer, at, value in ((a, y, pair[:1]), (a + sz, y, pair[1:]), (a, y + sy, got[1:])):
                    row = mid_window.at(layer, at)
                    x[0, row : row + 1, :] = value
                row = mid_window.at(a, y)
                x[1, row : row + 1, :] = sides([lines(sx, sy, sz)[:1] for sx in signs], 0)
            got = [unfolded(lines(sx, 0, sz), mid.height) for sx in signs]
            x[1, mid_window.layer(a), :] = sides(got, 0)
            x[1, mid_window.layer(a + sz), :] = sides(got, 1)
            x[2, mid_window.layer(a), :] = sides(got, 2)
        for sy in signs:
            y = -1 if sy < 0 else mid.height
            got = [unfolded(lines(sx, sy, 0), mid.depth) for sx in signs]
            x[1, mid_window.row(y), :] = sides(got, 0)
            x[1, mid_window.row(y + sy), :] = sides(got, 1)
            x[2, mid_window.row(y), :] = sides(got, 2)

    def full(window, lines, ends, side_lines, side_ends):
        line, none = window.line, jnp.zeros((window.line, LANES), F32)
        packed = jnp.concatenate([none, side_ends[:line, :], side_lines[...], side_ends[line:, :], none])
        return (
            lambda c: jnp.concatenate([none, ends[c, :line, :], lines[c], ends[c, line:, :], none]),
            lambda c: unpack_side(packed, c, window.grid.dup),
        )

    def gradient_factors(mobility, pressure, trans, trans_before, *rest):
        got, (inner, layer_out, line_out, side_out, ends) = rest[:swaps], rest[swaps:]
        faces = second_round.faces(0, got, range(3, 7))
        rims = [Rim(fine, f, ends, c) for c, f in enumerate(faces)]
        lines = pl.ds(0, depth, stride=height)
        drops = []
        for dim in range(3):
            drops.append(0.25 * trans[dim] * (pressure[0] - rims[3].following(pressure[0], dim)))
        side_drop = 0.25 * trans_before[2] * (faces[3][2][0] - pressure[0])
        sides = []
        for c in range(3):
            value = mobility[c]
            for dim in range(3):
                inner[3 * dim + c] = drops[dim] * (value + rims[c].following(value, dim))
            drop = 0.25 * trans_before[0, :height, :] * (faces[3][0][0] - pressure[0, :height, :])
            layer_out[c] = drop * (faces[c][0][0] + mobility[c, :height, :])
            drop = 0.25 * trans_before[1, lines, :] * (faces[3][1][0] - pressure[0, lines, :])
            line_out[c] = drop * (faces[c][1][0] + mobility[c, lines, :])
            sides.append(side_drop * (faces[c][2][0] + value))
        side_out[...] = pack_sides(sides, 1)

    gradient_inputs = call(
        gradient_factors,
        (mobility, pressure, trans, trans_before, *second_got),
        [out(9, rows, LANES), out(3, height, LANES), out(3, depth, LANES), out(rows, LANES)],
        [(4, rows, LANES)],
    )

    def final_kernel(
        everyone,
        x_windows,
        mid_around,
        mid_beside,
        low_around,
        low_beside,
        mid_ends,
        mid_side_ends,
        low_ends,
        low_side_ends,
        layer_halos,
        line_halos,
        side_halos,
        adj_known,
        adj_factor,
        couplings,
        terms,
        layer_terms,
        line_terms,
        side_terms,
        adj_out,
        grad_out,
        *scratch,
    ):
        last_temp, low_x, low_temp, x, temp, ends, around, beside, value_ref, adj, grad, sems = scratch
        added = spread_last(solve_last(everyone, last_temp), low_temp)
        low_values = low_windows(everyone, low_temp, low_x)
        pair = full(low_window, low_around, low_ends, low_beside, low_side_ends)
        results = smooth(low_values, added, pair, low_window.line, low.dup)
        inner = slice(low_window.line, (low.depth + 3) * low_window.line)
        added = [spread_rows(v[inner], low.depth + 2, low_window.line, temp) for v in results]
        x[...] = x_windows[...]
        mid_edges(everyone, x)
        pair = full(mid_window, mid_around, mid_ends, mid_beside, mid_side_ends)
        around[...], beside[...] = smooth([x[k] for k in range(3)], added, pair, mid_window.line, mid.dup)

        def own(ref):
            lines = [ref[mid_window.layer(a), :] for a in range(mid.depth)]
            return spread_rows(jnp.concatenate(lines), mid.depth, mid.height, temp)

        def layer(ref, a):
            return spread_lines(ref[mid_window.layer(a), :], temp)

        def lines(ref, y):
            return spread_lines(ref[mid_window.row(y), :], temp)

        def one_row(a, y):
            at = mid_window.at(a, y)
            return around[at : at + 1, :]

        value, side = own(around), own(beside)
        value_ref[...] = value
        layers = [(a, layer(around, a), layer(beside, a)) for a in (-1, mid.depth)]
        rows_y = [(y, lines(around, y), lines(beside, y)) for y in (-1, mid.height)]
        rim = Rim(fine, [[v[1] for v in layers], [v[1] for v in rows_y], (side, side)], ends, 0)

        def gain(value, shifts, coupling):
            total = (1.0 - OMEGA) * value
            for k in range(6):
                total = total - coupling(k) * shifts[k]
            return total

        shifts = [shift(value, dim) for dim in range(3) for shift in (rim.previous, rim.following)]
        own_gain = gain(value, shifts, lambda k: couplings[k])
        for c in range(3):
            adj[c] = adj_known[c] + adj_factor[c] * own_gain
        copies = [pltpu.make_async_copy(adj, adj_out, sems.at[3])]
        copies[0].start()

        def along_x(value, side):
            lane = lane_of(value)
            return [jnp.where(lane < 1, side, roll(value, 1, 1)), jnp.where(lane >= LANES - 1, side, roll(value, -1, 1))]

        def ended(value, low, high):
            row = lax.broadcasted_iota(jnp.int32, value.shape, 0)
            n = value.shape[0]
            return [jnp.where(row == 0, low, roll(value, 1, 0)), jnp.where(row == n - 1, high, roll(value, -1, 0))]

        layer_gains, line_gains = [], []
        for k, (a, here, there) in enumerate(layers):
            shifts = [here, value[:height]] if k == 0 else [value[rows - height :], here]
            shifts += ended(here, one_row(a, -1), one_row(a, mid.height)) + along_x(here, there)
            layer_gains.append(gain(here, shifts, lambda c: layer_halos[c, k * height : (k + 1) * height, :]))
        for k, (y, here, there) in enumerate(rows_y):
            inside = value_ref[pl.ds(0 if k == 0 else height - 1, depth, stride=height), :]
            shifts = ended(here, one_row(-1, y), one_row(mid.depth, y))
            shifts += ([here, inside] if k == 0 else [inside, here]) + along_x(here, there)
            line_gains.append(gain(here, shifts, lambda c: line_halos[c, k * depth : (k + 1) * depth, :]))
        lane = lane_of(side)
        side_rim = Rim(fine, [[v[2] for v in layers], [v[2] for v in rows_y], (side, side)], ends, 1)
        shifts = [shift(side, dim) for dim in range(2) for shift in (side_rim.previous, side_rim.following)]
        shifts += [jnp.where(lane < LANES // 2, side, value), jnp.where(lane < LANES // 2, value, side)]

        def side_halo(c):
            return unpack_side(side_halos[c // 2], 1, 1) if c % 2 else side_halos[c // 2]

        side_gain = gain(side, shifts, side_halo)
        adj_rims = []
        for c in range(3):
            known, factor = 9 + c, 6 + c
            faces = [
                [
                    layer_halos[known, k * height : (k + 1) * height, :]
                    + layer_halos[factor, k * height : (k + 1) * height, :] * layer_gains[k]
                    for k in range(2)
                ],
                [
                    line_halos[known, k * depth : (k + 1) * depth, :] + line_halos[factor, k * depth : (k + 1) * depth, :] * line_gains[k]
                    for k in range(2)
                ],
                (side_halo(known) + side_halo(factor) * side_gain,) * 2,
            ]
            adj_rims.append(Rim(fine, faces, ends, 2 + c))
        values = [adj[c] for c in range(3)]
        lines = pl.ds(0, depth, stride=height)
        parts = []
        for c in range(3):
            layer, line, side = (adj_rims[c].faces[dim][0] for dim in range(3))
            parts.append(
                (
                    layer_terms[c] * (layer - values[c][:height]),
                    line_terms[c] * (line - adj[c, lines, :]),
                    unpack_side(side_terms[...], c, 1) * (side - values[c]),
                )
            )
        below = Rim(fine, [(sum(p[dim] for p in parts),) * 2 for dim in range(3)], ends, 5)
        for dim in range(3):
            here = 0.0
            for c in range(3):
                here = here + terms[3 * dim + c] * (values[c] - adj_rims[c].following(values[c], dim))
            grad[dim] = here + below.previous(here, dim)
            copies.append(pltpu.make_async_copy(grad.at[dim], grad_out.at[dim], sems.at[dim]))
            copies[-1].start()
        for copy in copies:
            copy.wait()

    adjoint, gradient = call(
        final_kernel,
        (everyone, x_windows, mid_around, mid_beside, low_around, low_beside, *halo_inputs)
        + (adj_known, adj_factor, fine_couplings, *gradient_inputs),
        [out(3, rows, LANES)] * 2,
        [
            (min(sizes[0], last_groups), 2 * last_rows, LANES),
            (3, low_window.rows, LANES),
            (max(low_window.rows, 96), LANES),
            (3, mid_window.rows, LANES),
            (mid_window.rows, LANES),
            (6, rows, LANES),
            (mid_window.rows, LANES),
            (mid_window.rows, LANES),
            (rows, LANES),
            (3, rows, LANES),
            (3, rows, LANES),
            pltpu.SemaphoreType.DMA((4,)),
        ],
        far_outputs=2,
    )
    shape = (3, depth, height, width)
    return adjoint.reshape(shape), gradient.reshape(shape)


def solution(mesh):
    cells = P("layer", "gy", "gx")
    fields = P(None, "layer", "gy", "gx")
    return jax.shard_map(
        local,
        mesh=mesh,
        in_specs=(
            fields,
            cells,
            fields,
            fields,
            fields,
            fields,
            fields,
            fields,
            fields,
            fields,
            cells,
            fields,
        ),
        out_specs=(fields, fields),
        check_vma=False,
    )
```

time: 62.2 us -> 56 us (0.900)
  waiting for transfers between devices: 21.4 us -> 16.2 us
  starting transfers between devices: 30.4 us -> 28.1 us
  Pallas kernels: 7.7 us -> 9.45 us
    all_to_all x1, waiting for transfers between devices: 13 us -> 6.58 us  [local(): everyone = lax.all_to_all(sent, AXES, 0, 0)]
    ppermute x30 -> x25, starting transfers between devices: 27.6 us -> 24.6 us  [swap(): lax.ppermute(b, AXES, pair_route(BY_DIM[dim], phase))]
    pallas_call x10 -> x11, Pallas kernels: 7.7 us -> 9.45 us  [call(): pl.pallas_call(kernel, out_shape=list(outputs), in_specs=specs(len(inputs...]
    ppermute x30 -> x25, waiting for transfers between devices: 8.41 us -> 9.64 us  [swap(): lax.ppermute(b, AXES, pair_route(BY_DIM[dim], phase))]
    all_to_all x1, starting transfers between devices: 2.81 us -> 3.51 us  [local(): everyone = lax.all_to_all(sent, AXES, 0, 0)]
  transfers between devices with their start and end apart: 31 -> 26, of which waited for: 10 -> 8; matrix products, arithmetic and copies ran while one was open for 1% -> 0% of each run, Pallas kernels for 1% -> 2%
where the time goes in v5:
time: 56 us; the launch traced here: 55.7 us
  starting transfers between devices  28.1 us (50%)
  waiting for transfers between devices  16.2 us (29%)
  Pallas kernels  9.45 us (17%)
  local copies, waits for them, and re-layouts  1.05 us (2%)
  between operations  0.89 us (2%)
    ppermute x25, starting transfers between devices, swap(): lax.ppermute(b, AXES, pair_route(BY_DIM[dim], phase))  24.6 us
    ppermute x25, waiting for transfers between devices, swap(): lax.ppermute(b, AXES, pair_route(BY_DIM[dim], phase))  9.64 us
    pallas_call x11, Pallas kernels, call(): pl.pallas_call(kernel, out_shape=list(outputs), in_specs=specs(len(inputs...  9.45 us
    all_to_all x1, waiting for transfers between devices, local(): everyone = lax.all_to_all(sent, AXES, 0, 0)  6.58 us
    all_to_all x1, starting transfers between devices, local(): everyone = lax.all_to_all(sent, AXES, 0, 0)  3.51 us
  transfers between devices with their start and end apart: 26, of which 8 were waited for; matrix products, arithmetic and copies ran while one was open for 0% of the time, Pallas kernels for 2%

profile of v5, /device:TPU:0, one launch (start us, length us, event | category | flops | bytes accessed | tf_op | source)
XLA Modules:
  0.0 55.7 jit_solution(18353178971275111300)
XLA Ops:
  0.7 1.8 %shard_map.131 = (f32[3,128,128]{2,1,0:T(8,128)S(1)}, f32[3,128,128]{2,1,0:T(8,128)S(1)}, f32[9,128,128]{2,1,0:T(8,128)S(1)}, f32[3,128,128]{2,1,0:T(8,128)S(1)}...) custom-call(f32[3,128,128]{2,1,0:T(8,128)} %bitcast.37, ...), custom_call_target="tpu_custom_call" | custom-call | tf_op jit(solution)/shard_map/pallas_call | solution.py:389
  3.0 4.1 %collective-permute-start.1 = (f32[76,128]{1,0:T(8,128)S(1)}, f32[76,128]{1,0:T(8,128)S(1)}, u32[]{:S(2)}, u32[]{:S(2)}) collective-permute-start(f32[76,128]{1,0:T(8,128)S(1)} %get-tuple-element.68), channel_id=1, source_target_pairs={{0,1},{1,0},{2,3},{3,2},{4,5},{5,4},{6,7},{7,6},{8,9},{9,8},{10,11... | collective-permute-start | bytes 116744 | tf_op jit(solution)/shard_map/ppermute | solution.py:49
  7.1 1.5 %collective-permute-start.2 = (f32[38,128]{1,0:T(8,128)S(1)}, f32[38,128]{1,0:T(8,128)S(1)}, u32[]{:S(2)}, u32[]{:S(2)}) collective-permute-start(f32[38,128]{1,0:T(8,128)S(1)} %get-tuple-element.69), channel_id=1, source_target_pairs={{0,4},{1,5},{2,6},{3,7},{4,0},{5,1},{6,2},{7,3},{8,12},{9,13},{10,... | collective-permute-start | bytes 58376 | tf_op jit(solution)/shard_map/ppermute | solution.py:49
  8.7 1.5 %collective-permute-start.4 = (f32[24,128]{1,0:T(8,128)S(1)}, f32[24,128]{1,0:T(8,128)S(1)}, u32[]{:S(2)}, u32[]{:S(2)}) collective-permute-start(f32[24,128]{1,0:T(8,128)S(1)} %get-tuple-element.71), channel_id=1, source_target_pairs={{0,8},{1,9},{2,10},{3,11},{4,12},{5,13},{6,14},{7,15},{8,0},{9,1},... | collective-permute-start | bytes 36872 | tf_op jit(solution)/shard_map/ppermute | solution.py:49
  10.2 1.5 %collective-permute-done.3.rest_3_ = f32[24,128]{1,0:T(8,128)S(1)} collective-permute-done((f32[24,128]{1,0:T(8,128)S(1)}, f32[24,128]{1,0:T(8,128)S(1)}, u32[]{:S(2)}, u32[]{:S(2)}) %collective-permute-start.3) | collective-permute-done | bytes 12320 | tf_op jit(solution)/shard_map/ppermute | solution.py:49
  11.8 0.9 %copy-done.2 = f32[3,8,16,128]{3,2,1,0:T(8,128)S(1)} copy-done((f32[3,8,16,128]{3,2,1,0:T(8,128)S(1)}, f32[3,8,16,128]{3,2,1,0:T(8,128)}, u32[]{:S(2)}) %copy-start.2) | copy-done | bytes 196632
  13.8 1.5 %collective-permute-start.6 = (f32[128,128]{1,0:T(8,128)S(1)}, f32[128,128]{1,0:T(8,128)S(1)}, u32[]{:S(2)}, u32[]{:S(2)}) collective-permute-start(f32[128,128]{1,0:T(8,128)S(1)} %get-tuple-element.79), channel_id=1, source_target_pairs={{0,1},{1,0},{2,3},{3,2},{4,5},{5,4},{6,7},{7,6},{8,9},{9,8},{10,11... | collective-permute-start | bytes 196616 | tf_op jit(solution)/shard_map/ppermute | solution.py:49
  16.3 1.2 %collective-permute-start.9 = (f32[8,128]{1,0:T(8,128)S(1)}, f32[8,128]{1,0:T(8,128)S(1)}, u32[]{:S(2)}, u32[]{:S(2)}) collective-permute-start(f32[8,128]{1,0:T(8,128)S(1)} %get-tuple-element.82), channel_id=1, source_target_pairs={{0,8},{1,9},{2,10},{3,11},{4,12},{5,13},{6,14},{7,15},{8,0},{9,1},... | collective-permute-start | bytes 12296 | tf_op jit(solution)/shard_map/ppermute | solution.py:49
  17.7 1.3 %collective-permute-done.8.rest_3_ = f32[8,128]{1,0:T(8,128)S(1)} collective-permute-done((f32[8,128]{1,0:T(8,128)S(1)}, f32[8,128]{1,0:T(8,128)S(1)}, u32[]{:S(2)}, u32[]{:S(2)}) %collective-permute-start.8) | collective-permute-done | bytes 4128 | tf_op jit(solution)/shard_map/ppermute | solution.py:49
  20.1 1.0 %collective-permute-start.11 = (f32[64,128]{1,0:T(8,128)S(1)}, f32[64,128]{1,0:T(8,128)S(1)}, u32[]{:S(2)}, u32[]{:S(2)}) collective-permute-start(f32[64,128]{1,0:T(8,128)S(1)} %get-tuple-element.85), channel_id=1, source_target_pairs={{0,1},{1,0},{2,3},{3,2},{4,5},{5,4},{6,7},{7,6},{8,9},{9,8},{10,11... | collective-permute-start | bytes 98312 | tf_op jit(solution)/shard_map/ppermute | solution.py:49
  21.0 1.2 %collective-permute-start.12 = (f32[32,128]{1,0:T(8,128)S(1)}, f32[32,128]{1,0:T(8,128)S(1)}, u32[]{:S(2)}, u32[]{:S(2)}) collective-permute-start(f32[32,128]{1,0:T(8,128)S(1)} %get-tuple-element.86), channel_id=1, source_target_pairs={{0,4},{1,5},{2,6},{3,7},{4,0},{5,1},{6,2},{7,3},{8,12},{9,13},{10,... | collective-permute-start | bytes 49160 | tf_op jit(solution)/shard_map/ppermute | solution.py:49
  22.6 1.1 %collective-permute-start.14 = (f32[24,128]{1,0:T(8,128)S(1)}, f32[24,128]{1,0:T(8,128)S(1)}, u32[]{:S(2)}, u32[]{:S(2)}) collective-permute-start(f32[24,128]{1,0:T(8,128)S(1)} %get-tuple-element.88), channel_id=1, source_target_pairs={{0,8},{1,9},{2,10},{3,11},{4,12},{5,13},{6,14},{7,15},{8,0},{9,1},... | collective-permute-start | bytes 36872 | tf_op jit(solution)/shard_map/ppermute | solution.py:49
  23.8 1.5 %collective-permute-done.13.rest_3_ = f32[24,128]{1,0:T(8,128)S(1)} collective-permute-done((f32[24,128]{1,0:T(8,128)S(1)}, f32[24,128]{1,0:T(8,128)S(1)}, u32[]{:S(2)}, u32[]{:S(2)}) %collective-permute-start.13) | collective-permute-done | bytes 12320 | tf_op jit(solution)/shard_map/ppermute | solution.py:49
  26.6 0.9 %collective-permute-start.19 = (f32[8,128]{1,0:T(8,128)S(1)}, f32[8,128]{1,0:T(8,128)S(1)}, u32[]{:S(2)}, u32[]{:S(2)}) collective-permute-start(f32[8,128]{1,0:T(8,128)S(1)} %get-tuple-element.97), channel_id=1, source_target_pairs={{0,8},{1,9},{2,10},{3,11},{4,12},{5,13},{6,14},{7,15},{8,0},{9,1},... | collective-permute-start | bytes 12296 | tf_op jit(solution)/shard_map/ppermute | solution.py:49
  28.4 1.6 %collective-permute-start.16 = (f32[112,128]{1,0:T(8,128)S(1)}, f32[112,128]{1,0:T(8,128)S(1)}, u32[]{:S(2)}, u32[]{:S(2)}) collective-permute-start(f32[112,128]{1,0:T(8,128)S(1)} %get-tuple-element.94), channel_id=1, source_target_pairs={{0,1},{1,0},{2,3},{3,2},{4,5},{5,4},{6,7},{7,6},{8,9},{9,8},{10,11... | collective-permute-start | bytes 172040 | tf_op jit(solution)/shard_map/ppermute | solution.py:49
  30.1 1.6 %collective-permute-done.17.rest_2_.rest_7_ = f32[98,128]{1,0:T(8,128)S(1)} collective-permute-done((f32[98,128]{1,0:T(8,128)S(1)}, f32[98,128]{1,0:T(8,128)S(1)}, u32[]{:S(2)}, u32[]{:S(2)}) %collective-permute-start.17) | collective-permute-done | bytes 50208 | tf_op jit(solution)/shard_map/ppermute | solution.py:49
  31.7 1.1 %collective-permute-done.16.rest_1_.rest_6_ = f32[112,128]{1,0:T(8,128)S(1)} collective-permute-done((f32[112,128]{1,0:T(8,128)S(1)}, f32[112,128]{1,0:T(8,128)S(1)}, u32[]{:S(2)}, u32[]{:S(2)}) %collective-permute-start.16) | collective-permute-done | bytes 57376 | tf_op jit(solution)/shard_map/ppermute | solution.py:49
  34.1 1.2 %collective-permute-start.22 = (f32[32,128]{1,0:T(8,128)S(1)}, f32[32,128]{1,0:T(8,128)S(1)}, u32[]{:S(2)}, u32[]{:S(2)}) collective-permute-start(f32[32,128]{1,0:T(8,128)S(1)} %get-tuple-element.101), channel_id=1, source_target_pairs={{0,4},{1,5},{2,6},{3,7},{4,0},{5,1},{6,2},{7,3},{8,12},{9,13},{10,... | collective-permute-start | bytes 49160 | tf_op jit(solution)/shard_map/ppermute | solution.py:49
  35.2 3.1 %collective-permute-start.21 = (f32[160,128]{1,0:T(8,128)S(1)}, f32[160,128]{1,0:T(8,128)S(1)}, u32[]{:S(2)}, u32[]{:S(2)}) collective-permute-start(f32[160,128]{1,0:T(8,128)S(1)} %get-tuple-element.100), channel_id=1, source_target_pairs={{0,1},{1,0},{2,3},{3,2},{4,5},{5,4},{6,7},{7,6},{8,9},{9,8},{10,11... | collective-permute-start | bytes 245768 | tf_op jit(solution)/shard_map/ppermute | solution.py:49
  38.5 2.3 %collective-permute-done.21.rest_1_.rest_11_ = f32[160,128]{1,0:T(8,128)S(1)} collective-permute-done((f32[160,128]{1,0:T(8,128)S(1)}, f32[160,128]{1,0:T(8,128)S(1)}, u32[]{:S(2)}, u32[]{:S(2)}) %collective-permute-start.21) | collective-permute-done | bytes 81952 | tf_op jit(solution)/shard_map/ppermute | solution.py:49
  40.8 1.3 %shard_map.138 = f32[32,8,128]{2,1,0:T(8,128)} custom-call(f32[32,128]{1,0:T(8,128)S(1)} %get-tuple-element.98.x, f32[7,32,128]{2,1,0:T(8,128)S(1)} %get-tuple-element.74.one, f32[6,32,128]{2,1,0:T(8,128)S(1)} %get-tuple-element.76.mid_couplings.mid_own, f32[7,8,128]{2,1,0:T(8,128)S(1)} %get-tuple-element.75.two, f32[4,128]{1,0:T(4,128)S(1)} %reshape.57.last, ...), custom_call_target="tpu_custom_call" | custom-call | tf_op jit(solution)/shard_map/pallas_call | solution.py:389
  42.0 3.5 %all-to-all-start = ((f32[32,8,128]{2,1,0:T(8,128)}), f32[32,8,128]{2,1,0:T(8,128)S(1)}, u32[]{:S(2)}, u32[]{:S(2)}) async-start(f32[32,8,128]{2,1,0:T(8,128)} %shard_map.138), calls=%async_computation | async-start | bytes 262144 | tf_op jit(solution)/shard_map/all_to_all | solution.py:761
  46.7 6.6 %all-to-all-done.everyone = f32[32,8,128]{2,1,0:T(8,128)S(1)} async-done(((f32[32,8,128]{2,1,0:T(8,128)}), f32[32,8,128]{2,1,0:T(8,128)S(1)}, u32[]{:S(2)}, u32[]{:S(2)}) %all-to-all-start) | async-done | bytes 131104 | tf_op jit(solution)/shard_map/all_to_all | solution.py:761
  53.3 2.4 %shard_map.141 = (f32[3,128,128]{2,1,0:T(8,128)}, f32[3,128,128]{2,1,0:T(8,128)}) custom-call(f32[32,8,128]{2,1,0:T(8,128)S(1)} %all-to-all-done.everyone, f32[3,128,128]{2,1,0:T(8,128)S(1)} %get-tuple-element.104.x_windows, f32[6,64,128]{2,1,0:T(8,128)S(1)} %get-tuple-element.105.mid_around, f32[64,128]{1,0:T(8,128)S(1)} %get-tuple-element.106.mid_beside, ...), custom_call_target="tpu_custom_call" | custom-call | tf_op jit(solution)/shard_map/pallas_call | solution.py:389
  (62 shorter events, 9.0 us)
Async XLA Ops:
  2.4 9.3 %collective-permute-start = (f32[76,128]{1,0:T(8,128)S(1)}, f32[76,128]{1,0:T(8,128)S(1)}, u32[]{:S(2)}, u32[]{:S(2)}) collective-permute-start(f32[76,128]{1,0:T(8,128)S(1)} %get-tuple-element.67), channel_id=1, source_target_pairs={{0,8},{1,2},{2,1},{3,11},{4,12},{5,6},{6,5},{7,15},{8,0},{9,10},{1... | collective-permute-start | bytes 116744 | tf_op jit(solution)/shard_map/ppermute | solution.py:49
  3.0 8.8 %collective-permute-start.1 = (f32[76,128]{1,0:T(8,128)S(1)}, f32[76,128]{1,0:T(8,128)S(1)}, u32[]{:S(2)}, u32[]{:S(2)}) collective-permute-start(f32[76,128]{1,0:T(8,128)S(1)} %get-tuple-element.68), channel_id=1, source_target_pairs={{0,1},{1,0},{2,3},{3,2},{4,5},{5,4},{6,7},{7,6},{8,9},{9,8},{10,11... | collective-permute-start | bytes 116744 | tf_op jit(solution)/shard_map/ppermute | solution.py:49
  7.1 4.7 %collective-permute-start.2 = (f32[38,128]{1,0:T(8,128)S(1)}, f32[38,128]{1,0:T(8,128)S(1)}, u32[]{:S(2)}, u32[]{:S(2)}) collective-permute-start(f32[38,128]{1,0:T(8,128)S(1)} %get-tuple-element.69), channel_id=1, source_target_pairs={{0,4},{1,5},{2,6},{3,7},{4,0},{5,1},{6,2},{7,3},{8,12},{9,13},{10,... | collective-permute-start | bytes 58376 | tf_op jit(solution)/shard_map/ppermute | solution.py:49
  8.6 3.2 %collective-permute-start.3 = (f32[24,128]{1,0:T(8,128)S(1)}, f32[24,128]{1,0:T(8,128)S(1)}, u32[]{:S(2)}, u32[]{:S(2)}) collective-permute-start(f32[24,128]{1,0:T(8,128)S(1)} %get-tuple-element.70), channel_id=1, source_target_pairs={{0,24},{1,25},{2,26},{3,27},{4,28},{5,29},{6,30},{7,31},{8,16},{9,... | collective-permute-start | bytes 36872 | tf_op jit(solution)/shard_map/ppermute | solution.py:49
  8.7 3.1 %collective-permute-start.4 = (f32[24,128]{1,0:T(8,128)S(1)}, f32[24,128]{1,0:T(8,128)S(1)}, u32[]{:S(2)}, u32[]{:S(2)}) collective-permute-start(f32[24,128]{1,0:T(8,128)S(1)} %get-tuple-element.71), channel_id=1, source_target_pairs={{0,8},{1,9},{2,10},{3,11},{4,12},{5,13},{6,14},{7,15},{8,0},{9,1},... | collective-permute-start | bytes 36872 | tf_op jit(solution)/shard_map/ppermute | solution.py:49
  13.6 5.6 %collective-permute-start.5 = (f32[128,128]{1,0:T(8,128)S(1)}, f32[128,128]{1,0:T(8,128)S(1)}, u32[]{:S(2)}, u32[]{:S(2)}) collective-permute-start(f32[128,128]{1,0:T(8,128)S(1)} %get-tuple-element.78), channel_id=1, source_target_pairs={{0,8},{1,2},{2,1},{3,11},{4,12},{5,6},{6,5},{7,15},{8,0},{9,10},{1... | collective-permute-start | bytes 196616 | tf_op jit(solution)/shard_map/ppermute | solution.py:49
  13.8 5.5 %collective-permute-start.6 = (f32[128,128]{1,0:T(8,128)S(1)}, f32[128,128]{1,0:T(8,128)S(1)}, u32[]{:S(2)}, u32[]{:S(2)}) collective-permute-start(f32[128,128]{1,0:T(8,128)S(1)} %get-tuple-element.79), channel_id=1, source_target_pairs={{0,1},{1,0},{2,3},{3,2},{4,5},{5,4},{6,7},{7,6},{8,9},{9,8},{10,11... | collective-permute-start | bytes 196616 | tf_op jit(solution)/shard_map/ppermute | solution.py:49
  15.3 3.9 %collective-permute-start.7 = (f32[64,128]{1,0:T(8,128)S(1)}, f32[64,128]{1,0:T(8,128)S(1)}, u32[]{:S(2)}, u32[]{:S(2)}) collective-permute-start(f32[64,128]{1,0:T(8,128)S(1)} %get-tuple-element.80), channel_id=1, source_target_pairs={{0,4},{1,5},{2,6},{3,7},{4,0},{5,1},{6,2},{7,3},{8,12},{9,13},{10,... | collective-permute-start | bytes 98312 | tf_op jit(solution)/shard_map/ppermute | solution.py:49
  15.9 3.0 %collective-permute-start.8 = (f32[8,128]{1,0:T(8,128)S(1)}, f32[8,128]{1,0:T(8,128)S(1)}, u32[]{:S(2)}, u32[]{:S(2)}) collective-permute-start(f32[8,128]{1,0:T(8,128)S(1)} %get-tuple-element.81), channel_id=1, source_target_pairs={{0,24},{1,25},{2,26},{3,27},{4,28},{5,29},{6,30},{7,31},{8,16},{9,... | collective-permute-start | bytes 12296 | tf_op jit(solution)/shard_map/ppermute | solution.py:49
  20.0 5.4 %collective-permute-start.10 = (f32[64,128]{1,0:T(8,128)S(1)}, f32[64,128]{1,0:T(8,128)S(1)}, u32[]{:S(2)}, u32[]{:S(2)}) collective-permute-start(f32[64,128]{1,0:T(8,128)S(1)} %get-tuple-element.84), channel_id=1, source_target_pairs={{0,8},{1,2},{2,1},{3,11},{4,12},{5,6},{6,5},{7,15},{8,0},{9,10},{1... | collective-permute-start | bytes 98312 | tf_op jit(solution)/shard_map/ppermute | solution.py:49
  20.1 5.3 %collective-permute-start.11 = (f32[64,128]{1,0:T(8,128)S(1)}, f32[64,128]{1,0:T(8,128)S(1)}, u32[]{:S(2)}, u32[]{:S(2)}) collective-permute-start(f32[64,128]{1,0:T(8,128)S(1)} %get-tuple-element.85), channel_id=1, source_target_pairs={{0,1},{1,0},{2,3},{3,2},{4,5},{5,4},{6,7},{7,6},{8,9},{9,8},{10,11... | collective-permute-start | bytes 98312 | tf_op jit(solution)/shard_map/ppermute | solution.py:49
  21.0 4.4 %collective-permute-start.12 = (f32[32,128]{1,0:T(8,128)S(1)}, f32[32,128]{1,0:T(8,128)S(1)}, u32[]{:S(2)}, u32[]{:S(2)}) collective-permute-start(f32[32,128]{1,0:T(8,128)S(1)} %get-tuple-element.86), channel_id=1, source_target_pairs={{0,4},{1,5},{2,6},{3,7},{4,0},{5,1},{6,2},{7,3},{8,12},{9,13},{10,... | collective-permute-start | bytes 49160 | tf_op jit(solution)/shard_map/ppermute | solution.py:49
  22.2 3.2 %collective-permute-start.13 = (f32[24,128]{1,0:T(8,128)S(1)}, f32[24,128]{1,0:T(8,128)S(1)}, u32[]{:S(2)}, u32[]{:S(2)}) collective-permute-start(f32[24,128]{1,0:T(8,128)S(1)} %get-tuple-element.87), channel_id=1, source_target_pairs={{0,24},{1,25},{2,26},{3,27},{4,28},{5,29},{6,30},{7,31},{8,16},{9,... | collective-permute-start | bytes 36872 | tf_op jit(solution)/shard_map/ppermute | solution.py:49
  26.0 4.0 %collective-permute-start.18 = (f32[8,128]{1,0:T(8,128)S(1)}, f32[8,128]{1,0:T(8,128)S(1)}, u32[]{:S(2)}, u32[]{:S(2)}) collective-permute-start(f32[8,128]{1,0:T(8,128)S(1)} %get-tuple-element.96), channel_id=1, source_target_pairs={{0,24},{1,25},{2,26},{3,27},{4,28},{5,29},{6,30},{7,31},{8,16},{9,... | collective-permute-start | bytes 12296 | tf_op jit(solution)/shard_map/ppermute | solution.py:49
  26.6 3.5 %collective-permute-start.19 = (f32[8,128]{1,0:T(8,128)S(1)}, f32[8,128]{1,0:T(8,128)S(1)}, u32[]{:S(2)}, u32[]{:S(2)}) collective-permute-start(f32[8,128]{1,0:T(8,128)S(1)} %get-tuple-element.97), channel_id=1, source_target_pairs={{0,8},{1,9},{2,10},{3,11},{4,12},{5,13},{6,14},{7,15},{8,0},{9,1},... | collective-permute-start | bytes 12296 | tf_op jit(solution)/shard_map/ppermute | solution.py:49
  27.5 4.1 %collective-permute-start.17 = (f32[98,128]{1,0:T(8,128)S(1)}, f32[98,128]{1,0:T(8,128)S(1)}, u32[]{:S(2)}, u32[]{:S(2)}) collective-permute-start(f32[98,128]{1,0:T(8,128)S(1)} %get-tuple-element.95), channel_id=1, source_target_pairs={{0,4},{1,5},{2,6},{3,7},{4,0},{5,1},{6,2},{7,3},{8,12},{9,13},{10,... | collective-permute-start | bytes 150536 | tf_op jit(solution)/shard_map/ppermute | solution.py:49
  28.4 3.3 %collective-permute-start.15 = (f32[112,128]{1,0:T(8,128)S(1)}, f32[112,128]{1,0:T(8,128)S(1)}, u32[]{:S(2)}, u32[]{:S(2)}) collective-permute-start(f32[112,128]{1,0:T(8,128)S(1)} %get-tuple-element.93), channel_id=1, source_target_pairs={{0,8},{1,2},{2,1},{3,11},{4,12},{5,6},{6,5},{7,15},{8,0},{9,10},{1... | collective-permute-start | bytes 172040 | tf_op jit(solution)/shard_map/ppermute | solution.py:49
  28.4 4.3 %collective-permute-start.16 = (f32[112,128]{1,0:T(8,128)S(1)}, f32[112,128]{1,0:T(8,128)S(1)}, u32[]{:S(2)}, u32[]{:S(2)}) collective-permute-start(f32[112,128]{1,0:T(8,128)S(1)} %get-tuple-element.94), channel_id=1, source_target_pairs={{0,1},{1,0},{2,3},{3,2},{4,5},{5,4},{6,7},{7,6},{8,9},{9,8},{10,11... | collective-permute-start | bytes 172040 | tf_op jit(solution)/shard_map/ppermute | solution.py:49
  33.2 5.3 %collective-permute-start.23 = (f32[16,128]{1,0:T(8,128)S(1)}, f32[16,128]{1,0:T(8,128)S(1)}, u32[]{:S(2)}, u32[]{:S(2)}) collective-permute-start(f32[16,128]{1,0:T(8,128)S(1)} %get-tuple-element.102), channel_id=1, source_target_pairs={{0,24},{1,25},{2,26},{3,27},{4,28},{5,29},{6,30},{7,31},{8,16},{9,... | collective-permute-start | bytes 24584 | tf_op jit(solution)/shard_map/ppermute | solution.py:49
  33.3 5.2 %collective-permute-start.24 = (f32[16,128]{1,0:T(8,128)S(1)}, f32[16,128]{1,0:T(8,128)S(1)}, u32[]{:S(2)}, u32[]{:S(2)}) collective-permute-start(f32[16,128]{1,0:T(8,128)S(1)} %get-tuple-element.103), channel_id=1, source_target_pairs={{0,8},{1,9},{2,10},{3,11},{4,12},{5,13},{6,14},{7,15},{8,0},{9,1},... | collective-permute-start | bytes 24584 | tf_op jit(solution)/shard_map/ppermute | solution.py:49
  34.1 4.4 %collective-permute-start.22 = (f32[32,128]{1,0:T(8,128)S(1)}, f32[32,128]{1,0:T(8,128)S(1)}, u32[]{:S(2)}, u32[]{:S(2)}) collective-permute-start(f32[32,128]{1,0:T(8,128)S(1)} %get-tuple-element.101), channel_id=1, source_target_pairs={{0,4},{1,5},{2,6},{3,7},{4,0},{5,1},{6,2},{7,3},{8,12},{9,13},{10,... | collective-permute-start | bytes 49160 | tf_op jit(solution)/shard_map/ppermute | solution.py:49
  35.2 3.3 %collective-permute-start.20 = (f32[160,128]{1,0:T(8,128)S(1)}, f32[160,128]{1,0:T(8,128)S(1)}, u32[]{:S(2)}, u32[]{:S(2)}) collective-permute-start(f32[160,128]{1,0:T(8,128)S(1)} %get-tuple-element.99), channel_id=1, source_target_pairs={{0,8},{1,2},{2,1},{3,11},{4,12},{5,6},{6,5},{7,15},{8,0},{9,10},{1... | collective-permute-start | bytes 245768 | tf_op jit(solution)/shard_map/ppermute | solution.py:49
  35.2 5.5 %collective-permute-start.21 = (f32[160,128]{1,0:T(8,128)S(1)}, f32[160,128]{1,0:T(8,128)S(1)}, u32[]{:S(2)}, u32[]{:S(2)}) collective-permute-start(f32[160,128]{1,0:T(8,128)S(1)} %get-tuple-element.100), channel_id=1, source_target_pairs={{0,1},{1,0},{2,3},{3,2},{4,5},{5,4},{6,7},{7,6},{8,9},{9,8},{10,11... | collective-permute-start | bytes 245768 | tf_op jit(solution)/shard_map/ppermute | solution.py:49
  42.0 11.3 %all-to-all-start = ((f32[32,8,128]{2,1,0:T(8,128)}), f32[32,8,128]{2,1,0:T(8,128)S(1)}, u32[]{:S(2)}, u32[]{:S(2)}) async-start(f32[32,8,128]{2,1,0:T(8,128)} %shard_map.138), calls=%async_computation | async-start | bytes 262144 | tf_op jit(solution)/shard_map/all_to_all | solution.py:761
  (11 other events, 60.0 us)

commit v6 on v5

--- a/solution.py
+++ b/solution.py
@@ -15,7 +15,6 @@
 AXES = ("gx", "gy", "layer")
 BY_DIM = ("layer", "gy", "gx")
 ORDER = ((0, 1), (0, 0), (1, 1), (1, 0), (2, 1), (2, 0))
-HIGHEST = lax.Precision.HIGHEST
 F32 = jnp.float32
 
 
@@ -41,12 +40,12 @@
     return min(lax.axis_size(BY_DIM[dim]), 3) - 1
 
 
-def sends():
-    return [(dim, phase) for dim, phase in ORDER if phase < phases(dim)]
-
-
-def swap(buffers):
-    return [lax.ppermute(b, AXES, pair_route(BY_DIM[dim], phase)) for b, (dim, phase) in zip(buffers, sends())]
+def sends(dims=(0, 1, 2)):
+    return [(dim, phase) for dim, phase in ORDER if dim in dims and phase < phases(dim)]
+
+
+def swap(buffers, dims=(0, 1, 2)):
+    return [lax.ppermute(b, AXES, pair_route(BY_DIM[dim], phase)) for b, (dim, phase) in zip(buffers, sends(dims))]
 
 
 class Grid:
@@ -62,8 +61,8 @@
 
 
 class Message:
-    def __init__(self, *parts):
-        self.parts = parts
+    def __init__(self, *parts, dims=(0, 1, 2)):
+        self.parts, self.dims = parts, dims
 
     def size(self, part, dim):
         part = self.parts[part]
@@ -77,12 +76,12 @@
         return sum(self.size(i, dim) for i in range(part))
 
     def buffers(self):
-        return [jax.ShapeDtypeStruct((self.start(len(self.parts), dim), LANES), F32) for dim, phase in sends()]
+        return [jax.ShapeDtypeStruct((self.start(len(self.parts), dim), LANES), F32) for dim, phase in sends(self.dims)]
 
     def put(self, dim, rows, first, last, out):
         if phases(dim) == 0:
             return
-        out = dict(zip(sends(), out))
+        out = dict(zip(sends(self.dims), out))
         even = lax.axis_index(BY_DIM[dim]) % 2 == 0
         out[dim, 0][rows] = jnp.where(even, last, first)
         if phases(dim) == 2:
@@ -121,7 +120,7 @@
     def both(self, dim, rows, got):
         if phases(dim) == 0:
             return (jnp.zeros((rows.stop - rows.start, LANES), F32),) * 2
-        got = dict(zip(sends(), got))
+        got = dict(zip(sends(self.dims), got))
         me, n = lax.axis_index(BY_DIM[dim]), lax.axis_size(BY_DIM[dim])
         even = me % 2 == 0
         one = got[dim, 0][rows]
@@ -374,8 +373,18 @@
     return jnp.where(hit(lax.broadcasted_iota(jnp.int32, shape, 0), lax.broadcasted_iota(jnp.int32, shape, 1)), 1.0, 0.0).astype(F32)
 
 
-def matmul(a, b):
-    return jnp.dot(a, b, precision=HIGHEST, preferred_element_type=F32)
+def matmul(values, ones):
+    n = values.shape[0]
+    extra = -n % 16
+    if extra:
+        values = jnp.concatenate([values, jnp.zeros((extra, values.shape[1]), F32)])
+    parts = []
+    for _ in range(3):
+        parts.append(values.astype(jnp.bfloat16))
+        values = values - parts[-1].astype(F32)
+    product = jnp.dot(jnp.concatenate(parts), ones.astype(jnp.bfloat16), preferred_element_type=F32)
+    step = n + extra
+    return (product[2 * step : 2 * step + n] + product[step : step + n]) + product[:n]
 
 
 def call(kernel, inputs, outputs, scratch=(), far_inputs=0, far_outputs=0):
@@ -422,10 +431,12 @@
     swaps = len(sends())
     rows = fine.rows
     first_round = Message((fine, 4), (mid, 1), (low, 1))
-    second_round = Message((fine, 8))
-    third_round = Message((fine, 4), (mid, 6, 2), (low, 6, 2))
-    fourth_round = Message((fine, 7), {1: 7 * mid.depth}, {1: 7 * low.depth})
-    fifth_round = Message((fine, 3), (mid, 2), {0: 4 * mid_window.line}, {0: 4 * low_window.line})
+    second_round = Message((fine, 4))
+    third_round = Message((fine, 8), (mid, 6, 2), (low, 6, 2))
+    fourth_round = Message((fine, 1), {1: 7 * mid.depth}, {1: 7 * low.depth}, (fine, 6, 1, 2))
+    fifth_round = Message((fine, 3, 1, 2), (mid, 2), {2: 3 * depth})
+    late_round = Message((fine, 9, 0), {0: 4 * mid_window.line}, {0: 4 * low_window.line}, dims=(0,))
+    late = len(sends((0,)))
 
     def flat(array):
         return array.reshape(array.shape[:-3] + (rows, width))
@@ -512,19 +523,23 @@
             result[2 * dim] = scale * rim.previous(coefs[2 + 2 * dim], dim)
             result[2 * dim + 1] = scale * rim.following(coefs[1 + 2 * dim], dim)
 
-    def coarse_couplings(one, two, *rest):
-        got, outs, scratch = rest[:swaps], rest[swaps : swaps + 2], rest[swaps + 2 :]
+    def coarse_couplings(mobility, one, two, *rest):
+        got, outs, mobility_out, scratch = rest[:swaps], rest[swaps : swaps + 2], rest[swaps + 2], rest[swaps + 3 :]
+        fetch = pltpu.make_async_copy(mobility, mobility_out, scratch[2])
+        fetch.start()
         for part, coefs, result, ends in ((1, one, outs[0], scratch[0]), (2, two, outs[1], scratch[1])):
             couplings(coefs, first_round.halos(part, got, ends)[0], result)
-
-    mid_couplings, low_couplings = call(
+        fetch.wait()
+
+    mid_couplings, low_couplings, mobility_near = call(
         coarse_couplings,
-        (one, two, *got),
-        [out(6, mid.rows, LANES), out(6, low.rows, LANES)],
-        [(1, mid.rows, LANES), (1, low.rows, LANES)],
-    )
-
-    def sweep_one(rhs, it, frozen, diag, trans, mobility, pressure, stencil, *rest):
+        (mobility, one, two, *got),
+        [out(6, mid.rows, LANES), out(6, low.rows, LANES), out(3, rows, LANES)],
+        [(1, mid.rows, LANES), (1, low.rows, LANES), pltpu.SemaphoreType.DMA],
+        far_inputs=1,
+    )
+
+    def sweep_one(rhs, it, frozen, diag, trans, stencil, *rest):
         got, (it_out, before_out), buffers, ends = rest[:swaps], rest[swaps : swaps + 2], rest[swaps + 2 : -1], rest[-1]
         rims = first_round.halos(0, got, ends)
         trans_before = [rims[3].previous(trans[dim], dim) for dim in range(3)]
@@ -534,12 +549,11 @@
             before_out[c] = trans_before[c]
             it_out[c] = values[c] + block_row(frozen, c, rest)
         channels = [(loader(it_out, c),) * 2 for c in range(3)]
-        channels += [(loader(mobility, c),) * 2 for c in range(3)] + [(loader(pressure, 0),) * 2]
         second_round.emit(0, [channels + faces for faces in coupling_faces(stencil)], buffers)
 
     iterate, trans_before, *buffers = call(
         sweep_one,
-        (rhs, iterate, frozen, diag, trans, mobility, pressure, stencil, *got),
+        (rhs, iterate, frozen, diag, trans, stencil, *got),
         [out(3, rows, LANES)] * 2 + second_round.buffers(),
         [(4, rows, LANES)],
     )
@@ -548,7 +562,9 @@
     def same(ref, channels):
         return [(loader(ref, c),) * 2 for c in channels]
 
-    def sweep_two(rhs, it, frozen, diag, trans, trans_before, active, weights, mid_couplings, low_couplings, *rest):
+    def sweep_two(
+        rhs, it, frozen, diag, trans, trans_before, active, weights, mobility, pressure, mid_couplings, low_couplings, *rest
+    ):
         got, it_out, buffers, ends = rest[:swaps], rest[swaps], rest[swaps + 1 : -1], rest[-1]
         rims = second_round.halos(0, got, ends, range(3))
         values = [it[c] for c in range(3)]
@@ -556,13 +572,15 @@
         for c in range(3):
             it_out[c] = values[c] + block_row(frozen, c, rest)
         factors = [(lambda at, c=c: active[at, :].astype(F32) * weights[c, at, :],) * 2 for c in range(3)]
-        third_round.emit(0, [same(it_out, range(1)) + factors] * 3, buffers)
+        states = same(mobility, range(3)) + same(pressure, range(1))
+        third_round.emit(0, [same(it_out, range(1)) + factors + states] * 3, buffers)
         third_round.emit(1, [same(mid_couplings, range(6))] * 3, buffers)
         third_round.emit(2, [same(low_couplings, range(6))] * 3, buffers)
 
     iterate, *buffers = call(
         sweep_two,
-        (rhs, iterate, frozen, diag, trans, trans_before, active, weights, mid_couplings, low_couplings, *second_got),
+        (rhs, iterate, frozen, diag, trans, trans_before, active, weights, mobility_near, pressure)
+        + (mid_couplings, low_couplings, *second_got),
         [out(3, rows, LANES)] + third_round.buffers(),
         [(3, rows, LANES)],
     )
@@ -570,7 +588,7 @@
 
     def fine_kernel(stencil, *rest):
         got, (result, ends) = rest[:swaps], rest[swaps:]
-        couplings(stencil, second_round.halos(0, got, ends, [7])[0], result)
+        couplings(stencil, second_round.halos(0, got, ends, [3])[0], result)
 
     (fine_couplings,) = call(fine_kernel, (stencil, *second_got), [out(6, rows, LANES)], [(1, rows, LANES)])
 
@@ -583,8 +601,8 @@
         b = rhs[0] - system_row(0, [it[c] for c in range(3)], rim, diag, trans, trans_before)
         b_out[...] = b
         x_out[...] = b * (OMEGA / stencil[0])
-        ours = same(fine_couplings, range(6))
-        fourth_round.emit(0, [faces + ours for faces in products(stencil, x_out)], buffers)
+        fourth_round.emit(0, products(stencil, x_out), buffers)
+        fourth_round.emit(3, [same(fine_couplings, range(6))] * 3, buffers)
         for part, grid, values, side in ((1, mid, mid_couplings, mid_side), (2, low, low_couplings, low_side)):
             side[...] = pack_sides([beside_of(*faces[2]) for faces in third_round.faces(part, got)], grid.dup)
             ends = []
@@ -602,9 +620,9 @@
     )
     fourth_got = swap(buffers)
 
-    def residual_kernel(b, x, stencil, one, it, active, weights, mid_own, mid_side, low_own, low_side, *rest):
-        got, (x_out, adj_out, factor_out), windows = rest[:swaps], rest[swaps : swaps + 3], rest[swaps + 3 : swaps + 7]
-        buffers, (ends, temp) = rest[swaps + 7 : -2], rest[-2:]
+    def residual_kernel(b, x, stencil, one, it, active, weights, *rest):
+        got, (x_out, adj_out, factor_out), buffers = rest[:swaps], rest[swaps : swaps + 3], rest[swaps + 3 : -2]
+        ends, temp = rest[-2:]
         (rim,) = fourth_round.halos(0, got, ends, [0])
         off = off_apply(stencil, x[...], rim)
         residual = (1.0 - OMEGA) * b[...] - off
@@ -616,13 +634,24 @@
             adj_out[c] = mask * it[c] + factor * q
         coarse = pair_sum_rows(pair_sum_x(residual, 1), depth, height, temp)
         x_out[...] = coarse * (OMEGA / one[0])
-        fifth_round.emit(0, [same(adj_out, range(3))] * 3, buffers)
         near = (lambda at: x_out[at, :],) * 2
         channels = []
         for step in (mid.height, 1):
             channels.append([near, (lambda at, s=step: x_out[moved(at, s), :], lambda at, s=step: x_out[moved(at, -s), :])])
         channels.append([near, (lambda at: roll(x_out[at, :], -mid.dup, 1), lambda at: roll(x_out[at, :], mid.dup, 1))])
         fifth_round.emit(1, channels, buffers)
+        fifth_round.emit(0, [same(adj_out, range(3))] * 3, buffers)
+
+    x_mid, adj_known, adj_factor, *buffers = call(
+        residual_kernel,
+        (b_fine, x_fine, stencil, one, iterate, active, weights, *fourth_got),
+        [out(mid.rows, LANES), out(3, rows, LANES), out(3, rows, LANES)] + fifth_round.buffers(),
+        [(1, rows, LANES), (rows // 2, LANES)],
+    )
+    fifth_got = swap(buffers)
+
+    def lines_kernel(mid_own, mid_side, low_own, low_side, *rest):
+        got, windows = rest[:swaps], rest[swaps:]
         for part, window, own, side, ours, theirs in (
             (1, mid_window, mid_own, mid_side, windows[0], windows[1]),
             (2, low_window, low_own, low_side, windows[2], windows[3]),
@@ -638,23 +667,13 @@
                     ref[at : at + grid.height, :] = source[a * grid.height : (a + 1) * grid.height, :]
                 for y, half in zip((-1, grid.height), halves):
                     ref[pl.ds(window.rim + y, grid.depth, stride=line), :] = half[c * grid.depth : (c + 1) * grid.depth]
-            ends = []
-            for a in (0, grid.depth - 1):
-                lines = slice(a * line, (a + 1) * line)
-                parts = [fold(jnp.concatenate([ours[c, lines, :], ours[c + 1, lines, :]])) for c in (0, 2, 4)]
-                ends.append(jnp.concatenate(parts + [theirs[lines, :]]))
-            fifth_round.put_rows(part + 1, 0, *ends, buffers)
 
     mid_lines, low_lines = (mid.depth * mid_window.line, LANES), (low.depth * low_window.line, LANES)
-    x_mid, adj_known, adj_factor, mid_around, mid_beside, low_around, low_beside, *buffers = call(
-        residual_kernel,
-        (b_fine, x_fine, stencil, one, iterate, active, weights, mid_couplings, mid_side, low_couplings, low_side, *fourth_got),
-        [out(mid.rows, LANES), out(3, rows, LANES), out(3, rows, LANES)]
-        + [out(6, *mid_lines), out(*mid_lines), out(6, *low_lines), out(*low_lines)]
-        + fifth_round.buffers(),
-        [(1, rows, LANES), (rows // 2, LANES)],
-    )
-    fifth_got = swap(buffers)
+    mid_around, mid_beside, low_around, low_beside = call(
+        lines_kernel,
+        (mid_couplings, mid_side, low_couplings, low_side, *fourth_got),
+        [out(6, *mid_lines), out(*mid_lines), out(6, *low_lines), out(*low_lines)],
+    )
 
     def device(*steps):
         at = [lax.axis_index(name) for name in AXES]
@@ -683,7 +702,7 @@
         return jnp.where(lane < 2, parts[0], jnp.where(lane < 4, parts[1], jnp.where(lane < 6, parts[2], 0.0)))
 
     def low_kernel(x, one, mid_couplings, two, last, *rest):
-        got, (sent, ends, temp) = rest[:swaps], rest[swaps:]
+        got, (sent, mark, ends, temp) = rest[:swaps], rest[swaps:]
         (rim,) = fifth_round.halos(1, got, ends, [0])
         value = x[...]
         total = (1.0 - OMEGA) * value
@@ -720,6 +739,7 @@
             packed = jnp.where(phase == k, field[k * keep : (k + 1) * keep], packed)
         filled = jnp.concatenate([packed, upper, lower, jnp.zeros((2, LANES), F32)])
         sent[...] = jnp.broadcast_to(filled[None], (count, block, LANES))
+        mark[...] = filled
 
         def near(sign, size):
             return 0 if sign < 0 else size - 1
@@ -752,17 +772,33 @@
             for sx in signs:
                 sent[device(sx, sy, 0), own_at : own_at + 2, :] = folded(columns(along(y), along(y - sy), sx))
 
-    (sent,) = call(
+    sent, mark = call(
         low_kernel,
         (x_mid, one, mid_couplings, two, last, *fifth_got),
-        [out(count, block, LANES)],
+        [out(count, block, LANES), out(block, LANES)],
         [(1, mid.rows, LANES), (mid.rows // 2, LANES)],
     )
     everyone = lax.all_to_all(sent, AXES, 0, 0)
 
-    def window_kernel(x, *rest):
-        gots, (x_out, *lines, layers_out, lines_out, sides_out) = [rest[k * swaps : (k + 1) * swaps] for k in range(3)], rest[3 * swaps :]
-        third, fourth, fifth = gots
+    def late_kernel(mark, adj, couplings, mid_around, mid_beside, low_around, low_beside, *buffers):
+        late_round.emit(0, [same(adj, range(3)) + same(couplings, range(6))], buffers)
+        for part, window, ours, theirs in ((1, mid_window, mid_around, mid_beside), (2, low_window, low_around, low_beside)):
+            ends = []
+            for a in (0, window.grid.depth - 1):
+                lines = slice(a * window.line, (a + 1) * window.line)
+                parts = [fold(jnp.concatenate([ours[c, lines, :], ours[c + 1, lines, :]])) for c in (0, 2, 4)]
+                ends.append(jnp.concatenate(parts + [theirs[lines, :]]))
+            late_round.put_rows(part, 0, *ends, buffers)
+
+    buffers = call(
+        late_kernel,
+        (mark, adj_known, fine_couplings, mid_around, mid_beside, low_around, low_beside),
+        late_round.buffers(),
+    )
+    late_got = swap(buffers, (0,))
+
+    def window_kernel(mark, x, *rest):
+        (third, fourth, fifth), (x_out, lines_out, sides_out) = [rest[k * swaps : (k + 1) * swaps] for k in range(3)], rest[3 * swaps :]
         x_out[...] = jnp.zeros(x_out.shape, F32)
         near, far = fifth_round.faces(1, fifth)
         mid_window.fill(x_out.at[0], x[...])
@@ -773,32 +809,44 @@
                 x_out[0, mid_window.layer(layer), :] = value
             for y, value in zip((-1 - step, mid.height + step), faces[1]):
                 x_out[0, mid_window.row(y), :] = value
-        for part, window, ours, theirs in ((2, mid_window, *lines[:2]), (3, low_window, *lines[2:])):
+        channels = fourth_round.faces(3, fourth) + third_round.faces(0, third, range(1, 4)) + fifth_round.faces(0, fifth)
+        for c, faces in enumerate(channels):
+            lines_out[c] = jnp.concatenate(faces[1])
+        sides = [beside_of(*faces[2]) for faces in channels]
+        for c in range(6):
+            sides_out[c] = pack_sides(sides[2 * c : 2 * c + 2], 1)
+
+    x_windows, line_halos, side_halos = call(
+        window_kernel,
+        (mark, x_mid, *third_got, *fourth_got, *fifth_got),
+        [out(3, mid_window.rows, LANES), out(12, 2 * depth, LANES), out(6, rows, LANES)],
+    )
+
+    def ends_kernel(*rest):
+        third, got, (*lines, layers_out) = rest[:swaps], rest[swaps : swaps + late], rest[swaps + late :]
+        for part, window, ours, theirs in ((1, mid_window, *lines[:2]), (2, low_window, *lines[2:])):
             line = window.line
-            for k, half in enumerate(fifth_round.rows(part, 0, fifth)):
+            for k, half in enumerate(late_round.rows(part, 0, got)):
                 at = slice(k * line, (k + 1) * line)
                 for pair in range(3):
                     both = unfold(half[pair * line : (pair + 1) * line])
                     ours[2 * pair, at, :] = both[:line]
                     ours[2 * pair + 1, at, :] = both[line:]
                 theirs[at, :] = half[3 * line :]
-        channels = fourth_round.faces(0, fourth, range(1, 7)) + third_round.faces(0, third, range(1, 4)) + fifth_round.faces(0, fifth)
+        channels = late_round.faces(0, got)
+        channels = channels[3:] + third_round.faces(0, third, range(1, 4)) + channels[:3]
         for c, faces in enumerate(channels):
             layers_out[c] = jnp.concatenate(faces[0])
-            lines_out[c] = jnp.concatenate(faces[1])
-        sides = [beside_of(*faces[2]) for faces in channels]
-        for c in range(6):
-            sides_out[c] = pack_sides(sides[2 * c : 2 * c + 2], 1)
 
     mid_ends, low_ends = (2 * mid_window.line, LANES), (2 * low_window.line, LANES)
-    x_windows, *halo_inputs = call(
-        window_kernel,
-        (x_mid, *third_got, *fourth_got, *fifth_got),
-        [out(3, mid_window.rows, LANES), out(6, *mid_ends), out(*mid_ends), out(6, *low_ends), out(*low_ends)]
-        + [out(12, 2 * height, LANES), out(12, 2 * depth, LANES), out(6, rows, LANES)],
+    *ends, layer_halos = call(
+        ends_kernel,
+        (*third_got, *late_got),
+        [out(6, *mid_ends), out(*mid_ends), out(6, *low_ends), out(*low_ends), out(12, 2 * height, LANES)],
     )
 
     last_rows, last_line = sizes[2] * sizes[1] * last_height, sizes[1] * last_height
+    last_base = -(-(last_line + low_window.rim) // 8) * 8
 
     def solve_last(everyone, temp):
         channels = [[] for _ in range(2 * last_groups)]
@@ -841,17 +889,19 @@
         layers = low.depth // 2 + 2
         dup = 2 * low.dup
 
-        def picked(i, j):
-            return j == (gz * (low.depth // 2) + i // half - 1) * last_line + gy * last_height + i % half - reach
-
         def taken(i, j):
             own = (j < LANES) & (i == gx * last_width + j // dup)
             before = (j >= LANES) & (j < LANES + low.dup) & (i == gx * last_width - 1)
             after = (j >= 2 * LANES - low.dup) & (i == (gx + 1) * last_width)
             return own | before | after
 
-        chosen = matmul(one_hot((layers * half, last_rows), picked), field)
-        both = matmul(chosen, one_hot((field.shape[1], 2 * LANES), taken))
+        at = last_base + (gz * (low.depth // 2) - 1) * last_line + gy * last_height - reach
+        tiles = []
+        for tile in range(0, field.shape[1], LANES):
+            temp[...] = jnp.zeros(temp.shape, F32)
+            temp[last_base : last_base + last_rows, :] = field[:, tile : tile + LANES]
+            tiles.append(jnp.concatenate([temp[pl.ds(at + k * last_line, half), :] for k in range(layers)]))
+        both = matmul(jnp.concatenate(tiles, axis=1), one_hot((field.shape[1], 2 * LANES), taken))
         return [spread_rows(both[:, k * LANES : (k + 1) * LANES], layers, half, temp) for k in range(2)]
 
     def low_windows(everyone, temp, result):
@@ -923,7 +973,7 @@
 
     def gradient_factors(mobility, pressure, trans, trans_before, *rest):
         got, (inner, layer_out, line_out, side_out, ends) = rest[:swaps], rest[swaps:]
-        faces = second_round.faces(0, got, range(3, 7))
+        faces = third_round.faces(0, got, range(4, 8))
         rims = [Rim(fine, f, ends, c) for c, f in enumerate(faces)]
         lines = pl.ds(0, depth, stride=height)
         drops = []
@@ -944,7 +994,7 @@
 
     gradient_inputs = call(
         gradient_factors,
-        (mobility, pressure, trans, trans_before, *second_got),
+        (mobility, pressure, trans, trans_before, *third_got),
         [out(9, rows, LANES), out(3, height, LANES), out(3, depth, LANES), out(rows, LANES)],
         [(4, rows, LANES)],
     )
@@ -1088,13 +1138,13 @@
 
     adjoint, gradient = call(
         final_kernel,
-        (everyone, x_windows, mid_around, mid_beside, low_around, low_beside, *halo_inputs)
-        + (adj_known, adj_factor, fine_couplings, *gradient_inputs),
+        (everyone, x_windows, mid_around, mid_beside, low_around, low_beside, *ends, layer_halos)
+        + (line_halos, side_halos, adj_known, adj_factor, fine_couplings, *gradient_inputs),
         [out(3, rows, LANES)] * 2,
         [
             (min(sizes[0], last_groups), 2 * last_rows, LANES),
             (3, low_window.rows, LANES),
-            (max(low_window.rows, 96), LANES),
+            (max(low_window.rows, 96, 2 * last_base + last_rows), LANES),
             (3, mid_window.rows, LANES),
             (mid_window.rows, LANES),
             (6, rows, LANES),

time: 56 us -> 53.4 us (0.954)
  waiting for transfers between devices: 16.2 us -> 12.5 us
  starting transfers between devices: 28.1 us -> 29.4 us
  local copies, waits for them, and re-layouts: 1.05 us -> 0.13 us
  Pallas kernels: 9.45 us -> 10.3 us
    all_to_all x1, waiting for transfers between devices: 6.58 us -> 0.02 us  [local(): everyone = lax.all_to_all(sent, AXES, 0, 0)]
    ppermute x25 -> x27, waiting for transfers between devices: 9.64 us -> 12.5 us  [swap(): lax.ppermute(b, AXES, pair_route(BY_DIM[dim], phase))]
    ppermute x25 -> x27, starting transfers between devices: 24.6 us -> 26.7 us  [swap(): lax.ppermute(b, AXES, pair_route(BY_DIM[dim], phase))]
    unnamed x16 -> x14, local copies, waits for them, and re-layouts: 0.95 us -> 0.03 us
    pallas_call x11 -> x14, Pallas kernels: 9.45 us -> 10.3 us  [call(): pl.pallas_call(kernel, out_shape=list(outputs), in_specs=specs(len(inputs...]
    all_to_all x1, starting transfers between devices: 3.51 us -> 2.64 us  [local(): everyone = lax.all_to_all(sent, AXES, 0, 0)]
  transfers between devices with their start and end apart: 26 -> 28, of which waited for: 8 -> 9; matrix products, arithmetic and copies ran while one was open for 0% -> 0% of each run, Pallas kernels for 2% -> 5%
where the time goes in v6:
time: 53.4 us; the launch traced here: 53.2 us
  starting transfers between devices  29.4 us (55%)
  waiting for transfers between devices  12.5 us (23%)
  Pallas kernels  10.3 us (19%)
  between operations  0.89 us (2%)
    ppermute x27, starting transfers between devices, swap(): lax.ppermute(b, AXES, pair_route(BY_DIM[dim], phase))  26.7 us
    ppermute x27, waiting for transfers between devices, swap(): lax.ppermute(b, AXES, pair_route(BY_DIM[dim], phase))  12.5 us
    pallas_call x14, Pallas kernels, call(): pl.pallas_call(kernel, out_shape=list(outputs), in_specs=specs(len(inputs...  10.3 us
    all_to_all x1, starting transfers between devices, local(): everyone = lax.all_to_all(sent, AXES, 0, 0)  2.64 us
  transfers between devices with their start and end apart: 28, of which 9 were waited for; matrix products, arithmetic and copies ran while one was open for 0% of the time, Pallas kernels for 5%

profile of v6, /device:TPU:0, one launch (start us, length us, event | category | flops | bytes accessed | tf_op | source)
XLA Modules:
  0.0 53.2 jit_solution(15501144377959217650)
XLA Ops:
  0.7 1.7 %shard_map.131 = (f32[3,128,128]{2,1,0:T(8,128)S(1)}, f32[3,128,128]{2,1,0:T(8,128)S(1)}, f32[9,128,128]{2,1,0:T(8,128)S(1)}, f32[3,128,128]{2,1,0:T(8,128)S(1)}...) custom-call(f32[3,128,128]{2,1,0:T(8,128)} %bitcast.37, ...), custom_call_target="tpu_custom_call" | custom-call | tf_op jit(solution)/shard_map/pallas_call | solution.py:398
  2.9 4.1 %collective-permute-start.1 = (f32[76,128]{1,0:T(8,128)S(1)}, f32[76,128]{1,0:T(8,128)S(1)}, u32[]{:S(2)}, u32[]{:S(2)}) collective-permute-start(f32[76,128]{1,0:T(8,128)S(1)} %get-tuple-element.73), channel_id=1, source_target_pairs={{0,1},{1,0},{2,3},{3,2},{4,5},{5,4},{6,7},{7,6},{8,9},{9,8},{10,11... | collective-permute-start | bytes 116744 | tf_op jit(solution)/shard_map/ppermute | solution.py:48
  7.1 1.5 %collective-permute-start.2 = (f32[38,128]{1,0:T(8,128)S(1)}, f32[38,128]{1,0:T(8,128)S(1)}, u32[]{:S(2)}, u32[]{:S(2)}) collective-permute-start(f32[38,128]{1,0:T(8,128)S(1)} %get-tuple-element.74), channel_id=1, source_target_pairs={{0,4},{1,5},{2,6},{3,7},{4,0},{5,1},{6,2},{7,3},{8,12},{9,13},{10,... | collective-permute-start | bytes 58376 | tf_op jit(solution)/shard_map/ppermute | solution.py:48
  8.7 1.5 %collective-permute-start.4 = (f32[24,128]{1,0:T(8,128)S(1)}, f32[24,128]{1,0:T(8,128)S(1)}, u32[]{:S(2)}, u32[]{:S(2)}) collective-permute-start(f32[24,128]{1,0:T(8,128)S(1)} %get-tuple-element.76), channel_id=1, source_target_pairs={{0,8},{1,9},{2,10},{3,11},{4,12},{5,13},{6,14},{7,15},{8,0},{9,1},... | collective-permute-start | bytes 36872 | tf_op jit(solution)/shard_map/ppermute | solution.py:48
  10.2 1.5 %collective-permute-done.3.rest_3_ = f32[24,128]{1,0:T(8,128)S(1)} collective-permute-done((f32[24,128]{1,0:T(8,128)S(1)}, f32[24,128]{1,0:T(8,128)S(1)}, u32[]{:S(2)}, u32[]{:S(2)}) %collective-permute-start.3) | collective-permute-done | bytes 12320 | tf_op jit(solution)/shard_map/ppermute | solution.py:48
  12.7 1.5 %collective-permute-start.6 = (f32[64,128]{1,0:T(8,128)S(1)}, f32[64,128]{1,0:T(8,128)S(1)}, u32[]{:S(2)}, u32[]{:S(2)}) collective-permute-start(f32[64,128]{1,0:T(8,128)S(1)} %get-tuple-element.85), channel_id=1, source_target_pairs={{0,1},{1,0},{2,3},{3,2},{4,5},{5,4},{6,7},{7,6},{8,9},{9,8},{10,11... | collective-permute-start | bytes 98312 | tf_op jit(solution)/shard_map/ppermute | solution.py:48
  15.2 1.2 %collective-permute-start.9 = (f32[8,128]{1,0:T(8,128)S(1)}, f32[8,128]{1,0:T(8,128)S(1)}, u32[]{:S(2)}, u32[]{:S(2)}) collective-permute-start(f32[8,128]{1,0:T(8,128)S(1)} %get-tuple-element.88), channel_id=1, source_target_pairs={{0,8},{1,9},{2,10},{3,11},{4,12},{5,13},{6,14},{7,15},{8,0},{9,1},... | collective-permute-start | bytes 12296 | tf_op jit(solution)/shard_map/ppermute | solution.py:48
  16.4 1.0 %shard_map.133 = (f32[6,32,128]{2,1,0:T(8,128)S(1)}, f32[6,8,128]{2,1,0:T(8,128)S(1)}, f32[3,128,128]{2,1,0:T(8,128)S(1)}) custom-call(f32[3,128,128]{2,1,0:T(8,128)} %bitcast.27, f32[7,32,128]{2,1,0:T(8,128)S(1)} %get-tuple-element.79.one, f32[7,8,128]{2,1,0:T(8,128)S(1)} %get-tuple-element.80.two, f32[76,128]{1,0:T(8,128)S(1)} %collective-permute-done.rest_0_, ...), custom_call_target="tpu_custom_call" | custom-call | tf_op jit(solution)/shard_map/pallas_call | solution.py:398
  18.0 0.9 %shard_map.134 = (f32[3,128,128]{2,1,0:T(8,128)S(1)}, f32[128,128]{1,0:T(8,128)S(1)}, f32[128,128]{1,0:T(8,128)S(1)}, f32[64,128]{1,0:T(8,128)S(1)}, f32[24,128]{1,0:T(8,128)S(1)}, /*index=5*/f32[24,128]{1,0:T(8,128)S(1)}) custom-call(f32[3,128,128]{2,1,0:T(8,128)S(1)} %get-tuple-element.68.rhs, f32[3,128,128]{2,1,0:T(8,128)S(1)} %get-tuple-element.77.it, ...), custom_call_target="tpu_custom_call" | custom-call | tf_op jit(solution)/shard_map/pallas_call | solution.py:398
  19.0 0.9 %collective-permute-start.11 = (f32[128,128]{1,0:T(8,128)S(1)}, f32[128,128]{1,0:T(8,128)S(1)}, u32[]{:S(2)}, u32[]{:S(2)}) collective-permute-start(f32[128,128]{1,0:T(8,128)S(1)} %get-tuple-element.91), channel_id=1, source_target_pairs={{0,1},{1,0},{2,3},{3,2},{4,5},{5,4},{6,7},{7,6},{8,9},{9,8},{10,11... | collective-permute-start | bytes 196616 | tf_op jit(solution)/shard_map/ppermute | solution.py:48
  19.9 1.4 %collective-permute-start.12 = (f32[64,128]{1,0:T(8,128)S(1)}, f32[64,128]{1,0:T(8,128)S(1)}, u32[]{:S(2)}, u32[]{:S(2)}) collective-permute-start(f32[64,128]{1,0:T(8,128)S(1)} %get-tuple-element.92), channel_id=1, source_target_pairs={{0,4},{1,5},{2,6},{3,7},{4,0},{5,1},{6,2},{7,3},{8,12},{9,13},{10,... | collective-permute-start | bytes 98312 | tf_op jit(solution)/shard_map/ppermute | solution.py:48
  21.6 1.1 %collective-permute-start.14 = (f32[24,128]{1,0:T(8,128)S(1)}, f32[24,128]{1,0:T(8,128)S(1)}, u32[]{:S(2)}, u32[]{:S(2)}) collective-permute-start(f32[24,128]{1,0:T(8,128)S(1)} %get-tuple-element.94), channel_id=1, source_target_pairs={{0,8},{1,9},{2,10},{3,11},{4,12},{5,13},{6,14},{7,15},{8,0},{9,1},... | collective-permute-start | bytes 36872 | tf_op jit(solution)/shard_map/ppermute | solution.py:48
  22.9 1.5 %collective-permute-done.13.rest_3_ = f32[24,128]{1,0:T(8,128)S(1)} collective-permute-done((f32[24,128]{1,0:T(8,128)S(1)}, f32[24,128]{1,0:T(8,128)S(1)}, u32[]{:S(2)}, u32[]{:S(2)}) %collective-permute-start.13) | collective-permute-done | bytes 12320 | tf_op jit(solution)/shard_map/ppermute | solution.py:48
  25.2 1.6 %collective-permute-start.16 = (f32[16,128]{1,0:T(8,128)S(1)}, f32[16,128]{1,0:T(8,128)S(1)}, u32[]{:S(2)}, u32[]{:S(2)}) collective-permute-start(f32[16,128]{1,0:T(8,128)S(1)} %get-tuple-element.98), channel_id=1, source_target_pairs={{0,1},{1,0},{2,3},{3,2},{4,5},{5,4},{6,7},{7,6},{8,9},{9,8},{10,11... | collective-permute-start | bytes 24584 | tf_op jit(solution)/shard_map/ppermute | solution.py:48
  27.4 0.9 %collective-permute-start.19 = (f32[16,128]{1,0:T(8,128)S(1)}, f32[16,128]{1,0:T(8,128)S(1)}, u32[]{:S(2)}, u32[]{:S(2)}) collective-permute-start(f32[16,128]{1,0:T(8,128)S(1)} %get-tuple-element.101), channel_id=1, source_target_pairs={{0,8},{1,9},{2,10},{3,11},{4,12},{5,13},{6,14},{7,15},{8,0},{9,1},... | collective-permute-start | bytes 24584 | tf_op jit(solution)/shard_map/ppermute | solution.py:48
  28.3 1.0 %collective-permute-start.17 = (f32[98,128]{1,0:T(8,128)S(1)}, f32[98,128]{1,0:T(8,128)S(1)}, u32[]{:S(2)}, u32[]{:S(2)}) collective-permute-start(f32[98,128]{1,0:T(8,128)S(1)} %get-tuple-element.99), channel_id=1, source_target_pairs={{0,4},{1,5},{2,6},{3,7},{4,0},{5,1},{6,2},{7,3},{8,12},{9,13},{10,... | collective-permute-start | bytes 150536 | tf_op jit(solution)/shard_map/ppermute | solution.py:48
  29.9 2.5 %collective-permute-done.17.rest_2_.rest_7_ = f32[98,128]{1,0:T(8,128)S(1)} collective-permute-done((f32[98,128]{1,0:T(8,128)S(1)}, f32[98,128]{1,0:T(8,128)S(1)}, u32[]{:S(2)}, u32[]{:S(2)}) %collective-permute-start.17) | collective-permute-done | bytes 50208 | tf_op jit(solution)/shard_map/ppermute | solution.py:48
  32.9 2.0 %collective-permute-start.21 = (f32[16,128]{1,0:T(8,128)S(1)}, f32[16,128]{1,0:T(8,128)S(1)}, u32[]{:S(2)}, u32[]{:S(2)}) collective-permute-start(f32[16,128]{1,0:T(8,128)S(1)} %get-tuple-element.104), channel_id=1, source_target_pairs={{0,1},{1,0},{2,3},{3,2},{4,5},{5,4},{6,7},{7,6},{8,9},{9,8},{10,11... | collective-permute-start | bytes 24584 | tf_op jit(solution)/shard_map/ppermute | solution.py:48
  36.6 2.0 %collective-permute-done.22.rest_2_.rest_12_ = f32[32,128]{1,0:T(8,128)S(1)} collective-permute-done((f32[32,128]{1,0:T(8,128)S(1)}, f32[32,128]{1,0:T(8,128)S(1)}, u32[]{:S(2)}, u32[]{:S(2)}) %collective-permute-start.22) | collective-permute-done | bytes 16416 | tf_op jit(solution)/shard_map/ppermute | solution.py:48
  38.9 1.2 %shard_map.138 = (f32[32,8,128]{2,1,0:T(8,128)}, f32[8,128]{1,0:T(8,128)S(1)}) custom-call(f32[32,128]{1,0:T(8,128)S(1)} %get-tuple-element.102.x, f32[7,32,128]{2,1,0:T(8,128)S(1)} %get-tuple-element.79.one, f32[6,32,128]{2,1,0:T(8,128)S(1)} %get-tuple-element.82.mid_couplings.mid_own, f32[7,8,128]{2,1,0:T(8,128)S(1)} %get-tuple-element.80.two, ...), custom_call_target="tpu_custom_call" | custom-call | tf_op jit(solution)/shard_map/pallas_call | solution.py:398
  40.2 2.6 %all-to-all-start = ((f32[32,8,128]{2,1,0:T(8,128)}), f32[32,8,128]{2,1,0:T(8,128)S(1)}, u32[]{:S(2)}, u32[]{:S(2)}) async-start(f32[32,8,128]{2,1,0:T(8,128)} %get-tuple-element.108), calls=%async_computation | async-start | bytes 262144 | tf_op jit(solution)/shard_map/all_to_all | solution.py:781
  43.2 3.0 %collective-permute-start.26 = (f32[240,128]{1,0:T(8,128)S(1)}, f32[240,128]{1,0:T(8,128)S(1)}, u32[]{:S(2)}, u32[]{:S(2)}) collective-permute-start(f32[240,128]{1,0:T(8,128)S(1)} %get-tuple-element.119), channel_id=1, source_target_pairs={{0,1},{1,0},{2,3},{3,2},{4,5},{5,4},{6,7},{7,6},{8,9},{9,8},{10,11... | collective-permute-start | bytes 368648 | tf_op jit(solution)/shard_map/ppermute | solution.py:48
  47.3 3.5 %collective-permute-done.26.rest_6_ = f32[240,128]{1,0:T(8,128)S(1)} collective-permute-done((f32[240,128]{1,0:T(8,128)S(1)}, f32[240,128]{1,0:T(8,128)S(1)}, u32[]{:S(2)}, u32[]{:S(2)}) %collective-permute-start.26) | collective-permute-done | bytes 122912 | tf_op jit(solution)/shard_map/ppermute | solution.py:48
  50.9 2.3 %shard_map.144 = (f32[3,128,128]{2,1,0:T(8,128)}, f32[3,128,128]{2,1,0:T(8,128)}) custom-call(f32[32,8,128]{2,1,0:T(8,128)S(1)} %all-to-all-done.everyone, f32[3,128,128]{2,1,0:T(8,128)S(1)} %get-tuple-element.110.x_windows, f32[6,64,128]{2,1,0:T(8,128)S(1)} %get-tuple-element.113.mid_around, f32[64,128]{1,0:T(8,128)S(1)} %get-tuple-element.114.mid_beside, ...), custom_call_target="tpu_custom_call" | custom-call | tf_op jit(solution)/shard_map/pallas_call | solution.py:398
  (67 shorter events, 9.6 us)
Async XLA Ops:
  2.4 9.3 %collective-permute-start = (f32[76,128]{1,0:T(8,128)S(1)}, f32[76,128]{1,0:T(8,128)S(1)}, u32[]{:S(2)}, u32[]{:S(2)}) collective-permute-start(f32[76,128]{1,0:T(8,128)S(1)} %get-tuple-element.72), channel_id=1, source_target_pairs={{0,8},{1,2},{2,1},{3,11},{4,12},{5,6},{6,5},{7,15},{8,0},{9,10},{1... | collective-permute-start | bytes 116744 | tf_op jit(solution)/shard_map/ppermute | solution.py:48
  2.9 8.8 %collective-permute-start.1 = (f32[76,128]{1,0:T(8,128)S(1)}, f32[76,128]{1,0:T(8,128)S(1)}, u32[]{:S(2)}, u32[]{:S(2)}) collective-permute-start(f32[76,128]{1,0:T(8,128)S(1)} %get-tuple-element.73), channel_id=1, source_target_pairs={{0,1},{1,0},{2,3},{3,2},{4,5},{5,4},{6,7},{7,6},{8,9},{9,8},{10,11... | collective-permute-start | bytes 116744 | tf_op jit(solution)/shard_map/ppermute | solution.py:48
  7.1 4.7 %collective-permute-start.2 = (f32[38,128]{1,0:T(8,128)S(1)}, f32[38,128]{1,0:T(8,128)S(1)}, u32[]{:S(2)}, u32[]{:S(2)}) collective-permute-start(f32[38,128]{1,0:T(8,128)S(1)} %get-tuple-element.74), channel_id=1, source_target_pairs={{0,4},{1,5},{2,6},{3,7},{4,0},{5,1},{6,2},{7,3},{8,12},{9,13},{10,... | collective-permute-start | bytes 58376 | tf_op jit(solution)/shard_map/ppermute | solution.py:48
  8.6 3.2 %collective-permute-start.3 = (f32[24,128]{1,0:T(8,128)S(1)}, f32[24,128]{1,0:T(8,128)S(1)}, u32[]{:S(2)}, u32[]{:S(2)}) collective-permute-start(f32[24,128]{1,0:T(8,128)S(1)} %get-tuple-element.75), channel_id=1, source_target_pairs={{0,24},{1,25},{2,26},{3,27},{4,28},{5,29},{6,30},{7,31},{8,16},{9,... | collective-permute-start | bytes 36872 | tf_op jit(solution)/shard_map/ppermute | solution.py:48
  8.7 3.1 %collective-permute-start.4 = (f32[24,128]{1,0:T(8,128)S(1)}, f32[24,128]{1,0:T(8,128)S(1)}, u32[]{:S(2)}, u32[]{:S(2)}) collective-permute-start(f32[24,128]{1,0:T(8,128)S(1)} %get-tuple-element.76), channel_id=1, source_target_pairs={{0,8},{1,9},{2,10},{3,11},{4,12},{5,13},{6,14},{7,15},{8,0},{9,1},... | collective-permute-start | bytes 36872 | tf_op jit(solution)/shard_map/ppermute | solution.py:48
  12.5 5.5 %collective-permute-start.5 = (f32[64,128]{1,0:T(8,128)S(1)}, f32[64,128]{1,0:T(8,128)S(1)}, u32[]{:S(2)}, u32[]{:S(2)}) collective-permute-start(f32[64,128]{1,0:T(8,128)S(1)} %get-tuple-element.84), channel_id=1, source_target_pairs={{0,8},{1,2},{2,1},{3,11},{4,12},{5,6},{6,5},{7,15},{8,0},{9,10},{1... | collective-permute-start | bytes 98312 | tf_op jit(solution)/shard_map/ppermute | solution.py:48
  12.7 5.3 %collective-permute-start.6 = (f32[64,128]{1,0:T(8,128)S(1)}, f32[64,128]{1,0:T(8,128)S(1)}, u32[]{:S(2)}, u32[]{:S(2)}) collective-permute-start(f32[64,128]{1,0:T(8,128)S(1)} %get-tuple-element.85), channel_id=1, source_target_pairs={{0,1},{1,0},{2,3},{3,2},{4,5},{5,4},{6,7},{7,6},{8,9},{9,8},{10,11... | collective-permute-start | bytes 98312 | tf_op jit(solution)/shard_map/ppermute | solution.py:48
  14.2 3.7 %collective-permute-start.7 = (f32[32,128]{1,0:T(8,128)S(1)}, f32[32,128]{1,0:T(8,128)S(1)}, u32[]{:S(2)}, u32[]{:S(2)}) collective-permute-start(f32[32,128]{1,0:T(8,128)S(1)} %get-tuple-element.86), channel_id=1, source_target_pairs={{0,4},{1,5},{2,6},{3,7},{4,0},{5,1},{6,2},{7,3},{8,12},{9,13},{10,... | collective-permute-start | bytes 49160 | tf_op jit(solution)/shard_map/ppermute | solution.py:48
  18.9 5.6 %collective-permute-start.10 = (f32[128,128]{1,0:T(8,128)S(1)}, f32[128,128]{1,0:T(8,128)S(1)}, u32[]{:S(2)}, u32[]{:S(2)}) collective-permute-start(f32[128,128]{1,0:T(8,128)S(1)} %get-tuple-element.90), channel_id=1, source_target_pairs={{0,8},{1,2},{2,1},{3,11},{4,12},{5,6},{6,5},{7,15},{8,0},{9,10},{1... | collective-permute-start | bytes 196616 | tf_op jit(solution)/shard_map/ppermute | solution.py:48
  19.0 5.4 %collective-permute-start.11 = (f32[128,128]{1,0:T(8,128)S(1)}, f32[128,128]{1,0:T(8,128)S(1)}, u32[]{:S(2)}, u32[]{:S(2)}) collective-permute-start(f32[128,128]{1,0:T(8,128)S(1)} %get-tuple-element.91), channel_id=1, source_target_pairs={{0,1},{1,0},{2,3},{3,2},{4,5},{5,4},{6,7},{7,6},{8,9},{9,8},{10,11... | collective-permute-start | bytes 196616 | tf_op jit(solution)/shard_map/ppermute | solution.py:48
  19.9 4.5 %collective-permute-start.12 = (f32[64,128]{1,0:T(8,128)S(1)}, f32[64,128]{1,0:T(8,128)S(1)}, u32[]{:S(2)}, u32[]{:S(2)}) collective-permute-start(f32[64,128]{1,0:T(8,128)S(1)} %get-tuple-element.92), channel_id=1, source_target_pairs={{0,4},{1,5},{2,6},{3,7},{4,0},{5,1},{6,2},{7,3},{8,12},{9,13},{10,... | collective-permute-start | bytes 98312 | tf_op jit(solution)/shard_map/ppermute | solution.py:48
  21.3 3.2 %collective-permute-start.13 = (f32[24,128]{1,0:T(8,128)S(1)}, f32[24,128]{1,0:T(8,128)S(1)}, u32[]{:S(2)}, u32[]{:S(2)}) collective-permute-start(f32[24,128]{1,0:T(8,128)S(1)} %get-tuple-element.93), channel_id=1, source_target_pairs={{0,24},{1,25},{2,26},{3,27},{4,28},{5,29},{6,30},{7,31},{8,16},{9,... | collective-permute-start | bytes 36872 | tf_op jit(solution)/shard_map/ppermute | solution.py:48
  25.1 4.2 %collective-permute-start.15 = (f32[16,128]{1,0:T(8,128)S(1)}, f32[16,128]{1,0:T(8,128)S(1)}, u32[]{:S(2)}, u32[]{:S(2)}) collective-permute-start(f32[16,128]{1,0:T(8,128)S(1)} %get-tuple-element.97), channel_id=1, source_target_pairs={{0,8},{1,2},{2,1},{3,11},{4,12},{5,6},{6,5},{7,15},{8,0},{9,10},{1... | collective-permute-start | bytes 24584 | tf_op jit(solution)/shard_map/ppermute | solution.py:48
  25.2 4.1 %collective-permute-start.16 = (f32[16,128]{1,0:T(8,128)S(1)}, f32[16,128]{1,0:T(8,128)S(1)}, u32[]{:S(2)}, u32[]{:S(2)}) collective-permute-start(f32[16,128]{1,0:T(8,128)S(1)} %get-tuple-element.98), channel_id=1, source_target_pairs={{0,1},{1,0},{2,3},{3,2},{4,5},{5,4},{6,7},{7,6},{8,9},{9,8},{10,11... | collective-permute-start | bytes 24584 | tf_op jit(solution)/shard_map/ppermute | solution.py:48
  26.8 3.1 %collective-permute-start.18 = (f32[16,128]{1,0:T(8,128)S(1)}, f32[16,128]{1,0:T(8,128)S(1)}, u32[]{:S(2)}, u32[]{:S(2)}) collective-permute-start(f32[16,128]{1,0:T(8,128)S(1)} %get-tuple-element.100), channel_id=1, source_target_pairs={{0,24},{1,25},{2,26},{3,27},{4,28},{5,29},{6,30},{7,31},{8,16},{9,... | collective-permute-start | bytes 24584 | tf_op jit(solution)/shard_map/ppermute | solution.py:48
  28.3 4.1 %collective-permute-start.17 = (f32[98,128]{1,0:T(8,128)S(1)}, f32[98,128]{1,0:T(8,128)S(1)}, u32[]{:S(2)}, u32[]{:S(2)}) collective-permute-start(f32[98,128]{1,0:T(8,128)S(1)} %get-tuple-element.99), channel_id=1, source_target_pairs={{0,4},{1,5},{2,6},{3,7},{4,0},{5,1},{6,2},{7,3},{8,12},{9,13},{10,... | collective-permute-start | bytes 150536 | tf_op jit(solution)/shard_map/ppermute | solution.py:48
  32.8 3.8 %collective-permute-start.20 = (f32[16,128]{1,0:T(8,128)S(1)}, f32[16,128]{1,0:T(8,128)S(1)}, u32[]{:S(2)}, u32[]{:S(2)}) collective-permute-start(f32[16,128]{1,0:T(8,128)S(1)} %get-tuple-element.103), channel_id=1, source_target_pairs={{0,8},{1,2},{2,1},{3,11},{4,12},{5,6},{6,5},{7,15},{8,0},{9,10},{1... | collective-permute-start | bytes 24584 | tf_op jit(solution)/shard_map/ppermute | solution.py:48
  32.9 3.7 %collective-permute-start.21 = (f32[16,128]{1,0:T(8,128)S(1)}, f32[16,128]{1,0:T(8,128)S(1)}, u32[]{:S(2)}, u32[]{:S(2)}) collective-permute-start(f32[16,128]{1,0:T(8,128)S(1)} %get-tuple-element.104), channel_id=1, source_target_pairs={{0,1},{1,0},{2,3},{3,2},{4,5},{5,4},{6,7},{7,6},{8,9},{9,8},{10,11... | collective-permute-start | bytes 24584 | tf_op jit(solution)/shard_map/ppermute | solution.py:48
  34.9 3.7 %collective-permute-start.22 = (f32[32,128]{1,0:T(8,128)S(1)}, f32[32,128]{1,0:T(8,128)S(1)}, u32[]{:S(2)}, u32[]{:S(2)}) collective-permute-start(f32[32,128]{1,0:T(8,128)S(1)} %get-tuple-element.105), channel_id=1, source_target_pairs={{0,4},{1,5},{2,6},{3,7},{4,0},{5,1},{6,2},{7,3},{8,12},{9,13},{10,... | collective-permute-start | bytes 49160 | tf_op jit(solution)/shard_map/ppermute | solution.py:48
  35.7 3.2 %collective-permute-start.23 = (f32[40,128]{1,0:T(8,128)S(1)}, f32[40,128]{1,0:T(8,128)S(1)}, u32[]{:S(2)}, u32[]{:S(2)}) collective-permute-start(f32[40,128]{1,0:T(8,128)S(1)} %get-tuple-element.106), channel_id=1, source_target_pairs={{0,24},{1,25},{2,26},{3,27},{4,28},{5,29},{6,30},{7,31},{8,16},{9,... | collective-permute-start | bytes 61448 | tf_op jit(solution)/shard_map/ppermute | solution.py:48
  35.7 3.2 %collective-permute-start.24 = (f32[40,128]{1,0:T(8,128)S(1)}, f32[40,128]{1,0:T(8,128)S(1)}, u32[]{:S(2)}, u32[]{:S(2)}) collective-permute-start(f32[40,128]{1,0:T(8,128)S(1)} %get-tuple-element.107), channel_id=1, source_target_pairs={{0,8},{1,9},{2,10},{3,11},{4,12},{5,13},{6,14},{7,15},{8,0},{9,1},... | collective-permute-start | bytes 61448 | tf_op jit(solution)/shard_map/ppermute | solution.py:48
  40.2 10.8 %all-to-all-start = ((f32[32,8,128]{2,1,0:T(8,128)}), f32[32,8,128]{2,1,0:T(8,128)S(1)}, u32[]{:S(2)}, u32[]{:S(2)}) async-start(f32[32,8,128]{2,1,0:T(8,128)} %get-tuple-element.108), calls=%async_computation | async-start | bytes 262144 | tf_op jit(solution)/shard_map/all_to_all | solution.py:781
  42.9 4.4 %collective-permute-start.25 = (f32[240,128]{1,0:T(8,128)S(1)}, f32[240,128]{1,0:T(8,128)S(1)}, u32[]{:S(2)}, u32[]{:S(2)}) collective-permute-start(f32[240,128]{1,0:T(8,128)S(1)} %get-tuple-element.118), channel_id=1, source_target_pairs={{0,8},{1,2},{2,1},{3,11},{4,12},{5,6},{6,5},{7,15},{8,0},{9,10},{1... | collective-permute-start | bytes 368648 | tf_op jit(solution)/shard_map/ppermute | solution.py:48
  43.2 7.6 %collective-permute-start.26 = (f32[240,128]{1,0:T(8,128)S(1)}, f32[240,128]{1,0:T(8,128)S(1)}, u32[]{:S(2)}, u32[]{:S(2)}) collective-permute-start(f32[240,128]{1,0:T(8,128)S(1)} %get-tuple-element.119), channel_id=1, source_target_pairs={{0,1},{1,0},{2,3},{3,2},{4,5},{5,4},{6,7},{7,6},{8,9},{9,8},{10,11... | collective-permute-start | bytes 368648 | tf_op jit(solution)/shard_map/ppermute | solution.py:48
  (12 other events, 49.1 us)

commit v7 on v6

--- a/solution.py
+++ b/solution.py
@@ -54,10 +54,15 @@
         self.rows = depth * height
         self.width = LANES // dup
         self.groups = self.rows // 8
-        self.stride = LANES // self.groups
 
     def lines(self, dim):
         return (self.height, self.depth)[dim]
+
+    def tiles(self, count):
+        return -(-2 * self.dup * count * self.groups // LANES)
+
+    def place(self, count, c, k):
+        return divmod(2 * self.dup * (count * k + c), LANES)
 
 
 class Message:
@@ -70,7 +75,7 @@
             return part.get(dim, 0)
         if dim not in part[2:] and len(part) > 2:
             return 0
-        return 8 if dim == 2 else part[1] * part[0].lines(dim)
+        return part[0].tiles(part[1]) * 8 if dim == 2 else part[1] * part[0].lines(dim)
 
     def start(self, part, dim):
         return sum(self.size(i, dim) for i in range(part))
@@ -83,9 +88,9 @@
             return
         out = dict(zip(sends(self.dims), out))
         even = lax.axis_index(BY_DIM[dim]) % 2 == 0
-        out[dim, 0][rows] = jnp.where(even, last, first)
+        out[dim, 0][rows] = last if first is last else jnp.where(even, last, first)
         if phases(dim) == 2:
-            out[dim, 1][rows] = jnp.where(even, first, last)
+            out[dim, 1][rows] = last if first is last else jnp.where(even, first, last)
 
     def put_rows(self, part, dim, first, last, out):
         start = self.start(part, dim)
@@ -99,15 +104,19 @@
                 continue
             start = self.start(part, dim)
             if dim == 2:
-                firsts, lasts = jnp.zeros((8, LANES), F32), jnp.zeros((8, LANES), F32)
+                count, dup = self.parts[part][1], grid.dup
+                tiles = [jnp.zeros((8, LANES), F32)] * grid.tiles(count)
                 for c, (first, last) in enumerate(channels[dim]):
                     for k in range(grid.groups):
-                        at = grid.stride * k + grid.dup * c
-                        here = (lane >= at) & (lane < at + grid.dup)
+                        tile, at = grid.place(count, c, k)
                         rows = slice(8 * k, 8 * k + 8)
-                        firsts = jnp.where(here, roll(first(rows), at, 1), firsts)
-                        lasts = jnp.where(here, roll(last(rows), at + grid.dup, 1), lasts)
-                self.put(dim, slice(start, start + 8), firsts, lasts, out)
+                        value = last(rows)
+                        if first is not last:
+                            value = jnp.where(lane < dup, first(rows), value)
+                        here = (lane >= at) & (lane < at + 2 * dup)
+                        tiles[tile] = jnp.where(here, roll(value, at + dup, 1), tiles[tile])
+                value = jnp.concatenate(tiles)
+                self.put(dim, slice(start, start + 8 * len(tiles)), value, value, out)
                 continue
             if dim == 0:
                 low, high = slice(0, grid.height), slice(grid.rows - grid.height, grid.rows)
@@ -143,13 +152,15 @@
                 continue
             start = self.start(part, dim)
             if dim == 2:
-                sides = self.both(dim, slice(start, start + 8), got)
+                dup = grid.dup
+                before, after = self.both(dim, slice(start, start + 8 * grid.tiles(count)), got)
+                merged = jnp.where(lane_of(before) % (2 * dup) < dup, roll(after, -dup, 1), roll(before, dup, 1))
                 for i, c in enumerate(channels):
-                    parts = []
-                    for side, lane in zip(sides, (0, LANES - grid.dup)):
-                        pieces = [roll(side, lane - grid.stride * k - grid.dup * c, 1) for k in range(grid.groups)]
-                        parts.append(jnp.concatenate(pieces))
-                    result[i][dim] = tuple(parts)
+                    pieces = []
+                    for k in range(grid.groups):
+                        tile, at = grid.place(count, c, k)
+                        pieces.append(roll(merged[8 * tile : 8 * tile + 8], -at - dup, 1))
+                    result[i][dim] = (jnp.concatenate(pieces),) * 2
             else:
                 size = grid.lines(dim)
                 for i, c in enumerate(channels):
@@ -313,6 +324,8 @@
 
 
 def beside_of(before, after):
+    if before is after:
+        return before
     return jnp.where(lane_of(before) < LANES // 2, before, after)
 
 
@@ -433,10 +446,9 @@
     first_round = Message((fine, 4), (mid, 1), (low, 1))
     second_round = Message((fine, 4))
     third_round = Message((fine, 8), (mid, 6, 2), (low, 6, 2))
-    fourth_round = Message((fine, 1), {1: 7 * mid.depth}, {1: 7 * low.depth}, (fine, 6, 1, 2))
-    fifth_round = Message((fine, 3, 1, 2), (mid, 2), {2: 3 * depth})
-    late_round = Message((fine, 9, 0), {0: 4 * mid_window.line}, {0: 4 * low_window.line}, dims=(0,))
-    late = len(sends((0,)))
+    fourth_round = Message((fine, 1), {1: 4 * mid.depth}, {1: 4 * low.depth}, {2: 4 * depth})
+    fifth_round = Message((mid, 2), {1: 2 * depth}, {2: 3 * depth})
+    late_round = Message((fine, 9), {0: 4 * mid_window.line}, {0: 4 * low_window.line})
 
     def flat(array):
         return array.reshape(array.shape[:-3] + (rows, width))
@@ -602,13 +614,12 @@
         b_out[...] = b
         x_out[...] = b * (OMEGA / stencil[0])
         fourth_round.emit(0, products(stencil, x_out), buffers)
-        fourth_round.emit(3, [same(fine_couplings, range(6))] * 3, buffers)
         for part, grid, values, side in ((1, mid, mid_couplings, mid_side), (2, low, low_couplings, low_side)):
             side[...] = pack_sides([beside_of(*faces[2]) for faces in third_round.faces(part, got)], grid.dup)
             ends = []
             for y in (0, grid.height - 1):
                 lines = pl.ds(y, grid.depth, stride=grid.height)
-                parts = [values[c, lines, :] for c in range(6)]
+                parts = [fold(jnp.concatenate([values[c, lines, :], values[c + 1, lines, :]])) for c in (0, 2, 4)]
                 ends.append(jnp.concatenate(parts + [side[lines, :]]))
             fourth_round.put_rows(part, 1, *ends, buffers)
 
@@ -639,8 +650,7 @@
         for step in (mid.height, 1):
             channels.append([near, (lambda at, s=step: x_out[moved(at, s), :], lambda at, s=step: x_out[moved(at, -s), :])])
         channels.append([near, (lambda at: roll(x_out[at, :], -mid.dup, 1), lambda at: roll(x_out[at, :], mid.dup, 1))])
-        fifth_round.emit(1, channels, buffers)
-        fifth_round.emit(0, [same(adj_out, range(3))] * 3, buffers)
+        fifth_round.emit(0, channels, buffers)
 
     x_mid, adj_known, adj_factor, *buffers = call(
         residual_kernel,
@@ -657,7 +667,10 @@
             (2, low_window, low_own, low_side, windows[2], windows[3]),
         ):
             grid, line = window.grid, window.line
-            halves = fourth_round.rows(part, 1, got)
+            halves = []
+            for half in fourth_round.rows(part, 1, got):
+                pairs = [unfold(half[k * grid.depth : (k + 1) * grid.depth]) for k in range(3)]
+                halves.append(jnp.concatenate(pairs + [half[3 * grid.depth :]]))
             ours[...] = jnp.zeros(ours.shape, F32)
             theirs[...] = jnp.zeros(theirs.shape, F32)
             pairs = [(ours.at[c], own.at[c], c) for c in range(6)] + [(theirs, side, 6)]
@@ -703,7 +716,7 @@
 
     def low_kernel(x, one, mid_couplings, two, last, *rest):
         got, (sent, mark, ends, temp) = rest[:swaps], rest[swaps:]
-        (rim,) = fifth_round.halos(1, got, ends, [0])
+        (rim,) = fifth_round.halos(0, got, ends, [0])
         value = x[...]
         total = (1.0 - OMEGA) * value
         for dim in range(3):
@@ -781,7 +794,7 @@
     everyone = lax.all_to_all(sent, AXES, 0, 0)
 
     def late_kernel(mark, adj, couplings, mid_around, mid_beside, low_around, low_beside, *buffers):
-        late_round.emit(0, [same(adj, range(3)) + same(couplings, range(6))], buffers)
+        late_round.emit(0, [same(couplings, range(6)) + same(adj, range(3))] * 3, buffers)
         for part, window, ours, theirs in ((1, mid_window, mid_around, mid_beside), (2, low_window, low_around, low_beside)):
             ends = []
             for a in (0, window.grid.depth - 1):
@@ -795,12 +808,12 @@
         (mark, adj_known, fine_couplings, mid_around, mid_beside, low_around, low_beside),
         late_round.buffers(),
     )
-    late_got = swap(buffers, (0,))
+    late_got = swap(buffers)
 
     def window_kernel(mark, x, *rest):
-        (third, fourth, fifth), (x_out, lines_out, sides_out) = [rest[k * swaps : (k + 1) * swaps] for k in range(3)], rest[3 * swaps :]
+        got, (x_out,) = rest[:swaps], rest[swaps:]
         x_out[...] = jnp.zeros(x_out.shape, F32)
-        near, far = fifth_round.faces(1, fifth)
+        near, far = fifth_round.faces(0, got)
         mid_window.fill(x_out.at[0], x[...])
         mid_window.fill(x_out.at[1], beside_of(*near[2]))
         mid_window.fill(x_out.at[2], beside_of(*far[2]))
@@ -809,41 +822,8 @@
                 x_out[0, mid_window.layer(layer), :] = value
             for y, value in zip((-1 - step, mid.height + step), faces[1]):
                 x_out[0, mid_window.row(y), :] = value
-        channels = fourth_round.faces(3, fourth) + third_round.faces(0, third, range(1, 4)) + fifth_round.faces(0, fifth)
-        for c, faces in enumerate(channels):
-            lines_out[c] = jnp.concatenate(faces[1])
-        sides = [beside_of(*faces[2]) for faces in channels]
-        for c in range(6):
-            sides_out[c] = pack_sides(sides[2 * c : 2 * c + 2], 1)
-
-    x_windows, line_halos, side_halos = call(
-        window_kernel,
-        (mark, x_mid, *third_got, *fourth_got, *fifth_got),
-        [out(3, mid_window.rows, LANES), out(12, 2 * depth, LANES), out(6, rows, LANES)],
-    )
-
-    def ends_kernel(*rest):
-        third, got, (*lines, layers_out) = rest[:swaps], rest[swaps : swaps + late], rest[swaps + late :]
-        for part, window, ours, theirs in ((1, mid_window, *lines[:2]), (2, low_window, *lines[2:])):
-            line = window.line
-            for k, half in enumerate(late_round.rows(part, 0, got)):
-                at = slice(k * line, (k + 1) * line)
-                for pair in range(3):
-                    both = unfold(half[pair * line : (pair + 1) * line])
-                    ours[2 * pair, at, :] = both[:line]
-                    ours[2 * pair + 1, at, :] = both[line:]
-                theirs[at, :] = half[3 * line :]
-        channels = late_round.faces(0, got)
-        channels = channels[3:] + third_round.faces(0, third, range(1, 4)) + channels[:3]
-        for c, faces in enumerate(channels):
-            layers_out[c] = jnp.concatenate(faces[0])
-
-    mid_ends, low_ends = (2 * mid_window.line, LANES), (2 * low_window.line, LANES)
-    *ends, layer_halos = call(
-        ends_kernel,
-        (*third_got, *late_got),
-        [out(6, *mid_ends), out(*mid_ends), out(6, *low_ends), out(*low_ends), out(12, 2 * height, LANES)],
-    )
+
+    (x_windows,) = call(window_kernel, (mark, x_mid, *fifth_got), [out(3, mid_window.rows, LANES)])
 
     last_rows, last_line = sizes[2] * sizes[1] * last_height, sizes[1] * last_height
     last_base = -(-(last_line + low_window.rim) // 8) * 8
@@ -963,13 +943,17 @@
             x[1, mid_window.row(y + sy), :] = sides(got, 1)
             x[2, mid_window.row(y), :] = sides(got, 2)
 
-    def full(window, lines, ends, side_lines, side_ends):
+    def full(part, window, lines, side_lines, got):
         line, none = window.line, jnp.zeros((window.line, LANES), F32)
-        packed = jnp.concatenate([none, side_ends[:line, :], side_lines[...], side_ends[line:, :], none])
-        return (
-            lambda c: jnp.concatenate([none, ends[c, :line, :], lines[c], ends[c, line:, :], none]),
-            lambda c: unpack_side(packed, c, window.grid.dup),
-        )
+        ends = late_round.rows(part, 0, got)
+        packed = jnp.concatenate([none, ends[0][3 * line :], side_lines[...], ends[1][3 * line :], none])
+
+        def around(c):
+            pair = slice(c // 2 * line, (c // 2 + 1) * line)
+            own = slice(c % 2 * line, (c % 2 + 1) * line)
+            return jnp.concatenate([none, unfold(ends[0][pair])[own], lines[c], unfold(ends[1][pair])[own], none])
+
+        return around, lambda c: unpack_side(packed, c, window.grid.dup)
 
     def gradient_factors(mobility, pressure, trans, trans_before, *rest):
         got, (inner, layer_out, line_out, side_out, ends) = rest[:swaps], rest[swaps:]
@@ -1006,13 +990,6 @@
         mid_beside,
         low_around,
         low_beside,
-        mid_ends,
-        mid_side_ends,
-        low_ends,
-        low_side_ends,
-        layer_halos,
-        line_halos,
-        side_halos,
         adj_known,
         adj_factor,
         couplings,
@@ -1020,20 +997,21 @@
         layer_terms,
         line_terms,
         side_terms,
-        adj_out,
-        grad_out,
-        *scratch,
+        *rest,
     ):
-        last_temp, low_x, low_temp, x, temp, ends, around, beside, value_ref, adj, grad, sems = scratch
-        added = spread_last(solve_last(everyone, last_temp), low_temp)
+        late_got, third_got, (adj_out, grad_out) = rest[:swaps], rest[swaps : 2 * swaps], rest[2 * swaps : 2 * swaps + 2]
+        last_temp, low_x, low_temp, x, temp, ends, around, beside, value_ref, adj, grad, sems = rest[2 * swaps + 2 :]
+        x[...] = x_windows[...]
+        mid_edges(everyone, x)
         low_values = low_windows(everyone, low_temp, low_x)
-        pair = full(low_window, low_around, low_ends, low_beside, low_side_ends)
+        added = spread_last(solve_last(everyone, last_temp), temp)
+        pair = full(2, low_window, low_around, low_beside, late_got)
         results = smooth(low_values, added, pair, low_window.line, low.dup)
         inner = slice(low_window.line, (low.depth + 3) * low_window.line)
         added = [spread_rows(v[inner], low.depth + 2, low_window.line, temp) for v in results]
-        x[...] = x_windows[...]
-        mid_edges(everyone, x)
-        pair = full(mid_window, mid_around, mid_ends, mid_beside, mid_side_ends)
+        pair = full(1, mid_window, mid_around, mid_beside, late_got)
+        beyond = late_round.faces(0, late_got)
+        factors = third_round.faces(0, third_got, range(1, 4))
         around[...], beside[...] = smooth([x[k] for k in range(3)], added, pair, mid_window.line, mid.dup)
 
         def own(ref):
@@ -1082,36 +1060,22 @@
         for k, (a, here, there) in enumerate(layers):
             shifts = [here, value[:height]] if k == 0 else [value[rows - height :], here]
             shifts += ended(here, one_row(a, -1), one_row(a, mid.height)) + along_x(here, there)
-            layer_gains.append(gain(here, shifts, lambda c: layer_halos[c, k * height : (k + 1) * height, :]))
+            layer_gains.append(gain(here, shifts, lambda c: beyond[c][0][k]))
         for k, (y, here, there) in enumerate(rows_y):
             inside = value_ref[pl.ds(0 if k == 0 else height - 1, depth, stride=height), :]
             shifts = ended(here, one_row(-1, y), one_row(mid.depth, y))
             shifts += ([here, inside] if k == 0 else [inside, here]) + along_x(here, there)
-            line_gains.append(gain(here, shifts, lambda c: line_halos[c, k * depth : (k + 1) * depth, :]))
+            line_gains.append(gain(here, shifts, lambda c: beyond[c][1][k]))
         lane = lane_of(side)
         side_rim = Rim(fine, [[v[2] for v in layers], [v[2] for v in rows_y], (side, side)], ends, 1)
         shifts = [shift(side, dim) for dim in range(2) for shift in (side_rim.previous, side_rim.following)]
         shifts += [jnp.where(lane < LANES // 2, side, value), jnp.where(lane < LANES // 2, value, side)]
-
-        def side_halo(c):
-            return unpack_side(side_halos[c // 2], 1, 1) if c % 2 else side_halos[c // 2]
-
-        side_gain = gain(side, shifts, side_halo)
+        side_gain = gain(side, shifts, lambda c: beyond[c][2][0])
         adj_rims = []
         for c in range(3):
-            known, factor = 9 + c, 6 + c
-            faces = [
-                [
-                    layer_halos[known, k * height : (k + 1) * height, :]
-                    + layer_halos[factor, k * height : (k + 1) * height, :] * layer_gains[k]
-                    for k in range(2)
-                ],
-                [
-                    line_halos[known, k * depth : (k + 1) * depth, :] + line_halos[factor, k * depth : (k + 1) * depth, :] * line_gains[k]
-                    for k in range(2)
-                ],
-                (side_halo(known) + side_halo(factor) * side_gain,) * 2,
-            ]
+            known, factor = beyond[6 + c], factors[c]
+            faces = [[known[dim][k] + factor[dim][k] * gains[k] for k in range(2)] for dim, gains in enumerate((layer_gains, line_gains))]
+            faces.append((known[2][0] + factor[2][0] * side_gain,) * 2)
             adj_rims.append(Rim(fine, faces, ends, 2 + c))
         values = [adj[c] for c in range(3)]
         lines = pl.ds(0, depth, stride=height)
@@ -1138,15 +1102,15 @@
 
     adjoint, gradient = call(
         final_kernel,
-        (everyone, x_windows, mid_around, mid_beside, low_around, low_beside, *ends, layer_halos)
-        + (line_halos, side_halos, adj_known, adj_factor, fine_couplings, *gradient_inputs),
+        (everyone, x_windows, mid_around, mid_beside, low_around, low_beside)
+        + (adj_known, adj_factor, fine_couplings, *gradient_inputs, *late_got, *third_got),
         [out(3, rows, LANES)] * 2,
         [
             (min(sizes[0], last_groups), 2 * last_rows, LANES),
             (3, low_window.rows, LANES),
             (max(low_window.rows, 96, 2 * last_base + last_rows), LANES),
             (3, mid_window.rows, LANES),
-            (mid_window.rows, LANES),
+            (max(mid_window.rows, 2 * last_base + last_rows), LANES),
             (6, rows, LANES),
             (mid_window.rows, LANES),
             (mid_window.rows, LANES),

time: 53.4 us -> 52.3 us (0.979)
  waiting for transfers between devices: 12.5 us -> 8.25 us
  starting transfers between devices: 29.4 us -> 33.3 us
  Pallas kernels: 10.3 us -> 9.54 us
    ppermute x27 -> x30, waiting for transfers between devices: 12.5 us -> 8.24 us  [swap(): lax.ppermute(b, AXES, pair_route(BY_DIM[dim], phase))]
    ppermute x27 -> x30, starting transfers between devices: 26.7 us -> 30.7 us  [swap(): lax.ppermute(b, AXES, pair_route(BY_DIM[dim], phase))]
    pallas_call x14 -> x13, Pallas kernels: 10.3 us -> 9.54 us  [call(): pl.pallas_call(kernel, out_shape=list(outputs), in_specs=specs(len(inputs...]
  transfers between devices with their start and end apart: 28 -> 31, of which waited for: 9 -> 9; matrix products, arithmetic and copies ran while one was open for 0% -> 0% of each run, Pallas kernels for 5% -> 4%
where the time goes in v7:
time: 52.3 us; the launch traced here: 52.1 us
  starting transfers between devices  33.3 us (64%)
  Pallas kernels  9.54 us (18%)
  waiting for transfers between devices  8.25 us (16%)
  between operations  0.88 us (2%)
    ppermute x30, starting transfers between devices, swap(): lax.ppermute(b, AXES, pair_route(BY_DIM[dim], phase))  30.7 us
    pallas_call x13, Pallas kernels, call(): pl.pallas_call(kernel, out_shape=list(outputs), in_specs=specs(len(inputs...  9.54 us
    ppermute x30, waiting for transfers between devices, swap(): lax.ppermute(b, AXES, pair_route(BY_DIM[dim], phase))  8.24 us
    all_to_all x1, starting transfers between devices, local(): everyone = lax.all_to_all(sent, AXES, 0, 0)  2.59 us
  transfers between devices with their start and end apart: 31, of which 9 were waited for; matrix products, arithmetic and copies ran while one was open for 0% of the time, Pallas kernels for 4%

profile of v7, /device:TPU:0, one launch (start us, length us, event | category | flops | bytes accessed | tf_op | source)
XLA Modules:
  0.0 52.1 jit_solution(12493844953399999207)
XLA Ops:
  0.7 1.7 %shard_map.131 = (f32[3,128,128]{2,1,0:T(8,128)S(1)}, f32[3,128,128]{2,1,0:T(8,128)S(1)}, f32[9,128,128]{2,1,0:T(8,128)S(1)}, f32[3,128,128]{2,1,0:T(8,128)S(1)}...) custom-call(f32[3,128,128]{2,1,0:T(8,128)} %bitcast.37, ...), custom_call_target="tpu_custom_call" | custom-call | tf_op jit(solution)/shard_map/pallas_call | solution.py:411
  2.9 4.1 %collective-permute-start.1 = (f32[76,128]{1,0:T(8,128)S(1)}, f32[76,128]{1,0:T(8,128)S(1)}, u32[]{:S(2)}, u32[]{:S(2)}) collective-permute-start(f32[76,128]{1,0:T(8,128)S(1)} %get-tuple-element.68), channel_id=1, source_target_pairs={{0,1},{1,0},{2,3},{3,2},{4,5},{5,4},{6,7},{7,6},{8,9},{9,8},{10,11... | collective-permute-start | bytes 116744 | tf_op jit(solution)/shard_map/ppermute | solution.py:48
  7.0 1.5 %collective-permute-start.2 = (f32[38,128]{1,0:T(8,128)S(1)}, f32[38,128]{1,0:T(8,128)S(1)}, u32[]{:S(2)}, u32[]{:S(2)}) collective-permute-start(f32[38,128]{1,0:T(8,128)S(1)} %get-tuple-element.69), channel_id=1, source_target_pairs={{0,4},{1,5},{2,6},{3,7},{4,0},{5,1},{6,2},{7,3},{8,12},{9,13},{10,... | collective-permute-start | bytes 58376 | tf_op jit(solution)/shard_map/ppermute | solution.py:48
  8.6 1.5 %collective-permute-start.4 = (f32[24,128]{1,0:T(8,128)S(1)}, f32[24,128]{1,0:T(8,128)S(1)}, u32[]{:S(2)}, u32[]{:S(2)}) collective-permute-start(f32[24,128]{1,0:T(8,128)S(1)} %get-tuple-element.71), channel_id=1, source_target_pairs={{0,8},{1,9},{2,10},{3,11},{4,12},{5,13},{6,14},{7,15},{8,0},{9,1},... | collective-permute-start | bytes 36872 | tf_op jit(solution)/shard_map/ppermute | solution.py:48
  10.1 1.5 %collective-permute-done.3.rest_3_ = f32[24,128]{1,0:T(8,128)S(1)} collective-permute-done((f32[24,128]{1,0:T(8,128)S(1)}, f32[24,128]{1,0:T(8,128)S(1)}, u32[]{:S(2)}, u32[]{:S(2)}) %collective-permute-start.3) | collective-permute-done | bytes 12320 | tf_op jit(solution)/shard_map/ppermute | solution.py:48
  12.5 1.5 %collective-permute-start.6 = (f32[64,128]{1,0:T(8,128)S(1)}, f32[64,128]{1,0:T(8,128)S(1)}, u32[]{:S(2)}, u32[]{:S(2)}) collective-permute-start(f32[64,128]{1,0:T(8,128)S(1)} %get-tuple-element.80), channel_id=1, source_target_pairs={{0,1},{1,0},{2,3},{3,2},{4,5},{5,4},{6,7},{7,6},{8,9},{9,8},{10,11... | collective-permute-start | bytes 98312 | tf_op jit(solution)/shard_map/ppermute | solution.py:48
  15.0 1.2 %collective-permute-start.9 = (f32[8,128]{1,0:T(8,128)S(1)}, f32[8,128]{1,0:T(8,128)S(1)}, u32[]{:S(2)}, u32[]{:S(2)}) collective-permute-start(f32[8,128]{1,0:T(8,128)S(1)} %get-tuple-element.83), channel_id=1, source_target_pairs={{0,8},{1,9},{2,10},{3,11},{4,12},{5,13},{6,14},{7,15},{8,0},{9,1},... | collective-permute-start | bytes 12296 | tf_op jit(solution)/shard_map/ppermute | solution.py:48
  16.2 1.1 %shard_map.133 = (f32[6,32,128]{2,1,0:T(8,128)S(1)}, f32[6,8,128]{2,1,0:T(8,128)S(1)}, f32[3,128,128]{2,1,0:T(8,128)S(1)}) custom-call(f32[3,128,128]{2,1,0:T(8,128)} %bitcast.27, f32[7,32,128]{2,1,0:T(8,128)S(1)} %get-tuple-element.74.one, f32[7,8,128]{2,1,0:T(8,128)S(1)} %get-tuple-element.75.two, f32[76,128]{1,0:T(8,128)S(1)} %collective-permute-done.rest_0_, ...), custom_call_target="tpu_custom_call" | custom-call | tf_op jit(solution)/shard_map/pallas_call | solution.py:411
  19.5 1.4 %collective-permute-start.12 = (f32[64,128]{1,0:T(8,128)S(1)}, f32[64,128]{1,0:T(8,128)S(1)}, u32[]{:S(2)}, u32[]{:S(2)}) collective-permute-start(f32[64,128]{1,0:T(8,128)S(1)} %get-tuple-element.87), channel_id=1, source_target_pairs={{0,4},{1,5},{2,6},{3,7},{4,0},{5,1},{6,2},{7,3},{8,12},{9,13},{10,... | collective-permute-start | bytes 98312 | tf_op jit(solution)/shard_map/ppermute | solution.py:48
  21.2 1.1 %collective-permute-start.14 = (f32[32,128]{1,0:T(8,128)S(1)}, f32[32,128]{1,0:T(8,128)S(1)}, u32[]{:S(2)}, u32[]{:S(2)}) collective-permute-start(f32[32,128]{1,0:T(8,128)S(1)} %get-tuple-element.89), channel_id=1, source_target_pairs={{0,8},{1,9},{2,10},{3,11},{4,12},{5,13},{6,14},{7,15},{8,0},{9,1},... | collective-permute-start | bytes 49160 | tf_op jit(solution)/shard_map/ppermute | solution.py:48
  22.5 1.6 %collective-permute-done.13.rest_3_.rest_8_ = f32[32,128]{1,0:T(8,128)S(1)} collective-permute-done((f32[32,128]{1,0:T(8,128)S(1)}, f32[32,128]{1,0:T(8,128)S(1)}, u32[]{:S(2)}, u32[]{:S(2)}) %collective-permute-start.13) | collective-permute-done | bytes 16416 | tf_op jit(solution)/shard_map/ppermute | solution.py:48
  24.6 1.6 %collective-permute-start.16 = (f32[16,128]{1,0:T(8,128)S(1)}, f32[16,128]{1,0:T(8,128)S(1)}, u32[]{:S(2)}, u32[]{:S(2)}) collective-permute-start(f32[16,128]{1,0:T(8,128)S(1)} %get-tuple-element.93), channel_id=1, source_target_pairs={{0,1},{1,0},{2,3},{3,2},{4,5},{5,4},{6,7},{7,6},{8,9},{9,8},{10,11... | collective-permute-start | bytes 24584 | tf_op jit(solution)/shard_map/ppermute | solution.py:48
  27.3 1.3 %collective-permute-start.19 = (f32[40,128]{1,0:T(8,128)S(1)}, f32[40,128]{1,0:T(8,128)S(1)}, u32[]{:S(2)}, u32[]{:S(2)}) collective-permute-start(f32[40,128]{1,0:T(8,128)S(1)} %get-tuple-element.96), channel_id=1, source_target_pairs={{0,8},{1,9},{2,10},{3,11},{4,12},{5,13},{6,14},{7,15},{8,0},{9,1},... | collective-permute-start | bytes 61448 | tf_op jit(solution)/shard_map/ppermute | solution.py:48
  28.6 1.3 %collective-permute-done.17.rest_2_ = f32[32,128]{1,0:T(8,128)S(1)} collective-permute-done((f32[32,128]{1,0:T(8,128)S(1)}, f32[32,128]{1,0:T(8,128)S(1)}, u32[]{:S(2)}, u32[]{:S(2)}) %collective-permute-start.17) | collective-permute-done | bytes 16416 | tf_op jit(solution)/shard_map/ppermute | solution.py:48
  31.0 1.8 %collective-permute-start.21 = (f32[16,128]{1,0:T(8,128)S(1)}, f32[16,128]{1,0:T(8,128)S(1)}, u32[]{:S(2)}, u32[]{:S(2)}) collective-permute-start(f32[16,128]{1,0:T(8,128)S(1)} %get-tuple-element.99), channel_id=1, source_target_pairs={{0,1},{1,0},{2,3},{3,2},{4,5},{5,4},{6,7},{7,6},{8,9},{9,8},{10,11... | collective-permute-start | bytes 24584 | tf_op jit(solution)/shard_map/ppermute | solution.py:48
  32.8 1.3 %collective-permute-start.22 = (f32[24,128]{1,0:T(8,128)S(1)}, f32[24,128]{1,0:T(8,128)S(1)}, u32[]{:S(2)}, u32[]{:S(2)}) collective-permute-start(f32[24,128]{1,0:T(8,128)S(1)} %get-tuple-element.100), channel_id=1, source_target_pairs={{0,4},{1,5},{2,6},{3,7},{4,0},{5,1},{6,2},{7,3},{8,12},{9,13},{10,... | collective-permute-start | bytes 36872 | tf_op jit(solution)/shard_map/ppermute | solution.py:48
  34.3 1.2 %collective-permute-start.24 = (f32[32,128]{1,0:T(8,128)S(1)}, f32[32,128]{1,0:T(8,128)S(1)}, u32[]{:S(2)}, u32[]{:S(2)}) collective-permute-start(f32[32,128]{1,0:T(8,128)S(1)} %get-tuple-element.102), channel_id=1, source_target_pairs={{0,8},{1,9},{2,10},{3,11},{4,12},{5,13},{6,14},{7,15},{8,0},{9,1},... | collective-permute-start | bytes 49160 | tf_op jit(solution)/shard_map/ppermute | solution.py:48
  37.3 1.3 %shard_map.138 = (f32[32,8,128]{2,1,0:T(8,128)}, f32[8,128]{1,0:T(8,128)S(1)}) custom-call(f32[32,128]{1,0:T(8,128)S(1)} %get-tuple-element.97.x, f32[7,32,128]{2,1,0:T(8,128)S(1)} %get-tuple-element.74.one, f32[6,32,128]{2,1,0:T(8,128)S(1)} %get-tuple-element.77.mid_couplings.mid_own, f32[7,8,128]{2,1,0:T(8,128)S(1)} %get-tuple-element.75.two, ...), custom_call_target="tpu_custom_call" | custom-call | tf_op jit(solution)/shard_map/pallas_call | solution.py:411
  38.6 2.6 %all-to-all-start = ((f32[32,8,128]{2,1,0:T(8,128)}), f32[32,8,128]{2,1,0:T(8,128)S(1)}, u32[]{:S(2)}, u32[]{:S(2)}) async-start(f32[32,8,128]{2,1,0:T(8,128)} %get-tuple-element.103), calls=%async_computation | async-start | bytes 262144 | tf_op jit(solution)/shard_map/all_to_all | solution.py:794
  41.8 3.0 %collective-permute-start.26 = (f32[240,128]{1,0:T(8,128)S(1)}, f32[240,128]{1,0:T(8,128)S(1)}, u32[]{:S(2)}, u32[]{:S(2)}) collective-permute-start(f32[240,128]{1,0:T(8,128)S(1)} %get-tuple-element.118), channel_id=1, source_target_pairs={{0,1},{1,0},{2,3},{3,2},{4,5},{5,4},{6,7},{7,6},{8,9},{9,8},{10,11... | collective-permute-start | bytes 368648 | tf_op jit(solution)/shard_map/ppermute | solution.py:48
  44.8 1.5 %collective-permute-start.27 = (f32[72,128]{1,0:T(8,128)S(1)}, f32[72,128]{1,0:T(8,128)S(1)}, u32[]{:S(2)}, u32[]{:S(2)}) collective-permute-start(f32[72,128]{1,0:T(8,128)S(1)} %get-tuple-element.119), channel_id=1, source_target_pairs={{0,4},{1,5},{2,6},{3,7},{4,0},{5,1},{6,2},{7,3},{8,12},{9,13},{10,... | collective-permute-start | bytes 110600 | tf_op jit(solution)/shard_map/ppermute | solution.py:48
  46.7 1.2 %collective-permute-start.29 = (f32[24,128]{1,0:T(8,128)S(1)}, f32[24,128]{1,0:T(8,128)S(1)}, u32[]{:S(2)}, u32[]{:S(2)}) collective-permute-start(f32[24,128]{1,0:T(8,128)S(1)} %get-tuple-element.121), channel_id=1, source_target_pairs={{0,8},{1,9},{2,10},{3,11},{4,12},{5,13},{6,14},{7,15},{8,0},{9,1},... | collective-permute-start | bytes 36872 | tf_op jit(solution)/shard_map/ppermute | solution.py:48
  48.4 1.2 %collective-permute-done.28.rest_3_ = f32[24,128]{1,0:T(8,128)S(1)} collective-permute-done((f32[24,128]{1,0:T(8,128)S(1)}, f32[24,128]{1,0:T(8,128)S(1)}, u32[]{:S(2)}, u32[]{:S(2)}) %collective-permute-start.28) | collective-permute-done | bytes 12320 | tf_op jit(solution)/shard_map/ppermute | solution.py:48
  49.6 2.4 %shard_map.143 = (f32[3,128,128]{2,1,0:T(8,128)}, f32[3,128,128]{2,1,0:T(8,128)}) custom-call(f32[32,8,128]{2,1,0:T(8,128)S(1)} %all-to-all-done.everyone, f32[3,128,128]{2,1,0:T(8,128)S(1)} %shard_map.139.x_windows, f32[6,64,128]{2,1,0:T(8,128)S(1)} %get-tuple-element.107.mid_around, f32[64,128]{1,0:T(8,128)S(1)} %get-tuple-element.108.mid_beside, ...), custom_call_target="tpu_custom_call" | custom-call | tf_op jit(solution)/shard_map/pallas_call | solution.py:411
  (72 shorter events, 11.2 us)
Async XLA Ops:
  2.3 9.3 %collective-permute-start = (f32[76,128]{1,0:T(8,128)S(1)}, f32[76,128]{1,0:T(8,128)S(1)}, u32[]{:S(2)}, u32[]{:S(2)}) collective-permute-start(f32[76,128]{1,0:T(8,128)S(1)} %get-tuple-element.67), channel_id=1, source_target_pairs={{0,8},{1,2},{2,1},{3,11},{4,12},{5,6},{6,5},{7,15},{8,0},{9,10},{1... | collective-permute-start | bytes 116744 | tf_op jit(solution)/shard_map/ppermute | solution.py:48
  2.9 8.8 %collective-permute-start.1 = (f32[76,128]{1,0:T(8,128)S(1)}, f32[76,128]{1,0:T(8,128)S(1)}, u32[]{:S(2)}, u32[]{:S(2)}) collective-permute-start(f32[76,128]{1,0:T(8,128)S(1)} %get-tuple-element.68), channel_id=1, source_target_pairs={{0,1},{1,0},{2,3},{3,2},{4,5},{5,4},{6,7},{7,6},{8,9},{9,8},{10,11... | collective-permute-start | bytes 116744 | tf_op jit(solution)/shard_map/ppermute | solution.py:48
  7.0 4.7 %collective-permute-start.2 = (f32[38,128]{1,0:T(8,128)S(1)}, f32[38,128]{1,0:T(8,128)S(1)}, u32[]{:S(2)}, u32[]{:S(2)}) collective-permute-start(f32[38,128]{1,0:T(8,128)S(1)} %get-tuple-element.69), channel_id=1, source_target_pairs={{0,4},{1,5},{2,6},{3,7},{4,0},{5,1},{6,2},{7,3},{8,12},{9,13},{10,... | collective-permute-start | bytes 58376 | tf_op jit(solution)/shard_map/ppermute | solution.py:48
  8.5 3.2 %collective-permute-start.3 = (f32[24,128]{1,0:T(8,128)S(1)}, f32[24,128]{1,0:T(8,128)S(1)}, u32[]{:S(2)}, u32[]{:S(2)}) collective-permute-start(f32[24,128]{1,0:T(8,128)S(1)} %get-tuple-element.70), channel_id=1, source_target_pairs={{0,24},{1,25},{2,26},{3,27},{4,28},{5,29},{6,30},{7,31},{8,16},{9,... | collective-permute-start | bytes 36872 | tf_op jit(solution)/shard_map/ppermute | solution.py:48
  12.3 5.5 %collective-permute-start.5 = (f32[64,128]{1,0:T(8,128)S(1)}, f32[64,128]{1,0:T(8,128)S(1)}, u32[]{:S(2)}, u32[]{:S(2)}) collective-permute-start(f32[64,128]{1,0:T(8,128)S(1)} %get-tuple-element.79), channel_id=1, source_target_pairs={{0,8},{1,2},{2,1},{3,11},{4,12},{5,6},{6,5},{7,15},{8,0},{9,10},{1... | collective-permute-start | bytes 98312 | tf_op jit(solution)/shard_map/ppermute | solution.py:48
  12.5 5.3 %collective-permute-start.6 = (f32[64,128]{1,0:T(8,128)S(1)}, f32[64,128]{1,0:T(8,128)S(1)}, u32[]{:S(2)}, u32[]{:S(2)}) collective-permute-start(f32[64,128]{1,0:T(8,128)S(1)} %get-tuple-element.80), channel_id=1, source_target_pairs={{0,1},{1,0},{2,3},{3,2},{4,5},{5,4},{6,7},{7,6},{8,9},{9,8},{10,11... | collective-permute-start | bytes 98312 | tf_op jit(solution)/shard_map/ppermute | solution.py:48
  14.0 3.7 %collective-permute-start.7 = (f32[32,128]{1,0:T(8,128)S(1)}, f32[32,128]{1,0:T(8,128)S(1)}, u32[]{:S(2)}, u32[]{:S(2)}) collective-permute-start(f32[32,128]{1,0:T(8,128)S(1)} %get-tuple-element.81), channel_id=1, source_target_pairs={{0,4},{1,5},{2,6},{3,7},{4,0},{5,1},{6,2},{7,3},{8,12},{9,13},{10,... | collective-permute-start | bytes 49160 | tf_op jit(solution)/shard_map/ppermute | solution.py:48
  18.5 5.7 %collective-permute-start.10 = (f32[128,128]{1,0:T(8,128)S(1)}, f32[128,128]{1,0:T(8,128)S(1)}, u32[]{:S(2)}, u32[]{:S(2)}) collective-permute-start(f32[128,128]{1,0:T(8,128)S(1)} %get-tuple-element.85), channel_id=1, source_target_pairs={{0,8},{1,2},{2,1},{3,11},{4,12},{5,6},{6,5},{7,15},{8,0},{9,10},{1... | collective-permute-start | bytes 196616 | tf_op jit(solution)/shard_map/ppermute | solution.py:48
  18.6 5.5 %collective-permute-start.11 = (f32[128,128]{1,0:T(8,128)S(1)}, f32[128,128]{1,0:T(8,128)S(1)}, u32[]{:S(2)}, u32[]{:S(2)}) collective-permute-start(f32[128,128]{1,0:T(8,128)S(1)} %get-tuple-element.86), channel_id=1, source_target_pairs={{0,1},{1,0},{2,3},{3,2},{4,5},{5,4},{6,7},{7,6},{8,9},{9,8},{10,11... | collective-permute-start | bytes 196616 | tf_op jit(solution)/shard_map/ppermute | solution.py:48
  19.5 4.6 %collective-permute-start.12 = (f32[64,128]{1,0:T(8,128)S(1)}, f32[64,128]{1,0:T(8,128)S(1)}, u32[]{:S(2)}, u32[]{:S(2)}) collective-permute-start(f32[64,128]{1,0:T(8,128)S(1)} %get-tuple-element.87), channel_id=1, source_target_pairs={{0,4},{1,5},{2,6},{3,7},{4,0},{5,1},{6,2},{7,3},{8,12},{9,13},{10,... | collective-permute-start | bytes 98312 | tf_op jit(solution)/shard_map/ppermute | solution.py:48
  20.9 3.3 %collective-permute-start.13 = (f32[32,128]{1,0:T(8,128)S(1)}, f32[32,128]{1,0:T(8,128)S(1)}, u32[]{:S(2)}, u32[]{:S(2)}) collective-permute-start(f32[32,128]{1,0:T(8,128)S(1)} %get-tuple-element.88), channel_id=1, source_target_pairs={{0,24},{1,25},{2,26},{3,27},{4,28},{5,29},{6,30},{7,31},{8,16},{9,... | collective-permute-start | bytes 49160 | tf_op jit(solution)/shard_map/ppermute | solution.py:48
  24.5 4.1 %collective-permute-start.15 = (f32[16,128]{1,0:T(8,128)S(1)}, f32[16,128]{1,0:T(8,128)S(1)}, u32[]{:S(2)}, u32[]{:S(2)}) collective-permute-start(f32[16,128]{1,0:T(8,128)S(1)} %get-tuple-element.92), channel_id=1, source_target_pairs={{0,8},{1,2},{2,1},{3,11},{4,12},{5,6},{6,5},{7,15},{8,0},{9,10},{1... | collective-permute-start | bytes 24584 | tf_op jit(solution)/shard_map/ppermute | solution.py:48
  24.6 4.0 %collective-permute-start.16 = (f32[16,128]{1,0:T(8,128)S(1)}, f32[16,128]{1,0:T(8,128)S(1)}, u32[]{:S(2)}, u32[]{:S(2)}) collective-permute-start(f32[16,128]{1,0:T(8,128)S(1)} %get-tuple-element.93), channel_id=1, source_target_pairs={{0,1},{1,0},{2,3},{3,2},{4,5},{5,4},{6,7},{7,6},{8,9},{9,8},{10,11... | collective-permute-start | bytes 24584 | tf_op jit(solution)/shard_map/ppermute | solution.py:48
  26.2 3.7 %collective-permute-start.17 = (f32[32,128]{1,0:T(8,128)S(1)}, f32[32,128]{1,0:T(8,128)S(1)}, u32[]{:S(2)}, u32[]{:S(2)}) collective-permute-start(f32[32,128]{1,0:T(8,128)S(1)} %get-tuple-element.94), channel_id=1, source_target_pairs={{0,4},{1,5},{2,6},{3,7},{4,0},{5,1},{6,2},{7,3},{8,12},{9,13},{10,... | collective-permute-start | bytes 49160 | tf_op jit(solution)/shard_map/ppermute | solution.py:48
  27.1 3.3 %collective-permute-start.18 = (f32[40,128]{1,0:T(8,128)S(1)}, f32[40,128]{1,0:T(8,128)S(1)}, u32[]{:S(2)}, u32[]{:S(2)}) collective-permute-start(f32[40,128]{1,0:T(8,128)S(1)} %get-tuple-element.95), channel_id=1, source_target_pairs={{0,24},{1,25},{2,26},{3,27},{4,28},{5,29},{6,30},{7,31},{8,16},{9,... | collective-permute-start | bytes 61448 | tf_op jit(solution)/shard_map/ppermute | solution.py:48
  30.9 4.7 %collective-permute-start.20 = (f32[16,128]{1,0:T(8,128)S(1)}, f32[16,128]{1,0:T(8,128)S(1)}, u32[]{:S(2)}, u32[]{:S(2)}) collective-permute-start(f32[16,128]{1,0:T(8,128)S(1)} %get-tuple-element.98), channel_id=1, source_target_pairs={{0,8},{1,2},{2,1},{3,11},{4,12},{5,6},{6,5},{7,15},{8,0},{9,10},{1... | collective-permute-start | bytes 24584 | tf_op jit(solution)/shard_map/ppermute | solution.py:48
  31.0 4.7 %collective-permute-start.21 = (f32[16,128]{1,0:T(8,128)S(1)}, f32[16,128]{1,0:T(8,128)S(1)}, u32[]{:S(2)}, u32[]{:S(2)}) collective-permute-start(f32[16,128]{1,0:T(8,128)S(1)} %get-tuple-element.99), channel_id=1, source_target_pairs={{0,1},{1,0},{2,3},{3,2},{4,5},{5,4},{6,7},{7,6},{8,9},{9,8},{10,11... | collective-permute-start | bytes 24584 | tf_op jit(solution)/shard_map/ppermute | solution.py:48
  32.8 3.7 %collective-permute-start.22 = (f32[24,128]{1,0:T(8,128)S(1)}, f32[24,128]{1,0:T(8,128)S(1)}, u32[]{:S(2)}, u32[]{:S(2)}) collective-permute-start(f32[24,128]{1,0:T(8,128)S(1)} %get-tuple-element.100), channel_id=1, source_target_pairs={{0,4},{1,5},{2,6},{3,7},{4,0},{5,1},{6,2},{7,3},{8,12},{9,13},{10,... | collective-permute-start | bytes 36872 | tf_op jit(solution)/shard_map/ppermute | solution.py:48
  34.1 3.2 %collective-permute-start.23 = (f32[32,128]{1,0:T(8,128)S(1)}, f32[32,128]{1,0:T(8,128)S(1)}, u32[]{:S(2)}, u32[]{:S(2)}) collective-permute-start(f32[32,128]{1,0:T(8,128)S(1)} %get-tuple-element.101), channel_id=1, source_target_pairs={{0,24},{1,25},{2,26},{3,27},{4,28},{5,29},{6,30},{7,31},{8,16},{9,... | collective-permute-start | bytes 49160 | tf_op jit(solution)/shard_map/ppermute | solution.py:48
  38.6 11.0 %all-to-all-start = ((f32[32,8,128]{2,1,0:T(8,128)}), f32[32,8,128]{2,1,0:T(8,128)S(1)}, u32[]{:S(2)}, u32[]{:S(2)}) async-start(f32[32,8,128]{2,1,0:T(8,128)} %get-tuple-element.103), calls=%async_computation | async-start | bytes 262144 | tf_op jit(solution)/shard_map/all_to_all | solution.py:794
  41.5 8.1 %collective-permute-start.25 = (f32[240,128]{1,0:T(8,128)S(1)}, f32[240,128]{1,0:T(8,128)S(1)}, u32[]{:S(2)}, u32[]{:S(2)}) collective-permute-start(f32[240,128]{1,0:T(8,128)S(1)} %get-tuple-element.117), channel_id=1, source_target_pairs={{0,8},{1,2},{2,1},{3,11},{4,12},{5,6},{6,5},{7,15},{8,0},{9,10},{1... | collective-permute-start | bytes 368648 | tf_op jit(solution)/shard_map/ppermute | solution.py:48
  41.8 7.8 %collective-permute-start.26 = (f32[240,128]{1,0:T(8,128)S(1)}, f32[240,128]{1,0:T(8,128)S(1)}, u32[]{:S(2)}, u32[]{:S(2)}) collective-permute-start(f32[240,128]{1,0:T(8,128)S(1)} %get-tuple-element.118), channel_id=1, source_target_pairs={{0,1},{1,0},{2,3},{3,2},{4,5},{5,4},{6,7},{7,6},{8,9},{9,8},{10,11... | collective-permute-start | bytes 368648 | tf_op jit(solution)/shard_map/ppermute | solution.py:48
  44.8 4.8 %collective-permute-start.27 = (f32[72,128]{1,0:T(8,128)S(1)}, f32[72,128]{1,0:T(8,128)S(1)}, u32[]{:S(2)}, u32[]{:S(2)}) collective-permute-start(f32[72,128]{1,0:T(8,128)S(1)} %get-tuple-element.119), channel_id=1, source_target_pairs={{0,4},{1,5},{2,6},{3,7},{4,0},{5,1},{6,2},{7,3},{8,12},{9,13},{10,... | collective-permute-start | bytes 110600 | tf_op jit(solution)/shard_map/ppermute | solution.py:48
  46.3 3.3 %collective-permute-start.28 = (f32[24,128]{1,0:T(8,128)S(1)}, f32[24,128]{1,0:T(8,128)S(1)}, u32[]{:S(2)}, u32[]{:S(2)}) collective-permute-start(f32[24,128]{1,0:T(8,128)S(1)} %get-tuple-element.120), channel_id=1, source_target_pairs={{0,24},{1,25},{2,26},{3,27},{4,28},{5,29},{6,30},{7,31},{8,16},{9,... | collective-permute-start | bytes 36872 | tf_op jit(solution)/shard_map/ppermute | solution.py:48
  (15 other events, 62.8 us)

commit v8 on v7

--- a/solution.py
+++ b/solution.py
@@ -61,8 +61,8 @@
     def tiles(self, count):
         return -(-2 * self.dup * count * self.groups // LANES)
 
-    def place(self, count, c, k):
-        return divmod(2 * self.dup * (count * k + c), LANES)
+    def place(self, c, k):
+        return divmod(2 * self.dup * (self.groups * c + k), LANES)
 
 
 class Message:
@@ -108,7 +108,7 @@
                 tiles = [jnp.zeros((8, LANES), F32)] * grid.tiles(count)
                 for c, (first, last) in enumerate(channels[dim]):
                     for k in range(grid.groups):
-                        tile, at = grid.place(count, c, k)
+                        tile, at = grid.place(c, k)
                         rows = slice(8 * k, 8 * k + 8)
                         value = last(rows)
                         if first is not last:
@@ -153,12 +153,11 @@
             start = self.start(part, dim)
             if dim == 2:
                 dup = grid.dup
-                before, after = self.both(dim, slice(start, start + 8 * grid.tiles(count)), got)
-                merged = jnp.where(lane_of(before) % (2 * dup) < dup, roll(after, -dup, 1), roll(before, dup, 1))
+                merged = self.sides(part, got)
                 for i, c in enumerate(channels):
                     pieces = []
                     for k in range(grid.groups):
-                        tile, at = grid.place(count, c, k)
+                        tile, at = grid.place(c, k)
                         pieces.append(roll(merged[8 * tile : 8 * tile + 8], -at - dup, 1))
                     result[i][dim] = (jnp.concatenate(pieces),) * 2
             else:
@@ -166,6 +165,18 @@
                 for i, c in enumerate(channels):
                     result[i][dim] = self.both(dim, slice(start + c * size, start + (c + 1) * size), got)
         return result
+
+    def sides(self, part, got):
+        grid, count = self.parts[part][:2]
+        start, dup = self.start(part, 2), grid.dup
+        before, after = self.both(2, slice(start, start + 8 * grid.tiles(count)), got)
+        return jnp.where(lane_of(before) % (2 * dup) < dup, roll(after, -dup, 1), roll(before, dup, 1))
+
+    def columns(self, part, got, channels=None):
+        grid, count = self.parts[part][:2]
+        merged = self.sides(part, got)
+        places = [grid.place(c, 0) for c in (range(count) if channels is None else channels)]
+        return [roll(merged[8 * tile : 8 * tile + 8], -at, 1) for tile, at in places]
 
     def halos(self, part, got, scratch, channels=None):
         return [Rim(self.parts[part][0], r, scratch, c) for c, r in enumerate(self.faces(part, got, channels))]
@@ -341,6 +352,26 @@
 
 def unpack_side(value, c, dup):
     return beside_of(roll(value, -dup * c, 1), roll(value, dup * c, 1))
+
+
+def pack_column(value):
+    tile = jnp.zeros((8, LANES), F32)
+    lane = lane_of(tile)
+    for k in range(value.shape[0] // 8):
+        tile = jnp.where((lane >= 2 * k) & (lane < 2 * k + 2), roll(value[8 * k : 8 * k + 8], 2 * k + 1, 1), tile)
+    return tile
+
+
+def unpack_column(tile, rows):
+    return jnp.concatenate([roll(tile, -2 * k - 1, 1) for k in range(rows // 8)])
+
+
+def column_ends(value, per, last):
+    step = per - 1 if last else 1
+    turned = pltpu.roll(value, step, 1, stride=per, stride_axis=0)
+    lane, row = lane_of(value), lax.broadcasted_iota(jnp.int32, value.shape, 0)
+    here = (lane // per == row) & (lane % per >= per - 2 if last else lane % per < 2)
+    return jnp.sum(jnp.where(here, turned, 0.0), axis=0, keepdims=True)
 
 
 def moved(rows, by):
@@ -446,9 +477,10 @@
     first_round = Message((fine, 4), (mid, 1), (low, 1))
     second_round = Message((fine, 4))
     third_round = Message((fine, 8), (mid, 6, 2), (low, 6, 2))
-    fourth_round = Message((fine, 1), {1: 4 * mid.depth}, {1: 4 * low.depth}, {2: 4 * depth})
-    fifth_round = Message((mid, 2), {1: 2 * depth}, {2: 3 * depth})
-    late_round = Message((fine, 9), {0: 4 * mid_window.line}, {0: 4 * low_window.line})
+    fourth_round = Message((fine, 1), {1: 4 * mid.depth}, {1: 4 * low.depth}, (fine, 6, 2), {2: 2 * depth})
+    fifth_round = Message((mid, 2), (fine, 3, 2), {1: 2 * depth}, {2: 2 * depth})
+    late_round = Message((fine, 9, 0, 1), {0: 4 * mid_window.line}, {0: 4 * low_window.line}, dims=(0, 1))
+    late = len(sends((0, 1)))
 
     def flat(array):
         return array.reshape(array.shape[:-3] + (rows, width))
@@ -614,6 +646,7 @@
         b_out[...] = b
         x_out[...] = b * (OMEGA / stencil[0])
         fourth_round.emit(0, products(stencil, x_out), buffers)
+        fourth_round.emit(3, [same(fine_couplings, range(6))] * 3, buffers)
         for part, grid, values, side in ((1, mid, mid_couplings, mid_side), (2, low, low_couplings, low_side)):
             side[...] = pack_sides([beside_of(*faces[2]) for faces in third_round.faces(part, got)], grid.dup)
             ends = []
@@ -651,6 +684,7 @@
             channels.append([near, (lambda at, s=step: x_out[moved(at, s), :], lambda at, s=step: x_out[moved(at, -s), :])])
         channels.append([near, (lambda at: roll(x_out[at, :], -mid.dup, 1), lambda at: roll(x_out[at, :], mid.dup, 1))])
         fifth_round.emit(0, channels, buffers)
+        fifth_round.emit(1, [same(adj_out, range(3))] * 3, buffers)
 
     x_mid, adj_known, adj_factor, *buffers = call(
         residual_kernel,
@@ -723,7 +757,7 @@
             total = total - mid_couplings[2 * dim] * rim.previous(value, dim)
             total = total - mid_couplings[2 * dim + 1] * rim.following(value, dim)
         residual = total * (one[0] * (1.0 / OMEGA))
-        b = pair_sum_rows(pair_sum_x(residual, mid.dup), mid.depth, mid.height, temp)
+        b = pair_sum_rows(pair_sum_x(residual, mid.dup), mid.depth, mid.height, temp.at[0])
         field = b * (OMEGA / two[0])
         to_next = [two[2 + 2 * dim] * field for dim in range(3)]
         to_previous = [two[1 + 2 * dim] * field for dim in range(3)]
@@ -739,7 +773,8 @@
             jnp.where(y == 0, -to_previous[1], jnp.where(y == low.height - 1, -to_next[1], 0.0)),
             jnp.where(lane < low.dup, -to_previous[2], jnp.where(lane >= LANES - low.dup, -to_next[2], 0.0)),
         ]
-        parts = [pair_sum_rows(pair_sum_x(v, low.dup), low.depth, low.height, temp) for v in [inner] + outer]
+        parts = [inner] + outer
+        parts = [pair_sum_rows(pair_sum_x(v, low.dup), low.depth, low.height, temp.at[1 + k]) for k, v in enumerate(parts)]
         parts = matmul(jnp.concatenate(parts), one_hot((LANES, LANES), lambda i, j: i == 2 * low.dup * j))
         parts = [parts[k * last_height : (k + 1) * last_height] for k in range(5)]
         upper = last[:last_height] + roll(parts[0], 7 * last_width, 1)
@@ -789,7 +824,7 @@
         low_kernel,
         (x_mid, one, mid_couplings, two, last, *fifth_got),
         [out(count, block, LANES), out(block, LANES)],
-        [(1, mid.rows, LANES), (mid.rows // 2, LANES)],
+        [(1, mid.rows, LANES), (6, mid.rows // 2, LANES)],
     )
     everyone = lax.all_to_all(sent, AXES, 0, 0)
 
@@ -808,7 +843,7 @@
         (mark, adj_known, fine_couplings, mid_around, mid_beside, low_around, low_beside),
         late_round.buffers(),
     )
-    late_got = swap(buffers)
+    late_got = swap(buffers, (0, 1))
 
     def window_kernel(mark, x, *rest):
         got, (x_out,) = rest[:swaps], rest[swaps:]
@@ -878,11 +913,11 @@
         at = last_base + (gz * (low.depth // 2) - 1) * last_line + gy * last_height - reach
         tiles = []
         for tile in range(0, field.shape[1], LANES):
-            temp[...] = jnp.zeros(temp.shape, F32)
-            temp[last_base : last_base + last_rows, :] = field[:, tile : tile + LANES]
-            tiles.append(jnp.concatenate([temp[pl.ds(at + k * last_line, half), :] for k in range(layers)]))
+            temp[12] = jnp.zeros(temp.shape[1:], F32)
+            temp[12, last_base : last_base + last_rows, :] = field[:, tile : tile + LANES]
+            tiles.append(jnp.concatenate([temp[12, pl.ds(at + k * last_line, half), :] for k in range(layers)]))
         both = matmul(jnp.concatenate(tiles, axis=1), one_hot((field.shape[1], 2 * LANES), taken))
-        return [spread_rows(both[:, k * LANES : (k + 1) * LANES], layers, half, temp) for k in range(2)]
+        return [spread_rows(both[:, k * LANES : (k + 1) * LANES], layers, half, temp.at[13 + k]) for k in range(2)]
 
     def low_windows(everyone, temp, result):
         around = [(sy, sz) for sz in (-1, 0, 1) for sy in (-1, 0, 1)]
@@ -999,8 +1034,10 @@
         side_terms,
         *rest,
     ):
-        late_got, third_got, (adj_out, grad_out) = rest[:swaps], rest[swaps : 2 * swaps], rest[2 * swaps : 2 * swaps + 2]
-        last_temp, low_x, low_temp, x, temp, ends, around, beside, value_ref, adj, grad, sems = rest[2 * swaps + 2 :]
+        late_got, third_got, fourth_got, fifth_got = (rest[max(0, k * swaps + late - swaps) : k * swaps + late] for k in range(4))
+        rest = rest[3 * swaps + late :]
+        adj_out, grad_out = rest[:2]
+        last_temp, low_x, low_temp, x, temp, ends, around, beside, value_ref, adj, grad, sems = rest[2:]
         x[...] = x_windows[...]
         mid_edges(everyone, x)
         low_values = low_windows(everyone, low_temp, low_x)
@@ -1008,30 +1045,32 @@
         pair = full(2, low_window, low_around, low_beside, late_got)
         results = smooth(low_values, added, pair, low_window.line, low.dup)
         inner = slice(low_window.line, (low.depth + 3) * low_window.line)
-        added = [spread_rows(v[inner], low.depth + 2, low_window.line, temp) for v in results]
+        added = [spread_rows(v[inner], low.depth + 2, low_window.line, temp.at[10 + k]) for k, v in enumerate(results)]
         pair = full(1, mid_window, mid_around, mid_beside, late_got)
         beyond = late_round.faces(0, late_got)
+        columns = fourth_round.columns(3, fourth_got) + third_round.columns(0, third_got, range(1, 4))
+        columns += fifth_round.columns(1, fifth_got)
         factors = third_round.faces(0, third_got, range(1, 4))
         around[...], beside[...] = smooth([x[k] for k in range(3)], added, pair, mid_window.line, mid.dup)
 
-        def own(ref):
+        def own(ref, slot):
             lines = [ref[mid_window.layer(a), :] for a in range(mid.depth)]
-            return spread_rows(jnp.concatenate(lines), mid.depth, mid.height, temp)
-
-        def layer(ref, a):
-            return spread_lines(ref[mid_window.layer(a), :], temp)
-
-        def lines(ref, y):
-            return spread_lines(ref[mid_window.row(y), :], temp)
+            return spread_rows(jnp.concatenate(lines), mid.depth, mid.height, temp.at[slot])
+
+        def layer(ref, a, slot):
+            return spread_lines(ref[mid_window.layer(a), :], temp.at[slot])
+
+        def lines(ref, y, slot):
+            return spread_lines(ref[mid_window.row(y), :], temp.at[slot])
 
         def one_row(a, y):
             at = mid_window.at(a, y)
             return around[at : at + 1, :]
 
-        value, side = own(around), own(beside)
+        value, side = own(around, 0), own(beside, 1)
         value_ref[...] = value
-        layers = [(a, layer(around, a), layer(beside, a)) for a in (-1, mid.depth)]
-        rows_y = [(y, lines(around, y), lines(beside, y)) for y in (-1, mid.height)]
+        layers = [(a, layer(around, a, k), layer(beside, a, k + 1)) for k, a in ((2, -1), (4, mid.depth))]
+        rows_y = [(y, lines(around, y, k), lines(beside, y, k + 1)) for k, y in ((6, -1), (8, mid.height))]
         rim = Rim(fine, [[v[1] for v in layers], [v[1] for v in rows_y], (side, side)], ends, 0)
 
         def gain(value, shifts, coupling):
@@ -1066,16 +1105,29 @@
             shifts = ended(here, one_row(-1, y), one_row(mid.depth, y))
             shifts += ([here, inside] if k == 0 else [inside, here]) + along_x(here, there)
             line_gains.append(gain(here, shifts, lambda c: beyond[c][1][k]))
-        lane = lane_of(side)
-        side_rim = Rim(fine, [[v[2] for v in layers], [v[2] for v in rows_y], (side, side)], ends, 1)
-        shifts = [shift(side, dim) for dim in range(2) for shift in (side_rim.previous, side_rim.following)]
-        shifts += [jnp.where(lane < LANES // 2, side, value), jnp.where(lane < LANES // 2, value, side)]
-        side_gain = gain(side, shifts, lambda c: beyond[c][2][0])
+        per = height // 4
+        beside_column, own_column = pack_column(side), pack_column(value)
+        lane, row = lane_of(own_column), lax.broadcasted_iota(jnp.int32, (8, LANES), 0)
+        ends_z = [pack_column(v[2]) for v in layers]
+        top = 2 * fine.groups - per
+        shifts = [
+            jnp.where(lane < per, ends_z[0], roll(beside_column, per, 1)),
+            jnp.where(lane >= top, roll(ends_z[1], top, 1), roll(beside_column, -per, 1)),
+        ]
+        up, down = roll(beside_column, 1, 0), roll(beside_column, -1, 0)
+        ends_y = [column_ends(rows_y[k][2], per, k == 1) for k in range(2)]
+        shifts += [
+            jnp.where(row > 0, up, jnp.where(lane % per < 2, ends_y[0], roll(up, 2, 1))),
+            jnp.where(row < 7, down, jnp.where(lane % per >= per - 2, ends_y[1], roll(down, -2, 1))),
+            jnp.where(lane % 2 == 1, beside_column, own_column),
+            jnp.where(lane % 2 == 1, own_column, beside_column),
+        ]
+        side_gain = gain(beside_column, shifts, lambda c: columns[c])
         adj_rims = []
         for c in range(3):
             known, factor = beyond[6 + c], factors[c]
             faces = [[known[dim][k] + factor[dim][k] * gains[k] for k in range(2)] for dim, gains in enumerate((layer_gains, line_gains))]
-            faces.append((known[2][0] + factor[2][0] * side_gain,) * 2)
+            faces.append((unpack_column(columns[9 + c] + columns[6 + c] * side_gain, rows),) * 2)
             adj_rims.append(Rim(fine, faces, ends, 2 + c))
         values = [adj[c] for c in range(3)]
         lines = pl.ds(0, depth, stride=height)
@@ -1103,14 +1155,14 @@
     adjoint, gradient = call(
         final_kernel,
         (everyone, x_windows, mid_around, mid_beside, low_around, low_beside)
-        + (adj_known, adj_factor, fine_couplings, *gradient_inputs, *late_got, *third_got),
+        + (adj_known, adj_factor, fine_couplings, *gradient_inputs, *late_got, *third_got, *fourth_got, *fifth_got),
         [out(3, rows, LANES)] * 2,
         [
             (min(sizes[0], last_groups), 2 * last_rows, LANES),
             (3, low_window.rows, LANES),
             (max(low_window.rows, 96, 2 * last_base + last_rows), LANES),
             (3, mid_window.rows, LANES),
-            (max(mid_window.rows, 2 * last_base + last_rows), LANES),
+            (15, max(mid_window.rows, 2 * last_base + last_rows), LANES),
             (6, rows, LANES),
             (mid_window.rows, LANES),
             (mid_window.rows, LANES),

time: 52.3 us -> 52 us (level)
  starting transfers between devices: 33.3 us -> 31.7 us
  waiting for transfers between devices: 8.25 us -> 9.73 us
    ppermute x30 -> x28, starting transfers between devices: 30.7 us -> 29.1 us  [swap(): lax.ppermute(b, AXES, pair_route(BY_DIM[dim], phase))]
    ppermute x30 -> x28, waiting for transfers between devices: 8.24 us -> 9.62 us  [swap(): lax.ppermute(b, AXES, pair_route(BY_DIM[dim], phase))]
  transfers between devices with their start and end apart: 31 -> 29, of which waited for: 9 -> 11; matrix products, arithmetic and copies ran while one was open for 0% -> 0% of each run, Pallas kernels for 4% -> 4%
where the time goes in v8:
time: 52 us; the launch traced here: 51.8 us
  starting transfers between devices  31.7 us (61%)
  waiting for transfers between devices  9.73 us (19%)
  Pallas kernels  9.35 us (18%)
  between operations  0.86 us (2%)
    ppermute x28, starting transfers between devices, swap(): lax.ppermute(b, AXES, pair_route(BY_DIM[dim], phase))  29.1 us
    ppermute x28, waiting for transfers between devices, swap(): lax.ppermute(b, AXES, pair_route(BY_DIM[dim], phase))  9.62 us
    pallas_call x13, Pallas kernels, call(): pl.pallas_call(kernel, out_shape=list(outputs), in_specs=specs(len(inputs...  9.35 us
    all_to_all x1, starting transfers between devices, local(): everyone = lax.all_to_all(sent, AXES, 0, 0)  2.59 us
  transfers between devices with their start and end apart: 29, of which 11 were waited for; matrix products, arithmetic and copies ran while one was open for 0% of the time, Pallas kernels for 4%

profile of v8, /device:TPU:0, one launch (start us, length us, event | category | flops | bytes accessed | tf_op | source)
XLA Modules:
  0.0 51.8 jit_solution(4012067125283780181)
XLA Ops:
  0.7 1.7 %shard_map.131 = (f32[3,128,128]{2,1,0:T(8,128)S(1)}, f32[3,128,128]{2,1,0:T(8,128)S(1)}, f32[9,128,128]{2,1,0:T(8,128)S(1)}, f32[3,128,128]{2,1,0:T(8,128)S(1)}...) custom-call(f32[3,128,128]{2,1,0:T(8,128)} %bitcast.37, ...), custom_call_target="tpu_custom_call" | custom-call | tf_op jit(solution)/shard_map/pallas_call | solution.py:442
  2.9 4.1 %collective-permute-start.1 = (f32[76,128]{1,0:T(8,128)S(1)}, f32[76,128]{1,0:T(8,128)S(1)}, u32[]{:S(2)}, u32[]{:S(2)}) collective-permute-start(f32[76,128]{1,0:T(8,128)S(1)} %get-tuple-element.66), channel_id=1, source_target_pairs={{0,1},{1,0},{2,3},{3,2},{4,5},{5,4},{6,7},{7,6},{8,9},{9,8},{10,11... | collective-permute-start | bytes 116744 | tf_op jit(solution)/shard_map/ppermute | solution.py:48
  7.0 1.5 %collective-permute-start.2 = (f32[38,128]{1,0:T(8,128)S(1)}, f32[38,128]{1,0:T(8,128)S(1)}, u32[]{:S(2)}, u32[]{:S(2)}) collective-permute-start(f32[38,128]{1,0:T(8,128)S(1)} %get-tuple-element.67), channel_id=1, source_target_pairs={{0,4},{1,5},{2,6},{3,7},{4,0},{5,1},{6,2},{7,3},{8,12},{9,13},{10,... | collective-permute-start | bytes 58376 | tf_op jit(solution)/shard_map/ppermute | solution.py:48
  8.6 1.5 %collective-permute-start.4 = (f32[24,128]{1,0:T(8,128)S(1)}, f32[24,128]{1,0:T(8,128)S(1)}, u32[]{:S(2)}, u32[]{:S(2)}) collective-permute-start(f32[24,128]{1,0:T(8,128)S(1)} %get-tuple-element.69), channel_id=1, source_target_pairs={{0,8},{1,9},{2,10},{3,11},{4,12},{5,13},{6,14},{7,15},{8,0},{9,1},... | collective-permute-start | bytes 36872 | tf_op jit(solution)/shard_map/ppermute | solution.py:48
  10.1 1.5 %collective-permute-done.3.rest_3_ = f32[24,128]{1,0:T(8,128)S(1)} collective-permute-done((f32[24,128]{1,0:T(8,128)S(1)}, f32[24,128]{1,0:T(8,128)S(1)}, u32[]{:S(2)}, u32[]{:S(2)}) %collective-permute-start.3) | collective-permute-done | bytes 12320 | tf_op jit(solution)/shard_map/ppermute | solution.py:48
  12.5 1.5 %collective-permute-start.6 = (f32[64,128]{1,0:T(8,128)S(1)}, f32[64,128]{1,0:T(8,128)S(1)}, u32[]{:S(2)}, u32[]{:S(2)}) collective-permute-start(f32[64,128]{1,0:T(8,128)S(1)} %get-tuple-element.78), channel_id=1, source_target_pairs={{0,1},{1,0},{2,3},{3,2},{4,5},{5,4},{6,7},{7,6},{8,9},{9,8},{10,11... | collective-permute-start | bytes 98312 | tf_op jit(solution)/shard_map/ppermute | solution.py:48
  15.0 1.2 %collective-permute-start.9 = (f32[8,128]{1,0:T(8,128)S(1)}, f32[8,128]{1,0:T(8,128)S(1)}, u32[]{:S(2)}, u32[]{:S(2)}) collective-permute-start(f32[8,128]{1,0:T(8,128)S(1)} %get-tuple-element.81), channel_id=1, source_target_pairs={{0,8},{1,9},{2,10},{3,11},{4,12},{5,13},{6,14},{7,15},{8,0},{9,1},... | collective-permute-start | bytes 12296 | tf_op jit(solution)/shard_map/ppermute | solution.py:48
  16.2 1.1 %shard_map.133 = (f32[6,32,128]{2,1,0:T(8,128)S(1)}, f32[6,8,128]{2,1,0:T(8,128)S(1)}, f32[3,128,128]{2,1,0:T(8,128)S(1)}) custom-call(f32[3,128,128]{2,1,0:T(8,128)} %bitcast.27, f32[7,32,128]{2,1,0:T(8,128)S(1)} %get-tuple-element.72.one, f32[7,8,128]{2,1,0:T(8,128)S(1)} %get-tuple-element.73.two, f32[76,128]{1,0:T(8,128)S(1)} %collective-permute-done.rest_0_, ...), custom_call_target="tpu_custom_call" | custom-call | tf_op jit(solution)/shard_map/pallas_call | solution.py:442
  19.5 1.4 %collective-permute-start.12 = (f32[64,128]{1,0:T(8,128)S(1)}, f32[64,128]{1,0:T(8,128)S(1)}, u32[]{:S(2)}, u32[]{:S(2)}) collective-permute-start(f32[64,128]{1,0:T(8,128)S(1)} %get-tuple-element.85), channel_id=1, source_target_pairs={{0,4},{1,5},{2,6},{3,7},{4,0},{5,1},{6,2},{7,3},{8,12},{9,13},{10,... | collective-permute-start | bytes 98312 | tf_op jit(solution)/shard_map/ppermute | solution.py:48
  21.2 1.1 %collective-permute-start.14 = (f32[32,128]{1,0:T(8,128)S(1)}, f32[32,128]{1,0:T(8,128)S(1)}, u32[]{:S(2)}, u32[]{:S(2)}) collective-permute-start(f32[32,128]{1,0:T(8,128)S(1)} %get-tuple-element.87), channel_id=1, source_target_pairs={{0,8},{1,9},{2,10},{3,11},{4,12},{5,13},{6,14},{7,15},{8,0},{9,1},... | collective-permute-start | bytes 49160 | tf_op jit(solution)/shard_map/ppermute | solution.py:48
  22.5 1.6 %collective-permute-done.13.rest_3_.rest_6_ = f32[32,128]{1,0:T(8,128)S(1)} collective-permute-done((f32[32,128]{1,0:T(8,128)S(1)}, f32[32,128]{1,0:T(8,128)S(1)}, u32[]{:S(2)}, u32[]{:S(2)}) %collective-permute-start.13) | collective-permute-done | bytes 16416 | tf_op jit(solution)/shard_map/ppermute | solution.py:48
  24.7 1.6 %collective-permute-start.16 = (f32[16,128]{1,0:T(8,128)S(1)}, f32[16,128]{1,0:T(8,128)S(1)}, u32[]{:S(2)}, u32[]{:S(2)}) collective-permute-start(f32[16,128]{1,0:T(8,128)S(1)} %get-tuple-element.91), channel_id=1, source_target_pairs={{0,1},{1,0},{2,3},{3,2},{4,5},{5,4},{6,7},{7,6},{8,9},{9,8},{10,11... | collective-permute-start | bytes 24584 | tf_op jit(solution)/shard_map/ppermute | solution.py:48
  26.3 0.9 %collective-permute-start.17 = (f32[32,128]{1,0:T(8,128)S(1)}, f32[32,128]{1,0:T(8,128)S(1)}, u32[]{:S(2)}, u32[]{:S(2)}) collective-permute-start(f32[32,128]{1,0:T(8,128)S(1)} %get-tuple-element.92), channel_id=1, source_target_pairs={{0,4},{1,5},{2,6},{3,7},{4,0},{5,1},{6,2},{7,3},{8,12},{9,13},{10,... | collective-permute-start | bytes 49160 | tf_op jit(solution)/shard_map/ppermute | solution.py:48
  27.4 1.3 %collective-permute-start.19 = (f32[40,128]{1,0:T(8,128)S(1)}, f32[40,128]{1,0:T(8,128)S(1)}, u32[]{:S(2)}, u32[]{:S(2)}) collective-permute-start(f32[40,128]{1,0:T(8,128)S(1)} %get-tuple-element.94), channel_id=1, source_target_pairs={{0,8},{1,9},{2,10},{3,11},{4,12},{5,13},{6,14},{7,15},{8,0},{9,1},... | collective-permute-start | bytes 61448 | tf_op jit(solution)/shard_map/ppermute | solution.py:48
  28.7 1.3 %collective-permute-done.17.rest_2_.rest_10_ = f32[32,128]{1,0:T(8,128)S(1)} collective-permute-done((f32[32,128]{1,0:T(8,128)S(1)}, f32[32,128]{1,0:T(8,128)S(1)}, u32[]{:S(2)}, u32[]{:S(2)}) %collective-permute-start.17) | collective-permute-done | bytes 16416 | tf_op jit(solution)/shard_map/ppermute | solution.py:48
  31.1 1.8 %collective-permute-start.21 = (f32[16,128]{1,0:T(8,128)S(1)}, f32[16,128]{1,0:T(8,128)S(1)}, u32[]{:S(2)}, u32[]{:S(2)}) collective-permute-start(f32[16,128]{1,0:T(8,128)S(1)} %get-tuple-element.97), channel_id=1, source_target_pairs={{0,1},{1,0},{2,3},{3,2},{4,5},{5,4},{6,7},{7,6},{8,9},{9,8},{10,11... | collective-permute-start | bytes 24584 | tf_op jit(solution)/shard_map/ppermute | solution.py:48
  32.9 1.3 %collective-permute-start.22 = (f32[24,128]{1,0:T(8,128)S(1)}, f32[24,128]{1,0:T(8,128)S(1)}, u32[]{:S(2)}, u32[]{:S(2)}) collective-permute-start(f32[24,128]{1,0:T(8,128)S(1)} %get-tuple-element.98), channel_id=1, source_target_pairs={{0,4},{1,5},{2,6},{3,7},{4,0},{5,1},{6,2},{7,3},{8,12},{9,13},{10,... | collective-permute-start | bytes 36872 | tf_op jit(solution)/shard_map/ppermute | solution.py:48
  34.4 1.2 %collective-permute-start.24 = (f32[32,128]{1,0:T(8,128)S(1)}, f32[32,128]{1,0:T(8,128)S(1)}, u32[]{:S(2)}, u32[]{:S(2)}) collective-permute-start(f32[32,128]{1,0:T(8,128)S(1)} %get-tuple-element.100), channel_id=1, source_target_pairs={{0,8},{1,9},{2,10},{3,11},{4,12},{5,13},{6,14},{7,15},{8,0},{9,1},... | collective-permute-start | bytes 49160 | tf_op jit(solution)/shard_map/ppermute | solution.py:48
  37.4 1.3 %shard_map.138 = (f32[32,8,128]{2,1,0:T(8,128)}, f32[8,128]{1,0:T(8,128)S(1)}) custom-call(f32[32,128]{1,0:T(8,128)S(1)} %get-tuple-element.95.x, f32[7,32,128]{2,1,0:T(8,128)S(1)} %get-tuple-element.72.one, f32[6,32,128]{2,1,0:T(8,128)S(1)} %get-tuple-element.75.mid_couplings.mid_own, f32[7,8,128]{2,1,0:T(8,128)S(1)} %get-tuple-element.73.two, ...), custom_call_target="tpu_custom_call" | custom-call | tf_op jit(solution)/shard_map/pallas_call | solution.py:442
  38.7 2.6 %all-to-all-start = ((f32[32,8,128]{2,1,0:T(8,128)}), f32[32,8,128]{2,1,0:T(8,128)S(1)}, u32[]{:S(2)}, u32[]{:S(2)}) async-start(f32[32,8,128]{2,1,0:T(8,128)} %get-tuple-element.101), calls=%async_computation | async-start | bytes 262144 | tf_op jit(solution)/shard_map/all_to_all | solution.py:829
  41.8 3.0 %collective-permute-start.26 = (f32[240,128]{1,0:T(8,128)S(1)}, f32[240,128]{1,0:T(8,128)S(1)}, u32[]{:S(2)}, u32[]{:S(2)}) collective-permute-start(f32[240,128]{1,0:T(8,128)S(1)} %get-tuple-element.116), channel_id=1, source_target_pairs={{0,1},{1,0},{2,3},{3,2},{4,5},{5,4},{6,7},{7,6},{8,9},{9,8},{10,11... | collective-permute-start | bytes 368648 | tf_op jit(solution)/shard_map/ppermute | solution.py:48
  44.8 1.5 %collective-permute-start.27 = (f32[72,128]{1,0:T(8,128)S(1)}, f32[72,128]{1,0:T(8,128)S(1)}, u32[]{:S(2)}, u32[]{:S(2)}) collective-permute-start(f32[72,128]{1,0:T(8,128)S(1)} %get-tuple-element.117), channel_id=1, source_target_pairs={{0,4},{1,5},{2,6},{3,7},{4,0},{5,1},{6,2},{7,3},{8,12},{9,13},{10,... | collective-permute-start | bytes 110600 | tf_op jit(solution)/shard_map/ppermute | solution.py:48
  46.8 2.1 %collective-permute-done.27.rest_2_ = f32[72,128]{1,0:T(8,128)S(1)} collective-permute-done((f32[72,128]{1,0:T(8,128)S(1)}, f32[72,128]{1,0:T(8,128)S(1)}, u32[]{:S(2)}, u32[]{:S(2)}) %collective-permute-start.27) | collective-permute-done | bytes 36896 | tf_op jit(solution)/shard_map/ppermute | solution.py:48
  49.4 2.3 %shard_map.143 = (f32[3,128,128]{2,1,0:T(8,128)}, f32[3,128,128]{2,1,0:T(8,128)}) custom-call(f32[32,8,128]{2,1,0:T(8,128)S(1)} %all-to-all-done.everyone, f32[3,128,128]{2,1,0:T(8,128)S(1)} %shard_map.139.x_windows, f32[6,64,128]{2,1,0:T(8,128)S(1)} %get-tuple-element.105.mid_around, f32[64,128]{1,0:T(8,128)S(1)} %get-tuple-element.106.mid_beside, ...), custom_call_target="tpu_custom_call" | custom-call | tf_op jit(solution)/shard_map/pallas_call | solution.py:442
  (68 shorter events, 10.4 us)
Async XLA Ops:
  2.3 9.3 %collective-permute-start = (f32[76,128]{1,0:T(8,128)S(1)}, f32[76,128]{1,0:T(8,128)S(1)}, u32[]{:S(2)}, u32[]{:S(2)}) collective-permute-start(f32[76,128]{1,0:T(8,128)S(1)} %get-tuple-element.65), channel_id=1, source_target_pairs={{0,8},{1,2},{2,1},{3,11},{4,12},{5,6},{6,5},{7,15},{8,0},{9,10},{1... | collective-permute-start | bytes 116744 | tf_op jit(solution)/shard_map/ppermute | solution.py:48
  2.9 8.8 %collective-permute-start.1 = (f32[76,128]{1,0:T(8,128)S(1)}, f32[76,128]{1,0:T(8,128)S(1)}, u32[]{:S(2)}, u32[]{:S(2)}) collective-permute-start(f32[76,128]{1,0:T(8,128)S(1)} %get-tuple-element.66), channel_id=1, source_target_pairs={{0,1},{1,0},{2,3},{3,2},{4,5},{5,4},{6,7},{7,6},{8,9},{9,8},{10,11... | collective-permute-start | bytes 116744 | tf_op jit(solution)/shard_map/ppermute | solution.py:48
  7.0 4.7 %collective-permute-start.2 = (f32[38,128]{1,0:T(8,128)S(1)}, f32[38,128]{1,0:T(8,128)S(1)}, u32[]{:S(2)}, u32[]{:S(2)}) collective-permute-start(f32[38,128]{1,0:T(8,128)S(1)} %get-tuple-element.67), channel_id=1, source_target_pairs={{0,4},{1,5},{2,6},{3,7},{4,0},{5,1},{6,2},{7,3},{8,12},{9,13},{10,... | collective-permute-start | bytes 58376 | tf_op jit(solution)/shard_map/ppermute | solution.py:48
  8.5 3.2 %collective-permute-start.3 = (f32[24,128]{1,0:T(8,128)S(1)}, f32[24,128]{1,0:T(8,128)S(1)}, u32[]{:S(2)}, u32[]{:S(2)}) collective-permute-start(f32[24,128]{1,0:T(8,128)S(1)} %get-tuple-element.68), channel_id=1, source_target_pairs={{0,24},{1,25},{2,26},{3,27},{4,28},{5,29},{6,30},{7,31},{8,16},{9,... | collective-permute-start | bytes 36872 | tf_op jit(solution)/shard_map/ppermute | solution.py:48
  12.3 5.5 %collective-permute-start.5 = (f32[64,128]{1,0:T(8,128)S(1)}, f32[64,128]{1,0:T(8,128)S(1)}, u32[]{:S(2)}, u32[]{:S(2)}) collective-permute-start(f32[64,128]{1,0:T(8,128)S(1)} %get-tuple-element.77), channel_id=1, source_target_pairs={{0,8},{1,2},{2,1},{3,11},{4,12},{5,6},{6,5},{7,15},{8,0},{9,10},{1... | collective-permute-start | bytes 98312 | tf_op jit(solution)/shard_map/ppermute | solution.py:48
  12.5 5.3 %collective-permute-start.6 = (f32[64,128]{1,0:T(8,128)S(1)}, f32[64,128]{1,0:T(8,128)S(1)}, u32[]{:S(2)}, u32[]{:S(2)}) collective-permute-start(f32[64,128]{1,0:T(8,128)S(1)} %get-tuple-element.78), channel_id=1, source_target_pairs={{0,1},{1,0},{2,3},{3,2},{4,5},{5,4},{6,7},{7,6},{8,9},{9,8},{10,11... | collective-permute-start | bytes 98312 | tf_op jit(solution)/shard_map/ppermute | solution.py:48
  14.0 3.7 %collective-permute-start.7 = (f32[32,128]{1,0:T(8,128)S(1)}, f32[32,128]{1,0:T(8,128)S(1)}, u32[]{:S(2)}, u32[]{:S(2)}) collective-permute-start(f32[32,128]{1,0:T(8,128)S(1)} %get-tuple-element.79), channel_id=1, source_target_pairs={{0,4},{1,5},{2,6},{3,7},{4,0},{5,1},{6,2},{7,3},{8,12},{9,13},{10,... | collective-permute-start | bytes 49160 | tf_op jit(solution)/shard_map/ppermute | solution.py:48
  18.5 5.7 %collective-permute-start.10 = (f32[128,128]{1,0:T(8,128)S(1)}, f32[128,128]{1,0:T(8,128)S(1)}, u32[]{:S(2)}, u32[]{:S(2)}) collective-permute-start(f32[128,128]{1,0:T(8,128)S(1)} %get-tuple-element.83), channel_id=1, source_target_pairs={{0,8},{1,2},{2,1},{3,11},{4,12},{5,6},{6,5},{7,15},{8,0},{9,10},{1... | collective-permute-start | bytes 196616 | tf_op jit(solution)/shard_map/ppermute | solution.py:48
  18.6 5.5 %collective-permute-start.11 = (f32[128,128]{1,0:T(8,128)S(1)}, f32[128,128]{1,0:T(8,128)S(1)}, u32[]{:S(2)}, u32[]{:S(2)}) collective-permute-start(f32[128,128]{1,0:T(8,128)S(1)} %get-tuple-element.84), channel_id=1, source_target_pairs={{0,1},{1,0},{2,3},{3,2},{4,5},{5,4},{6,7},{7,6},{8,9},{9,8},{10,11... | collective-permute-start | bytes 196616 | tf_op jit(solution)/shard_map/ppermute | solution.py:48
  19.5 4.6 %collective-permute-start.12 = (f32[64,128]{1,0:T(8,128)S(1)}, f32[64,128]{1,0:T(8,128)S(1)}, u32[]{:S(2)}, u32[]{:S(2)}) collective-permute-start(f32[64,128]{1,0:T(8,128)S(1)} %get-tuple-element.85), channel_id=1, source_target_pairs={{0,4},{1,5},{2,6},{3,7},{4,0},{5,1},{6,2},{7,3},{8,12},{9,13},{10,... | collective-permute-start | bytes 98312 | tf_op jit(solution)/shard_map/ppermute | solution.py:48
  20.9 3.3 %collective-permute-start.13 = (f32[32,128]{1,0:T(8,128)S(1)}, f32[32,128]{1,0:T(8,128)S(1)}, u32[]{:S(2)}, u32[]{:S(2)}) collective-permute-start(f32[32,128]{1,0:T(8,128)S(1)} %get-tuple-element.86), channel_id=1, source_target_pairs={{0,24},{1,25},{2,26},{3,27},{4,28},{5,29},{6,30},{7,31},{8,16},{9,... | collective-permute-start | bytes 49160 | tf_op jit(solution)/shard_map/ppermute | solution.py:48
  24.6 4.1 %collective-permute-start.15 = (f32[16,128]{1,0:T(8,128)S(1)}, f32[16,128]{1,0:T(8,128)S(1)}, u32[]{:S(2)}, u32[]{:S(2)}) collective-permute-start(f32[16,128]{1,0:T(8,128)S(1)} %get-tuple-element.90), channel_id=1, source_target_pairs={{0,8},{1,2},{2,1},{3,11},{4,12},{5,6},{6,5},{7,15},{8,0},{9,10},{1... | collective-permute-start | bytes 24584 | tf_op jit(solution)/shard_map/ppermute | solution.py:48
  24.7 4.0 %collective-permute-start.16 = (f32[16,128]{1,0:T(8,128)S(1)}, f32[16,128]{1,0:T(8,128)S(1)}, u32[]{:S(2)}, u32[]{:S(2)}) collective-permute-start(f32[16,128]{1,0:T(8,128)S(1)} %get-tuple-element.91), channel_id=1, source_target_pairs={{0,1},{1,0},{2,3},{3,2},{4,5},{5,4},{6,7},{7,6},{8,9},{9,8},{10,11... | collective-permute-start | bytes 24584 | tf_op jit(solution)/shard_map/ppermute | solution.py:48
  26.3 3.7 %collective-permute-start.17 = (f32[32,128]{1,0:T(8,128)S(1)}, f32[32,128]{1,0:T(8,128)S(1)}, u32[]{:S(2)}, u32[]{:S(2)}) collective-permute-start(f32[32,128]{1,0:T(8,128)S(1)} %get-tuple-element.92), channel_id=1, source_target_pairs={{0,4},{1,5},{2,6},{3,7},{4,0},{5,1},{6,2},{7,3},{8,12},{9,13},{10,... | collective-permute-start | bytes 49160 | tf_op jit(solution)/shard_map/ppermute | solution.py:48
  27.2 3.3 %collective-permute-start.18 = (f32[40,128]{1,0:T(8,128)S(1)}, f32[40,128]{1,0:T(8,128)S(1)}, u32[]{:S(2)}, u32[]{:S(2)}) collective-permute-start(f32[40,128]{1,0:T(8,128)S(1)} %get-tuple-element.93), channel_id=1, source_target_pairs={{0,24},{1,25},{2,26},{3,27},{4,28},{5,29},{6,30},{7,31},{8,16},{9,... | collective-permute-start | bytes 61448 | tf_op jit(solution)/shard_map/ppermute | solution.py:48
  27.4 3.2 %collective-permute-start.19 = (f32[40,128]{1,0:T(8,128)S(1)}, f32[40,128]{1,0:T(8,128)S(1)}, u32[]{:S(2)}, u32[]{:S(2)}) collective-permute-start(f32[40,128]{1,0:T(8,128)S(1)} %get-tuple-element.94), channel_id=1, source_target_pairs={{0,8},{1,9},{2,10},{3,11},{4,12},{5,13},{6,14},{7,15},{8,0},{9,1},... | collective-permute-start | bytes 61448 | tf_op jit(solution)/shard_map/ppermute | solution.py:48
  31.0 4.7 %collective-permute-start.20 = (f32[16,128]{1,0:T(8,128)S(1)}, f32[16,128]{1,0:T(8,128)S(1)}, u32[]{:S(2)}, u32[]{:S(2)}) collective-permute-start(f32[16,128]{1,0:T(8,128)S(1)} %get-tuple-element.96), channel_id=1, source_target_pairs={{0,8},{1,2},{2,1},{3,11},{4,12},{5,6},{6,5},{7,15},{8,0},{9,10},{1... | collective-permute-start | bytes 24584 | tf_op jit(solution)/shard_map/ppermute | solution.py:48
  31.1 4.7 %collective-permute-start.21 = (f32[16,128]{1,0:T(8,128)S(1)}, f32[16,128]{1,0:T(8,128)S(1)}, u32[]{:S(2)}, u32[]{:S(2)}) collective-permute-start(f32[16,128]{1,0:T(8,128)S(1)} %get-tuple-element.97), channel_id=1, source_target_pairs={{0,1},{1,0},{2,3},{3,2},{4,5},{5,4},{6,7},{7,6},{8,9},{9,8},{10,11... | collective-permute-start | bytes 24584 | tf_op jit(solution)/shard_map/ppermute | solution.py:48
  32.9 3.7 %collective-permute-start.22 = (f32[24,128]{1,0:T(8,128)S(1)}, f32[24,128]{1,0:T(8,128)S(1)}, u32[]{:S(2)}, u32[]{:S(2)}) collective-permute-start(f32[24,128]{1,0:T(8,128)S(1)} %get-tuple-element.98), channel_id=1, source_target_pairs={{0,4},{1,5},{2,6},{3,7},{4,0},{5,1},{6,2},{7,3},{8,12},{9,13},{10,... | collective-permute-start | bytes 36872 | tf_op jit(solution)/shard_map/ppermute | solution.py:48
  34.3 3.2 %collective-permute-start.23 = (f32[32,128]{1,0:T(8,128)S(1)}, f32[32,128]{1,0:T(8,128)S(1)}, u32[]{:S(2)}, u32[]{:S(2)}) collective-permute-start(f32[32,128]{1,0:T(8,128)S(1)} %get-tuple-element.99), channel_id=1, source_target_pairs={{0,24},{1,25},{2,26},{3,27},{4,28},{5,29},{6,30},{7,31},{8,16},{9,... | collective-permute-start | bytes 49160 | tf_op jit(solution)/shard_map/ppermute | solution.py:48
  38.7 10.7 %all-to-all-start = ((f32[32,8,128]{2,1,0:T(8,128)}), f32[32,8,128]{2,1,0:T(8,128)S(1)}, u32[]{:S(2)}, u32[]{:S(2)}) async-start(f32[32,8,128]{2,1,0:T(8,128)} %get-tuple-element.101), calls=%async_computation | async-start | bytes 262144 | tf_op jit(solution)/shard_map/all_to_all | solution.py:829
  41.5 7.4 %collective-permute-start.25 = (f32[240,128]{1,0:T(8,128)S(1)}, f32[240,128]{1,0:T(8,128)S(1)}, u32[]{:S(2)}, u32[]{:S(2)}) collective-permute-start(f32[240,128]{1,0:T(8,128)S(1)} %get-tuple-element.115), channel_id=1, source_target_pairs={{0,8},{1,2},{2,1},{3,11},{4,12},{5,6},{6,5},{7,15},{8,0},{9,10},{1... | collective-permute-start | bytes 368648 | tf_op jit(solution)/shard_map/ppermute | solution.py:48
  41.8 7.5 %collective-permute-start.26 = (f32[240,128]{1,0:T(8,128)S(1)}, f32[240,128]{1,0:T(8,128)S(1)}, u32[]{:S(2)}, u32[]{:S(2)}) collective-permute-start(f32[240,128]{1,0:T(8,128)S(1)} %get-tuple-element.116), channel_id=1, source_target_pairs={{0,1},{1,0},{2,3},{3,2},{4,5},{5,4},{6,7},{7,6},{8,9},{9,8},{10,11... | collective-permute-start | bytes 368648 | tf_op jit(solution)/shard_map/ppermute | solution.py:48
  44.8 4.1 %collective-permute-start.27 = (f32[72,128]{1,0:T(8,128)S(1)}, f32[72,128]{1,0:T(8,128)S(1)}, u32[]{:S(2)}, u32[]{:S(2)}) collective-permute-start(f32[72,128]{1,0:T(8,128)S(1)} %get-tuple-element.117), channel_id=1, source_target_pairs={{0,4},{1,5},{2,6},{3,7},{4,0},{5,1},{6,2},{7,3},{8,12},{9,13},{10,... | collective-permute-start | bytes 110600 | tf_op jit(solution)/shard_map/ppermute | solution.py:48
  (13 other events, 54.9 us)

commit v9 on v8

--- a/solution.py
+++ b/solution.py
@@ -96,6 +96,22 @@
         start = self.start(part, dim)
         self.put(dim, slice(start, start + self.size(part, dim)), first, last, out)
 
+    def packed(self, part, pairs):
+        grid = self.parts[part][0]
+        lane = lax.broadcasted_iota(jnp.int32, (8, LANES), 1)
+        count, dup = self.parts[part][1], grid.dup
+        tiles = [jnp.zeros((8, LANES), F32)] * grid.tiles(count)
+        for c, (first, last) in enumerate(pairs):
+            for k in range(grid.groups):
+                tile, at = grid.place(c, k)
+                rows = slice(8 * k, 8 * k + 8)
+                value = last(rows)
+                if first is not last:
+                    value = jnp.where(lane < dup, first(rows), value)
+                here = (lane >= at) & (lane < at + 2 * dup)
+                tiles[tile] = jnp.where(here, roll(value, at + dup, 1), tiles[tile])
+        return jnp.concatenate(tiles)
+
     def emit(self, part, channels, out):
         grid = self.parts[part][0]
         lane = lax.broadcasted_iota(jnp.int32, (8, LANES), 1)
@@ -104,19 +120,8 @@
                 continue
             start = self.start(part, dim)
             if dim == 2:
-                count, dup = self.parts[part][1], grid.dup
-                tiles = [jnp.zeros((8, LANES), F32)] * grid.tiles(count)
-                for c, (first, last) in enumerate(channels[dim]):
-                    for k in range(grid.groups):
-                        tile, at = grid.place(c, k)
-                        rows = slice(8 * k, 8 * k + 8)
-                        value = last(rows)
-                        if first is not last:
-                            value = jnp.where(lane < dup, first(rows), value)
-                        here = (lane >= at) & (lane < at + 2 * dup)
-                        tiles[tile] = jnp.where(here, roll(value, at + dup, 1), tiles[tile])
-                value = jnp.concatenate(tiles)
-                self.put(dim, slice(start, start + 8 * len(tiles)), value, value, out)
+                value = self.packed(part, channels[dim])
+                self.put(dim, slice(start, start + value.shape[0]), value, value, out)
                 continue
             if dim == 0:
                 low, high = slice(0, grid.height), slice(grid.rows - grid.height, grid.rows)
@@ -631,22 +636,26 @@
     third_got = swap(buffers)
 
     def fine_kernel(stencil, *rest):
-        got, (result, ends) = rest[:swaps], rest[swaps:]
+        got, (result, sides, ends) = rest[:swaps], rest[swaps:]
         couplings(stencil, second_round.halos(0, got, ends, [3])[0], result)
-
-    (fine_couplings,) = call(fine_kernel, (stencil, *second_got), [out(6, rows, LANES)], [(1, rows, LANES)])
+        sides[...] = fourth_round.packed(3, same(result, range(6)))
+
+    coupling_sides = out(8 * fine.tiles(6), LANES)
+    fine_couplings, coupling_sides = call(
+        fine_kernel, (stencil, *second_got), [out(6, rows, LANES), coupling_sides], [(1, rows, LANES)]
+    )
 
     def products(coefs, field):
         return [[(product(coefs, 1 + 2 * dim, field), product(coefs, 2 + 2 * dim, field))] for dim in range(3)]
 
-    def pressure_kernel(rhs, it, diag, trans, trans_before, stencil, fine_couplings, mid_couplings, low_couplings, *rest):
+    def pressure_kernel(rhs, it, diag, trans, trans_before, stencil, coupling_sides, mid_couplings, low_couplings, *rest):
         got, (b_out, x_out, mid_side, low_side), buffers = rest[:swaps], rest[swaps : swaps + 4], rest[swaps + 4 : -1]
         (rim,) = third_round.halos(0, got, rest[-1], [0])
         b = rhs[0] - system_row(0, [it[c] for c in range(3)], rim, diag, trans, trans_before)
         b_out[...] = b
         x_out[...] = b * (OMEGA / stencil[0])
         fourth_round.emit(0, products(stencil, x_out), buffers)
-        fourth_round.emit(3, [same(fine_couplings, range(6))] * 3, buffers)
+        fourth_round.put_rows(3, 2, coupling_sides[...], coupling_sides[...], buffers)
         for part, grid, values, side in ((1, mid, mid_couplings, mid_side), (2, low, low_couplings, low_side)):
             side[...] = pack_sides([beside_of(*faces[2]) for faces in third_round.faces(part, got)], grid.dup)
             ends = []
@@ -658,7 +667,7 @@
 
     b_fine, x_fine, mid_side, low_side, *buffers = call(
         pressure_kernel,
-        (rhs, iterate, diag, trans, trans_before, stencil, fine_couplings, mid_couplings, low_couplings, *third_got),
+        (rhs, iterate, diag, trans, trans_before, stencil, coupling_sides, mid_couplings, low_couplings, *third_got),
         [out(rows, LANES)] * 2 + [out(mid.rows, LANES), out(low.rows, LANES)] + fourth_round.buffers(),
         [(1, rows, LANES)],
     )

time: 52 us -> 51.9 us (level)
  no operation moved by 1% of the time
where the time goes in v9:
time: 51.9 us; the launch traced here: 51.6 us
  starting transfers between devices  31.7 us (61%)
  waiting for transfers between devices  9.65 us (19%)
  Pallas kernels  9.33 us (18%)
  between operations  0.86 us (2%)
    ppermute x28, starting transfers between devices, swap(): lax.ppermute(b, AXES, pair_route(BY_DIM[dim], phase))  29.1 us
    ppermute x28, waiting for transfers between devices, swap(): lax.ppermute(b, AXES, pair_route(BY_DIM[dim], phase))  9.53 us
    pallas_call x13, Pallas kernels, call(): pl.pallas_call(kernel, out_shape=list(outputs), in_specs=specs(len(inputs...  9.33 us
    all_to_all x1, starting transfers between devices, local(): everyone = lax.all_to_all(sent, AXES, 0, 0)  2.59 us
  transfers between devices with their start and end apart: 29, of which 11 were waited for; matrix products, arithmetic and copies ran while one was open for 0% of the time, Pallas kernels for 4%

profile of v9, /device:TPU:0, one launch (start us, length us, event | category | flops | bytes accessed | tf_op | source)
XLA Modules:
  0.0 51.6 jit_solution(8385373437436850439)
XLA Ops:
  0.7 1.7 %shard_map.131 = (f32[3,128,128]{2,1,0:T(8,128)S(1)}, f32[3,128,128]{2,1,0:T(8,128)S(1)}, f32[9,128,128]{2,1,0:T(8,128)S(1)}, f32[3,128,128]{2,1,0:T(8,128)S(1)}...) custom-call(f32[3,128,128]{2,1,0:T(8,128)} %bitcast.37, ...), custom_call_target="tpu_custom_call" | custom-call | tf_op jit(solution)/shard_map/pallas_call | solution.py:447
  2.9 4.1 %collective-permute-start.1 = (f32[76,128]{1,0:T(8,128)S(1)}, f32[76,128]{1,0:T(8,128)S(1)}, u32[]{:S(2)}, u32[]{:S(2)}) collective-permute-start(f32[76,128]{1,0:T(8,128)S(1)} %get-tuple-element.68), channel_id=1, source_target_pairs={{0,1},{1,0},{2,3},{3,2},{4,5},{5,4},{6,7},{7,6},{8,9},{9,8},{10,11... | collective-permute-start | bytes 116744 | tf_op jit(solution)/shard_map/ppermute | solution.py:48
  7.0 1.5 %collective-permute-start.2 = (f32[38,128]{1,0:T(8,128)S(1)}, f32[38,128]{1,0:T(8,128)S(1)}, u32[]{:S(2)}, u32[]{:S(2)}) collective-permute-start(f32[38,128]{1,0:T(8,128)S(1)} %get-tuple-element.69), channel_id=1, source_target_pairs={{0,4},{1,5},{2,6},{3,7},{4,0},{5,1},{6,2},{7,3},{8,12},{9,13},{10,... | collective-permute-start | bytes 58376 | tf_op jit(solution)/shard_map/ppermute | solution.py:48
  8.6 1.5 %collective-permute-start.4 = (f32[24,128]{1,0:T(8,128)S(1)}, f32[24,128]{1,0:T(8,128)S(1)}, u32[]{:S(2)}, u32[]{:S(2)}) collective-permute-start(f32[24,128]{1,0:T(8,128)S(1)} %get-tuple-element.71), channel_id=1, source_target_pairs={{0,8},{1,9},{2,10},{3,11},{4,12},{5,13},{6,14},{7,15},{8,0},{9,1},... | collective-permute-start | bytes 36872 | tf_op jit(solution)/shard_map/ppermute | solution.py:48
  10.1 1.5 %collective-permute-done.3.rest_3_ = f32[24,128]{1,0:T(8,128)S(1)} collective-permute-done((f32[24,128]{1,0:T(8,128)S(1)}, f32[24,128]{1,0:T(8,128)S(1)}, u32[]{:S(2)}, u32[]{:S(2)}) %collective-permute-start.3) | collective-permute-done | bytes 12320 | tf_op jit(solution)/shard_map/ppermute | solution.py:48
  12.5 1.5 %collective-permute-start.6 = (f32[64,128]{1,0:T(8,128)S(1)}, f32[64,128]{1,0:T(8,128)S(1)}, u32[]{:S(2)}, u32[]{:S(2)}) collective-permute-start(f32[64,128]{1,0:T(8,128)S(1)} %get-tuple-element.80), channel_id=1, source_target_pairs={{0,1},{1,0},{2,3},{3,2},{4,5},{5,4},{6,7},{7,6},{8,9},{9,8},{10,11... | collective-permute-start | bytes 98312 | tf_op jit(solution)/shard_map/ppermute | solution.py:48
  15.0 1.2 %collective-permute-start.9 = (f32[8,128]{1,0:T(8,128)S(1)}, f32[8,128]{1,0:T(8,128)S(1)}, u32[]{:S(2)}, u32[]{:S(2)}) collective-permute-start(f32[8,128]{1,0:T(8,128)S(1)} %get-tuple-element.83), channel_id=1, source_target_pairs={{0,8},{1,9},{2,10},{3,11},{4,12},{5,13},{6,14},{7,15},{8,0},{9,1},... | collective-permute-start | bytes 12296 | tf_op jit(solution)/shard_map/ppermute | solution.py:48
  16.3 1.1 %shard_map.133 = (f32[6,32,128]{2,1,0:T(8,128)S(1)}, f32[6,8,128]{2,1,0:T(8,128)S(1)}, f32[3,128,128]{2,1,0:T(8,128)S(1)}) custom-call(f32[3,128,128]{2,1,0:T(8,128)} %bitcast.27, f32[7,32,128]{2,1,0:T(8,128)S(1)} %get-tuple-element.74.one, f32[7,8,128]{2,1,0:T(8,128)S(1)} %get-tuple-element.75.two, f32[76,128]{1,0:T(8,128)S(1)} %collective-permute-done.rest_0_, ...), custom_call_target="tpu_custom_call" | custom-call | tf_op jit(solution)/shard_map/pallas_call | solution.py:447
  19.5 1.4 %collective-permute-start.12 = (f32[64,128]{1,0:T(8,128)S(1)}, f32[64,128]{1,0:T(8,128)S(1)}, u32[]{:S(2)}, u32[]{:S(2)}) collective-permute-start(f32[64,128]{1,0:T(8,128)S(1)} %get-tuple-element.88), channel_id=1, source_target_pairs={{0,4},{1,5},{2,6},{3,7},{4,0},{5,1},{6,2},{7,3},{8,12},{9,13},{10,... | collective-permute-start | bytes 98312 | tf_op jit(solution)/shard_map/ppermute | solution.py:48
  21.2 1.1 %collective-permute-start.14 = (f32[32,128]{1,0:T(8,128)S(1)}, f32[32,128]{1,0:T(8,128)S(1)}, u32[]{:S(2)}, u32[]{:S(2)}) collective-permute-start(f32[32,128]{1,0:T(8,128)S(1)} %get-tuple-element.90), channel_id=1, source_target_pairs={{0,8},{1,9},{2,10},{3,11},{4,12},{5,13},{6,14},{7,15},{8,0},{9,1},... | collective-permute-start | bytes 49160 | tf_op jit(solution)/shard_map/ppermute | solution.py:48
  22.6 1.5 %collective-permute-done.13.rest_3_.rest_6_ = f32[32,128]{1,0:T(8,128)S(1)} collective-permute-done((f32[32,128]{1,0:T(8,128)S(1)}, f32[32,128]{1,0:T(8,128)S(1)}, u32[]{:S(2)}, u32[]{:S(2)}) %collective-permute-start.13) | collective-permute-done | bytes 16416 | tf_op jit(solution)/shard_map/ppermute | solution.py:48
  24.6 1.6 %collective-permute-start.16 = (f32[16,128]{1,0:T(8,128)S(1)}, f32[16,128]{1,0:T(8,128)S(1)}, u32[]{:S(2)}, u32[]{:S(2)}) collective-permute-start(f32[16,128]{1,0:T(8,128)S(1)} %get-tuple-element.94), channel_id=1, source_target_pairs={{0,1},{1,0},{2,3},{3,2},{4,5},{5,4},{6,7},{7,6},{8,9},{9,8},{10,11... | collective-permute-start | bytes 24584 | tf_op jit(solution)/shard_map/ppermute | solution.py:48
  26.2 0.9 %collective-permute-start.17 = (f32[32,128]{1,0:T(8,128)S(1)}, f32[32,128]{1,0:T(8,128)S(1)}, u32[]{:S(2)}, u32[]{:S(2)}) collective-permute-start(f32[32,128]{1,0:T(8,128)S(1)} %get-tuple-element.95), channel_id=1, source_target_pairs={{0,4},{1,5},{2,6},{3,7},{4,0},{5,1},{6,2},{7,3},{8,12},{9,13},{10,... | collective-permute-start | bytes 49160 | tf_op jit(solution)/shard_map/ppermute | solution.py:48
  27.3 1.3 %collective-permute-start.19 = (f32[40,128]{1,0:T(8,128)S(1)}, f32[40,128]{1,0:T(8,128)S(1)}, u32[]{:S(2)}, u32[]{:S(2)}) collective-permute-start(f32[40,128]{1,0:T(8,128)S(1)} %get-tuple-element.97), channel_id=1, source_target_pairs={{0,8},{1,9},{2,10},{3,11},{4,12},{5,13},{6,14},{7,15},{8,0},{9,1},... | collective-permute-start | bytes 61448 | tf_op jit(solution)/shard_map/ppermute | solution.py:48
  28.6 1.3 %collective-permute-done.17.rest_2_.rest_10_ = f32[32,128]{1,0:T(8,128)S(1)} collective-permute-done((f32[32,128]{1,0:T(8,128)S(1)}, f32[32,128]{1,0:T(8,128)S(1)}, u32[]{:S(2)}, u32[]{:S(2)}) %collective-permute-start.17) | collective-permute-done | bytes 16416 | tf_op jit(solution)/shard_map/ppermute | solution.py:48
  31.0 1.8 %collective-permute-start.21 = (f32[16,128]{1,0:T(8,128)S(1)}, f32[16,128]{1,0:T(8,128)S(1)}, u32[]{:S(2)}, u32[]{:S(2)}) collective-permute-start(f32[16,128]{1,0:T(8,128)S(1)} %get-tuple-element.100), channel_id=1, source_target_pairs={{0,1},{1,0},{2,3},{3,2},{4,5},{5,4},{6,7},{7,6},{8,9},{9,8},{10,11... | collective-permute-start | bytes 24584 | tf_op jit(solution)/shard_map/ppermute | solution.py:48
  32.8 1.3 %collective-permute-start.22 = (f32[24,128]{1,0:T(8,128)S(1)}, f32[24,128]{1,0:T(8,128)S(1)}, u32[]{:S(2)}, u32[]{:S(2)}) collective-permute-start(f32[24,128]{1,0:T(8,128)S(1)} %get-tuple-element.101), channel_id=1, source_target_pairs={{0,4},{1,5},{2,6},{3,7},{4,0},{5,1},{6,2},{7,3},{8,12},{9,13},{10,... | collective-permute-start | bytes 36872 | tf_op jit(solution)/shard_map/ppermute | solution.py:48
  34.3 1.2 %collective-permute-start.24 = (f32[32,128]{1,0:T(8,128)S(1)}, f32[32,128]{1,0:T(8,128)S(1)}, u32[]{:S(2)}, u32[]{:S(2)}) collective-permute-start(f32[32,128]{1,0:T(8,128)S(1)} %get-tuple-element.103), channel_id=1, source_target_pairs={{0,8},{1,9},{2,10},{3,11},{4,12},{5,13},{6,14},{7,15},{8,0},{9,1},... | collective-permute-start | bytes 49160 | tf_op jit(solution)/shard_map/ppermute | solution.py:48
  37.3 1.3 %shard_map.138 = (f32[32,8,128]{2,1,0:T(8,128)}, f32[8,128]{1,0:T(8,128)S(1)}) custom-call(f32[32,128]{1,0:T(8,128)S(1)} %get-tuple-element.98.x, f32[7,32,128]{2,1,0:T(8,128)S(1)} %get-tuple-element.74.one, f32[6,32,128]{2,1,0:T(8,128)S(1)} %get-tuple-element.77.mid_couplings.mid_own, f32[7,8,128]{2,1,0:T(8,128)S(1)} %get-tuple-element.75.two, ...), custom_call_target="tpu_custom_call" | custom-call | tf_op jit(solution)/shard_map/pallas_call | solution.py:447
  38.6 2.6 %all-to-all-start = ((f32[32,8,128]{2,1,0:T(8,128)}), f32[32,8,128]{2,1,0:T(8,128)S(1)}, u32[]{:S(2)}, u32[]{:S(2)}) async-start(f32[32,8,128]{2,1,0:T(8,128)} %get-tuple-element.104), calls=%async_computation | async-start | bytes 262144 | tf_op jit(solution)/shard_map/all_to_all | solution.py:838
  41.7 3.0 %collective-permute-start.26 = (f32[240,128]{1,0:T(8,128)S(1)}, f32[240,128]{1,0:T(8,128)S(1)}, u32[]{:S(2)}, u32[]{:S(2)}) collective-permute-start(f32[240,128]{1,0:T(8,128)S(1)} %get-tuple-element.120), channel_id=1, source_target_pairs={{0,1},{1,0},{2,3},{3,2},{4,5},{5,4},{6,7},{7,6},{8,9},{9,8},{10,11... | collective-permute-start | bytes 368648 | tf_op jit(solution)/shard_map/ppermute | solution.py:48
  44.7 1.5 %collective-permute-start.27 = (f32[72,128]{1,0:T(8,128)S(1)}, f32[72,128]{1,0:T(8,128)S(1)}, u32[]{:S(2)}, u32[]{:S(2)}) collective-permute-start(f32[72,128]{1,0:T(8,128)S(1)} %get-tuple-element.121), channel_id=1, source_target_pairs={{0,4},{1,5},{2,6},{3,7},{4,0},{5,1},{6,2},{7,3},{8,12},{9,13},{10,... | collective-permute-start | bytes 110600 | tf_op jit(solution)/shard_map/ppermute | solution.py:48
  46.7 2.1 %collective-permute-done.27.rest_2_ = f32[72,128]{1,0:T(8,128)S(1)} collective-permute-done((f32[72,128]{1,0:T(8,128)S(1)}, f32[72,128]{1,0:T(8,128)S(1)}, u32[]{:S(2)}, u32[]{:S(2)}) %collective-permute-start.27) | collective-permute-done | bytes 36896 | tf_op jit(solution)/shard_map/ppermute | solution.py:48
  49.3 2.3 %shard_map.143 = (f32[3,128,128]{2,1,0:T(8,128)}, f32[3,128,128]{2,1,0:T(8,128)}) custom-call(f32[32,8,128]{2,1,0:T(8,128)S(1)} %all-to-all-done.everyone, f32[3,128,128]{2,1,0:T(8,128)S(1)} %shard_map.139.x_windows, f32[6,64,128]{2,1,0:T(8,128)S(1)} %get-tuple-element.108.mid_around, f32[64,128]{1,0:T(8,128)S(1)} %get-tuple-element.109.mid_beside, ...), custom_call_target="tpu_custom_call" | custom-call | tf_op jit(solution)/shard_map/pallas_call | solution.py:447
  (68 shorter events, 10.4 us)
Async XLA Ops:
  2.3 9.3 %collective-permute-start = (f32[76,128]{1,0:T(8,128)S(1)}, f32[76,128]{1,0:T(8,128)S(1)}, u32[]{:S(2)}, u32[]{:S(2)}) collective-permute-start(f32[76,128]{1,0:T(8,128)S(1)} %get-tuple-element.67), channel_id=1, source_target_pairs={{0,8},{1,2},{2,1},{3,11},{4,12},{5,6},{6,5},{7,15},{8,0},{9,10},{1... | collective-permute-start | bytes 116744 | tf_op jit(solution)/shard_map/ppermute | solution.py:48
  2.9 8.8 %collective-permute-start.1 = (f32[76,128]{1,0:T(8,128)S(1)}, f32[76,128]{1,0:T(8,128)S(1)}, u32[]{:S(2)}, u32[]{:S(2)}) collective-permute-start(f32[76,128]{1,0:T(8,128)S(1)} %get-tuple-element.68), channel_id=1, source_target_pairs={{0,1},{1,0},{2,3},{3,2},{4,5},{5,4},{6,7},{7,6},{8,9},{9,8},{10,11... | collective-permute-start | bytes 116744 | tf_op jit(solution)/shard_map/ppermute | solution.py:48
  7.0 4.7 %collective-permute-start.2 = (f32[38,128]{1,0:T(8,128)S(1)}, f32[38,128]{1,0:T(8,128)S(1)}, u32[]{:S(2)}, u32[]{:S(2)}) collective-permute-start(f32[38,128]{1,0:T(8,128)S(1)} %get-tuple-element.69), channel_id=1, source_target_pairs={{0,4},{1,5},{2,6},{3,7},{4,0},{5,1},{6,2},{7,3},{8,12},{9,13},{10,... | collective-permute-start | bytes 58376 | tf_op jit(solution)/shard_map/ppermute | solution.py:48
  8.5 3.2 %collective-permute-start.3 = (f32[24,128]{1,0:T(8,128)S(1)}, f32[24,128]{1,0:T(8,128)S(1)}, u32[]{:S(2)}, u32[]{:S(2)}) collective-permute-start(f32[24,128]{1,0:T(8,128)S(1)} %get-tuple-element.70), channel_id=1, source_target_pairs={{0,24},{1,25},{2,26},{3,27},{4,28},{5,29},{6,30},{7,31},{8,16},{9,... | collective-permute-start | bytes 36872 | tf_op jit(solution)/shard_map/ppermute | solution.py:48
  12.3 5.5 %collective-permute-start.5 = (f32[64,128]{1,0:T(8,128)S(1)}, f32[64,128]{1,0:T(8,128)S(1)}, u32[]{:S(2)}, u32[]{:S(2)}) collective-permute-start(f32[64,128]{1,0:T(8,128)S(1)} %get-tuple-element.79), channel_id=1, source_target_pairs={{0,8},{1,2},{2,1},{3,11},{4,12},{5,6},{6,5},{7,15},{8,0},{9,10},{1... | collective-permute-start | bytes 98312 | tf_op jit(solution)/shard_map/ppermute | solution.py:48
  12.5 5.3 %collective-permute-start.6 = (f32[64,128]{1,0:T(8,128)S(1)}, f32[64,128]{1,0:T(8,128)S(1)}, u32[]{:S(2)}, u32[]{:S(2)}) collective-permute-start(f32[64,128]{1,0:T(8,128)S(1)} %get-tuple-element.80), channel_id=1, source_target_pairs={{0,1},{1,0},{2,3},{3,2},{4,5},{5,4},{6,7},{7,6},{8,9},{9,8},{10,11... | collective-permute-start | bytes 98312 | tf_op jit(solution)/shard_map/ppermute | solution.py:48
  14.0 3.7 %collective-permute-start.7 = (f32[32,128]{1,0:T(8,128)S(1)}, f32[32,128]{1,0:T(8,128)S(1)}, u32[]{:S(2)}, u32[]{:S(2)}) collective-permute-start(f32[32,128]{1,0:T(8,128)S(1)} %get-tuple-element.81), channel_id=1, source_target_pairs={{0,4},{1,5},{2,6},{3,7},{4,0},{5,1},{6,2},{7,3},{8,12},{9,13},{10,... | collective-permute-start | bytes 49160 | tf_op jit(solution)/shard_map/ppermute | solution.py:48
  18.5 5.7 %collective-permute-start.10 = (f32[128,128]{1,0:T(8,128)S(1)}, f32[128,128]{1,0:T(8,128)S(1)}, u32[]{:S(2)}, u32[]{:S(2)}) collective-permute-start(f32[128,128]{1,0:T(8,128)S(1)} %get-tuple-element.86), channel_id=1, source_target_pairs={{0,8},{1,2},{2,1},{3,11},{4,12},{5,6},{6,5},{7,15},{8,0},{9,10},{1... | collective-permute-start | bytes 196616 | tf_op jit(solution)/shard_map/ppermute | solution.py:48
  18.6 5.5 %collective-permute-start.11 = (f32[128,128]{1,0:T(8,128)S(1)}, f32[128,128]{1,0:T(8,128)S(1)}, u32[]{:S(2)}, u32[]{:S(2)}) collective-permute-start(f32[128,128]{1,0:T(8,128)S(1)} %get-tuple-element.87), channel_id=1, source_target_pairs={{0,1},{1,0},{2,3},{3,2},{4,5},{5,4},{6,7},{7,6},{8,9},{9,8},{10,11... | collective-permute-start | bytes 196616 | tf_op jit(solution)/shard_map/ppermute | solution.py:48
  19.5 4.6 %collective-permute-start.12 = (f32[64,128]{1,0:T(8,128)S(1)}, f32[64,128]{1,0:T(8,128)S(1)}, u32[]{:S(2)}, u32[]{:S(2)}) collective-permute-start(f32[64,128]{1,0:T(8,128)S(1)} %get-tuple-element.88), channel_id=1, source_target_pairs={{0,4},{1,5},{2,6},{3,7},{4,0},{5,1},{6,2},{7,3},{8,12},{9,13},{10,... | collective-permute-start | bytes 98312 | tf_op jit(solution)/shard_map/ppermute | solution.py:48
  20.9 3.3 %collective-permute-start.13 = (f32[32,128]{1,0:T(8,128)S(1)}, f32[32,128]{1,0:T(8,128)S(1)}, u32[]{:S(2)}, u32[]{:S(2)}) collective-permute-start(f32[32,128]{1,0:T(8,128)S(1)} %get-tuple-element.89), channel_id=1, source_target_pairs={{0,24},{1,25},{2,26},{3,27},{4,28},{5,29},{6,30},{7,31},{8,16},{9,... | collective-permute-start | bytes 49160 | tf_op jit(solution)/shard_map/ppermute | solution.py:48
  24.5 4.1 %collective-permute-start.15 = (f32[16,128]{1,0:T(8,128)S(1)}, f32[16,128]{1,0:T(8,128)S(1)}, u32[]{:S(2)}, u32[]{:S(2)}) collective-permute-start(f32[16,128]{1,0:T(8,128)S(1)} %get-tuple-element.93), channel_id=1, source_target_pairs={{0,8},{1,2},{2,1},{3,11},{4,12},{5,6},{6,5},{7,15},{8,0},{9,10},{1... | collective-permute-start | bytes 24584 | tf_op jit(solution)/shard_map/ppermute | solution.py:48
  24.6 4.0 %collective-permute-start.16 = (f32[16,128]{1,0:T(8,128)S(1)}, f32[16,128]{1,0:T(8,128)S(1)}, u32[]{:S(2)}, u32[]{:S(2)}) collective-permute-start(f32[16,128]{1,0:T(8,128)S(1)} %get-tuple-element.94), channel_id=1, source_target_pairs={{0,1},{1,0},{2,3},{3,2},{4,5},{5,4},{6,7},{7,6},{8,9},{9,8},{10,11... | collective-permute-start | bytes 24584 | tf_op jit(solution)/shard_map/ppermute | solution.py:48
  26.2 3.7 %collective-permute-start.17 = (f32[32,128]{1,0:T(8,128)S(1)}, f32[32,128]{1,0:T(8,128)S(1)}, u32[]{:S(2)}, u32[]{:S(2)}) collective-permute-start(f32[32,128]{1,0:T(8,128)S(1)} %get-tuple-element.95), channel_id=1, source_target_pairs={{0,4},{1,5},{2,6},{3,7},{4,0},{5,1},{6,2},{7,3},{8,12},{9,13},{10,... | collective-permute-start | bytes 49160 | tf_op jit(solution)/shard_map/ppermute | solution.py:48
  27.1 3.3 %collective-permute-start.18 = (f32[40,128]{1,0:T(8,128)S(1)}, f32[40,128]{1,0:T(8,128)S(1)}, u32[]{:S(2)}, u32[]{:S(2)}) collective-permute-start(f32[40,128]{1,0:T(8,128)S(1)} %get-tuple-element.96), channel_id=1, source_target_pairs={{0,24},{1,25},{2,26},{3,27},{4,28},{5,29},{6,30},{7,31},{8,16},{9,... | collective-permute-start | bytes 61448 | tf_op jit(solution)/shard_map/ppermute | solution.py:48
  27.3 3.2 %collective-permute-start.19 = (f32[40,128]{1,0:T(8,128)S(1)}, f32[40,128]{1,0:T(8,128)S(1)}, u32[]{:S(2)}, u32[]{:S(2)}) collective-permute-start(f32[40,128]{1,0:T(8,128)S(1)} %get-tuple-element.97), channel_id=1, source_target_pairs={{0,8},{1,9},{2,10},{3,11},{4,12},{5,13},{6,14},{7,15},{8,0},{9,1},... | collective-permute-start | bytes 61448 | tf_op jit(solution)/shard_map/ppermute | solution.py:48
  30.9 4.7 %collective-permute-start.20 = (f32[16,128]{1,0:T(8,128)S(1)}, f32[16,128]{1,0:T(8,128)S(1)}, u32[]{:S(2)}, u32[]{:S(2)}) collective-permute-start(f32[16,128]{1,0:T(8,128)S(1)} %get-tuple-element.99), channel_id=1, source_target_pairs={{0,8},{1,2},{2,1},{3,11},{4,12},{5,6},{6,5},{7,15},{8,0},{9,10},{1... | collective-permute-start | bytes 24584 | tf_op jit(solution)/shard_map/ppermute | solution.py:48
  31.0 4.7 %collective-permute-start.21 = (f32[16,128]{1,0:T(8,128)S(1)}, f32[16,128]{1,0:T(8,128)S(1)}, u32[]{:S(2)}, u32[]{:S(2)}) collective-permute-start(f32[16,128]{1,0:T(8,128)S(1)} %get-tuple-element.100), channel_id=1, source_target_pairs={{0,1},{1,0},{2,3},{3,2},{4,5},{5,4},{6,7},{7,6},{8,9},{9,8},{10,11... | collective-permute-start | bytes 24584 | tf_op jit(solution)/shard_map/ppermute | solution.py:48
  32.8 3.7 %collective-permute-start.22 = (f32[24,128]{1,0:T(8,128)S(1)}, f32[24,128]{1,0:T(8,128)S(1)}, u32[]{:S(2)}, u32[]{:S(2)}) collective-permute-start(f32[24,128]{1,0:T(8,128)S(1)} %get-tuple-element.101), channel_id=1, source_target_pairs={{0,4},{1,5},{2,6},{3,7},{4,0},{5,1},{6,2},{7,3},{8,12},{9,13},{10,... | collective-permute-start | bytes 36872 | tf_op jit(solution)/shard_map/ppermute | solution.py:48
  34.1 3.2 %collective-permute-start.23 = (f32[32,128]{1,0:T(8,128)S(1)}, f32[32,128]{1,0:T(8,128)S(1)}, u32[]{:S(2)}, u32[]{:S(2)}) collective-permute-start(f32[32,128]{1,0:T(8,128)S(1)} %get-tuple-element.102), channel_id=1, source_target_pairs={{0,24},{1,25},{2,26},{3,27},{4,28},{5,29},{6,30},{7,31},{8,16},{9,... | collective-permute-start | bytes 49160 | tf_op jit(solution)/shard_map/ppermute | solution.py:48
  38.6 10.7 %all-to-all-start = ((f32[32,8,128]{2,1,0:T(8,128)}), f32[32,8,128]{2,1,0:T(8,128)S(1)}, u32[]{:S(2)}, u32[]{:S(2)}) async-start(f32[32,8,128]{2,1,0:T(8,128)} %get-tuple-element.104), calls=%async_computation | async-start | bytes 262144 | tf_op jit(solution)/shard_map/all_to_all | solution.py:838
  41.4 7.4 %collective-permute-start.25 = (f32[240,128]{1,0:T(8,128)S(1)}, f32[240,128]{1,0:T(8,128)S(1)}, u32[]{:S(2)}, u32[]{:S(2)}) collective-permute-start(f32[240,128]{1,0:T(8,128)S(1)} %get-tuple-element.119), channel_id=1, source_target_pairs={{0,8},{1,2},{2,1},{3,11},{4,12},{5,6},{6,5},{7,15},{8,0},{9,10},{1... | collective-permute-start | bytes 368648 | tf_op jit(solution)/shard_map/ppermute | solution.py:48
  41.7 7.5 %collective-permute-start.26 = (f32[240,128]{1,0:T(8,128)S(1)}, f32[240,128]{1,0:T(8,128)S(1)}, u32[]{:S(2)}, u32[]{:S(2)}) collective-permute-start(f32[240,128]{1,0:T(8,128)S(1)} %get-tuple-element.120), channel_id=1, source_target_pairs={{0,1},{1,0},{2,3},{3,2},{4,5},{5,4},{6,7},{7,6},{8,9},{9,8},{10,11... | collective-permute-start | bytes 368648 | tf_op jit(solution)/shard_map/ppermute | solution.py:48
  44.7 4.1 %collective-permute-start.27 = (f32[72,128]{1,0:T(8,128)S(1)}, f32[72,128]{1,0:T(8,128)S(1)}, u32[]{:S(2)}, u32[]{:S(2)}) collective-permute-start(f32[72,128]{1,0:T(8,128)S(1)} %get-tuple-element.121), channel_id=1, source_target_pairs={{0,4},{1,5},{2,6},{3,7},{4,0},{5,1},{6,2},{7,3},{8,12},{9,13},{10,... | collective-permute-start | bytes 110600 | tf_op jit(solution)/shard_map/ppermute | solution.py:48
  (13 other events, 54.9 us)
